TPU v7x, 256 devices: a whole 4x4x8 slice. The times are simulated.
256 devices in a mesh: section: 4 (over y_lo, core), fsdp: 64 (over x, z, y_hi).
Axes of the slice: x: 4, y: 4 (y_hi: 2, y_lo: 2; y = y_hi * 2 + y_lo), z: 8, core: 2. Of those that a mesh axis runs over, the one named last changes fastest.
Arguments:
- checkpoints: bfloat16 [4, 8192, 640], P('section', 'fsdp'), may hold values from -41 to 41
- cotangent: bfloat16 [8192, 640], P('fsdp'), may hold values from -6 to 6
- gains: float32 [4, 640], P('section'), may hold values from 0.25 to 1.75
- w_in: bfloat16 [4, 640, 2560], P('section', None, 'fsdp'), may hold values from -0.25 to 0.25
- w_out: bfloat16 [4, 2560, 640], P('section', 'fsdp'), may hold values from -0.125 to 0.125
- time_proj: bfloat16 [4, 256, 2560], P('section', None, 'fsdp'), may hold values from -0.375 to 0.375
- class_table: bfloat16 [4, 64, 2560], P('section', None, 'fsdp'), may hold values from -5 to 5
- timestep: int32 [8], replicated, may hold values from 0 to 999
- label: int32 [8], replicated, may hold values from 0 to 63
Outputs:
- section_input_grads: bfloat16 [4, 8192, 640], P('section', 'fsdp')
- w_in_grad: float32 [4, 640, 2560], P('section', None, 'fsdp')
- w_out_grad: float32 [4, 2560, 640], P('section', 'fsdp')
- gain_grad: float32 [4, 640], P('section')
All inputs are finite; a program needn't handle non-finite values.
Results may differ from a plain program's by a relative error of at most 0.013.
Values may be sent and summed in bfloat16 or wider, within the bound.
No kernel may reach another device: no remote copies, remote signals or barrier semaphores. Data moves between devices by JAX's collectives and lax.ppermute only.
A program may use at most 128 MiB of HBM per device.

v0:
```python
import math

import jax
import jax.numpy as jnp
from jax import lax
from jax.sharding import PartitionSpec as P

PIX = 1024


def passed_along(value, axis, by):
    count = lax.axis_size(axis)
    pairs = [(i, i + by) for i in range(count) if 0 <= i + by < count]
    return lax.ppermute(value, axis, pairs)


def time_features(timestep, freq_width):
    half_width = freq_width // 2
    freq_rates = jnp.exp(
        -math.log(10000.0) * jnp.arange(half_width, dtype=jnp.float32) / half_width
    )
    angles = timestep.astype(jnp.float32)[:, None] * freq_rates[None, :]
    return jnp.concatenate([jnp.cos(angles), jnp.sin(angles)], axis=1).astype(jnp.bfloat16)


def contract_last(left_side, right_side):
    return lax.dot_general(
        left_side, right_side, (((1,), (1,)), ((), ())), preferred_element_type=jnp.float32
    )


def contract_first(left_side, right_side):
    return lax.dot_general(
        left_side, right_side, (((0,), (0,)), ((), ())), preferred_element_type=jnp.float32
    )


def on_device(checkpoints, cotangent, gains, w_in, w_out, time_proj, class_table, timestep, label):
    row_count = checkpoints.shape[1]
    chan_width = checkpoints.shape[2]
    freq_width = time_proj.shape[1]
    section_count = lax.axis_size("section")
    fsdp_count = lax.axis_size("fsdp")
    section_index = lax.axis_index("section")
    start_row = lax.axis_index("fsdp") * row_count
    grad_scale = float(row_count * fsdp_count) ** (-0.5)
    inputs = checkpoints[0].astype(jnp.float32)
    gain_row = gains[0]
    mean_sq = jnp.mean(inputs * inputs, axis=1, keepdims=True)
    rscale = lax.rsqrt(mean_sq + 1e-06)
    normed = (inputs * rscale * gain_row).astype(jnp.bfloat16)
    time_feats = time_features(timestep, freq_width)
    class_picks = (
        label[:, None] == jnp.arange(class_table.shape[1], dtype=jnp.int32)[None, :]
    ).astype(jnp.bfloat16)
    row_sample = (start_row + jnp.arange(row_count, dtype=jnp.int32)) // PIX
    sample_map = (
        row_sample[:, None] == jnp.arange(timestep.shape[0], dtype=jnp.int32)[None, :]
    ).astype(jnp.float32)
    stacked = jnp.concatenate([w_in[0], time_proj[0], class_table[0]], axis=0)
    gathered = lax.all_gather(stacked, "fsdp", axis=1, tiled=True)
    w_in_full = gathered[:chan_width]
    weight_part = gathered[:chan_width]
    cond_small = jnp.dot(
        time_feats,
        gathered[chan_width : chan_width + freq_width],
        preferred_element_type=jnp.float32,
    ) + jnp.dot(
        class_picks, gathered[chan_width + freq_width :], preferred_element_type=jnp.float32
    )
    cond_rows = jnp.dot(sample_map, cond_small, precision=lax.Precision.HIGHEST)
    pre = jnp.dot(normed, weight_part, preferred_element_type=jnp.float32) + cond_rows
    w_out_full = lax.all_gather(w_out[0], "fsdp", axis=0, tiled=True)
    sigmoid_pre = jax.nn.sigmoid(pre)
    hidden = (pre * sigmoid_pre).astype(jnp.bfloat16)
    slope_pre = sigmoid_pre * (1.0 + pre * (1.0 - sigmoid_pre))
    last_section = section_count - 1
    grad_carry = jnp.where(section_index == last_section, cotangent, jnp.zeros_like(cotangent))
    kept_grad = jnp.zeros_like(cotangent)
    kept_carry = jnp.zeros_like(cotangent)
    kept_pre_grad = jnp.zeros(hidden.shape, jnp.bfloat16)
    kept_gain = jnp.zeros((chan_width,), jnp.float32)
    for turn_index in range(section_count):
        hidden_grad = contract_last(grad_carry, w_out_full)
        pre_grad = (hidden_grad * slope_pre).astype(jnp.bfloat16)
        normed_grad = contract_last(pre_grad, w_in_full)
        scaled_grad = normed_grad * gain_row
        inner_mean = jnp.mean(scaled_grad * inputs, axis=1, keepdims=True)
        grad_in = (
            grad_carry.astype(jnp.float32)
            + rscale * scaled_grad
            - inputs * (rscale * rscale * rscale) * inner_mean
        ).astype(jnp.bfloat16)
        is_active = section_index == last_section - turn_index
        kept_grad = jnp.where(is_active, grad_in, kept_grad)
        kept_carry = jnp.where(is_active, grad_carry, kept_carry)
        kept_pre_grad = jnp.where(is_active, pre_grad, kept_pre_grad)
        kept_gain = jnp.where(is_active, jnp.sum(normed_grad * inputs * rscale, axis=0), kept_gain)
        if turn_index < section_count - 1:
            grad_carry = passed_along(grad_in, "section", -1)
    w_in_term = contract_first(normed, kept_pre_grad) * grad_scale
    w_out_term = contract_first(hidden, kept_carry) * grad_scale
    w_in_part, w_out_part = (
        lax.psum_scatter(w_in_term, "fsdp", scatter_dimension=1, tiled=True),
        lax.psum_scatter(w_out_term, "fsdp", scatter_dimension=0, tiled=True),
    )
    gain_part = lax.psum(kept_gain * grad_scale, "fsdp")
    return (kept_grad[None], w_in_part[None], w_out_part[None], gain_part[None])


def solution(mesh):
    in_specs = (
        P("section", "fsdp", None),
        P("fsdp", None),
        P("section", None),
        P("section", None, "fsdp"),
        P("section", "fsdp", None),
        P("section", None, "fsdp"),
        P("section", None, "fsdp"),
        P(),
        P(),
    )
    out_specs = (
        P("section", "fsdp", None),
        P("section", None, "fsdp"),
        P("section", "fsdp", None),
        P("section", None),
    )
    return jax.shard_map(
        on_device, mesh=mesh, in_specs=in_specs, out_specs=out_specs, check_vma=False
    )
```

profile of v0, /device:TPU:8, one launch (start us, length us, event | category | flops | bytes accessed | tf_op | source)
XLA Modules:
  0.0 1056.1 jit_solution(16928092742461856931)
XLA Ops:
  7.2 1.5 pad_maximum_fusion
  8.8 0.7 all-gather.6.cloned.1.call-update
  10.2 0.7 reduce
  10.9 1.0 fusion.41
  12.1 134.2 %all-gather.4.cloned.1.call-done = bf16[960,2560]{0,1:T(8,128)(2,1)} async-done(((bf16[960,40]{0,1:T(8,128)(2,1)}), bf16[960,2560]{0,1:T(8,128)(2,1)}) %all-gather.4.cloned.1.call-update) | async-done | bytes 4915216 | tf_op jit(solution)/shard_map/all_gather | solution.py:61
  146.3 1.7 fusion.17
  148.1 1.4 convolution_add_fusion.1
  149.5 0.7 fusion.69
  150.3 3.2 convolution_add_fusion
  153.4 116.1 %all-gather.6.cloned.1.call-done = bf16[1,2560,640]{2,1,0:T(8,128)(2,1)} async-done(((bf16[1,40,640]{2,1,0:T(8,128)(2,1)}), bf16[1,2560,640]{2,1,0:T(8,128)(2,1)}) %all-gather.6.cloned.1.call-update) | async-done | bytes 3276816 | tf_op jit(solution)/shard_map/all_gather | solution.py:73
  269.5 3.1 fusion
  272.6 2.9 fusion.55
  275.8 2.2 collective-permute-start
  277.9 2.8 collective-permute-done
  280.8 1.3 fusion.1
  282.1 0.8 fusion.53
  283.1 3.8 collective-permute-start.1
  287.0 2.8 collective-permute-done.1
  289.8 1.2 fusion.2
  291.0 0.9 fusion.51
  292.1 3.8 collective-permute-start.2
  295.9 2.8 collective-permute-done.2
  298.7 4.8 convolution_multiply_fusion
  303.6 3.3 fusion.3
  306.9 0.8 copy-done.3
  307.8 3.8 convolution_multiply_fusion.1
  311.6 1.1 copy-done.4
  312.6 2.8 fusion.49
  315.5 181.8 %psum.7 = f32[1,640]{1,0:T(1,128)} all-reduce(f32[1,640]{1,0:T(1,128)S(1)} %broadcast_in_dim.34), channel_id=1, replica_groups=mesh['section'=4,'fsdp'=64] {'fsdp'}, use_global_device_ids=true, to_apply=%region_11.12 | all-reduce | flops 640 | bytes 5120 | tf_op jit(solution)/shard_map/psum | solution.py:107
  497.3 1.9 fusion.58
  499.2 178.7 %reduce-scatter.11.cloned.1.call-done = f32[40,640]{1,0:T(8,128)} async-done(((f32[2560,640]{1,0:T(8,128)}), f32[40,640]{1,0:T(8,128)}) %reduce-scatter.11.cloned.1.call-update) | async-done | bytes 102416
  677.9 371.7 %reduce-scatter.9.cloned.1.call-done = f32[640,40]{0,1:T(8,128)} async-done(((f32[640,2560]{0,1:T(8,128)}), f32[640,40]{0,1:T(8,128)}) %reduce-scatter.9.cloned.1.call-update) | async-done | bytes 102416
  (44 shorter events, 1.7 us)
Async XLA Ops:
  7.2 140.9 %copy-start.8 = (s32[8]{0:T(128)S(1)}, s32[8]{0:T(128)}, u32[]{:S(2)}) copy-start(s32[8]{0:T(128)} %param.17) | copy-start | bytes 100
  7.2 139.1 %all-gather.4.cloned.1.call-start = ((), (), s32[]{:S(2)}) async-start(), calls=%async_computation.2 | async-start | bytes 5324800 | tf_op jit(solution)/shard_map/all_gather | solution.py:61
  8.7 260.8 %all-gather.6.cloned.1.call-start = ((), (), s32[]{:S(2)}) async-start(), calls=%async_computation.3 | async-start | bytes 3328000 | tf_op jit(solution)/shard_map/all_gather | solution.py:73
  9.5 668.4 %reduce-scatter.11.cloned.1.call-start = ((), (), s32[]{:S(2)}) async-start(), calls=%async_computation.5 | async-start | bytes 6656000
  148.1 2.2 copy-start
  150.3 119.2 %copy-start.5 = (bf16[128,640]{1,0:T(8,128)(2,1)S(1)}, bf16[128,640]{1,0:T(8,128)(2,1)}, u32[]{:S(2)}) copy-start(bf16[128,640]{1,0:T(8,128)(2,1)} %param.10) | copy-start | bytes 491524
  272.6 8.1 copy-start.9
  275.5 6.5 slice-start
  275.7 6.3 slice-start.1
  275.8 5.0 collective-permute-start
  280.8 2.2 copy-start.6
  283.1 6.7 collective-permute-start.1
  289.8 2.1 copy-start.7
  291.0 0.9 copy-start.1
  292.1 6.6 collective-permute-start.2
  303.5 746.0 %reduce-scatter.9.cloned.1.call-start = ((), (), s32[]{:S(2)}) async-start(), calls=%async_computation.4 | async-start | bytes 6656000
  303.6 4.2 copy-start.2
  306.9 0.9 copy-start.3
  311.6 1.1 copy-start.4
Sparse Core Ops, SparseCore 0:
  12.1 134.1 all-gather.3
  149.8 119.6 all-gather.5
  303.7 374.1 reduce-scatter.10
  681.0 368.4 reduce-scatter.8
where the time goes:
time: 1060 us
  waiting for transfers between devices  810 us (76%)
  blocking collectives  182 us (17%)
  matrix products  32 us (3%)
  between operations  14 us (1%)
    unnamed x6, waiting for transfers between devices  551 us
    psum x1, blocking collectives, on_device(): gain_part = lax.psum(kept_gain * grad_scale, 'fsdp')  182 us
    all_gather x1, waiting for transfers between devices, on_device(): gathered = lax.all_gather(stacked, 'fsdp', axis=1, tiled=True)  134 us
    all_gather x1, waiting for transfers between devices, on_device(): w_out_full = lax.all_gather(w_out[0], 'fsdp', axis=0, tiled=True)  116 us
  transfers between devices with their start and end apart: 7, of which 7 were waited for; matrix products, arithmetic and copies ran while one was open for 2% of the time, Pallas kernels for 0%

commit v1 on v0

v1 whole, which is shorter than its diff:
```python
import math

import jax
import jax.numpy as jnp
from jax import lax
from jax.sharding import Mesh, PartitionSpec as P

SAMPLES = 8
COLUMN = ("yl", "core", "z", "yh")
PLANE = ("x", "yl", "yh")
PEERS = 16
ALL = ("yl", "core", "x", "z", "yh")


def home_to_work(flip):
    pairs = []
    for i in range(64):
        sec, z2, z10, yh = i >> 4, (i >> 3) & 1, (i >> 1) & 3, i & 1
        pairs.append((i, (z10 << 4) | ((z2 ^ flip) << 3) | (sec << 1) | yh))
    return pairs


def work_to_home(flip):
    return [(j, i) for i, j in home_to_work(flip)]


def next_section():
    pairs = []
    for z in range(8):
        if z % 4:
            pairs.append((z, z - 1))
    return pairs


def across_cores(value):
    return lax.ppermute(value, "core", [(0, 1), (1, 0)])


def time_features(timestep, freq_width):
    half_width = freq_width // 2
    freq_rates = jnp.exp(
        -math.log(10000.0) * jnp.arange(half_width, dtype=jnp.float32) / half_width
    )
    angles = timestep.astype(jnp.float32)[:, None] * freq_rates[None, :]
    return jnp.concatenate([jnp.cos(angles), jnp.sin(angles)], axis=1).astype(jnp.bfloat16)


def contract_last(left_side, right_side):
    return lax.dot_general(
        left_side, right_side, (((1,), (1,)), ((), ())), preferred_element_type=jnp.float32
    )


def contract_first(left_side, right_side):
    return lax.dot_general(
        left_side, right_side, (((0,), (0,)), ((), ())), preferred_element_type=jnp.float32
    )


def matmul(left_side, right_side):
    return jnp.dot(left_side, right_side, preferred_element_type=jnp.float32)


def two_parts(value):
    high = lax.reduce_precision(value, 8, 7)
    return high.astype(jnp.bfloat16), (value - high).astype(jnp.bfloat16)


def gathered(chunk):
    copies = jnp.broadcast_to(chunk[None], (PEERS,) + chunk.shape)
    full = lax.all_to_all(copies, PLANE, 0, 0, tiled=True)
    return full.reshape(PEERS * chunk.shape[0], chunk.shape[1])


def on_device(checkpoints, cotangent, gains, w_in, w_out, time_proj, class_table, timestep, label):
    row_count, chan = checkpoints.shape[1:]
    own = w_in.shape[2]
    grad_scale = float(row_count * 64) ** (-0.5)
    section = lax.axis_index("z") % 4
    sample = 2 * lax.axis_index("x") + lax.axis_index("z") // 4

    time_feats = time_features(timestep, time_proj.shape[1])
    picks = (
        label[:, None] == jnp.arange(class_table.shape[1], dtype=jnp.int32)[None, :]
    ).astype(jnp.bfloat16)
    cond = lax.dot_general(
        time_proj[0], time_feats, (((0,), (1,)), ((), ())), preferred_element_type=jnp.float32
    ) + lax.dot_general(
        class_table[0], picks, (((0,), (1,)), ((), ())), preferred_element_type=jnp.float32
    )
    cond_high, cond_low = two_parts(cond)
    w_in_rows = jnp.concatenate(
        [
            w_in[0].T,
            cond_high,
            cond_low,
            jnp.zeros((own, 128 - 2 * SAMPLES), jnp.bfloat16),
        ],
        axis=1,
    )

    w_in_pair = jnp.concatenate(
        [lax.ppermute(w_in_rows, COLUMN, home_to_work(flip)) for flip in (0, 1)], axis=0
    )
    w_out_pair = jnp.concatenate(
        [lax.ppermute(w_out[0], COLUMN, home_to_work(flip)) for flip in (0, 1)], axis=0
    )
    x_rows = lax.ppermute(checkpoints[0], COLUMN, home_to_work(0))
    cot_rows = lax.ppermute(cotangent, COLUMN, home_to_work(0))
    gain_row = lax.ppermute(gains, COLUMN, home_to_work(0))

    w_in_near = gathered(w_in_pair)
    w_in_far = across_cores(w_in_near)
    w_out_near = gathered(w_out_pair)
    w_out_far = across_cores(w_out_near)

    inputs = x_rows.astype(jnp.float32)
    rscale = lax.rsqrt(jnp.mean(inputs * inputs, axis=1, keepdims=True) + 1e-06)
    normed = (inputs * rscale * gain_row).astype(jnp.bfloat16)
    lane = jnp.arange(128, dtype=jnp.int32)
    pick = ((lane == sample) | (lane == sample + SAMPLES)).astype(jnp.bfloat16)
    normed_wide = jnp.concatenate(
        [normed, jnp.broadcast_to(pick[None], (row_count, 128))], axis=1
    )

    def activation(weight):
        pre = contract_last(normed_wide, weight)
        sig = jax.nn.sigmoid(pre)
        return (pre * sig).astype(jnp.bfloat16), sig * (1.0 + pre * (1.0 - sig))

    hidden_near, slope_near = activation(w_in_near)
    hidden_far, slope_far = activation(w_in_far)

    def block_backward(grad):
        pg_near = (contract_last(grad, w_out_near) * slope_near).astype(jnp.bfloat16)
        pg_far = (contract_last(grad, w_out_far) * slope_far).astype(jnp.bfloat16)
        normed_grad = matmul(pg_near, w_in_near[:, :chan]) + matmul(pg_far, w_in_far[:, :chan])
        scaled = normed_grad * gain_row
        inner = jnp.mean(scaled * inputs, axis=1, keepdims=True)
        grad_in = (
            grad.astype(jnp.float32)
            + rscale * scaled
            - inputs * (rscale * rscale * rscale) * inner
        ).astype(jnp.bfloat16)
        return grad_in, normed_grad, pg_near, pg_far

    grad = jnp.where(section == 3, cot_rows, jnp.zeros_like(cot_rows))
    kept = grad
    for _ in range(3):
        grad = lax.ppermute(block_backward(grad)[0], "z", next_section())
        kept = kept + grad
    grad_in, normed_grad, pg_near, pg_far = block_backward(kept)

    grad_home = lax.ppermute(grad_in, COLUMN, work_to_home(0))
    gain_part = jnp.sum(normed_grad * inputs * rscale, axis=0, keepdims=True)
    gain_chip = gain_part + across_cores(gain_part)

    def chip_sum(left_near, left_far, right):
        far = contract_first(left_far, right).astype(jnp.bfloat16)
        near = contract_first(left_near, right)
        return near + across_cores(far).astype(jnp.float32)

    w_out_chip = chip_sum(hidden_near, hidden_far, kept).astype(jnp.bfloat16)
    w_in_chip = chip_sum(pg_near, pg_far, normed).astype(jnp.bfloat16)

    def plane_sum(chunks):
        parts = lax.all_to_all(chunks, PLANE, 0, 0, tiled=True)
        return jnp.sum(parts.astype(jnp.float32), axis=0)

    def sum_home(total):
        return sum(
            lax.ppermute(total[flip], COLUMN, work_to_home(flip)).astype(jnp.float32)
            for flip in (0, 1)
        )

    w_out_total = plane_sum(w_out_chip.reshape(PEERS, 2 * own, chan))
    gain_rows = jnp.concatenate(
        two_parts(gain_chip) + (jnp.zeros((6, chan), jnp.bfloat16),), axis=0
    )
    w_in_total = plane_sum(
        jnp.concatenate(
            [
                w_in_chip.reshape(PEERS, 2 * own, chan),
                jnp.broadcast_to(gain_rows[None], (PEERS, 8, chan)),
            ],
            axis=1,
        )
    )
    w_out_home = sum_home(w_out_total.reshape(2, own, chan).astype(jnp.bfloat16))
    gain_plane = w_in_total[2 * own : 2 * own + 1] + w_in_total[2 * own + 1 : 2 * own + 2]
    gain_rows_2 = jnp.concatenate(
        two_parts(gain_plane) + (jnp.zeros((6, chan), jnp.bfloat16),), axis=0
    )
    w_in_sum = w_in_total[: 2 * own].reshape(2, own, chan).astype(jnp.bfloat16)
    w_in_home = sum_home(
        jnp.concatenate([w_in_sum, jnp.broadcast_to(gain_rows_2[None], (2, 8, chan))], axis=1)
    )
    gain_home = (w_in_home[own : own + 1] + w_in_home[own + 1 : own + 2]) * grad_scale
    return (
        grad_home[None],
        (w_in_home[:own].T * grad_scale)[None],
        (w_out_home * grad_scale)[None],
        gain_home,
    )


def solution(mesh):
    fine = Mesh(mesh.devices.reshape(2, 2, 4, 8, 2), ALL)
    section, fsdp = ("yl", "core"), ("x", "z", "yh")
    in_specs = (
        P(section, fsdp, None),
        P(fsdp, None),
        P(section, None),
        P(section, None, fsdp),
        P(section, fsdp, None),
        P(section, None, fsdp),
        P(section, None, fsdp),
        P(),
        P(),
    )
    out_specs = (
        P(section, fsdp, None),
        P(section, None, fsdp),
        P(section, fsdp, None),
        P(section, None),
    )
    return jax.shard_map(
        on_device, mesh=fine, in_specs=in_specs, out_specs=out_specs, check_vma=False
    )
```

time: 1060 us -> 230 us (0.22)
  the two profiles are of different devices: /device:TPU:8 before, /device:TPU:9 now
where the time goes in v1:
time: 230 us; the launch traced here: 228 us
  waiting for transfers between devices  89.7 us (39%)
  starting transfers between devices  82.6 us (36%)
  matrix products  38.9 us (17%)
  other arithmetic  11.1 us (5%)
  local copies, waits for them, and re-layouts  4.34 us (2%)
    all_to_all x2, waiting for transfers between devices, gathered(): full = lax.all_to_all(copies, PLANE, 0, 0, tiled=True)  26.2 us
    dot_general x8, matrix products, matmul(): return jnp.dot(left_side, right_side, preferred_element_type=jnp.float32)  23.3 us
    all_to_all x2, waiting for transfers between devices, plane_sum(): parts = lax.all_to_all(chunks, PLANE, 0, 0, tiled=True)  21.2 us
    ppermute x3, waiting for transfers between devices, on_device(): grad = lax.ppermute(block_backward(grad)[0], 'z', next_section())  21.1 us
    ppermute x4, starting transfers between devices, sum_home(): lax.ppermute(total[flip], COLUMN, work_to_home(flip)).astype(jnp.float32)  13.2 us
    ppermute x5, starting transfers between devices, across_cores(): return lax.ppermute(value, 'core', [(0, 1), (1, 0)])  12.3 us
    all_to_all x2, starting transfers between devices, gathered(): full = lax.all_to_all(copies, PLANE, 0, 0, tiled=True)  11.8 us
    ppermute x2, starting transfers between devices, on_device(): lax.ppermute(w_in_rows, COLUMN, home_to_work(flip))  10.3 us
  transfers between devices with their start and end apart: 24, of which 14 were waited for; matrix products, arithmetic and copies ran while one was open for 11% of the time, Pallas kernels for 0%

profile of v1, /device:TPU:9, one launch (start us, length us, event | category | flops | bytes accessed | tf_op | source)
XLA Modules:
  0.0 227.7 jit_solution(14658790456139804790)
XLA Ops:
  3.6 6.1 %collective-permute-start.6 = (bf16[40,768]{1,0:T(8,128)(2,1)S(1)}, bf16[40,768]{1,0:T(8,128)(2,1)S(1)}, u32[]{:S(2)}, u32[]{:S(2)}) collective-permute-start(bf16[40,768]{1,0:T(8,128)(2,1)S(1)} %maximum_maximum_fusion), channel_id=1, source_target_pairs={{0,8},{1,9},{2,72},{3,73},{4,136},{5,137},{6,200},{7,201},{8,0},{9... | collective-permute-start | bytes 184328 | tf_op jit(solution)/shard_map/ppermute | solution.py:103
  9.7 4.2 %collective-permute-start.5 = (bf16[40,768]{1,0:T(8,128)(2,1)S(1)}, bf16[40,768]{1,0:T(8,128)(2,1)S(1)}, u32[]{:S(2)}, u32[]{:S(2)}) collective-permute-start(bf16[40,768]{1,0:T(8,128)(2,1)S(1)} %maximum_maximum_fusion), channel_id=1, source_target_pairs={{0,0},{1,1},{2,64},{3,65},{4,128},{5,129},{6,192},{7,193},{8,8},{9... | collective-permute-start | bytes 184328 | tf_op jit(solution)/shard_map/ppermute | solution.py:103
  14.2 3.7 %collective-permute-done.5 = bf16[40,768]{1,0:T(8,128)(2,1)S(1)} collective-permute-done((bf16[40,768]{1,0:T(8,128)(2,1)S(1)}, bf16[40,768]{1,0:T(8,128)(2,1)S(1)}, u32[]{:S(2)}, u32[]{:S(2)}) %collective-permute-start.5) | collective-permute-done | bytes 61472 | tf_op jit(solution)/shard_map/ppermute | solution.py:103
  19.3 7.1 %all-to-all-start.1 = ((bf16[16,80,768]{2,1,0:T(8,128)(2,1)}), bf16[16,80,768]{2,1,0:T(8,128)(2,1)S(1)}, u32[]{:S(2)}, u32[]{:S(2)}) async-start(bf16[16,80,768]{2,1,0:T(8,128)(2,1)} %broadcast_in_dim.26), calls=%async_computation.1 | async-start | bytes 3932160 | tf_op jit(solution)/shard_map/all_to_all | solution.py:71
  28.3 3.3 %collective-permute-start.2 = (bf16[40,640]{1,0:T(8,128)(2,1)S(1)}, bf16[40,640]{1,0:T(8,128)(2,1)S(1)}, u32[]{:S(2)}, u32[]{:S(2)}) collective-permute-start(bf16[40,640]{1,0:T(8,128)(2,1)S(1)} %bitcast.68), channel_id=1, source_target_pairs={{0,0},{1,1},{2,64},{3,65},{4,128},{5,129},{6,192},{7,193},{8,8},{9... | collective-permute-start | bytes 153608 | tf_op jit(solution)/shard_map/ppermute | solution.py:106
  32.8 4.9 %collective-permute-done.2 = bf16[40,640]{1,0:T(8,128)(2,1)S(1)} collective-permute-done((bf16[40,640]{1,0:T(8,128)(2,1)S(1)}, bf16[40,640]{1,0:T(8,128)(2,1)S(1)}, u32[]{:S(2)}, u32[]{:S(2)}) %collective-permute-start.2) | collective-permute-done | bytes 51232 | tf_op jit(solution)/shard_map/ppermute | solution.py:106
  37.7 17.9 %all-to-all-done.1 = bf16[16,80,768]{2,1,0:T(8,128)(2,1)S(1)} async-done(((bf16[16,80,768]{2,1,0:T(8,128)(2,1)}), bf16[16,80,768]{2,1,0:T(8,128)(2,1)S(1)}, u32[]{:S(2)}, u32[]{:S(2)}) %all-to-all-start.1) | async-done | bytes 1966112 | tf_op jit(solution)/shard_map/all_to_all | solution.py:71
  56.9 4.7 %all-to-all-start = ((bf16[16,80,640]{2,1,0:T(8,128)(2,1)}), bf16[16,80,640]{2,1,0:T(8,128)(2,1)}, u32[]{:S(2)}, u32[]{:S(2)}) async-start(bf16[16,80,640]{2,1,0:T(8,128)(2,1)} %broadcast_in_dim.23), calls=%async_computation | async-start | bytes 3276800 | tf_op jit(solution)/shard_map/all_to_all | solution.py:71
  61.6 3.5 %collective-permute-start.8 = (bf16[1280,768]{1,0:T(8,128)(2,1)S(1)}, bf16[1280,768]{1,0:T(8,128)(2,1)}, u32[]{:S(2)}, u32[]{:S(2)}) collective-permute-start(bf16[1280,768]{1,0:T(8,128)(2,1)S(1)} %bitcast.55), channel_id=1, source_target_pairs={{0,64},{64,0},{1,65},{65,1},{2,66},{66,2},{3,67},{67,3},{4,68},{68... | collective-permute-start | bytes 5898248 | tf_op jit(solution)/shard_map/ppermute | solution.py:36
  67.7 5.6 %collective-permute-start.4 = (f32[1,640]{1,0:T(1,128)S(1)}, f32[1,640]{1,0:T(1,128)S(1)}, u32[]{:S(2)}, u32[]{:S(2)}) collective-permute-start(f32[1,640]{1,0:T(1,128)S(1)} %copy-done.7), channel_id=1, source_target_pairs={{0,0},{1,1},{2,64},{3,65},{4,128},{5,129},{6,192},{7,193},{8,8},{9... | collective-permute-start | bytes 7688 | tf_op jit(solution)/shard_map/ppermute | solution.py:110
  76.0 8.3 %all-to-all-done = bf16[16,80,640]{2,1,0:T(8,128)(2,1)} async-done(((bf16[16,80,640]{2,1,0:T(8,128)(2,1)}), bf16[16,80,640]{2,1,0:T(8,128)(2,1)}, u32[]{:S(2)}, u32[]{:S(2)}) %all-to-all-start) | async-done | bytes 1638432 | tf_op jit(solution)/shard_map/all_to_all | solution.py:71
  84.2 5.3 %collective-permute-start.7 = (bf16[1280,640]{1,0:T(8,128)(2,1)}, bf16[1280,640]{1,0:T(8,128)(2,1)}, u32[]{:S(2)}, u32[]{:S(2)}) collective-permute-start(bf16[1280,640]{1,0:T(8,128)(2,1)} %bitcast.2), channel_id=1, source_target_pairs={{0,64},{64,0},{1,65},{65,1},{2,66},{66,2},{3,67},{67,3},{4,68},{68... | collective-permute-start | bytes 4915208 | tf_op jit(solution)/shard_map/ppermute | solution.py:36
  90.7 3.2 %fusion.18 = f32[128,640]{1,0:T(8,128)} fusion(bf16[1280,640]{1,0:T(8,128)(2,1)} %bitcast.2, bf16[1280,768]{1,0:T(8,128)(2,1)S(1)} %bitcast.57, bf16[128,640]{1,0:T(8,128)(2,1)S(1)} %collective-permute-done, pred[]{:T(512)S(6)} %eq.38, f32[128,1280]{1,0:T(8,128)S(1)} %fusion.56), kind=kOutput, calls=%fused_computation.32 | convolution fusion | flops 420986880 | bytes 4423681 | tf_op jit(solution)/shard_map/dot_general | solution.py:61
  93.9 3.2 %fusion.55 = f32[128,1280]{1,0:T(8,128)} fusion(bf16[1280,768]{1,0:T(8,128)(2,1)} %collective-permute-done.8, bf16[128,640]{1,0:T(8,128)(2,1)S(1)} %fusion.46, bf16[768]{0:T(1024)(128)(2,1)S(1)} %pad.19.clone), kind=kOutput, calls=%fused_computation.87 | convolution fusion | flops 252051456 | bytes 2786816 | tf_op jit(solution)/shard_map/dot_general | solution.py:49
  97.1 3.3 %fusion.47 = (f32[128]{0:T(128)S(1)}, f32[128,640]{1,0:T(8,128)S(1)}) fusion(bf16[128,640]{1,0:T(8,128)(2,1)S(1)} %collective-permute-done.1, f32[640]{0:T(1024)S(1)} %reduce.1, f32[128,640]{1,0:T(8,128)} %fusion.18, bf16[1280,768]{1,0:T(8,128)(2,1)} %collective-permute-done.8, bf16[1280,640]{1,0:T(8,128)(2,1)} %collective-permute-done.7, ...), kind=kOutput, calls=%fused_computation.77 | convolution fusion | flops 421396352 | bytes 4918273 | tf_op jit(solution)/shard_map/dot_general | solution.py:61
  101.9 6.4 %collective-permute-done.9 = bf16[128,640]{1,0:T(8,128)(2,1)S(1)} collective-permute-done((bf16[128,640]{1,0:T(8,128)(2,1)S(1)}, bf16[128,640]{1,0:T(8,128)(2,1)S(1)}, u32[]{:S(2)}, u32[]{:S(2)}) %collective-permute-start.9) | collective-permute-done | bytes 163872 | tf_op jit(solution)/shard_map/ppermute | solution.py:150
  108.3 3.2 %fusion.15 = f32[128,640]{1,0:T(8,128)} fusion(bf16[128,640]{1,0:T(8,128)(2,1)S(1)} %collective-permute-done.9, bf16[1280,640]{1,0:T(8,128)(2,1)} %bitcast.2, bf16[1280,768]{1,0:T(8,128)(2,1)S(1)} %bitcast.58, f32[128,1280]{1,0:T(8,128)S(1)} %fusion.56), kind=kOutput, calls=%fused_computation.29 | convolution fusion | flops 420904960 | bytes 4423680 | tf_op jit(solution)/shard_map/dot_general | solution.py:61
  111.5 3.9 %fusion.48 = (f32[128]{0:T(128)S(1)}, f32[128,640]{1,0:T(8,128)}) fusion(bf16[128,640]{1,0:T(8,128)(2,1)S(1)} %collective-permute-done.1, f32[640]{0:T(1024)S(1)} %reduce.1, f32[128,640]{1,0:T(8,128)} %fusion.15, bf16[1280,768]{1,0:T(8,128)(2,1)} %collective-permute-done.8, bf16[128,640]{1,0:T(8,128)(2,1)S(1)} %collective-permute-done.9, ...), kind=kOutput, calls=%fused_computation.78 | convolution fusion | flops 421314432 | bytes 4918272 | tf_op jit(solution)/shard_map/dot_general | solution.py:61
  117.9 9.6 %collective-permute-done.10 = bf16[128,640]{1,0:T(8,128)(2,1)S(1)} collective-permute-done((bf16[128,640]{1,0:T(8,128)(2,1)S(1)}, bf16[128,640]{1,0:T(8,128)(2,1)S(1)}, u32[]{:S(2)}, u32[]{:S(2)}) %collective-permute-start.10) | collective-permute-done | bytes 163872 | tf_op jit(solution)/shard_map/ppermute | solution.py:150
  127.5 3.3 %fusion.12 = f32[128,640]{1,0:T(8,128)} fusion(bf16[128,640]{1,0:T(8,128)(2,1)S(1)} %collective-permute-done.10, bf16[1280,640]{1,0:T(8,128)(2,1)} %bitcast.2, bf16[1280,768]{1,0:T(8,128)(2,1)S(1)} %bitcast.59, f32[128,1280]{1,0:T(8,128)S(1)} %fusion.56), kind=kOutput, calls=%fused_computation.26 | convolution fusion | flops 420904960 | bytes 4423680 | tf_op jit(solution)/shard_map/dot_general | solution.py:61
  130.8 3.9 %fusion.49 = (f32[128]{0:T(128)S(1)}, f32[128,640]{1,0:T(8,128)}) fusion(bf16[128,640]{1,0:T(8,128)(2,1)S(1)} %collective-permute-done.1, f32[640]{0:T(1024)S(1)} %reduce.1, f32[128,640]{1,0:T(8,128)} %fusion.12, bf16[1280,768]{1,0:T(8,128)(2,1)} %collective-permute-done.8, bf16[128,640]{1,0:T(8,128)(2,1)S(1)} %collective-permute-done.10, ...), kind=kOutput, calls=%fused_computation.79 | convolution fusion | flops 421314432 | bytes 4918272 | tf_op jit(solution)/shard_map/dot_general | solution.py:61
  137.3 5.1 %collective-permute-done.11 = bf16[128,640]{1,0:T(8,128)(2,1)S(1)} collective-permute-done((bf16[128,640]{1,0:T(8,128)(2,1)S(1)}, bf16[128,640]{1,0:T(8,128)(2,1)S(1)}, u32[]{:S(2)}, u32[]{:S(2)}) %collective-permute-start.11) | collective-permute-done | bytes 163872 | tf_op jit(solution)/shard_map/ppermute | solution.py:150
  152.3 6.1 %all-to-all-start.3 = ((bf16[16,80,640]{2,1,0:T(8,128)(2,1)}), bf16[16,80,640]{2,1,0:T(8,128)(2,1)}, u32[]{:S(2)}, u32[]{:S(2)}) async-start(bf16[16,80,640]{2,1,0:T(8,128)(2,1)} %bitcast.62), calls=%async_computation.3 | async-start | bytes 3276800 | tf_op jit(solution)/shard_map/all_to_all | solution.py:167
  168.8 15.5 %all-to-all-done.3 = bf16[16,80,640]{2,1,0:T(8,128)(2,1)} async-done(((bf16[16,80,640]{2,1,0:T(8,128)(2,1)}), bf16[16,80,640]{2,1,0:T(8,128)(2,1)}, u32[]{:S(2)}, u32[]{:S(2)}) %all-to-all-start.3) | async-done | bytes 1638432 | tf_op jit(solution)/shard_map/all_to_all | solution.py:167
  184.3 3.6 %all-to-all-start.2 = ((bf16[16,88,640]{2,1,0:T(8,128)(2,1)}), bf16[16,88,640]{2,1,0:T(8,128)(2,1)S(1)}, u32[]{:S(2)}, u32[]{:S(2)}) async-start(bf16[16,88,640]{2,1,0:T(8,128)(2,1)} %pad_maximum_fusion), calls=%async_computation.2 | async-start | bytes 3604480 | tf_op jit(solution)/shard_map/all_to_all | solution.py:167
  188.1 5.5 %collective-permute-start.12 = (bf16[128,640]{1,0:T(8,128)(2,1)S(1)}, bf16[128,640]{1,0:T(8,128)(2,1)S(1)}, u32[]{:S(2)}, u32[]{:S(2)}) collective-permute-start(bf16[128,640]{1,0:T(8,128)(2,1)S(1)} %fusion.43), channel_id=1, source_target_pairs={{0,0},{1,1},{64,2},{65,3},{128,4},{129,5},{192,6},{193,7},{8,8},{9... | collective-permute-start | bytes 491528 | tf_op jit(solution)/shard_map/ppermute | solution.py:154
  193.6 6.2 %collective-permute-done.12 = bf16[128,640]{1,0:T(8,128)(2,1)S(1)} collective-permute-done((bf16[128,640]{1,0:T(8,128)(2,1)S(1)}, bf16[128,640]{1,0:T(8,128)(2,1)S(1)}, u32[]{:S(2)}, u32[]{:S(2)}) %collective-permute-start.12) | collective-permute-done | bytes 163872 | tf_op jit(solution)/shard_map/ppermute | solution.py:154
  202.9 3.5 %collective-permute-start.18 = (bf16[40,640]{1,0:T(8,128)(2,1)S(1)}, bf16[40,640]{1,0:T(8,128)(2,1)S(1)}, u32[]{:S(2)}, u32[]{:S(2)}) collective-permute-start(bf16[40,640]{1,0:T(8,128)(2,1)S(1)} %get-tuple-element.10), channel_id=1, source_target_pairs={{0,0},{1,1},{64,2},{65,3},{128,4},{129,5},{192,6},{193,7},{8,8},{9... | collective-permute-start | bytes 153608 | tf_op jit(solution)/shard_map/ppermute | solution.py:172
  206.4 5.8 %all-to-all-done.2 = bf16[16,88,640]{2,1,0:T(8,128)(2,1)S(1)} async-done(((bf16[16,88,640]{2,1,0:T(8,128)(2,1)}), bf16[16,88,640]{2,1,0:T(8,128)(2,1)S(1)}, u32[]{:S(2)}, u32[]{:S(2)}) %all-to-all-start.2) | async-done | bytes 1802272 | tf_op jit(solution)/shard_map/all_to_all | solution.py:167
  212.6 4.2 %collective-permute-start.16 = (bf16[48,640]{1,0:T(8,128)(2,1)S(1)}, bf16[48,640]{1,0:T(8,128)(2,1)S(1)}, u32[]{:S(2)}, u32[]{:S(2)}) collective-permute-start(bf16[48,640]{1,0:T(8,128)(2,1)S(1)} %get-tuple-element.9), channel_id=1, source_target_pairs={{8,0},{9,1},{72,2},{73,3},{136,4},{137,5},{200,6},{201,7},{0,8},{1... | collective-permute-start | bytes 184328 | tf_op jit(solution)/shard_map/ppermute | solution.py:172
  216.8 4.1 %collective-permute-start.15 = (bf16[48,640]{1,0:T(8,128)(2,1)S(1)}, bf16[48,640]{1,0:T(8,128)(2,1)S(1)}, u32[]{:S(2)}, u32[]{:S(2)}) collective-permute-start(bf16[48,640]{1,0:T(8,128)(2,1)S(1)} %get-tuple-element.8), channel_id=1, source_target_pairs={{0,0},{1,1},{64,2},{65,3},{128,4},{129,5},{192,6},{193,7},{8,8},{9... | collective-permute-start | bytes 184328 | tf_op jit(solution)/shard_map/ppermute | solution.py:172
  221.6 4.2 %collective-permute-done.15 = bf16[48,640]{1,0:T(8,128)(2,1)S(1)} collective-permute-done((bf16[48,640]{1,0:T(8,128)(2,1)S(1)}, bf16[48,640]{1,0:T(8,128)(2,1)S(1)}, u32[]{:S(2)}, u32[]{:S(2)}) %collective-permute-start.15) | collective-permute-done | bytes 61472 | tf_op jit(solution)/shard_map/ppermute | solution.py:172
  (98 shorter events, 48.3 us)
Async XLA Ops:
  0.6 1.7 copy-start
  3.6 10.6 %collective-permute-start.6 = (bf16[40,768]{1,0:T(8,128)(2,1)S(1)}, bf16[40,768]{1,0:T(8,128)(2,1)S(1)}, u32[]{:S(2)}, u32[]{:S(2)}) collective-permute-start(bf16[40,768]{1,0:T(8,128)(2,1)S(1)} %maximum_maximum_fusion), channel_id=1, source_target_pairs={{0,8},{1,9},{2,72},{3,73},{4,136},{5,137},{6,200},{7,201},{8,0},{9... | collective-permute-start | bytes 184328 | tf_op jit(solution)/shard_map/ppermute | solution.py:103
  9.7 8.2 %collective-permute-start.5 = (bf16[40,768]{1,0:T(8,128)(2,1)S(1)}, bf16[40,768]{1,0:T(8,128)(2,1)S(1)}, u32[]{:S(2)}, u32[]{:S(2)}) collective-permute-start(bf16[40,768]{1,0:T(8,128)(2,1)S(1)} %maximum_maximum_fusion), channel_id=1, source_target_pairs={{0,0},{1,1},{2,64},{3,65},{4,128},{5,129},{6,192},{7,193},{8,8},{9... | collective-permute-start | bytes 184328 | tf_op jit(solution)/shard_map/ppermute | solution.py:103
  19.3 7.1 %copy-start.6 = (bf16[1,40,640]{2,1,0:T(8,128)(2,1)S(1)}, bf16[1,40,640]{2,1,0:T(8,128)(2,1)}, u32[]{:S(2)}) copy-start(bf16[1,40,640]{2,1,0:T(8,128)(2,1)} %param.13) | copy-start | bytes 153604
  19.3 36.2 %all-to-all-start.1 = ((bf16[16,80,768]{2,1,0:T(8,128)(2,1)}), bf16[16,80,768]{2,1,0:T(8,128)(2,1)S(1)}, u32[]{:S(2)}, u32[]{:S(2)}) async-start(bf16[16,80,768]{2,1,0:T(8,128)(2,1)} %broadcast_in_dim.26), calls=%async_computation.1 | async-start | bytes 3932160 | tf_op jit(solution)/shard_map/all_to_all | solution.py:71
  26.4 6.4 %collective-permute-start.3 = (bf16[40,640]{1,0:T(8,128)(2,1)S(1)}, bf16[40,640]{1,0:T(8,128)(2,1)S(1)}, u32[]{:S(2)}, u32[]{:S(2)}) collective-permute-start(bf16[40,640]{1,0:T(8,128)(2,1)S(1)} %bitcast.67), channel_id=1, source_target_pairs={{0,8},{1,9},{2,72},{3,73},{4,136},{5,137},{6,200},{7,201},{8,0},{9... | collective-permute-start | bytes 153608 | tf_op jit(solution)/shard_map/ppermute | solution.py:106
  28.3 9.4 %collective-permute-start.2 = (bf16[40,640]{1,0:T(8,128)(2,1)S(1)}, bf16[40,640]{1,0:T(8,128)(2,1)S(1)}, u32[]{:S(2)}, u32[]{:S(2)}) collective-permute-start(bf16[40,640]{1,0:T(8,128)(2,1)S(1)} %bitcast.68), channel_id=1, source_target_pairs={{0,0},{1,1},{2,64},{3,65},{4,128},{5,129},{6,192},{7,193},{8,8},{9... | collective-permute-start | bytes 153608 | tf_op jit(solution)/shard_map/ppermute | solution.py:106
  56.9 8.2 %copy-start.5 = (bf16[1,128,640]{2,1,0:T(8,128)(2,1)S(1)}, bf16[1,128,640]{2,1,0:T(8,128)(2,1)}, u32[]{:S(2)}) copy-start(bf16[1,128,640]{2,1,0:T(8,128)(2,1)} %param.9) | copy-start | bytes 491524
  56.9 10.8 %copy-start.7 = (f32[1,640]{1,0:T(1,128)S(1)}, f32[1,640]{1,0:T(1,128)}, u32[]{:S(2)}) copy-start(f32[1,640]{1,0:T(1,128)} %param.11) | copy-start | bytes 7684
  56.9 27.4 %all-to-all-start = ((bf16[16,80,640]{2,1,0:T(8,128)(2,1)}), bf16[16,80,640]{2,1,0:T(8,128)(2,1)}, u32[]{:S(2)}, u32[]{:S(2)}) async-start(bf16[16,80,640]{2,1,0:T(8,128)(2,1)} %broadcast_in_dim.23), calls=%async_computation | async-start | bytes 3276800 | tf_op jit(solution)/shard_map/all_to_all | solution.py:71
  61.6 32.4 %collective-permute-start.8 = (bf16[1280,768]{1,0:T(8,128)(2,1)S(1)}, bf16[1280,768]{1,0:T(8,128)(2,1)}, u32[]{:S(2)}, u32[]{:S(2)}) collective-permute-start(bf16[1280,768]{1,0:T(8,128)(2,1)S(1)} %bitcast.55), channel_id=1, source_target_pairs={{0,64},{64,0},{1,65},{65,1},{2,66},{66,2},{3,67},{67,3},{4,68},{68... | collective-permute-start | bytes 5898248 | tf_op jit(solution)/shard_map/ppermute | solution.py:36
  65.0 24.6 %collective-permute-start.1 = (bf16[128,640]{1,0:T(8,128)(2,1)S(1)}, bf16[128,640]{1,0:T(8,128)(2,1)S(1)}, u32[]{:S(2)}, u32[]{:S(2)}) collective-permute-start(bf16[128,640]{1,0:T(8,128)(2,1)S(1)} %bitcast.66), channel_id=1, source_target_pairs={{0,0},{1,1},{2,64},{3,65},{4,128},{5,129},{6,192},{7,193},{8,8},{9... | collective-permute-start | bytes 491528 | tf_op jit(solution)/shard_map/ppermute | solution.py:108
  67.7 21.9 %collective-permute-start.4 = (f32[1,640]{1,0:T(1,128)S(1)}, f32[1,640]{1,0:T(1,128)S(1)}, u32[]{:S(2)}, u32[]{:S(2)}) collective-permute-start(f32[1,640]{1,0:T(1,128)S(1)} %copy-done.7), channel_id=1, source_target_pairs={{0,0},{1,1},{2,64},{3,65},{4,128},{5,129},{6,192},{7,193},{8,8},{9... | collective-permute-start | bytes 7688 | tf_op jit(solution)/shard_map/ppermute | solution.py:110
  73.3 17.4 %collective-permute-start = (bf16[128,640]{1,0:T(8,128)(2,1)}, bf16[128,640]{1,0:T(8,128)(2,1)S(1)}, u32[]{:S(2)}, u32[]{:S(2)}) collective-permute-start(bf16[128,640]{1,0:T(8,128)(2,1)} %param.10), channel_id=1, source_target_pairs={{0,0},{1,1},{2,64},{3,65},{4,128},{5,129},{6,192},{7,193},{8,8},{9... | collective-permute-start | bytes 491528 | tf_op jit(solution)/shard_map/ppermute | solution.py:109
  84.2 12.9 %collective-permute-start.7 = (bf16[1280,640]{1,0:T(8,128)(2,1)}, bf16[1280,640]{1,0:T(8,128)(2,1)}, u32[]{:S(2)}, u32[]{:S(2)}) collective-permute-start(bf16[1280,640]{1,0:T(8,128)(2,1)} %bitcast.2), channel_id=1, source_target_pairs={{0,64},{64,0},{1,65},{65,1},{2,66},{66,2},{3,67},{67,3},{4,68},{68... | collective-permute-start | bytes 4915208 | tf_op jit(solution)/shard_map/ppermute | solution.py:36
  100.6 7.7 %collective-permute-start.9 = (bf16[128,640]{1,0:T(8,128)(2,1)S(1)}, bf16[128,640]{1,0:T(8,128)(2,1)S(1)}, u32[]{:S(2)}, u32[]{:S(2)}) collective-permute-start(bf16[128,640]{1,0:T(8,128)(2,1)S(1)} %fusion.37), channel_id=1, source_target_pairs={{2,0},{4,2},{6,4},{10,8},{12,10},{14,12},{3,1},{5,3},{7,5},{11,9},... | collective-permute-start | bytes 491528 | tf_op jit(solution)/shard_map/ppermute | solution.py:150
  116.6 10.9 %collective-permute-start.10 = (bf16[128,640]{1,0:T(8,128)(2,1)S(1)}, bf16[128,640]{1,0:T(8,128)(2,1)S(1)}, u32[]{:S(2)}, u32[]{:S(2)}) collective-permute-start(bf16[128,640]{1,0:T(8,128)(2,1)S(1)} %fusion.39), channel_id=1, source_target_pairs={{2,0},{4,2},{6,4},{10,8},{12,10},{14,12},{3,1},{5,3},{7,5},{11,9},... | collective-permute-start | bytes 491528 | tf_op jit(solution)/shard_map/ppermute | solution.py:150
  127.5 7.3 %copy-start.2 = (bf16[128,640]{1,0:T(8,128)(2,1)}, bf16[128,640]{1,0:T(8,128)(2,1)S(1)}, u32[]{:S(2)}) copy-start(bf16[128,640]{1,0:T(8,128)(2,1)S(1)} %collective-permute-done.10) | copy-start | bytes 491524
  134.8 8.7 %copy-start.1 = (f32[128,1280]{1,0:T(8,128)S(1)}, f32[128,1280]{1,0:T(8,128)}, u32[]{:S(2)}) copy-start(f32[128,1280]{1,0:T(8,128)} %fusion.55) | copy-start | bytes 1966084
  136.0 6.4 %collective-permute-start.11 = (bf16[128,640]{1,0:T(8,128)(2,1)S(1)}, bf16[128,640]{1,0:T(8,128)(2,1)S(1)}, u32[]{:S(2)}, u32[]{:S(2)}) collective-permute-start(bf16[128,640]{1,0:T(8,128)(2,1)S(1)} %fusion.41), channel_id=1, source_target_pairs={{2,0},{4,2},{6,4},{10,8},{12,10},{14,12},{3,1},{5,3},{7,5},{11,9},... | collective-permute-start | bytes 491528 | tf_op jit(solution)/shard_map/ppermute | solution.py:150
  144.1 6.3 %collective-permute-start.17 = (bf16[1280,640]{1,0:T(8,128)(2,1)S(1)}, bf16[1280,640]{1,0:T(8,128)(2,1)S(1)}, u32[]{:S(2)}, u32[]{:S(2)}) collective-permute-start(bf16[1280,640]{1,0:T(8,128)(2,1)S(1)} %convolution_convert_fusion), channel_id=1, source_target_pairs={{0,64},{64,0},{1,65},{65,1},{2,66},{66,2},{3,67},{67,3},{4,68},{68... | collective-permute-start | bytes 4915208 | tf_op jit(solution)/shard_map/ppermute | solution.py:36
  148.5 3.8 %copy-start.3 = (bf16[128,1280]{1,0:T(8,128)(2,1)}, bf16[128,1280]{1,0:T(8,128)(2,1)S(1)}, u32[]{:S(2)}) copy-start(bf16[128,1280]{1,0:T(8,128)(2,1)S(1)} %fusion.9) | copy-start | bytes 983044
  150.4 15.0 %collective-permute-start.13 = (bf16[1280,640]{1,0:T(8,128)(2,1)}, bf16[1280,640]{1,0:T(8,128)(2,1)}, u32[]{:S(2)}, u32[]{:S(2)}) collective-permute-start(bf16[1280,640]{1,0:T(8,128)(2,1)} %convolution_convert_fusion.1), channel_id=1, source_target_pairs={{0,64},{64,0},{1,65},{65,1},{2,66},{66,2},{3,67},{67,3},{4,68},{68... | collective-permute-start | bytes 4915208 | tf_op jit(solution)/shard_map/ppermute | solution.py:36
  152.3 32.0 %all-to-all-start.3 = ((bf16[16,80,640]{2,1,0:T(8,128)(2,1)}), bf16[16,80,640]{2,1,0:T(8,128)(2,1)}, u32[]{:S(2)}, u32[]{:S(2)}) async-start(bf16[16,80,640]{2,1,0:T(8,128)(2,1)} %bitcast.62), calls=%async_computation.3 | async-start | bytes 3276800 | tf_op jit(solution)/shard_map/all_to_all | solution.py:167
  160.4 1.0 copy-start.4
  163.3 2.0 collective-permute-start.14
  184.3 27.9 %all-to-all-start.2 = ((bf16[16,88,640]{2,1,0:T(8,128)(2,1)}), bf16[16,88,640]{2,1,0:T(8,128)(2,1)S(1)}, u32[]{:S(2)}, u32[]{:S(2)}) async-start(bf16[16,88,640]{2,1,0:T(8,128)(2,1)} %pad_maximum_fusion), calls=%async_computation.2 | async-start | bytes 3604480 | tf_op jit(solution)/shard_map/all_to_all | solution.py:167
  188.1 11.7 %collective-permute-start.12 = (bf16[128,640]{1,0:T(8,128)(2,1)S(1)}, bf16[128,640]{1,0:T(8,128)(2,1)S(1)}, u32[]{:S(2)}, u32[]{:S(2)}) collective-permute-start(bf16[128,640]{1,0:T(8,128)(2,1)S(1)} %fusion.43), channel_id=1, source_target_pairs={{0,0},{1,1},{64,2},{65,3},{128,4},{129,5},{192,6},{193,7},{8,8},{9... | collective-permute-start | bytes 491528 | tf_op jit(solution)/shard_map/ppermute | solution.py:154
  201.5 19.4 %collective-permute-start.19 = (bf16[40,640]{1,0:T(8,128)(2,1)S(1)}, bf16[40,640]{1,0:T(8,128)(2,1)S(1)}, u32[]{:S(2)}, u32[]{:S(2)}) collective-permute-start(bf16[40,640]{1,0:T(8,128)(2,1)S(1)} %get-tuple-element.11), channel_id=1, source_target_pairs={{8,0},{9,1},{72,2},{73,3},{136,4},{137,5},{200,6},{201,7},{0,8},{1... | collective-permute-start | bytes 153608 | tf_op jit(solution)/shard_map/ppermute | solution.py:172
  202.9 18.0 %collective-permute-start.18 = (bf16[40,640]{1,0:T(8,128)(2,1)S(1)}, bf16[40,640]{1,0:T(8,128)(2,1)S(1)}, u32[]{:S(2)}, u32[]{:S(2)}) collective-permute-start(bf16[40,640]{1,0:T(8,128)(2,1)S(1)} %get-tuple-element.10), channel_id=1, source_target_pairs={{0,0},{1,1},{64,2},{65,3},{128,4},{129,5},{192,6},{193,7},{8,8},{9... | collective-permute-start | bytes 153608 | tf_op jit(solution)/shard_map/ppermute | solution.py:172
  212.6 9.0 %collective-permute-start.16 = (bf16[48,640]{1,0:T(8,128)(2,1)S(1)}, bf16[48,640]{1,0:T(8,128)(2,1)S(1)}, u32[]{:S(2)}, u32[]{:S(2)}) collective-permute-start(bf16[48,640]{1,0:T(8,128)(2,1)S(1)} %get-tuple-element.9), channel_id=1, source_target_pairs={{8,0},{9,1},{72,2},{73,3},{136,4},{137,5},{200,6},{201,7},{0,8},{1... | collective-permute-start | bytes 184328 | tf_op jit(solution)/shard_map/ppermute | solution.py:172
  216.8 9.0 %collective-permute-start.15 = (bf16[48,640]{1,0:T(8,128)(2,1)S(1)}, bf16[48,640]{1,0:T(8,128)(2,1)S(1)}, u32[]{:S(2)}, u32[]{:S(2)}) collective-permute-start(bf16[48,640]{1,0:T(8,128)(2,1)S(1)} %get-tuple-element.8), channel_id=1, source_target_pairs={{0,0},{1,1},{64,2},{65,3},{128,4},{129,5},{192,6},{193,7},{8,8},{9... | collective-permute-start | bytes 184328 | tf_op jit(solution)/shard_map/ppermute | solution.py:172

commit v2 on v1

v2 whole, which is shorter than its diff:
```python
import math

import jax
import jax.numpy as jnp
from jax import lax
from jax.experimental import pallas as pl
from jax.experimental.pallas import tpu as pltpu
from jax.sharding import Mesh, PartitionSpec as P

SAMPLES = 8
COLUMN = ("yl", "core", "z", "yh")
PLANE = ("x", "yl", "yh")
PEERS = 16
TILE = 640
VMEM_LIMIT = 28 << 20
ALL = ("yl", "core", "x", "z", "yh")


def home_to_work(flip):
    pairs = []
    for i in range(64):
        sec, z2, z10, yh = i >> 4, (i >> 3) & 1, (i >> 1) & 3, i & 1
        pairs.append((i, (z10 << 4) | ((z2 ^ flip) << 3) | (sec << 1) | yh))
    return pairs


def work_to_home(flip):
    return [(j, i) for i, j in home_to_work(flip)]


def next_section():
    pairs = []
    for z in range(8):
        if z % 4:
            pairs.append((z, z - 1))
    return pairs


def across_cores(value):
    return lax.ppermute(value, "core", [(0, 1), (1, 0)])


def time_features(timestep, freq_width):
    half_width = freq_width // 2
    freq_rates = jnp.exp(
        -math.log(10000.0) * jnp.arange(half_width, dtype=jnp.float32) / half_width
    )
    angles = timestep.astype(jnp.float32)[:, None] * freq_rates[None, :]
    return jnp.concatenate([jnp.cos(angles), jnp.sin(angles)], axis=1).astype(jnp.bfloat16)


def dot_rows(left_side, right_side):
    return lax.dot_general(
        left_side, right_side, (((1,), (1,)), ((), ())), preferred_element_type=jnp.float32
    )


def dot_plain(left_side, right_side):
    return lax.dot_general(
        left_side, right_side, (((1,), (0,)), ((), ())), preferred_element_type=jnp.float32
    )


def dot_first(left_side, right_side):
    return lax.dot_general(
        left_side, right_side, (((0,), (0,)), ((), ())), preferred_element_type=jnp.float32
    )


def two_parts(value):
    high = lax.reduce_precision(value, 8, 7)
    return high.astype(jnp.bfloat16), (value - high).astype(jnp.bfloat16)


def row_norm(x_ref):
    inputs = x_ref[...].astype(jnp.float32)
    rscale = lax.rsqrt(jnp.mean(inputs * inputs, axis=1, keepdims=True) + 1e-06)
    return rscale, inputs * rscale


def activation_kernel(x_ref, gain_ref, w_ref, cond_ref, normed_ref, hidden_ref, slope_ref):
    _, unit = row_norm(x_ref)
    normed = (unit * gain_ref[...]).astype(jnp.bfloat16)
    normed_ref[...] = normed
    for at in range(0, w_ref.shape[0], TILE):
        cols = pl.ds(at, TILE)
        pre = dot_rows(normed, w_ref[cols, :]) + cond_ref[:, cols]
        sig = jax.nn.sigmoid(pre)
        hidden_ref[:, cols] = (pre * sig).astype(jnp.bfloat16)
        slope_ref[:, cols] = sig * (1.0 + pre * (1.0 - sig))


def turn_body(g_ref, x_ref, gain_ref, halves, keep):
    grad = g_ref[...]
    total = None
    for w_in_ref, w_out_ref, slope_ref, pg_ref in halves:
        for at in range(0, w_in_ref.shape[0], TILE):
            cols = pl.ds(at, TILE)
            pre_grad = (dot_rows(grad, w_out_ref[cols, :]) * slope_ref[:, cols]).astype(
                jnp.bfloat16
            )
            if keep:
                pg_ref[:, cols] = pre_grad
            term = dot_plain(pre_grad, w_in_ref[cols, :])
            total = term if total is None else total + term
    rscale, unit = row_norm(x_ref)
    scaled = total * gain_ref[...]
    inner = jnp.mean(scaled * unit, axis=1, keepdims=True)
    grad_in = grad.astype(jnp.float32) + rscale * (scaled - unit * inner)
    return grad_in.astype(jnp.bfloat16), total * unit


def turn_kernel(g, x, gain, wi_n, wo_n, sl_n, wi_f, wo_f, sl_f, out):
    halves = ((wi_n, wo_n, sl_n, None), (wi_f, wo_f, sl_f, None))
    out[...] = turn_body(g, x, gain, halves, False)[0]


def last_turn_kernel(
    g, x, gain, wi_n, wo_n, sl_n, wi_f, wo_f, sl_f, normed, out, gain_out, pg_n, pg_f, far_out
):
    halves = ((wi_n, wo_n, sl_n, pg_n), (wi_f, wo_f, sl_f, pg_f))
    grad_in, terms = turn_body(g, x, gain, halves, True)
    out[...] = grad_in
    gain_out[...] = jnp.sum(terms, axis=0, keepdims=True)
    for at in range(0, pg_f.shape[1], TILE):
        cols = pl.ds(at, TILE)
        far_out[cols, :] = dot_first(pg_f[:, cols], normed[...]).astype(jnp.bfloat16)


def outer_kernel(left, right, out):
    for at in range(0, left.shape[1], TILE):
        cols = pl.ds(at, TILE)
        out[cols, :] = dot_first(left[:, cols], right[...]).astype(jnp.bfloat16)


def near_kernel(pg, normed, in_far, hidden, grad, out_far, sums):
    peers, rows = sums.shape[0], sums.shape[1] // 2
    span = 8
    for first, (left, right, far) in enumerate(((pg, normed, in_far), (hidden, grad, out_far))):
        for at in range(0, peers, span):
            cols = pl.ds(at * rows, span * rows)
            total = dot_first(left[:, cols], right[...]) + far[cols, :].astype(jnp.float32)
            total = total.astype(jnp.bfloat16)
            for k in range(span):
                sums[at + k, pl.ds(first * rows, rows), :] = total[k * rows : (k + 1) * rows, :]


def kernel(body, outs, flops=0):
    whole = pl.BlockSpec(memory_space=pltpu.VMEM)
    shapes = [jax.ShapeDtypeStruct(*out) for out in outs]

    def call(*operands):
        result = pl.pallas_call(
            body,
            out_shape=shapes,
            in_specs=[whole] * len(operands),
            out_specs=[whole] * len(shapes),
            compiler_params=pltpu.CompilerParams(vmem_limit_bytes=VMEM_LIMIT),
            cost_estimate=pl.CostEstimate(flops=flops, bytes_accessed=4 << 20, transcendentals=0),
        )(*operands)
        return result if len(shapes) > 1 else result[0]

    return call


def on_device(checkpoints, cotangent, gains, w_in, w_out, time_proj, class_table, timestep, label):
    rows, chan = checkpoints.shape[1:]
    own = w_in.shape[2]
    half = PEERS * 2 * own
    grad_scale = float(rows * 64) ** (-0.5)
    section = lax.axis_index("z") % 4
    sample = 2 * lax.axis_index("x") + lax.axis_index("z") // 4
    bf16, f32 = jnp.bfloat16, jnp.float32

    time_feats = time_features(timestep, time_proj.shape[1])
    picks = (
        label[:, None] == jnp.arange(class_table.shape[1], dtype=jnp.int32)[None, :]
    ).astype(bf16)
    cond = dot_plain(time_feats, time_proj[0]) + dot_plain(picks, class_table[0])
    cond_row = jnp.concatenate([part.reshape(1, -1) for part in two_parts(cond)], axis=1)
    shard = jnp.concatenate(
        [w_in[0].T, w_out[0], cond_row, jnp.zeros((7, chan), bf16)], axis=0
    )

    one, two = (lax.ppermute(shard, COLUMN, home_to_work(flip)) for flip in (0, 1))
    chunk = jnp.concatenate(
        [
            one[:own],
            two[:own],
            one[own : 2 * own],
            two[own : 2 * own],
            one[2 * own : 2 * own + 1],
            two[2 * own : 2 * own + 1],
            jnp.zeros((6, chan), bf16),
        ],
        axis=0,
    )
    full = lax.all_to_all(
        jnp.broadcast_to(chunk[None], (PEERS,) + chunk.shape), PLANE, 0, 0, tiled=True
    )
    x_rows = lax.ppermute(checkpoints[0], COLUMN, home_to_work(0))
    cot_rows = lax.ppermute(cotangent, COLUMN, home_to_work(0))
    gain_row = lax.ppermute(gains, COLUMN, home_to_work(0))

    wi_n = full[:, : 2 * own].reshape(half, chan)
    wi_f = across_cores(wi_n)
    wo_n = full[:, 2 * own : 4 * own].reshape(half, chan)
    wo_f = across_cores(wo_n)
    conds = full[:, 4 * own : 4 * own + 2].astype(f32).reshape(PEERS * 2, 2, SAMPLES, own)
    cond_n = lax.dynamic_index_in_dim(conds, sample, 2, False).sum(axis=1).reshape(1, half)
    cond_f = across_cores(cond_n)

    flops = 2 * rows * half * chan
    activate = kernel(
        activation_kernel, [((rows, chan), bf16), ((rows, half), bf16), ((rows, half), f32)], flops
    )
    normed, hidden_n, slope_n = activate(x_rows, gain_row, wi_n, cond_n)
    _, hidden_f, slope_f = activate(x_rows, gain_row, wi_f, cond_f)

    turn = kernel(turn_kernel, [((rows, chan), bf16)], 4 * flops)
    held = (x_rows, gain_row, wi_n, wo_n, slope_n, wi_f, wo_f, slope_f)
    grad = jnp.where(section == 3, cot_rows, jnp.zeros_like(cot_rows))
    kept = grad
    for _ in range(3):
        grad = lax.ppermute(turn(grad, *held), "z", next_section())
        kept = kept + grad

    far_out = kernel(outer_kernel, [((half, chan), bf16)], flops)(hidden_f, kept)
    recv_out = across_cores(far_out)
    last_turn = kernel(
        last_turn_kernel,
        [
            ((rows, chan), bf16),
            ((1, chan), f32),
            ((rows, half), bf16),
            ((rows, half), bf16),
            ((half, chan), bf16),
        ],
        5 * flops,
    )
    grad_in, gain_part, pg_n, _, far_in = last_turn(kept, *held, normed)
    recv_in = across_cores(far_in)
    sums = kernel(near_kernel, [((PEERS, 4 * own, chan), bf16)], 2 * flops)(
        pg_n, normed, recv_in, hidden_n, kept, recv_out
    )
    parts = lax.all_to_all(sums, PLANE, 0, 0, tiled=True)

    grad_home = lax.ppermute(grad_in, COLUMN, work_to_home(0))
    gain_sum = gain_part
    for axis, size, bit in (("core", 2, 1), ("x", 4, 1), ("x", 4, 2), ("yl", 2, 1), ("yh", 2, 1), ("z", 8, 4)):
        gain_sum = gain_sum + lax.ppermute(gain_sum, axis, [(i, i ^ bit) for i in range(size)])
    gain_home = lax.ppermute(gain_sum, COLUMN, work_to_home(0)) * grad_scale

    total = jnp.sum(parts.astype(f32), axis=0).astype(bf16).reshape(2, 2, own, chan)
    home = sum(
        lax.ppermute(total[:, flip], COLUMN, work_to_home(flip)).astype(f32) for flip in (0, 1)
    )
    return (
        grad_home[None],
        (home[0].T * grad_scale)[None],
        (home[1] * grad_scale)[None],
        gain_home,
    )


def solution(mesh):
    fine = Mesh(mesh.devices.reshape(2, 2, 4, 8, 2), ALL)
    section, fsdp = ("yl", "core"), ("x", "z", "yh")
    in_specs = (
        P(section, fsdp, None),
        P(fsdp, None),
        P(section, None),
        P(section, None, fsdp),
        P(section, fsdp, None),
        P(section, None, fsdp),
        P(section, None, fsdp),
        P(),
        P(),
    )
    out_specs = (
        P(section, fsdp, None),
        P(section, None, fsdp),
        P(section, fsdp, None),
        P(section, None),
    )
    return jax.shard_map(
        on_device, mesh=fine, in_specs=in_specs, out_specs=out_specs, check_vma=False
    )
```

time: 230 us -> 256 us (1.11)
  blocking collectives: 0 us -> 44.8 us
  matrix products: 38.9 us -> 1.02 us
  Pallas kernels: 0 us -> 22.4 us
  waiting for transfers between devices: 89.7 us -> 79.7 us
  starting transfers between devices: 82.6 us -> 91.2 us
  other arithmetic: 11.1 us -> 6.95 us
    all_to_all x4 -> x1, waiting for transfers between devices: 47.4 us -> 0.01 us  [on_device(): parts = lax.all_to_all(sums, PLANE, 0, 0, tiled=True)]
    all_to_all x0 -> x1, blocking collectives: none -> 44.8 us  [on_device(): lax.all_to_all(jnp.broadcast_to(chunk[None], (PEERS,) + chunk.shape), PLA...]
    ppermute x11 -> x14, waiting for transfers between devices: 35.3 us -> 76.1 us  [the longest x6 49.1 us: on_device(): lax.ppermute(gain_sum, axis, [(i, i ^ bit) for i in range(size)])]
    dot_general x18 -> x2, matrix products: 38.9 us -> 1.02 us  [dot_plain(): lax.dot_general(left_side, right_side, (((1,), (0,)), ((), ())), preferre...]
    pallas_call x0 -> x8, Pallas kernels: none -> 22.4 us  [call(): pl.pallas_call(body, out_shape=shapes, in_specs=[whole] * len(operands),...]
    ppermute x11 -> x14, starting transfers between devices: 32.5 us -> 45.3 us  [the longest x6 20.1 us: on_device(): lax.ppermute(gain_sum, axis, [(i, i ^ bit) for i in range(size)])]
    all_to_all x4 -> x1, starting transfers between devices: 21.4 us -> 8.82 us  [on_device(): parts = lax.all_to_all(sums, PLANE, 0, 0, tiled=True)]
    ppermute x1, waiting for transfers between devices: 6.21 us -> 0.01 us  [on_device(): grad_home = lax.ppermute(grad_in, COLUMN, work_to_home(0))]
  transfers between devices with their start and end apart: 24 -> 24, of which waited for: 14 -> 14; matrix products, arithmetic and copies ran while one was open for 11% -> 3% of each run, Pallas kernels for 0% -> 3%
where the time goes in v2:
time: 256 us; the launch traced here: 254 us
  starting transfers between devices  91.2 us (36%)
  waiting for transfers between devices  79.7 us (31%)
  blocking collectives  44.8 us (18%)
  Pallas kernels  22.4 us (9%)
  other arithmetic  6.95 us (3%)
  local copies, waits for them, and re-layouts  6.62 us (3%)
    ppermute x6, waiting for transfers between devices, on_device(): lax.ppermute(gain_sum, axis, [(i, i ^ bit) for i in range(size)])  49.1 us
    all_to_all x1, blocking collectives, on_device(): lax.all_to_all(jnp.broadcast_to(chunk[None], (PEERS,) + chunk.shape), PLA...  44.8 us
    pallas_call x8, Pallas kernels, call(): pl.pallas_call(body, out_shape=shapes, in_specs=[whole] * len(operands),...  22.4 us
    ppermute x6, starting transfers between devices, on_device(): lax.ppermute(gain_sum, axis, [(i, i ^ bit) for i in range(size)])  20.1 us
    ppermute x3, waiting for transfers between devices, on_device(): grad = lax.ppermute(turn(grad, *held), 'z', next_section())  14.3 us
    ppermute x5, starting transfers between devices, across_cores(): return lax.ppermute(value, 'core', [(0, 1), (1, 0)])  11.7 us
    ppermute x2, starting transfers between devices, on_device(): lax.ppermute(shard, COLUMN, home_to_work(flip))  10.4 us
    ppermute x1, starting transfers between devices, on_device(): grad_home = lax.ppermute(grad_in, COLUMN, work_to_home(0))  9.82 us
  transfers between devices with their start and end apart: 24, of which 14 were waited for; matrix products, arithmetic and copies ran while one was open for 3% of the time, Pallas kernels for 3%

profile of v2, /device:TPU:9, one launch (start us, length us, event | category | flops | bytes accessed | tf_op | source)
XLA Modules:
  0.0 253.6 jit_solution(12496423044818547173)
XLA Ops:
  3.7 6.1 %collective-permute-start.4 = (bf16[88,640]{1,0:T(8,128)(2,1)S(1)}, bf16[88,640]{1,0:T(8,128)(2,1)S(1)}, u32[]{:S(2)}, u32[]{:S(2)}) collective-permute-start(bf16[88,640]{1,0:T(8,128)(2,1)S(1)} %maximum_maximum_fusion), channel_id=1, source_target_pairs={{0,8},{1,9},{2,72},{3,73},{4,136},{5,137},{6,200},{7,201},{8,0},{9... | collective-permute-start | bytes 337928 | tf_op jit(solution)/shard_map/ppermute | solution.py:185
  9.8 4.2 %collective-permute-start.3 = (bf16[88,640]{1,0:T(8,128)(2,1)S(1)}, bf16[88,640]{1,0:T(8,128)(2,1)S(1)}, u32[]{:S(2)}, u32[]{:S(2)}) collective-permute-start(bf16[88,640]{1,0:T(8,128)(2,1)S(1)} %maximum_maximum_fusion), channel_id=1, source_target_pairs={{0,0},{1,1},{2,64},{3,65},{4,128},{5,129},{6,192},{7,193},{8,8},{9... | collective-permute-start | bytes 337928 | tf_op jit(solution)/shard_map/ppermute | solution.py:185
  14.0 3.5 %collective-permute-done.4 = bf16[88,640]{1,0:T(8,128)(2,1)S(1)} collective-permute-done((bf16[88,640]{1,0:T(8,128)(2,1)S(1)}, bf16[88,640]{1,0:T(8,128)(2,1)S(1)}, u32[]{:S(2)}, u32[]{:S(2)}) %collective-permute-start.4) | collective-permute-done | bytes 112672 | tf_op jit(solution)/shard_map/ppermute | solution.py:185
  19.3 44.8 %all_to_all.10 = bf16[16,168,640]{2,1,0:T(8,128)(2,1)S(1)} all-to-all(bf16[16,168,640]{2,1,0:T(8,128)(2,1)S(1)} %broadcast_in_dim.29), channel_id=1, replica_groups=mesh['yl'=2,'core'=2,'x'=4,'z'=8,'yh'=2] {'x','yl','yh'}, dimensions={0} | all-to-all | bytes 6881280 | tf_op jit(solution)/shard_map/all_to_all | solution.py:198
  65.8 4.5 %collective-permute-start.5 = (bf16[1280,640]{1,0:T(8,128)(2,1)S(1)}, bf16[1280,640]{1,0:T(8,128)(2,1)}, u32[]{:S(2)}, u32[]{:S(2)}) collective-permute-start(bf16[1280,640]{1,0:T(8,128)(2,1)S(1)} %bitcast.29), channel_id=1, source_target_pairs={{0,64},{64,0},{1,65},{65,1},{2,66},{66,2},{3,67},{67,3},{4,68},{68... | collective-permute-start | bytes 4915208 | tf_op jit(solution)/shard_map/ppermute | solution.py:40
  70.3 7.2 %collective-permute-start = (bf16[128,640]{1,0:T(8,128)(2,1)}, bf16[128,640]{1,0:T(8,128)(2,1)}, u32[]{:S(2)}, u32[]{:S(2)}) collective-permute-start(bf16[128,640]{1,0:T(8,128)(2,1)} %param.10), channel_id=1, source_target_pairs={{0,0},{1,1},{2,64},{3,65},{4,128},{5,129},{6,192},{7,193},{8,8},{9... | collective-permute-start | bytes 491528 | tf_op jit(solution)/shard_map/ppermute | solution.py:202
  77.5 1.9 collective-permute-start.2
  79.4 6.3 %collective-permute-start.1 = (bf16[128,640]{1,0:T(8,128)(2,1)}, bf16[128,640]{1,0:T(8,128)(2,1)S(1)}, u32[]{:S(2)}, u32[]{:S(2)}) collective-permute-start(bf16[128,640]{1,0:T(8,128)(2,1)} %bitcast), channel_id=1, source_target_pairs={{0,0},{1,1},{2,64},{3,65},{4,128},{5,129},{6,192},{7,193},{8,8},{9... | collective-permute-start | bytes 491528 | tf_op jit(solution)/shard_map/ppermute | solution.py:201
  89.5 2.2 collective-permute-start.7
  92.5 2.2 shard_map.121
  94.8 3.9 %shard_map.122 = bf16[128,640]{1,0:T(8,128)(2,1)S(1)} custom-call(bf16[128,640]{1,0:T(8,128)(2,1)S(1)} %copy-done.1, bf16[128,640]{1,0:T(8,128)(2,1)S(1)} %collective-permute-done.1.x_ref.x, f32[1,640]{1,0:T(1,128)S(1)} %collective-permute-done.2.gain_ref.gain, bf16[1280,640]{1,0:T(8,128)(2,1)S(1)} %bitcast.31, bf16[1280,640]{1,0:T(8,128)(2,1)S(1)} %bitcast.36, ...), custom_call_target="tpu_custom_call" | custom-call | flops 838860800 | bytes 4194304 | tf_op jit(solution)/shard_map/pallas_call | solution.py:153
  100.0 4.8 %collective-permute-done.8.g = bf16[128,640]{1,0:T(8,128)(2,1)S(1)} collective-permute-done((bf16[128,640]{1,0:T(8,128)(2,1)S(1)}, bf16[128,640]{1,0:T(8,128)(2,1)S(1)}, u32[]{:S(2)}, u32[]{:S(2)}) %collective-permute-start.8) | collective-permute-done | bytes 163872 | tf_op jit(solution)/shard_map/ppermute | solution.py:225
  104.8 3.9 %shard_map.123 = bf16[128,640]{1,0:T(8,128)(2,1)S(1)} custom-call(bf16[128,640]{1,0:T(8,128)(2,1)S(1)} %collective-permute-done.8.g, bf16[128,640]{1,0:T(8,128)(2,1)S(1)} %collective-permute-done.1.x_ref.x, f32[1,640]{1,0:T(1,128)S(1)} %collective-permute-done.2.gain_ref.gain, bf16[1280,640]{1,0:T(8,128)(2,1)S(1)} %bitcast.32, ...), custom_call_target="tpu_custom_call" | custom-call | flops 838860800 | bytes 4194304 | tf_op jit(solution)/shard_map/pallas_call | solution.py:153
  110.0 4.8 %collective-permute-done.9.g = bf16[128,640]{1,0:T(8,128)(2,1)S(1)} collective-permute-done((bf16[128,640]{1,0:T(8,128)(2,1)S(1)}, bf16[128,640]{1,0:T(8,128)(2,1)S(1)}, u32[]{:S(2)}, u32[]{:S(2)}) %collective-permute-start.9) | collective-permute-done | bytes 163872 | tf_op jit(solution)/shard_map/ppermute | solution.py:225
  114.8 3.9 %shard_map.124 = bf16[128,640]{1,0:T(8,128)(2,1)S(1)} custom-call(bf16[128,640]{1,0:T(8,128)(2,1)S(1)} %collective-permute-done.9.g, bf16[128,640]{1,0:T(8,128)(2,1)S(1)} %collective-permute-done.1.x_ref.x, f32[1,640]{1,0:T(1,128)S(1)} %collective-permute-done.2.gain_ref.gain, bf16[1280,640]{1,0:T(8,128)(2,1)S(1)} %bitcast.33, ...), custom_call_target="tpu_custom_call" | custom-call | flops 838860800 | bytes 4194304 | tf_op jit(solution)/shard_map/pallas_call | solution.py:153
  120.0 4.8 %collective-permute-done.10 = bf16[128,640]{1,0:T(8,128)(2,1)S(1)} collective-permute-done((bf16[128,640]{1,0:T(8,128)(2,1)S(1)}, bf16[128,640]{1,0:T(8,128)(2,1)S(1)}, u32[]{:S(2)}, u32[]{:S(2)}) %collective-permute-start.10) | collective-permute-done | bytes 163872 | tf_op jit(solution)/shard_map/ppermute | solution.py:225
  125.5 5.0 %collective-permute-start.13 = (bf16[1280,640]{1,0:T(8,128)(2,1)S(1)}, bf16[1280,640]{1,0:T(8,128)(2,1)S(1)}, u32[]{:S(2)}, u32[]{:S(2)}) collective-permute-start(bf16[1280,640]{1,0:T(8,128)(2,1)S(1)} %shard_map.126), channel_id=1, source_target_pairs={{0,64},{64,0},{1,65},{65,1},{2,66},{66,2},{3,67},{67,3},{4,68},{68... | collective-permute-start | bytes 4915208 | tf_op jit(solution)/shard_map/ppermute | solution.py:40
  130.5 4.4 %shard_map.125 = (bf16[128,640]{1,0:T(8,128)(2,1)S(1)}, f32[1,640]{1,0:T(1,128)S(1)}, bf16[128,1280]{1,0:T(8,128)(2,1)S(1)}, bf16[128,1280]{1,0:T(8,128)(2,1)}, bf16[1280,640]{1,0:T(8,128)(2,1)S(1)}) custom-call(bf16[128,640]{1,0:T(8,128)(2,1)S(1)} %add_add_fusion.g.right.grad, bf16[128,640]{1,0:T(8,128)(2,1)S(1)} %collective-permute-done.1.x_ref.x, ...), custom_call_target="tpu_custom_call" | custom-call | flops 1048576000 | bytes 4194304 | tf_op jit(solution)/shard_map/pallas_call | solution.py:153
  135.5 3.5 %collective-permute-done.12.in_far = bf16[1280,640]{1,0:T(8,128)(2,1)S(1)} collective-permute-done((bf16[1280,640]{1,0:T(8,128)(2,1)S(1)}, bf16[1280,640]{1,0:T(8,128)(2,1)S(1)}, u32[]{:S(2)}, u32[]{:S(2)}) %collective-permute-start.12) | collective-permute-done | bytes 1638432 | tf_op jit(solution)/shard_map/ppermute | solution.py:40
  139.0 2.7 %shard_map.127 = bf16[16,160,640]{2,1,0:T(8,128)(2,1)} custom-call(bf16[128,1280]{1,0:T(8,128)(2,1)S(1)} %get-tuple-element.17.pg, bf16[128,640]{1,0:T(8,128)(2,1)S(1)} %get-tuple-element.15.normed, bf16[1280,640]{1,0:T(8,128)(2,1)S(1)} %collective-permute-done.12.in_far, bf16[128,1280]{1,0:T(8,128)(2,1)S(1)} %get-tuple-element.19.hidden, ...), custom_call_target="tpu_custom_call" | custom-call | flops 419430400 | bytes 4194304 | tf_op jit(solution)/shard_map/pallas_call | solution.py:153
  141.7 8.8 %all-to-all-start.1 = ((bf16[16,160,640]{2,1,0:T(8,128)(2,1)}), bf16[16,160,640]{2,1,0:T(8,128)(2,1)S(1)}, u32[]{:S(2)}, u32[]{:S(2)}) async-start(bf16[16,160,640]{2,1,0:T(8,128)(2,1)} %shard_map.127), calls=%async_computation.1 | async-start | bytes 6553600 | tf_op jit(solution)/shard_map/all_to_all | solution.py:246
  153.3 42.2 %collective-permute-done.17 = f32[1,640]{1,0:T(1,128)S(1)} collective-permute-done((f32[1,640]{1,0:T(1,128)S(1)}, f32[1,640]{1,0:T(1,128)S(1)}, u32[]{:S(2)}, u32[]{:S(2)}) %collective-permute-start.17) | collective-permute-done | bytes 2592 | tf_op jit(solution)/shard_map/ppermute | solution.py:251
  195.5 3.9 %collective-permute-done.18 = f32[1,640]{1,0:T(1,128)S(1)} collective-permute-done((f32[1,640]{1,0:T(1,128)S(1)}, f32[1,640]{1,0:T(1,128)S(1)}, u32[]{:S(2)}, u32[]{:S(2)}) %collective-permute-start.18) | collective-permute-done | bytes 2592 | tf_op jit(solution)/shard_map/ppermute | solution.py:251
  199.4 15.2 %collective-permute-start.19 = (f32[1,640]{1,0:T(1,128)S(1)}, f32[1,640]{1,0:T(1,128)S(1)}, u32[]{:S(2)}, u32[]{:S(2)}) collective-permute-start(f32[1,640]{1,0:T(1,128)S(1)} %add.55), channel_id=1, source_target_pairs={{0,128},{128,0},{1,129},{129,1},{2,130},{130,2},{3,131},{131,3},{4... | collective-permute-start | bytes 7688 | tf_op jit(solution)/shard_map/ppermute | solution.py:251
  215.5 2.7 %collective-permute-start.20 = (f32[1,640]{1,0:T(1,128)S(1)}, f32[1,640]{1,0:T(1,128)S(1)}, u32[]{:S(2)}, u32[]{:S(2)}) collective-permute-start(f32[1,640]{1,0:T(1,128)S(1)} %add.56), channel_id=1, source_target_pairs={{0,1},{1,0},{2,3},{3,2},{4,5},{5,4},{6,7},{7,6},{8,9},{9,8},{10,11... | collective-permute-start | bytes 7688 | tf_op jit(solution)/shard_map/ppermute | solution.py:251
  219.8 9.8 %collective-permute-start.11 = (bf16[128,640]{1,0:T(8,128)(2,1)S(1)}, bf16[128,640]{1,0:T(8,128)(2,1)}, u32[]{:S(2)}, u32[]{:S(2)}) collective-permute-start(bf16[128,640]{1,0:T(8,128)(2,1)S(1)} %copy-done.3), channel_id=1, source_target_pairs={{0,0},{1,1},{64,2},{65,3},{128,4},{129,5},{192,6},{193,7},{8,8},{9... | collective-permute-start | bytes 491528 | tf_op jit(solution)/shard_map/ppermute | solution.py:248
  229.6 7.4 %collective-permute-start.22 = (f32[1,640]{1,0:T(1,128)S(1)}, f32[1,640]{1,0:T(1,128)S(1)}, u32[]{:S(2)}, u32[]{:S(2)}) collective-permute-start(f32[1,640]{1,0:T(1,128)S(1)} %add.58), channel_id=1, source_target_pairs={{0,0},{1,1},{64,2},{65,3},{128,4},{129,5},{192,6},{193,7},{8,8},{9... | collective-permute-start | bytes 7688 | tf_op jit(solution)/shard_map/ppermute | solution.py:252
  239.2 1.9 collective-permute-start.14
  241.2 1.6 collective-permute-start.15
  243.4 6.0 %collective-permute-done.14 = bf16[2,40,640]{2,1,0:T(8,128)(2,1)S(1)} collective-permute-done((bf16[2,40,640]{2,1,0:T(8,128)(2,1)S(1)}, bf16[2,40,640]{2,1,0:T(8,128)(2,1)S(1)}, u32[]{:S(2)}, u32[]{:S(2)}) %collective-permute-start.14) | collective-permute-done | bytes 102432 | tf_op jit(solution)/shard_map/ppermute | solution.py:256
  249.4 1.9 collective-permute-done.15
  252.0 1.6 copy.16
  (73 shorter events, 24.9 us)
Async XLA Ops:
  0.6 1.7 copy-start
  3.7 13.9 %collective-permute-start.4 = (bf16[88,640]{1,0:T(8,128)(2,1)S(1)}, bf16[88,640]{1,0:T(8,128)(2,1)S(1)}, u32[]{:S(2)}, u32[]{:S(2)}) collective-permute-start(bf16[88,640]{1,0:T(8,128)(2,1)S(1)} %maximum_maximum_fusion), channel_id=1, source_target_pairs={{0,8},{1,9},{2,72},{3,73},{4,136},{5,137},{6,200},{7,201},{8,0},{9... | collective-permute-start | bytes 337928 | tf_op jit(solution)/shard_map/ppermute | solution.py:185
  9.8 9.1 %collective-permute-start.3 = (bf16[88,640]{1,0:T(8,128)(2,1)S(1)}, bf16[88,640]{1,0:T(8,128)(2,1)S(1)}, u32[]{:S(2)}, u32[]{:S(2)}) collective-permute-start(bf16[88,640]{1,0:T(8,128)(2,1)S(1)} %maximum_maximum_fusion), channel_id=1, source_target_pairs={{0,0},{1,1},{2,64},{3,65},{4,128},{5,129},{6,192},{7,193},{8,8},{9... | collective-permute-start | bytes 337928 | tf_op jit(solution)/shard_map/ppermute | solution.py:185
  64.1 1.7 copy-start.4
  64.1 13.4 %copy-start.5 = (f32[1,640]{1,0:T(1,128)S(1)}, f32[1,640]{1,0:T(1,128)}, u32[]{:S(2)}) copy-start(f32[1,640]{1,0:T(1,128)} %param.11) | copy-start | bytes 7684
  65.8 26.8 %collective-permute-start.5 = (bf16[1280,640]{1,0:T(8,128)(2,1)S(1)}, bf16[1280,640]{1,0:T(8,128)(2,1)}, u32[]{:S(2)}, u32[]{:S(2)}) collective-permute-start(bf16[1280,640]{1,0:T(8,128)(2,1)S(1)} %bitcast.29), channel_id=1, source_target_pairs={{0,64},{64,0},{1,65},{65,1},{2,66},{66,2},{3,67},{67,3},{4,68},{68... | collective-permute-start | bytes 4915208 | tf_op jit(solution)/shard_map/ppermute | solution.py:40
  70.3 24.5 %collective-permute-start.6 = (bf16[1280,640]{1,0:T(8,128)(2,1)S(1)}, bf16[1280,640]{1,0:T(8,128)(2,1)}, u32[]{:S(2)}, u32[]{:S(2)}) collective-permute-start(bf16[1280,640]{1,0:T(8,128)(2,1)S(1)} %bitcast.35), channel_id=1, source_target_pairs={{0,64},{64,0},{1,65},{65,1},{2,66},{66,2},{3,67},{67,3},{4,68},{68... | collective-permute-start | bytes 4915208 | tf_op jit(solution)/shard_map/ppermute | solution.py:40
  70.3 15.5 %collective-permute-start = (bf16[128,640]{1,0:T(8,128)(2,1)}, bf16[128,640]{1,0:T(8,128)(2,1)}, u32[]{:S(2)}, u32[]{:S(2)}) collective-permute-start(bf16[128,640]{1,0:T(8,128)(2,1)} %param.10), channel_id=1, source_target_pairs={{0,0},{1,1},{2,64},{3,65},{4,128},{5,129},{6,192},{7,193},{8,8},{9... | collective-permute-start | bytes 491528 | tf_op jit(solution)/shard_map/ppermute | solution.py:202
  77.5 14.2 %collective-permute-start.2 = (f32[1,640]{1,0:T(1,128)S(1)}, f32[1,640]{1,0:T(1,128)S(1)}, u32[]{:S(2)}, u32[]{:S(2)}) collective-permute-start(f32[1,640]{1,0:T(1,128)S(1)} %copy-done.5), channel_id=1, source_target_pairs={{0,0},{1,1},{2,64},{3,65},{4,128},{5,129},{6,192},{7,193},{8,8},{9... | collective-permute-start | bytes 7688 | tf_op jit(solution)/shard_map/ppermute | solution.py:203
  79.4 12.3 %collective-permute-start.1 = (bf16[128,640]{1,0:T(8,128)(2,1)}, bf16[128,640]{1,0:T(8,128)(2,1)S(1)}, u32[]{:S(2)}, u32[]{:S(2)}) collective-permute-start(bf16[128,640]{1,0:T(8,128)(2,1)} %bitcast), channel_id=1, source_target_pairs={{0,0},{1,1},{2,64},{3,65},{4,128},{5,129},{6,192},{7,193},{8,8},{9... | collective-permute-start | bytes 491528 | tf_op jit(solution)/shard_map/ppermute | solution.py:201
  89.5 5.3 %copy-start.1 = (bf16[128,640]{1,0:T(8,128)(2,1)S(1)}, bf16[128,640]{1,0:T(8,128)(2,1)}, u32[]{:S(2)}) copy-start(bf16[128,640]{1,0:T(8,128)(2,1)} %broadcast_select_fusion.g) | copy-start | bytes 491524
  89.5 3.0 %collective-permute-start.7 = (f32[1,1280]{1,0:T(1,128)S(1)}, f32[1,1280]{1,0:T(1,128)S(1)}, u32[]{:S(2)}, u32[]{:S(2)}) collective-permute-start(f32[1,1280]{1,0:T(1,128)S(1)} %reshape.48.cond_ref), channel_id=1, source_target_pairs={{0,64},{64,0},{1,65},{65,1},{2,66},{66,2},{3,67},{67,3},{4,68},{68... | collective-permute-start | bytes 15368 | tf_op jit(solution)/shard_map/ppermute | solution.py:40
  98.7 6.1 %collective-permute-start.8 = (bf16[128,640]{1,0:T(8,128)(2,1)S(1)}, bf16[128,640]{1,0:T(8,128)(2,1)S(1)}, u32[]{:S(2)}, u32[]{:S(2)}) collective-permute-start(bf16[128,640]{1,0:T(8,128)(2,1)S(1)} %shard_map.122), channel_id=1, source_target_pairs={{2,0},{4,2},{6,4},{10,8},{12,10},{14,12},{3,1},{5,3},{7,5},{11,9},... | collective-permute-start | bytes 491528 | tf_op jit(solution)/shard_map/ppermute | solution.py:225
  108.7 6.1 %collective-permute-start.9 = (bf16[128,640]{1,0:T(8,128)(2,1)S(1)}, bf16[128,640]{1,0:T(8,128)(2,1)S(1)}, u32[]{:S(2)}, u32[]{:S(2)}) collective-permute-start(bf16[128,640]{1,0:T(8,128)(2,1)S(1)} %shard_map.123), channel_id=1, source_target_pairs={{2,0},{4,2},{6,4},{10,8},{12,10},{14,12},{3,1},{5,3},{7,5},{11,9},... | collective-permute-start | bytes 491528 | tf_op jit(solution)/shard_map/ppermute | solution.py:225
  118.7 6.1 %collective-permute-start.10 = (bf16[128,640]{1,0:T(8,128)(2,1)S(1)}, bf16[128,640]{1,0:T(8,128)(2,1)S(1)}, u32[]{:S(2)}, u32[]{:S(2)}) collective-permute-start(bf16[128,640]{1,0:T(8,128)(2,1)S(1)} %shard_map.124), channel_id=1, source_target_pairs={{2,0},{4,2},{6,4},{10,8},{12,10},{14,12},{3,1},{5,3},{7,5},{11,9},... | collective-permute-start | bytes 491528 | tf_op jit(solution)/shard_map/ppermute | solution.py:225
  125.5 10.0 %collective-permute-start.13 = (bf16[1280,640]{1,0:T(8,128)(2,1)S(1)}, bf16[1280,640]{1,0:T(8,128)(2,1)S(1)}, u32[]{:S(2)}, u32[]{:S(2)}) collective-permute-start(bf16[1280,640]{1,0:T(8,128)(2,1)S(1)} %shard_map.126), channel_id=1, source_target_pairs={{0,64},{64,0},{1,65},{65,1},{2,66},{66,2},{3,67},{67,3},{4,68},{68... | collective-permute-start | bytes 4915208 | tf_op jit(solution)/shard_map/ppermute | solution.py:40
  134.8 0.7 copy-start.2
  135.5 3.5 %collective-permute-start.12 = (bf16[1280,640]{1,0:T(8,128)(2,1)S(1)}, bf16[1280,640]{1,0:T(8,128)(2,1)S(1)}, u32[]{:S(2)}, u32[]{:S(2)}) collective-permute-start(bf16[1280,640]{1,0:T(8,128)(2,1)S(1)} %get-tuple-element.18), channel_id=1, source_target_pairs={{0,64},{64,0},{1,65},{65,1},{2,66},{66,2},{3,67},{67,3},{4,68},{68... | collective-permute-start | bytes 4915208 | tf_op jit(solution)/shard_map/ppermute | solution.py:40
  141.7 78.0 %copy-start.3 = (bf16[128,640]{1,0:T(8,128)(2,1)S(1)}, bf16[128,640]{1,0:T(8,128)(2,1)}, u32[]{:S(2)}) copy-start(bf16[128,640]{1,0:T(8,128)(2,1)} %copy-done.2) | copy-start | bytes 491524
  141.7 95.3 %all-to-all-start.1 = ((bf16[16,160,640]{2,1,0:T(8,128)(2,1)}), bf16[16,160,640]{2,1,0:T(8,128)(2,1)S(1)}, u32[]{:S(2)}, u32[]{:S(2)}) async-start(bf16[16,160,640]{2,1,0:T(8,128)(2,1)} %shard_map.127), calls=%async_computation.1 | async-start | bytes 6553600 | tf_op jit(solution)/shard_map/all_to_all | solution.py:246
  150.5 1.5 collective-permute-start.16
  152.1 43.4 %collective-permute-start.17 = (f32[1,640]{1,0:T(1,128)S(1)}, f32[1,640]{1,0:T(1,128)S(1)}, u32[]{:S(2)}, u32[]{:S(2)}) collective-permute-start(f32[1,640]{1,0:T(1,128)S(1)} %add.53), channel_id=1, source_target_pairs={{0,16},{16,0},{32,48},{48,32},{1,17},{17,1},{33,49},{49,33},{2,18}... | collective-permute-start | bytes 7688 | tf_op jit(solution)/shard_map/ppermute | solution.py:251
  195.4 3.9 %collective-permute-start.18 = (f32[1,640]{1,0:T(1,128)S(1)}, f32[1,640]{1,0:T(1,128)S(1)}, u32[]{:S(2)}, u32[]{:S(2)}) collective-permute-start(f32[1,640]{1,0:T(1,128)S(1)} %add.54), channel_id=1, source_target_pairs={{0,32},{16,48},{32,0},{48,16},{1,33},{17,49},{33,1},{49,17},{2,34}... | collective-permute-start | bytes 7688 | tf_op jit(solution)/shard_map/ppermute | solution.py:251
  199.4 16.1 %collective-permute-start.19 = (f32[1,640]{1,0:T(1,128)S(1)}, f32[1,640]{1,0:T(1,128)S(1)}, u32[]{:S(2)}, u32[]{:S(2)}) collective-permute-start(f32[1,640]{1,0:T(1,128)S(1)} %add.55), channel_id=1, source_target_pairs={{0,128},{128,0},{1,129},{129,1},{2,130},{130,2},{3,131},{131,3},{4... | collective-permute-start | bytes 7688 | tf_op jit(solution)/shard_map/ppermute | solution.py:251
  215.5 3.9 %collective-permute-start.20 = (f32[1,640]{1,0:T(1,128)S(1)}, f32[1,640]{1,0:T(1,128)S(1)}, u32[]{:S(2)}, u32[]{:S(2)}) collective-permute-start(f32[1,640]{1,0:T(1,128)S(1)} %add.56), channel_id=1, source_target_pairs={{0,1},{1,0},{2,3},{3,2},{4,5},{5,4},{6,7},{7,6},{8,9},{9,8},{10,11... | collective-permute-start | bytes 7688 | tf_op jit(solution)/shard_map/ppermute | solution.py:251
  219.5 10.1 %collective-permute-start.21 = (f32[1,640]{1,0:T(1,128)S(1)}, f32[1,640]{1,0:T(1,128)S(1)}, u32[]{:S(2)}, u32[]{:S(2)}) collective-permute-start(f32[1,640]{1,0:T(1,128)S(1)} %add.57), channel_id=1, source_target_pairs={{0,8},{2,10},{4,12},{6,14},{8,0},{10,2},{12,4},{14,6},{1,9},{3,11}... | collective-permute-start | bytes 7688 | tf_op jit(solution)/shard_map/ppermute | solution.py:251
  219.8 23.6 %collective-permute-start.11 = (bf16[128,640]{1,0:T(8,128)(2,1)S(1)}, bf16[128,640]{1,0:T(8,128)(2,1)}, u32[]{:S(2)}, u32[]{:S(2)}) collective-permute-start(bf16[128,640]{1,0:T(8,128)(2,1)S(1)} %copy-done.3), channel_id=1, source_target_pairs={{0,0},{1,1},{64,2},{65,3},{128,4},{129,5},{192,6},{193,7},{8,8},{9... | collective-permute-start | bytes 491528 | tf_op jit(solution)/shard_map/ppermute | solution.py:248
  229.6 13.2 %collective-permute-start.22 = (f32[1,640]{1,0:T(1,128)S(1)}, f32[1,640]{1,0:T(1,128)S(1)}, u32[]{:S(2)}, u32[]{:S(2)}) collective-permute-start(f32[1,640]{1,0:T(1,128)S(1)} %add.58), channel_id=1, source_target_pairs={{0,0},{1,1},{64,2},{65,3},{128,4},{129,5},{192,6},{193,7},{8,8},{9... | collective-permute-start | bytes 7688 | tf_op jit(solution)/shard_map/ppermute | solution.py:252
  239.2 10.1 %collective-permute-start.14 = (bf16[2,40,640]{2,1,0:T(8,128)(2,1)S(1)}, bf16[2,40,640]{2,1,0:T(8,128)(2,1)S(1)}, u32[]{:S(2)}, u32[]{:S(2)}) collective-permute-start(bf16[2,40,640]{2,1,0:T(8,128)(2,1)S(1)} %get-tuple-element.26), channel_id=1, source_target_pairs={{0,0},{1,1},{64,2},{65,3},{128,4},{129,5},{192,6},{193,7},{8,8},{9... | collective-permute-start | bytes 307208 | tf_op jit(solution)/shard_map/ppermute | solution.py:256
  241.2 10.1 %collective-permute-start.15 = (bf16[2,40,640]{2,1,0:T(8,128)(2,1)S(1)}, bf16[2,40,640]{2,1,0:T(8,128)(2,1)S(1)}, u32[]{:S(2)}, u32[]{:S(2)}) collective-permute-start(bf16[2,40,640]{2,1,0:T(8,128)(2,1)S(1)} %get-tuple-element.27), channel_id=1, source_target_pairs={{8,0},{9,1},{72,2},{73,3},{136,4},{137,5},{200,6},{201,7},{0,8},{1... | collective-permute-start | bytes 307208 | tf_op jit(solution)/shard_map/ppermute | solution.py:256

commit v3 on v2

--- a/solution.py
+++ b/solution.py
@@ -9,9 +9,10 @@
 
 SAMPLES = 8
 COLUMN = ("yl", "core", "z", "yh")
-PLANE = ("x", "yl", "yh")
-PEERS = 16
+PLANE = ("yl", "core", "x", "yh")
+SIDE = 4
 TILE = 640
+PAD = 16
 VMEM_LIMIT = 28 << 20
 ALL = ("yl", "core", "x", "z", "yh")
 
@@ -36,6 +37,19 @@
     return pairs
 
 
+def along(stage, shift):
+    pairs = []
+    for i in range(32):
+        yl, core, x, yh = i >> 4, (i >> 3) & 1, (i >> 1) & 3, i & 1
+        if (core == 0) == (stage == 1):
+            x = (x + shift) % SIDE
+        else:
+            y = (2 * yh + yl + shift) % SIDE
+            yl, yh = y % 2, y // 2
+        pairs.append((i, (yl << 4) | (core << 3) | (x << 1) | yh))
+    return pairs
+
+
 def across_cores(value):
     return lax.ppermute(value, "core", [(0, 1), (1, 0)])
 
@@ -78,13 +92,32 @@
     return rscale, inputs * rscale
 
 
-def activation_kernel(x_ref, gain_ref, w_ref, cond_ref, normed_ref, hidden_ref, slope_ref):
+def activation_kernel(
+    x_ref, gain_ref, select_ref, b0, b1, b2, b3, w_in_ref, w_out_ref, normed_ref, hidden_ref, slope_ref
+):
+    blocks = (b0, b1, b2, b3)
+    step = b0.shape[0] // SIDE
+    rows = (step - PAD) // 2
+    half = 2 * SIDE * SIDE * (rows // 2)
+    extras = []
+    for n, block in enumerate(blocks):
+        for k in range(SIDE):
+            to = pl.ds((n * SIDE + k) * rows, rows)
+            w_in_ref[to, :] = block[pl.ds(k * step, rows), :]
+            w_out_ref[to, :] = block[pl.ds(k * step + rows, rows), :]
+            extras.append(block[pl.ds(k * step + 2 * rows, PAD), :])
     _, unit = row_norm(x_ref)
     normed = (unit * gain_ref[...]).astype(jnp.bfloat16)
     normed_ref[...] = normed
-    for at in range(0, w_ref.shape[0], TILE):
+    extras = jnp.concatenate(extras, axis=0)
+    for at in range(0, half, TILE):
         cols = pl.ds(at, TILE)
-        pre = dot_rows(normed, w_ref[cols, :]) + cond_ref[:, cols]
+        spread = dot_plain(extras, select_ref[:, cols])
+        line = lax.broadcasted_iota(jnp.int32, spread.shape, 0)
+        shard = (lax.broadcasted_iota(jnp.int32, spread.shape, 1) + at) // (rows // 2)
+        mine = (line // PAD * 2 + line % PAD == shard) & (line % PAD < 2)
+        cond = jnp.sum(jnp.where(mine, spread, 0.0), axis=0, keepdims=True)
+        pre = dot_rows(normed, w_in_ref[cols, :]) + cond
         sig = jax.nn.sigmoid(pre)
         hidden_ref[:, cols] = (pre * sig).astype(jnp.bfloat16)
         slope_ref[:, cols] = sig * (1.0 + pre * (1.0 - sig))
@@ -133,16 +166,40 @@
         out[cols, :] = dot_first(left[:, cols], right[...]).astype(jnp.bfloat16)
 
 
-def near_kernel(pg, normed, in_far, hidden, grad, out_far, sums):
-    peers, rows = sums.shape[0], sums.shape[1] // 2
-    span = 8
+def high_low_rows(value):
+    line = lax.broadcasted_iota(jnp.int32, (PAD, value.shape[1]), 0)
+    high = value.astype(jnp.bfloat16).astype(jnp.float32)
+    rows = jnp.where(line == 0, high, jnp.where(line == 1, value - high, 0.0))
+    return rows.astype(jnp.bfloat16)
+
+
+def near_kernel(pg, normed, in_far, hidden, grad, out_far, gain_here, gain_there, *sums):
+    rows = (sums[0].shape[0] - PAD) // SIDE // 2
     for first, (left, right, far) in enumerate(((pg, normed, in_far), (hidden, grad, out_far))):
-        for at in range(0, peers, span):
-            cols = pl.ds(at * rows, span * rows)
+        for at in range(0, left.shape[1], TILE):
+            cols = pl.ds(at, TILE)
             total = dot_first(left[:, cols], right[...]) + far[cols, :].astype(jnp.float32)
             total = total.astype(jnp.bfloat16)
-            for k in range(span):
-                sums[at + k, pl.ds(first * rows, rows), :] = total[k * rows : (k + 1) * rows, :]
+            for k in range(TILE // rows):
+                peer = at // rows + k
+                to = pl.ds((peer % SIDE * 2 + first) * rows, rows)
+                sums[peer // SIDE][to, :] = total[k * rows : (k + 1) * rows, :]
+    gain = high_low_rows(gain_here[...] + gain_there[...])
+    for out in sums:
+        out[pl.ds(out.shape[0] - PAD, PAD), :] = gain
+
+
+def stage_sum_kernel(s0, s1, s2, s3, *outs):
+    rows = outs[0].shape[0] - PAD
+    for k, out in enumerate(outs):
+        cut = pl.ds(k * rows, rows)
+        total = sum(s[cut, :].astype(jnp.float32) for s in (s0, s1, s2, s3))
+        out[pl.ds(0, rows), :] = total.astype(jnp.bfloat16)
+    tail = pl.ds(s0.shape[0] - PAD, PAD)
+    total = sum(s[tail, :].astype(jnp.float32) for s in (s0, s1, s2, s3))
+    gain = high_low_rows(jnp.sum(total, axis=0, keepdims=True))
+    for out in outs:
+        out[pl.ds(rows, PAD), :] = gain
 
 
 def kernel(body, outs, flops=0):
@@ -166,7 +223,7 @@
 def on_device(checkpoints, cotangent, gains, w_in, w_out, time_proj, class_table, timestep, label):
     rows, chan = checkpoints.shape[1:]
     own = w_in.shape[2]
-    half = PEERS * 2 * own
+    half = SIDE * SIDE * 2 * own
     grad_scale = float(rows * 64) ** (-0.5)
     section = lax.axis_index("z") % 4
     sample = 2 * lax.axis_index("x") + lax.axis_index("z") // 4
@@ -183,6 +240,12 @@
     )
 
     one, two = (lax.ppermute(shard, COLUMN, home_to_work(flip)) for flip in (0, 1))
+    x_rows = lax.ppermute(checkpoints[0], COLUMN, home_to_work(0))
+    cot_rows = lax.ppermute(cotangent, COLUMN, home_to_work(0))
+    gain_row = lax.ppermute(gains, COLUMN, home_to_work(0))
+    one, two, x_rows, cot_rows, gain_row = lax.optimization_barrier(
+        (one, two, x_rows, cot_rows, gain_row)
+    )
     chunk = jnp.concatenate(
         [
             one[:own],
@@ -191,31 +254,36 @@
             two[own : 2 * own],
             one[2 * own : 2 * own + 1],
             two[2 * own : 2 * own + 1],
-            jnp.zeros((6, chan), bf16),
+            jnp.zeros((PAD - 2, chan), bf16),
         ],
         axis=0,
     )
-    full = lax.all_to_all(
-        jnp.broadcast_to(chunk[None], (PEERS,) + chunk.shape), PLANE, 0, 0, tiled=True
-    )
-    x_rows = lax.ppermute(checkpoints[0], COLUMN, home_to_work(0))
-    cot_rows = lax.ppermute(cotangent, COLUMN, home_to_work(0))
-    gain_row = lax.ppermute(gains, COLUMN, home_to_work(0))
-
-    wi_n = full[:, : 2 * own].reshape(half, chan)
-    wi_f = across_cores(wi_n)
-    wo_n = full[:, 2 * own : 4 * own].reshape(half, chan)
-    wo_f = across_cores(wo_n)
-    conds = full[:, 4 * own : 4 * own + 2].astype(f32).reshape(PEERS * 2, 2, SAMPLES, own)
-    cond_n = lax.dynamic_index_in_dim(conds, sample, 2, False).sum(axis=1).reshape(1, half)
-    cond_f = across_cores(cond_n)
+    quarter = jnp.concatenate(
+        [chunk] + [lax.ppermute(chunk, PLANE, along(1, k)) for k in range(1, SIDE)], axis=0
+    )
+    near = [quarter] + [lax.ppermute(quarter, PLANE, along(2, k)) for k in range(1, SIDE)]
+    far = [across_cores(block) for block in near]
+
+    entry = jnp.arange(chan, dtype=jnp.int32)[:, None]
+    hidden_col = jnp.arange(half, dtype=jnp.int32)[None, :]
+    select = (
+        (entry % own == hidden_col % own) & (entry // own % SAMPLES == sample)
+    ).astype(bf16)
 
     flops = 2 * rows * half * chan
     activate = kernel(
-        activation_kernel, [((rows, chan), bf16), ((rows, half), bf16), ((rows, half), f32)], flops
-    )
-    normed, hidden_n, slope_n = activate(x_rows, gain_row, wi_n, cond_n)
-    _, hidden_f, slope_f = activate(x_rows, gain_row, wi_f, cond_f)
+        activation_kernel,
+        [
+            ((half, chan), bf16),
+            ((half, chan), bf16),
+            ((rows, chan), bf16),
+            ((rows, half), bf16),
+            ((rows, half), f32),
+        ],
+        2 * flops,
+    )
+    wi_n, wo_n, normed, hidden_n, slope_n = activate(x_rows, gain_row, select, *near)
+    wi_f, wo_f, _, hidden_f, slope_f = activate(x_rows, gain_row, select, *far)
 
     turn = kernel(turn_kernel, [((rows, chan), bf16)], 4 * flops)
     held = (x_rows, gain_row, wi_n, wo_n, slope_n, wi_f, wo_f, slope_f)
@@ -240,26 +308,43 @@
     )
     grad_in, gain_part, pg_n, _, far_in = last_turn(kept, *held, normed)
     recv_in = across_cores(far_in)
-    sums = kernel(near_kernel, [((PEERS, 4 * own, chan), bf16)], 2 * flops)(
-        pg_n, normed, recv_in, hidden_n, kept, recv_out
-    )
-    parts = lax.all_to_all(sums, PLANE, 0, 0, tiled=True)
-
+    gain_there = across_cores(gain_part)
+    sums = kernel(near_kernel, [((SIDE * 4 * own + PAD, chan), bf16)] * SIDE, 2 * flops)(
+        pg_n, normed, recv_in, hidden_n, kept, recv_out, gain_part, gain_there
+    )
     grad_home = lax.ppermute(grad_in, COLUMN, work_to_home(0))
-    gain_sum = gain_part
-    for axis, size, bit in (("core", 2, 1), ("x", 4, 1), ("x", 4, 2), ("yl", 2, 1), ("yh", 2, 1), ("z", 8, 4)):
-        gain_sum = gain_sum + lax.ppermute(gain_sum, axis, [(i, i ^ bit) for i in range(size)])
-    gain_home = lax.ppermute(gain_sum, COLUMN, work_to_home(0)) * grad_scale
-
-    total = jnp.sum(parts.astype(f32), axis=0).astype(bf16).reshape(2, 2, own, chan)
+
+    parts = [sums[0]] + [
+        lax.ppermute(sums[k], PLANE, along(2, SIDE - k)) for k in range(1, SIDE)
+    ]
+    sums = kernel(stage_sum_kernel, [((4 * own + PAD, chan), bf16)] * SIDE)(*parts)
+    parts = [sums[0]] + [
+        lax.ppermute(sums[k], PLANE, along(1, SIDE - k)) for k in range(1, SIDE)
+    ]
+    total = sum(part.astype(f32) for part in parts)
+    gain_lines = list(two_parts(total[4 * own : 4 * own + 1] + total[4 * own + 1 : 4 * own + 2]))
+    gain_lines.append(jnp.zeros((6, chan), bf16))
+    total = total.astype(bf16)
     home = sum(
-        lax.ppermute(total[:, flip], COLUMN, work_to_home(flip)).astype(f32) for flip in (0, 1)
+        lax.ppermute(
+            jnp.concatenate(
+                [
+                    total[flip * own : (flip + 1) * own],
+                    total[(2 + flip) * own : (3 + flip) * own],
+                    *gain_lines,
+                ],
+                axis=0,
+            ),
+            COLUMN,
+            work_to_home(flip),
+        ).astype(f32)
+        for flip in (0, 1)
     )
     return (
         grad_home[None],
-        (home[0].T * grad_scale)[None],
-        (home[1] * grad_scale)[None],
-        gain_home,
+        (home[:own].T * grad_scale)[None],
+        (home[own : 2 * own] * grad_scale)[None],
+        (home[2 * own : 2 * own + 1] + home[2 * own + 1 : 2 * own + 2]) * grad_scale,
     )
 
 

time: 256 us -> 165 us (0.64)
  blocking collectives: 44.8 us -> 0 us
  starting transfers between devices: 91.2 us -> 65.5 us
  Pallas kernels: 22.4 us -> 16.5 us
  waiting for transfers between devices: 79.7 us -> 74.3 us
  local copies, waits for them, and re-layouts: 6.62 us -> 1.97 us
  other arithmetic: 6.95 us -> 3.79 us
    all_to_all x1 -> x0, blocking collectives: 44.8 us -> none  [on_device(): lax.all_to_all(jnp.broadcast_to(chunk[None], (PEERS,) + chunk.shape), PLA...]
    all_to_all x1 -> x0, starting transfers between devices: 8.82 us -> none  [on_device(): parts = lax.all_to_all(sums, PLANE, 0, 0, tiled=True)]
    ppermute x9 -> x14, waiting for transfers between devices: 57 us -> 50.7 us  [the longest x3 20.7 us: on_device(): lax.ppermute(sums[k], PLANE, along(2, SIDE - k))]
    pallas_call x8 -> x9, Pallas kernels: 22.4 us -> 16.5 us  [call(): pl.pallas_call(body, out_shape=shapes, in_specs=[whole] * len(operands),...]
    ppermute x1, starting transfers between devices: 9.82 us -> 4.37 us  [on_device(): grad_home = lax.ppermute(grad_in, COLUMN, work_to_home(0))]
    ppermute x1, starting transfers between devices: 7.21 us -> 1.92 us  [on_device(): cot_rows = lax.ppermute(cotangent, COLUMN, home_to_work(0))]
    ppermute x2, waiting for transfers between devices: 4.81 us -> 0.01 us  [on_device(): lax.ppermute(shard, COLUMN, home_to_work(flip))]
    ppermute x9 -> x14, starting transfers between devices: 31.1 us -> 26.3 us  [the longest x2 9.54 us: on_device(): lax.ppermute(jnp.concatenate([total[flip * own:(flip + 1) * own], total[(...]
  transfers between devices with their start and end apart: 24 -> 30, of which waited for: 14 -> 15; matrix products, arithmetic and copies ran while one was open for 3% -> 2% of each run, Pallas kernels for 3% -> 3%
where the time goes in v3:
time: 165 us; the launch traced here: 164 us
  waiting for transfers between devices  74.3 us (45%)
  starting transfers between devices  65.5 us (40%)
  Pallas kernels  16.5 us (10%)
  other arithmetic  3.79 us (2%)
  local copies, waits for them, and re-layouts  1.97 us (1%)
    ppermute x3, waiting for transfers between devices, on_device(): lax.ppermute(sums[k], PLANE, along(2, SIDE - k))  20.7 us
    ppermute x3, waiting for transfers between devices, on_device(): grad = lax.ppermute(turn(grad, *held), 'z', next_section())  16.7 us
    pallas_call x9, Pallas kernels, call(): pl.pallas_call(body, out_shape=shapes, in_specs=[whole] * len(operands),...  16.5 us
    ppermute x3, waiting for transfers between devices, on_device(): lax.ppermute(quarter, PLANE, along(2, k))  16.3 us
    ppermute x2, starting transfers between devices, on_device(): lax.ppermute(shard, COLUMN, home_to_work(flip))  10 us
    ppermute x2, starting transfers between devices, on_device(): lax.ppermute(jnp.concatenate([total[flip * own:(flip + 1) * own], total[(...  9.54 us
    ppermute x7, starting transfers between devices, across_cores(): return lax.ppermute(value, 'core', [(0, 1), (1, 0)])  8.33 us
    ppermute x2, waiting for transfers between devices, on_device(): lax.ppermute(jnp.concatenate([total[flip * own:(flip + 1) * own], total[(...  7.88 us
  transfers between devices with their start and end apart: 30, of which 15 were waited for; matrix products, arithmetic and copies ran while one was open for 2% of the time, Pallas kernels for 3%

profile of v3, /device:TPU:9, one launch (start us, length us, event | category | flops | bytes accessed | tf_op | source)
XLA Modules:
  0.0 164.1 jit_solution(3551640647413775990)
XLA Ops:
  0.6 6.7 %collective-permute-start.2 = (bf16[128,640]{1,0:T(8,128)(2,1)}, bf16[128,640]{1,0:T(8,128)(2,1)S(1)}, u32[]{:S(2)}, u32[]{:S(2)}) collective-permute-start(bf16[128,640]{1,0:T(8,128)(2,1)} %bitcast.23), channel_id=1, source_target_pairs={{0,0},{1,1},{2,64},{3,65},{4,128},{5,129},{6,192},{7,193},{8,8},{9... | collective-permute-start | bytes 491528 | tf_op jit(solution)/shard_map/ppermute | solution.py:243
  7.4 1.9 %collective-permute-start.3 = (bf16[128,640]{1,0:T(8,128)(2,1)}, bf16[128,640]{1,0:T(8,128)(2,1)S(1)}, u32[]{:S(2)}, u32[]{:S(2)}) collective-permute-start(bf16[128,640]{1,0:T(8,128)(2,1)} %param.10), channel_id=1, source_target_pairs={{0,0},{1,1},{2,64},{3,65},{4,128},{5,129},{6,192},{7,193},{8,8},{9... | collective-permute-start | bytes 491528 | tf_op jit(solution)/shard_map/ppermute | solution.py:244
  12.3 6.3 %collective-permute-start = (bf16[88,640]{1,0:T(8,128)(2,1)S(1)}, bf16[88,640]{1,0:T(8,128)(2,1)S(1)}, u32[]{:S(2)}, u32[]{:S(2)}) collective-permute-start(bf16[88,640]{1,0:T(8,128)(2,1)S(1)} %maximum_maximum_fusion), channel_id=1, source_target_pairs={{0,0},{1,1},{2,64},{3,65},{4,128},{5,129},{6,192},{7,193},{8,8},{9... | collective-permute-start | bytes 337928 | tf_op jit(solution)/shard_map/ppermute | solution.py:242
  18.6 3.7 %collective-permute-start.1 = (bf16[88,640]{1,0:T(8,128)(2,1)S(1)}, bf16[88,640]{1,0:T(8,128)(2,1)S(1)}, u32[]{:S(2)}, u32[]{:S(2)}) collective-permute-start(bf16[88,640]{1,0:T(8,128)(2,1)S(1)} %maximum_maximum_fusion), channel_id=1, source_target_pairs={{0,8},{1,9},{2,72},{3,73},{4,136},{5,137},{6,200},{7,201},{8,0},{9... | collective-permute-start | bytes 337928 | tf_op jit(solution)/shard_map/ppermute | solution.py:242
  22.3 4.0 %collective-permute-start.4 = (f32[1,640]{1,0:T(1,128)}, f32[1,640]{1,0:T(1,128)S(1)}, u32[]{:S(2)}, u32[]{:S(2)}) collective-permute-start(f32[1,640]{1,0:T(1,128)} %param.11), channel_id=1, source_target_pairs={{0,0},{1,1},{2,64},{3,65},{4,128},{5,129},{6,192},{7,193},{8,8},{9... | collective-permute-start | bytes 7688 | tf_op jit(solution)/shard_map/ppermute | solution.py:245
  26.3 3.8 %collective-permute-done.4.gain_ref.gain = f32[1,640]{1,0:T(1,128)S(1)} collective-permute-done((f32[1,640]{1,0:T(1,128)}, f32[1,640]{1,0:T(1,128)S(1)}, u32[]{:S(2)}, u32[]{:S(2)}) %collective-permute-start.4) | collective-permute-done | bytes 2592 | tf_op jit(solution)/shard_map/ppermute | solution.py:245
  30.6 2.1 %collective-permute-start.6 = (bf16[176,640]{1,0:T(8,128)(2,1)S(1)}, bf16[176,640]{1,0:T(8,128)(2,1)S(1)}, u32[]{:S(2)}, u32[]{:S(2)}) collective-permute-start(bf16[176,640]{1,0:T(8,128)(2,1)S(1)} %concatenate.26), channel_id=1, source_target_pairs={{0,32},{1,33},{16,48},{17,49},{32,0},{33,1},{48,16},{49,17},{64,65... | collective-permute-start | bytes 675848 | tf_op jit(solution)/shard_map/ppermute | solution.py:262
  32.7 2.0 %collective-permute-start.7 = (bf16[176,640]{1,0:T(8,128)(2,1)S(1)}, bf16[176,640]{1,0:T(8,128)(2,1)S(1)}, u32[]{:S(2)}, u32[]{:S(2)}) collective-permute-start(bf16[176,640]{1,0:T(8,128)(2,1)S(1)} %concatenate.26), channel_id=1, source_target_pairs={{0,48},{1,49},{16,0},{17,1},{32,16},{33,17},{48,32},{49,33},{64,19... | collective-permute-start | bytes 675848 | tf_op jit(solution)/shard_map/ppermute | solution.py:262
  37.3 2.4 %collective-permute-done.7 = bf16[176,640]{1,0:T(8,128)(2,1)S(1)} collective-permute-done((bf16[176,640]{1,0:T(8,128)(2,1)S(1)}, bf16[176,640]{1,0:T(8,128)(2,1)S(1)}, u32[]{:S(2)}, u32[]{:S(2)}) %collective-permute-start.7) | collective-permute-done | bytes 225312 | tf_op jit(solution)/shard_map/ppermute | solution.py:262
  41.6 2.5 %collective-permute-start.9 = (bf16[704,640]{1,0:T(8,128)(2,1)S(1)}, bf16[704,640]{1,0:T(8,128)(2,1)S(1)}, u32[]{:S(2)}, u32[]{:S(2)}) collective-permute-start(bf16[704,640]{1,0:T(8,128)(2,1)S(1)} %concatenate.27.b0), channel_id=1, source_target_pairs={{0,1},{1,0},{16,17},{17,16},{32,33},{33,32},{48,49},{49,48},{64,96... | collective-permute-start | bytes 2703368 | tf_op jit(solution)/shard_map/ppermute | solution.py:264
  46.8 7.0 %collective-permute-done.8.b1 = bf16[704,640]{1,0:T(8,128)(2,1)S(1)} collective-permute-done((bf16[704,640]{1,0:T(8,128)(2,1)S(1)}, bf16[704,640]{1,0:T(8,128)(2,1)S(1)}, u32[]{:S(2)}, u32[]{:S(2)}) %collective-permute-start.8) | collective-permute-done | bytes 901152 | tf_op jit(solution)/shard_map/ppermute | solution.py:264
  55.0 9.2 %collective-permute-done.9.b2 = bf16[704,640]{1,0:T(8,128)(2,1)S(1)} collective-permute-done((bf16[704,640]{1,0:T(8,128)(2,1)S(1)}, bf16[704,640]{1,0:T(8,128)(2,1)S(1)}, u32[]{:S(2)}, u32[]{:S(2)}) %collective-permute-start.9) | collective-permute-done | bytes 901152 | tf_op jit(solution)/shard_map/ppermute | solution.py:264
  64.3 2.1 %collective-permute-start.14 = (bf16[704,640]{1,0:T(8,128)(2,1)}, bf16[704,640]{1,0:T(8,128)(2,1)}, u32[]{:S(2)}, u32[]{:S(2)}) collective-permute-start(bf16[704,640]{1,0:T(8,128)(2,1)} %collective-permute-done.10.b3), channel_id=1, source_target_pairs={{0,64},{64,0},{1,65},{65,1},{2,66},{66,2},{3,67},{67,3},{4,68},{68... | collective-permute-start | bytes 2703368 | tf_op jit(solution)/shard_map/ppermute | solution.py:54
  67.0 2.5 %shard_map.120 = (bf16[1280,640]{1,0:T(8,128)(2,1)S(1)}, bf16[1280,640]{1,0:T(8,128)(2,1)S(1)}, bf16[128,640]{1,0:T(8,128)(2,1)S(1)}, bf16[128,1280]{1,0:T(8,128)(2,1)S(1)}, f32[128,1280]{1,0:T(8,128)S(1)}) custom-call(bf16[128,640]{1,0:T(8,128)(2,1)S(1)} %collective-permute-done.2.x_ref.x, f32[1,640]{1,0:T(1,128)S(1)} %collective-permute-done.4.gain_ref.gain, ...), custom_call_target="tpu_custom_call" | custom-call | flops 419430400 | bytes 4194304 | tf_op jit(solution)/shard_map/pallas_call | solution.py:210
  69.6 3.3 %shard_map.121 = (bf16[1280,640]{1,0:T(8,128)(2,1)S(1)}, bf16[1280,640]{1,0:T(8,128)(2,1)S(1)}, bf16[128,640]{1,0:T(8,128)(2,1)}, bf16[128,1280]{1,0:T(8,128)(2,1)S(1)}, f32[128,1280]{1,0:T(8,128)S(1)}) custom-call(bf16[128,640]{1,0:T(8,128)(2,1)S(1)} %collective-permute-done.2.x_ref.x, f32[1,640]{1,0:T(1,128)S(1)} %collective-permute-done.4.gain_ref.gain, ...), custom_call_target="tpu_custom_call" | custom-call | flops 419430400 | bytes 4194304 | tf_op jit(solution)/shard_map/pallas_call | solution.py:210
  73.0 2.0 %shard_map.122 = bf16[128,640]{1,0:T(8,128)(2,1)S(1)} custom-call(bf16[128,640]{1,0:T(8,128)(2,1)S(1)} %broadcast_select_fusion.g, bf16[128,640]{1,0:T(8,128)(2,1)S(1)} %collective-permute-done.2.x_ref.x, f32[1,640]{1,0:T(1,128)S(1)} %collective-permute-done.4.gain_ref.gain, bf16[1280,640]{1,0:T(8,128)(2,1)S(1)} %get-tuple-element.35.wi_n, ...), custom_call_target="tpu_custom_call" | custom-call | flops 838860800 | bytes 4194304 | tf_op jit(solution)/shard_map/pallas_call | solution.py:210
  76.3 6.4 %collective-permute-done.15.g = bf16[128,640]{1,0:T(8,128)(2,1)S(1)} collective-permute-done((bf16[128,640]{1,0:T(8,128)(2,1)S(1)}, bf16[128,640]{1,0:T(8,128)(2,1)S(1)}, u32[]{:S(2)}, u32[]{:S(2)}) %collective-permute-start.15) | collective-permute-done | bytes 163872 | tf_op jit(solution)/shard_map/ppermute | solution.py:293
  82.7 2.0 %shard_map.123 = bf16[128,640]{1,0:T(8,128)(2,1)S(1)} custom-call(bf16[128,640]{1,0:T(8,128)(2,1)S(1)} %collective-permute-done.15.g, bf16[128,640]{1,0:T(8,128)(2,1)S(1)} %collective-permute-done.2.x_ref.x, f32[1,640]{1,0:T(1,128)S(1)} %collective-permute-done.4.gain_ref.gain, bf16[1280,640]{1,0:T(8,128)(2,1)S(1)} %get-tuple-element.35.wi_n, ...), custom_call_target="tpu_custom_call" | custom-call | flops 838860800 | bytes 4194304 | tf_op jit(solution)/shard_map/pallas_call | solution.py:210
  86.0 5.5 %collective-permute-done.16.g = bf16[128,640]{1,0:T(8,128)(2,1)S(1)} collective-permute-done((bf16[128,640]{1,0:T(8,128)(2,1)S(1)}, bf16[128,640]{1,0:T(8,128)(2,1)S(1)}, u32[]{:S(2)}, u32[]{:S(2)}) %collective-permute-start.16) | collective-permute-done | bytes 163872 | tf_op jit(solution)/shard_map/ppermute | solution.py:293
  91.5 2.0 %shard_map.124 = bf16[128,640]{1,0:T(8,128)(2,1)S(1)} custom-call(bf16[128,640]{1,0:T(8,128)(2,1)S(1)} %collective-permute-done.16.g, bf16[128,640]{1,0:T(8,128)(2,1)S(1)} %collective-permute-done.2.x_ref.x, f32[1,640]{1,0:T(1,128)S(1)} %collective-permute-done.4.gain_ref.gain, bf16[1280,640]{1,0:T(8,128)(2,1)S(1)} %get-tuple-element.35.wi_n, ...), custom_call_target="tpu_custom_call" | custom-call | flops 838860800 | bytes 4194304 | tf_op jit(solution)/shard_map/pallas_call | solution.py:210
  94.8 4.8 %collective-permute-done.17 = bf16[128,640]{1,0:T(8,128)(2,1)S(1)} collective-permute-done((bf16[128,640]{1,0:T(8,128)(2,1)S(1)}, bf16[128,640]{1,0:T(8,128)(2,1)S(1)}, u32[]{:S(2)}, u32[]{:S(2)}) %collective-permute-start.17) | collective-permute-done | bytes 163872 | tf_op jit(solution)/shard_map/ppermute | solution.py:293
  100.3 2.9 %collective-permute-start.20 = (bf16[1280,640]{1,0:T(8,128)(2,1)S(1)}, bf16[1280,640]{1,0:T(8,128)(2,1)S(1)}, u32[]{:S(2)}, u32[]{:S(2)}) collective-permute-start(bf16[1280,640]{1,0:T(8,128)(2,1)S(1)} %shard_map.126), channel_id=1, source_target_pairs={{0,64},{64,0},{1,65},{65,1},{2,66},{66,2},{3,67},{67,3},{4,68},{68... | collective-permute-start | bytes 4915208 | tf_op jit(solution)/shard_map/ppermute | solution.py:54
  103.2 2.5 %shard_map.125 = (bf16[128,640]{1,0:T(8,128)(2,1)S(1)}, f32[1,640]{1,0:T(1,128)S(1)}, bf16[128,1280]{1,0:T(8,128)(2,1)S(1)}, bf16[128,1280]{1,0:T(8,128)(2,1)}, bf16[1280,640]{1,0:T(8,128)(2,1)S(1)}) custom-call(bf16[128,640]{1,0:T(8,128)(2,1)S(1)} %add_add_fusion.g.right.grad, bf16[128,640]{1,0:T(8,128)(2,1)S(1)} %collective-permute-done.2.x_ref.x, ...), custom_call_target="tpu_custom_call" | custom-call | flops 1048576000 | bytes 4194304 | tf_op jit(solution)/shard_map/pallas_call | solution.py:210
  106.1 3.0 %collective-permute-done.21.gain_there = f32[1,640]{1,0:T(1,128)S(1)} collective-permute-done((f32[1,640]{1,0:T(1,128)S(1)}, f32[1,640]{1,0:T(1,128)S(1)}, u32[]{:S(2)}, u32[]{:S(2)}) %collective-permute-start.21) | collective-permute-done | bytes 2592 | tf_op jit(solution)/shard_map/ppermute | solution.py:54
  110.2 2.3 %collective-permute-start.22 = (bf16[656,640]{1,0:T(8,128)(2,1)S(1)}, bf16[656,640]{1,0:T(8,128)(2,1)S(1)}, u32[]{:S(2)}, u32[]{:S(2)}) collective-permute-start(bf16[656,640]{1,0:T(8,128)(2,1)S(1)} %get-tuple-element.49), channel_id=1, source_target_pairs={{0,129},{1,128},{16,145},{17,144},{32,161},{33,160},{48,177},{49,1... | collective-permute-start | bytes 2519048 | tf_op jit(solution)/shard_map/ppermute | solution.py:318
  113.8 17.3 %collective-permute-done.22.s1 = bf16[656,640]{1,0:T(8,128)(2,1)S(1)} collective-permute-done((bf16[656,640]{1,0:T(8,128)(2,1)S(1)}, bf16[656,640]{1,0:T(8,128)(2,1)S(1)}, u32[]{:S(2)}, u32[]{:S(2)}) %collective-permute-start.22) | collective-permute-done | bytes 839712 | tf_op jit(solution)/shard_map/ppermute | solution.py:318
  131.0 3.4 %collective-permute-done.24.s3 = bf16[656,640]{1,0:T(8,128)(2,1)S(1)} collective-permute-done((bf16[656,640]{1,0:T(8,128)(2,1)S(1)}, bf16[656,640]{1,0:T(8,128)(2,1)S(1)}, u32[]{:S(2)}, u32[]{:S(2)}) %collective-permute-start.24) | collective-permute-done | bytes 839712 | tf_op jit(solution)/shard_map/ppermute | solution.py:318
  137.1 2.0 %collective-permute-start.27 = (bf16[176,640]{1,0:T(8,128)(2,1)S(1)}, bf16[176,640]{1,0:T(8,128)(2,1)S(1)}, u32[]{:S(2)}, u32[]{:S(2)}) collective-permute-start(bf16[176,640]{1,0:T(8,128)(2,1)S(1)} %get-tuple-element.55), channel_id=1, source_target_pairs={{0,16},{1,17},{16,32},{17,33},{32,48},{33,49},{48,0},{49,1},{64,19... | collective-permute-start | bytes 675848 | tf_op jit(solution)/shard_map/ppermute | solution.py:322
  139.1 4.4 %collective-permute-start.18 = (bf16[128,640]{1,0:T(8,128)(2,1)S(1)}, bf16[128,640]{1,0:T(8,128)(2,1)S(1)}, u32[]{:S(2)}, u32[]{:S(2)}) collective-permute-start(bf16[128,640]{1,0:T(8,128)(2,1)S(1)} %get-tuple-element.42), channel_id=1, source_target_pairs={{0,0},{1,1},{64,2},{65,3},{128,4},{129,5},{192,6},{193,7},{8,8},{9... | collective-permute-start | bytes 491528 | tf_op jit(solution)/shard_map/ppermute | solution.py:315
  144.6 7.2 %collective-permute-start.28 = (bf16[88,640]{1,0:T(8,128)(2,1)S(1)}, bf16[88,640]{1,0:T(8,128)(2,1)S(1)}, u32[]{:S(2)}, u32[]{:S(2)}) collective-permute-start(bf16[88,640]{1,0:T(8,128)(2,1)S(1)} %concatenate.28), channel_id=1, source_target_pairs={{0,0},{1,1},{64,2},{65,3},{128,4},{129,5},{192,6},{193,7},{8,8},{9... | collective-permute-start | bytes 337928 | tf_op jit(solution)/shard_map/ppermute | solution.py:329
  151.9 2.3 %collective-permute-start.29 = (bf16[88,640]{1,0:T(8,128)(2,1)S(1)}, bf16[88,640]{1,0:T(8,128)(2,1)S(1)}, u32[]{:S(2)}, u32[]{:S(2)}) collective-permute-start(bf16[88,640]{1,0:T(8,128)(2,1)S(1)} %concatenate.29), channel_id=1, source_target_pairs={{8,0},{9,1},{72,2},{73,3},{136,4},{137,5},{200,6},{201,7},{0,8},{1... | collective-permute-start | bytes 337928 | tf_op jit(solution)/shard_map/ppermute | solution.py:329
  154.4 7.7 %collective-permute-done.29 = bf16[88,640]{1,0:T(8,128)(2,1)S(1)} collective-permute-done((bf16[88,640]{1,0:T(8,128)(2,1)S(1)}, bf16[88,640]{1,0:T(8,128)(2,1)S(1)}, u32[]{:S(2)}, u32[]{:S(2)}) %collective-permute-start.29) | collective-permute-done | bytes 112672 | tf_op jit(solution)/shard_map/ppermute | solution.py:329
  (72 shorter events, 25.9 us)
Async XLA Ops:
  0.6 10.3 %copy-start = (bf16[1,256,40]{1,2,0:T(8,128)(2,1)S(1)}, bf16[1,256,40]{1,2,0:T(8,128)(2,1)}, u32[]{:S(2)}) copy-start(bf16[1,256,40]{1,2,0:T(8,128)(2,1)} %param.14) | copy-start | bytes 61444
  0.6 29.5 %collective-permute-start.2 = (bf16[128,640]{1,0:T(8,128)(2,1)}, bf16[128,640]{1,0:T(8,128)(2,1)S(1)}, u32[]{:S(2)}, u32[]{:S(2)}) collective-permute-start(bf16[128,640]{1,0:T(8,128)(2,1)} %bitcast.23), channel_id=1, source_target_pairs={{0,0},{1,1},{2,64},{3,65},{4,128},{5,129},{6,192},{7,193},{8,8},{9... | collective-permute-start | bytes 491528 | tf_op jit(solution)/shard_map/ppermute | solution.py:243
  7.4 22.8 %collective-permute-start.3 = (bf16[128,640]{1,0:T(8,128)(2,1)}, bf16[128,640]{1,0:T(8,128)(2,1)S(1)}, u32[]{:S(2)}, u32[]{:S(2)}) collective-permute-start(bf16[128,640]{1,0:T(8,128)(2,1)} %param.10), channel_id=1, source_target_pairs={{0,0},{1,1},{2,64},{3,65},{4,128},{5,129},{6,192},{7,193},{8,8},{9... | collective-permute-start | bytes 491528 | tf_op jit(solution)/shard_map/ppermute | solution.py:244
  12.3 17.8 %collective-permute-start = (bf16[88,640]{1,0:T(8,128)(2,1)S(1)}, bf16[88,640]{1,0:T(8,128)(2,1)S(1)}, u32[]{:S(2)}, u32[]{:S(2)}) collective-permute-start(bf16[88,640]{1,0:T(8,128)(2,1)S(1)} %maximum_maximum_fusion), channel_id=1, source_target_pairs={{0,0},{1,1},{2,64},{3,65},{4,128},{5,129},{6,192},{7,193},{8,8},{9... | collective-permute-start | bytes 337928 | tf_op jit(solution)/shard_map/ppermute | solution.py:242
  18.6 11.5 %collective-permute-start.1 = (bf16[88,640]{1,0:T(8,128)(2,1)S(1)}, bf16[88,640]{1,0:T(8,128)(2,1)S(1)}, u32[]{:S(2)}, u32[]{:S(2)}) collective-permute-start(bf16[88,640]{1,0:T(8,128)(2,1)S(1)} %maximum_maximum_fusion), channel_id=1, source_target_pairs={{0,8},{1,9},{2,72},{3,73},{4,136},{5,137},{6,200},{7,201},{8,0},{9... | collective-permute-start | bytes 337928 | tf_op jit(solution)/shard_map/ppermute | solution.py:242
  22.3 7.8 %collective-permute-start.4 = (f32[1,640]{1,0:T(1,128)}, f32[1,640]{1,0:T(1,128)S(1)}, u32[]{:S(2)}, u32[]{:S(2)}) collective-permute-start(f32[1,640]{1,0:T(1,128)} %param.11), channel_id=1, source_target_pairs={{0,0},{1,1},{2,64},{3,65},{4,128},{5,129},{6,192},{7,193},{8,8},{9... | collective-permute-start | bytes 7688 | tf_op jit(solution)/shard_map/ppermute | solution.py:245
  30.5 5.2 %collective-permute-start.5 = (bf16[176,640]{1,0:T(8,128)(2,1)S(1)}, bf16[176,640]{1,0:T(8,128)(2,1)S(1)}, u32[]{:S(2)}, u32[]{:S(2)}) collective-permute-start(bf16[176,640]{1,0:T(8,128)(2,1)S(1)} %concatenate.26), channel_id=1, source_target_pairs={{0,16},{1,17},{16,32},{17,33},{32,48},{33,49},{48,0},{49,1},{64,19... | collective-permute-start | bytes 675848 | tf_op jit(solution)/shard_map/ppermute | solution.py:262
  30.6 6.8 %collective-permute-start.6 = (bf16[176,640]{1,0:T(8,128)(2,1)S(1)}, bf16[176,640]{1,0:T(8,128)(2,1)S(1)}, u32[]{:S(2)}, u32[]{:S(2)}) collective-permute-start(bf16[176,640]{1,0:T(8,128)(2,1)S(1)} %concatenate.26), channel_id=1, source_target_pairs={{0,32},{1,33},{16,48},{17,49},{32,0},{33,1},{48,16},{49,17},{64,65... | collective-permute-start | bytes 675848 | tf_op jit(solution)/shard_map/ppermute | solution.py:262
  32.7 7.0 %collective-permute-start.7 = (bf16[176,640]{1,0:T(8,128)(2,1)S(1)}, bf16[176,640]{1,0:T(8,128)(2,1)S(1)}, u32[]{:S(2)}, u32[]{:S(2)}) collective-permute-start(bf16[176,640]{1,0:T(8,128)(2,1)S(1)} %concatenate.26), channel_id=1, source_target_pairs={{0,48},{1,49},{16,0},{17,1},{32,16},{33,17},{48,32},{49,33},{64,19... | collective-permute-start | bytes 675848 | tf_op jit(solution)/shard_map/ppermute | solution.py:262
  40.3 13.5 %collective-permute-start.8 = (bf16[704,640]{1,0:T(8,128)(2,1)S(1)}, bf16[704,640]{1,0:T(8,128)(2,1)S(1)}, u32[]{:S(2)}, u32[]{:S(2)}) collective-permute-start(bf16[704,640]{1,0:T(8,128)(2,1)S(1)} %concatenate.27.b0), channel_id=1, source_target_pairs={{0,128},{1,129},{16,144},{17,145},{32,160},{33,161},{48,176},{49,1... | collective-permute-start | bytes 2703368 | tf_op jit(solution)/shard_map/ppermute | solution.py:264
  41.6 22.7 %collective-permute-start.9 = (bf16[704,640]{1,0:T(8,128)(2,1)S(1)}, bf16[704,640]{1,0:T(8,128)(2,1)S(1)}, u32[]{:S(2)}, u32[]{:S(2)}) collective-permute-start(bf16[704,640]{1,0:T(8,128)(2,1)S(1)} %concatenate.27.b0), channel_id=1, source_target_pairs={{0,1},{1,0},{16,17},{17,16},{32,33},{33,32},{48,49},{49,48},{64,96... | collective-permute-start | bytes 2703368 | tf_op jit(solution)/shard_map/ppermute | solution.py:264
  44.0 20.3 %collective-permute-start.10 = (bf16[704,640]{1,0:T(8,128)(2,1)S(1)}, bf16[704,640]{1,0:T(8,128)(2,1)}, u32[]{:S(2)}, u32[]{:S(2)}) collective-permute-start(bf16[704,640]{1,0:T(8,128)(2,1)S(1)} %concatenate.27.b0), channel_id=1, source_target_pairs={{0,129},{1,128},{16,145},{17,144},{32,161},{33,160},{48,177},{49,1... | collective-permute-start | bytes 2703368 | tf_op jit(solution)/shard_map/ppermute | solution.py:264
  45.2 24.4 %collective-permute-start.11 = (bf16[704,640]{1,0:T(8,128)(2,1)S(1)}, bf16[704,640]{1,0:T(8,128)(2,1)}, u32[]{:S(2)}, u32[]{:S(2)}) collective-permute-start(bf16[704,640]{1,0:T(8,128)(2,1)S(1)} %concatenate.27.b0), channel_id=1, source_target_pairs={{0,64},{64,0},{1,65},{65,1},{2,66},{66,2},{3,67},{67,3},{4,68},{68... | collective-permute-start | bytes 2703368 | tf_op jit(solution)/shard_map/ppermute | solution.py:54
  53.8 15.8 %collective-permute-start.12 = (bf16[704,640]{1,0:T(8,128)(2,1)S(1)}, bf16[704,640]{1,0:T(8,128)(2,1)}, u32[]{:S(2)}, u32[]{:S(2)}) collective-permute-start(bf16[704,640]{1,0:T(8,128)(2,1)S(1)} %collective-permute-done.8.b1), channel_id=1, source_target_pairs={{0,64},{64,0},{1,65},{65,1},{2,66},{66,2},{3,67},{67,3},{4,68},{68... | collective-permute-start | bytes 2703368 | tf_op jit(solution)/shard_map/ppermute | solution.py:54
  64.3 5.3 %collective-permute-start.13 = (bf16[704,640]{1,0:T(8,128)(2,1)S(1)}, bf16[704,640]{1,0:T(8,128)(2,1)}, u32[]{:S(2)}, u32[]{:S(2)}) collective-permute-start(bf16[704,640]{1,0:T(8,128)(2,1)S(1)} %collective-permute-done.9.b2), channel_id=1, source_target_pairs={{0,64},{64,0},{1,65},{65,1},{2,66},{66,2},{3,67},{67,3},{4,68},{68... | collective-permute-start | bytes 2703368 | tf_op jit(solution)/shard_map/ppermute | solution.py:54
  64.3 5.3 %collective-permute-start.14 = (bf16[704,640]{1,0:T(8,128)(2,1)}, bf16[704,640]{1,0:T(8,128)(2,1)}, u32[]{:S(2)}, u32[]{:S(2)}) collective-permute-start(bf16[704,640]{1,0:T(8,128)(2,1)} %collective-permute-done.10.b3), channel_id=1, source_target_pairs={{0,64},{64,0},{1,65},{65,1},{2,66},{66,2},{3,67},{67,3},{4,68},{68... | collective-permute-start | bytes 2703368 | tf_op jit(solution)/shard_map/ppermute | solution.py:54
  75.0 7.7 %collective-permute-start.15 = (bf16[128,640]{1,0:T(8,128)(2,1)S(1)}, bf16[128,640]{1,0:T(8,128)(2,1)S(1)}, u32[]{:S(2)}, u32[]{:S(2)}) collective-permute-start(bf16[128,640]{1,0:T(8,128)(2,1)S(1)} %shard_map.122), channel_id=1, source_target_pairs={{2,0},{4,2},{6,4},{10,8},{12,10},{14,12},{3,1},{5,3},{7,5},{11,9},... | collective-permute-start | bytes 491528 | tf_op jit(solution)/shard_map/ppermute | solution.py:293
  84.7 6.8 %collective-permute-start.16 = (bf16[128,640]{1,0:T(8,128)(2,1)S(1)}, bf16[128,640]{1,0:T(8,128)(2,1)S(1)}, u32[]{:S(2)}, u32[]{:S(2)}) collective-permute-start(bf16[128,640]{1,0:T(8,128)(2,1)S(1)} %shard_map.123), channel_id=1, source_target_pairs={{2,0},{4,2},{6,4},{10,8},{12,10},{14,12},{3,1},{5,3},{7,5},{11,9},... | collective-permute-start | bytes 491528 | tf_op jit(solution)/shard_map/ppermute | solution.py:293
  93.5 6.1 %collective-permute-start.17 = (bf16[128,640]{1,0:T(8,128)(2,1)S(1)}, bf16[128,640]{1,0:T(8,128)(2,1)S(1)}, u32[]{:S(2)}, u32[]{:S(2)}) collective-permute-start(bf16[128,640]{1,0:T(8,128)(2,1)S(1)} %shard_map.124), channel_id=1, source_target_pairs={{2,0},{4,2},{6,4},{10,8},{12,10},{14,12},{3,1},{5,3},{7,5},{11,9},... | collective-permute-start | bytes 491528 | tf_op jit(solution)/shard_map/ppermute | solution.py:293
  100.3 8.9 %collective-permute-start.20 = (bf16[1280,640]{1,0:T(8,128)(2,1)S(1)}, bf16[1280,640]{1,0:T(8,128)(2,1)S(1)}, u32[]{:S(2)}, u32[]{:S(2)}) collective-permute-start(bf16[1280,640]{1,0:T(8,128)(2,1)S(1)} %shard_map.126), channel_id=1, source_target_pairs={{0,64},{64,0},{1,65},{65,1},{2,66},{66,2},{3,67},{67,3},{4,68},{68... | collective-permute-start | bytes 4915208 | tf_op jit(solution)/shard_map/ppermute | solution.py:54
  105.6 3.5 %collective-permute-start.19 = (bf16[1280,640]{1,0:T(8,128)(2,1)S(1)}, bf16[1280,640]{1,0:T(8,128)(2,1)S(1)}, u32[]{:S(2)}, u32[]{:S(2)}) collective-permute-start(bf16[1280,640]{1,0:T(8,128)(2,1)S(1)} %get-tuple-element.44), channel_id=1, source_target_pairs={{0,64},{64,0},{1,65},{65,1},{2,66},{66,2},{3,67},{67,3},{4,68},{68... | collective-permute-start | bytes 4915208 | tf_op jit(solution)/shard_map/ppermute | solution.py:54
  105.7 3.5 %collective-permute-start.21 = (f32[1,640]{1,0:T(1,128)S(1)}, f32[1,640]{1,0:T(1,128)S(1)}, u32[]{:S(2)}, u32[]{:S(2)}) collective-permute-start(f32[1,640]{1,0:T(1,128)S(1)} %get-tuple-element.47.gain_here), channel_id=1, source_target_pairs={{0,64},{64,0},{1,65},{65,1},{2,66},{66,2},{3,67},{67,3},{4,68},{68... | collective-permute-start | bytes 7688 | tf_op jit(solution)/shard_map/ppermute | solution.py:54
  110.2 20.8 %collective-permute-start.22 = (bf16[656,640]{1,0:T(8,128)(2,1)S(1)}, bf16[656,640]{1,0:T(8,128)(2,1)S(1)}, u32[]{:S(2)}, u32[]{:S(2)}) collective-permute-start(bf16[656,640]{1,0:T(8,128)(2,1)S(1)} %get-tuple-element.49), channel_id=1, source_target_pairs={{0,129},{1,128},{16,145},{17,144},{32,161},{33,160},{48,177},{49,1... | collective-permute-start | bytes 2519048 | tf_op jit(solution)/shard_map/ppermute | solution.py:318
  112.5 18.5 %collective-permute-start.23 = (bf16[656,640]{1,0:T(8,128)(2,1)S(1)}, bf16[656,640]{1,0:T(8,128)(2,1)S(1)}, u32[]{:S(2)}, u32[]{:S(2)}) collective-permute-start(bf16[656,640]{1,0:T(8,128)(2,1)S(1)} %get-tuple-element.50), channel_id=1, source_target_pairs={{0,1},{1,0},{16,17},{17,16},{32,33},{33,32},{48,49},{49,48},{64,96... | collective-permute-start | bytes 2519048 | tf_op jit(solution)/shard_map/ppermute | solution.py:318
  113.7 20.8 %collective-permute-start.24 = (bf16[656,640]{1,0:T(8,128)(2,1)S(1)}, bf16[656,640]{1,0:T(8,128)(2,1)S(1)}, u32[]{:S(2)}, u32[]{:S(2)}) collective-permute-start(bf16[656,640]{1,0:T(8,128)(2,1)S(1)} %get-tuple-element.51), channel_id=1, source_target_pairs={{0,128},{1,129},{16,144},{17,145},{32,160},{33,161},{48,176},{49,1... | collective-permute-start | bytes 2519048 | tf_op jit(solution)/shard_map/ppermute | solution.py:318
  134.9 8.5 %collective-permute-start.25 = (bf16[176,640]{1,0:T(8,128)(2,1)S(1)}, bf16[176,640]{1,0:T(8,128)(2,1)S(1)}, u32[]{:S(2)}, u32[]{:S(2)}) collective-permute-start(bf16[176,640]{1,0:T(8,128)(2,1)S(1)} %get-tuple-element.53), channel_id=1, source_target_pairs={{0,48},{1,49},{16,0},{17,1},{32,16},{33,17},{48,32},{49,33},{64,19... | collective-permute-start | bytes 675848 | tf_op jit(solution)/shard_map/ppermute | solution.py:322
  136.3 7.2 %collective-permute-start.26 = (bf16[176,640]{1,0:T(8,128)(2,1)S(1)}, bf16[176,640]{1,0:T(8,128)(2,1)S(1)}, u32[]{:S(2)}, u32[]{:S(2)}) collective-permute-start(bf16[176,640]{1,0:T(8,128)(2,1)S(1)} %get-tuple-element.54), channel_id=1, source_target_pairs={{0,32},{1,33},{16,48},{17,49},{32,0},{33,1},{48,16},{49,17},{64,65... | collective-permute-start | bytes 675848 | tf_op jit(solution)/shard_map/ppermute | solution.py:322
  137.1 7.2 %collective-permute-start.27 = (bf16[176,640]{1,0:T(8,128)(2,1)S(1)}, bf16[176,640]{1,0:T(8,128)(2,1)S(1)}, u32[]{:S(2)}, u32[]{:S(2)}) collective-permute-start(bf16[176,640]{1,0:T(8,128)(2,1)S(1)} %get-tuple-element.55), channel_id=1, source_target_pairs={{0,16},{1,17},{16,32},{17,33},{32,48},{33,49},{48,0},{49,1},{64,19... | collective-permute-start | bytes 675848 | tf_op jit(solution)/shard_map/ppermute | solution.py:322
  139.1 15.1 %collective-permute-start.18 = (bf16[128,640]{1,0:T(8,128)(2,1)S(1)}, bf16[128,640]{1,0:T(8,128)(2,1)S(1)}, u32[]{:S(2)}, u32[]{:S(2)}) collective-permute-start(bf16[128,640]{1,0:T(8,128)(2,1)S(1)} %get-tuple-element.42), channel_id=1, source_target_pairs={{0,0},{1,1},{64,2},{65,3},{128,4},{129,5},{192,6},{193,7},{8,8},{9... | collective-permute-start | bytes 491528 | tf_op jit(solution)/shard_map/ppermute | solution.py:315
  144.6 9.8 %collective-permute-start.28 = (bf16[88,640]{1,0:T(8,128)(2,1)S(1)}, bf16[88,640]{1,0:T(8,128)(2,1)S(1)}, u32[]{:S(2)}, u32[]{:S(2)}) collective-permute-start(bf16[88,640]{1,0:T(8,128)(2,1)S(1)} %concatenate.28), channel_id=1, source_target_pairs={{0,0},{1,1},{64,2},{65,3},{128,4},{129,5},{192,6},{193,7},{8,8},{9... | collective-permute-start | bytes 337928 | tf_op jit(solution)/shard_map/ppermute | solution.py:329
  151.9 10.2 %collective-permute-start.29 = (bf16[88,640]{1,0:T(8,128)(2,1)S(1)}, bf16[88,640]{1,0:T(8,128)(2,1)S(1)}, u32[]{:S(2)}, u32[]{:S(2)}) collective-permute-start(bf16[88,640]{1,0:T(8,128)(2,1)S(1)} %concatenate.29), channel_id=1, source_target_pairs={{8,0},{9,1},{72,2},{73,3},{136,4},{137,5},{200,6},{201,7},{0,8},{1... | collective-permute-start | bytes 337928 | tf_op jit(solution)/shard_map/ppermute | solution.py:329

commit v4 on v3

--- a/solution.py
+++ b/solution.py
@@ -11,8 +11,8 @@
 COLUMN = ("yl", "core", "z", "yh")
 PLANE = ("yl", "core", "x", "yh")
 SIDE = 4
-TILE = 640
 PAD = 16
+LINES = 8
 VMEM_LIMIT = 28 << 20
 ALL = ("yl", "core", "x", "z", "yh")
 
@@ -30,11 +30,7 @@
 
 
 def next_section():
-    pairs = []
-    for z in range(8):
-        if z % 4:
-            pairs.append((z, z - 1))
-    return pairs
+    return [(z, (z - 1) % 8) for z in range(8)]
 
 
 def along(stage, shift):
@@ -86,6 +82,12 @@
     return high.astype(jnp.bfloat16), (value - high).astype(jnp.bfloat16)
 
 
+def three_parts(value):
+    high = lax.reduce_precision(value, 8, 7)
+    middle = lax.reduce_precision(value - high, 8, 7)
+    return [part.astype(jnp.bfloat16) for part in (high, middle, value - high - middle)]
+
+
 def row_norm(x_ref):
     inputs = x_ref[...].astype(jnp.float32)
     rscale = lax.rsqrt(jnp.mean(inputs * inputs, axis=1, keepdims=True) + 1e-06)
@@ -93,77 +95,71 @@
 
 
 def activation_kernel(
-    x_ref, gain_ref, select_ref, b0, b1, b2, b3, w_in_ref, w_out_ref, normed_ref, hidden_ref, slope_ref
+    x_ref, gain_ref, select_ref, b0, b1, w_in_ref, w_out_ref, normed_ref, hidden_ref, slope_ref
 ):
-    blocks = (b0, b1, b2, b3)
-    step = b0.shape[0] // SIDE
-    rows = (step - PAD) // 2
-    half = 2 * SIDE * SIDE * (rows // 2)
-    extras = []
-    for n, block in enumerate(blocks):
+    rows = (b0.shape[0] // SIDE - LINES) // 2
+    for n, block in enumerate((b0, b1)):
         for k in range(SIDE):
             to = pl.ds((n * SIDE + k) * rows, rows)
-            w_in_ref[to, :] = block[pl.ds(k * step, rows), :]
-            w_out_ref[to, :] = block[pl.ds(k * step + rows, rows), :]
-            extras.append(block[pl.ds(k * step + 2 * rows, PAD), :])
+            w_in_ref[to, :] = block[pl.ds(2 * k * rows, rows), :]
+            w_out_ref[to, :] = block[pl.ds((2 * k + 1) * rows, rows), :]
     _, unit = row_norm(x_ref)
     normed = (unit * gain_ref[...]).astype(jnp.bfloat16)
     normed_ref[...] = normed
-    extras = jnp.concatenate(extras, axis=0)
-    for at in range(0, half, TILE):
-        cols = pl.ds(at, TILE)
-        spread = dot_plain(extras, select_ref[:, cols])
-        line = lax.broadcasted_iota(jnp.int32, spread.shape, 0)
-        shard = (lax.broadcasted_iota(jnp.int32, spread.shape, 1) + at) // (rows // 2)
-        mine = (line // PAD * 2 + line % PAD == shard) & (line % PAD < 2)
-        cond = jnp.sum(jnp.where(mine, spread, 0.0), axis=0, keepdims=True)
-        pre = dot_rows(normed, w_in_ref[cols, :]) + cond
-        sig = jax.nn.sigmoid(pre)
-        hidden_ref[:, cols] = (pre * sig).astype(jnp.bfloat16)
-        slope_ref[:, cols] = sig * (1.0 + pre * (1.0 - sig))
-
-
-def turn_body(g_ref, x_ref, gain_ref, halves, keep):
+    tail = pl.ds(2 * SIDE * rows, SIDE * LINES)
+    extras = jnp.concatenate([b0[tail, :], b1[tail, :]], axis=0)
+    spread = dot_plain(extras, select_ref[...])
+    line = lax.broadcasted_iota(jnp.int32, spread.shape, 0)
+    shard = lax.broadcasted_iota(jnp.int32, spread.shape, 1) // (rows // 2)
+    mine = (line // LINES * 2 + line % LINES == shard) & (line % LINES < 2)
+    cond = jnp.sum(jnp.where(mine, spread, 0.0), axis=0, keepdims=True)
+    pre = dot_rows(normed, w_in_ref[...]) + cond
+    sig = jax.nn.sigmoid(pre)
+    hidden_ref[...] = (pre * sig).astype(jnp.bfloat16)
+    slope_ref[...] = sig * (1.0 + pre * (1.0 - sig))
+
+
+def turn_body(g_ref, x_ref, gain_ref, quarters):
     grad = g_ref[...]
     total = None
-    for w_in_ref, w_out_ref, slope_ref, pg_ref in halves:
-        for at in range(0, w_in_ref.shape[0], TILE):
-            cols = pl.ds(at, TILE)
-            pre_grad = (dot_rows(grad, w_out_ref[cols, :]) * slope_ref[:, cols]).astype(
-                jnp.bfloat16
-            )
-            if keep:
-                pg_ref[:, cols] = pre_grad
-            term = dot_plain(pre_grad, w_in_ref[cols, :])
-            total = term if total is None else total + term
+    pre_grads = []
+    for w_in_ref, w_out_ref, slope_ref in quarters:
+        pre_grad = dot_rows(grad, w_out_ref[...]) * slope_ref[...]
+        pre_grads.append(pre_grad.astype(jnp.bfloat16))
+        term = dot_plain(pre_grads[-1], w_in_ref[...])
+        total = term if total is None else total + term
     rscale, unit = row_norm(x_ref)
     scaled = total * gain_ref[...]
     inner = jnp.mean(scaled * unit, axis=1, keepdims=True)
     grad_in = grad.astype(jnp.float32) + rscale * (scaled - unit * inner)
-    return grad_in.astype(jnp.bfloat16), total * unit
-
-
-def turn_kernel(g, x, gain, wi_n, wo_n, sl_n, wi_f, wo_f, sl_f, out):
-    halves = ((wi_n, wo_n, sl_n, None), (wi_f, wo_f, sl_f, None))
-    out[...] = turn_body(g, x, gain, halves, False)[0]
-
-
-def last_turn_kernel(
-    g, x, gain, wi_n, wo_n, sl_n, wi_f, wo_f, sl_f, normed, out, gain_out, pg_n, pg_f, far_out
-):
-    halves = ((wi_n, wo_n, sl_n, pg_n), (wi_f, wo_f, sl_f, pg_f))
-    grad_in, terms = turn_body(g, x, gain, halves, True)
+    return grad_in.astype(jnp.bfloat16), total * unit, pre_grads
+
+
+def turn_kernel(g, x, gain, *refs):
+    quarters = [refs[i : i + 3] for i in range(0, 12, 3)]
+    refs[12][...] = turn_body(g, x, gain, quarters)[0]
+
+
+def last_turn_kernel(g, x, gain, *refs):
+    quarters = [refs[i : i + 3] for i in range(0, 12, 3)]
+    normed, out, gain_out, near_0, near_1, far_out = refs[12:]
+    grad_in, terms, pre_grads = turn_body(g, x, gain, quarters)
     out[...] = grad_in
     gain_out[...] = jnp.sum(terms, axis=0, keepdims=True)
-    for at in range(0, pg_f.shape[1], TILE):
-        cols = pl.ds(at, TILE)
-        far_out[cols, :] = dot_first(pg_f[:, cols], normed[...]).astype(jnp.bfloat16)
-
-
-def outer_kernel(left, right, out):
-    for at in range(0, left.shape[1], TILE):
-        cols = pl.ds(at, TILE)
-        out[cols, :] = dot_first(left[:, cols], right[...]).astype(jnp.bfloat16)
+    near_0[...], near_1[...] = pre_grads[:2]
+    for n, pre_grad in enumerate(pre_grads[2:]):
+        rows = pl.ds(n * pre_grad.shape[1], pre_grad.shape[1])
+        far_out[rows, :] = dot_first(pre_grad, normed[...]).astype(jnp.bfloat16)
+
+
+def outer_kernel(left_0, left_1, right, out):
+    for n, left in enumerate((left_0, left_1)):
+        rows = pl.ds(n * left.shape[1], left.shape[1])
+        out[rows, :] = dot_first(left[...], right[...]).astype(jnp.bfloat16)
+
+
+def copy_kernel(value, out):
+    out[...] = value[...]
 
 
 def high_low_rows(value):
@@ -173,15 +169,19 @@
     return rows.astype(jnp.bfloat16)
 
 
-def near_kernel(pg, normed, in_far, hidden, grad, out_far, gain_here, gain_there, *sums):
+def near_kernel(
+    pg_0, pg_1, normed, in_far, hidden_0, hidden_1, grad, out_far, gain_here, gain_there, *sums
+):
     rows = (sums[0].shape[0] - PAD) // SIDE // 2
-    for first, (left, right, far) in enumerate(((pg, normed, in_far), (hidden, grad, out_far))):
-        for at in range(0, left.shape[1], TILE):
-            cols = pl.ds(at, TILE)
-            total = dot_first(left[:, cols], right[...]) + far[cols, :].astype(jnp.float32)
+    products = (((pg_0, pg_1), normed, in_far), ((hidden_0, hidden_1), grad, out_far))
+    for first, (lefts, right, far) in enumerate(products):
+        for n, left in enumerate(lefts):
+            width = left.shape[1]
+            total = dot_first(left[...], right[...])
+            total = total + far[pl.ds(n * width, width), :].astype(jnp.float32)
             total = total.astype(jnp.bfloat16)
-            for k in range(TILE // rows):
-                peer = at // rows + k
+            for k in range(width // rows):
+                peer = n * width // rows + k
                 to = pl.ds((peer % SIDE * 2 + first) * rows, rows)
                 sums[peer // SIDE][to, :] = total[k * rows : (k + 1) * rows, :]
     gain = high_low_rows(gain_here[...] + gain_there[...])
@@ -240,12 +240,14 @@
     )
 
     one, two = (lax.ppermute(shard, COLUMN, home_to_work(flip)) for flip in (0, 1))
-    x_rows = lax.ppermute(checkpoints[0], COLUMN, home_to_work(0))
-    cot_rows = lax.ppermute(cotangent, COLUMN, home_to_work(0))
-    gain_row = lax.ppermute(gains, COLUMN, home_to_work(0))
-    one, two, x_rows, cot_rows, gain_row = lax.optimization_barrier(
-        (one, two, x_rows, cot_rows, gain_row)
-    )
+    packed = jnp.concatenate(
+        [checkpoints[0], cotangent, *three_parts(gains), jnp.zeros((PAD - 3, chan), bf16)], axis=0
+    )
+    packed = lax.ppermute(packed, COLUMN, home_to_work(0))
+    x_rows, cot_rows = packed[:rows], packed[rows : 2 * rows]
+    gain_row = packed[2 * rows : 2 * rows + 3].astype(f32)
+    gain_row = gain_row[0:1] + gain_row[1:2] + gain_row[2:3]
+
     chunk = jnp.concatenate(
         [
             one[:own],
@@ -254,18 +256,19 @@
             two[own : 2 * own],
             one[2 * own : 2 * own + 1],
             two[2 * own : 2 * own + 1],
-            jnp.zeros((PAD - 2, chan), bf16),
+            jnp.zeros((LINES - 2, chan), bf16),
         ],
         axis=0,
     )
+    chunks = [chunk] + [lax.ppermute(chunk, PLANE, along(1, k)) for k in range(1, SIDE)]
     quarter = jnp.concatenate(
-        [chunk] + [lax.ppermute(chunk, PLANE, along(1, k)) for k in range(1, SIDE)], axis=0
+        [part[: 4 * own] for part in chunks] + [part[4 * own :] for part in chunks], axis=0
     )
     near = [quarter] + [lax.ppermute(quarter, PLANE, along(2, k)) for k in range(1, SIDE)]
-    far = [across_cores(block) for block in near]
-
+
+    width = half // 2
     entry = jnp.arange(chan, dtype=jnp.int32)[:, None]
-    hidden_col = jnp.arange(half, dtype=jnp.int32)[None, :]
+    hidden_col = jnp.arange(width, dtype=jnp.int32)[None, :]
     select = (
         (entry % own == hidden_col % own) & (entry // own % SAMPLES == sample)
     ).astype(bf16)
@@ -274,45 +277,54 @@
     activate = kernel(
         activation_kernel,
         [
-            ((half, chan), bf16),
-            ((half, chan), bf16),
+            ((width, chan), bf16),
+            ((width, chan), bf16),
             ((rows, chan), bf16),
-            ((rows, half), bf16),
-            ((rows, half), f32),
+            ((rows, width), bf16),
+            ((rows, width), f32),
         ],
-        2 * flops,
-    )
-    wi_n, wo_n, normed, hidden_n, slope_n = activate(x_rows, gain_row, select, *near)
-    wi_f, wo_f, _, hidden_f, slope_f = activate(x_rows, gain_row, select, *far)
+        flops,
+    )
+    first_far = [across_cores(block) for block in near[:2]]
+    first = [activate(x_rows, gain_row, select, *blocks) for blocks in (near[:2], first_far)]
+    last_near, *first = lax.optimization_barrier((near[3], *first))
+    near, last_far = [near[2], last_near], [across_cores(near[2]), across_cores(last_near)]
+    second = [activate(x_rows, gain_row, select, *blocks) for blocks in (near, last_far)]
+    quarters = [first[0], second[0], first[1], second[1]]
+    normed = quarters[0][2]
+    hiddens = [quarter[3] for quarter in quarters]
+    held = [x_rows, gain_row]
+    for w_in_rows, w_out_rows, _, _, slope in quarters:
+        held += [w_in_rows, w_out_rows, slope]
 
     turn = kernel(turn_kernel, [((rows, chan), bf16)], 4 * flops)
-    held = (x_rows, gain_row, wi_n, wo_n, slope_n, wi_f, wo_f, slope_f)
     grad = jnp.where(section == 3, cot_rows, jnp.zeros_like(cot_rows))
     kept = grad
     for _ in range(3):
         grad = lax.ppermute(turn(grad, *held), "z", next_section())
         kept = kept + grad
 
-    far_out = kernel(outer_kernel, [((half, chan), bf16)], flops)(hidden_f, kept)
+    far_out = kernel(outer_kernel, [((half, chan), bf16)], flops)(*hiddens[2:], kept)
     recv_out = across_cores(far_out)
     last_turn = kernel(
         last_turn_kernel,
         [
             ((rows, chan), bf16),
             ((1, chan), f32),
-            ((rows, half), bf16),
-            ((rows, half), bf16),
+            ((rows, width), bf16),
+            ((rows, width), bf16),
             ((half, chan), bf16),
         ],
         5 * flops,
     )
-    grad_in, gain_part, pg_n, _, far_in = last_turn(kept, *held, normed)
+    grad_in, gain_part, pg_0, pg_1, far_in = last_turn(kept, *held, normed)
     recv_in = across_cores(far_in)
     gain_there = across_cores(gain_part)
     sums = kernel(near_kernel, [((SIDE * 4 * own + PAD, chan), bf16)] * SIDE, 2 * flops)(
-        pg_n, normed, recv_in, hidden_n, kept, recv_out, gain_part, gain_there
+        pg_0, pg_1, normed, recv_in, *hiddens[:2], kept, recv_out, gain_part, gain_there
     )
     grad_home = lax.ppermute(grad_in, COLUMN, work_to_home(0))
+    grad_home = kernel(copy_kernel, [((rows, chan), bf16)])(grad_home)
 
     parts = [sums[0]] + [
         lax.ppermute(sums[k], PLANE, along(2, SIDE - k)) for k in range(1, SIDE)
@@ -322,6 +334,7 @@
         lax.ppermute(sums[k], PLANE, along(1, SIDE - k)) for k in range(1, SIDE)
     ]
     total = sum(part.astype(f32) for part in parts)
+    total, grad_home = lax.optimization_barrier((total, grad_home))
     gain_lines = list(two_parts(total[4 * own : 4 * own + 1] + total[4 * own + 1 : 4 * own + 2]))
     gain_lines.append(jnp.zeros((6, chan), bf16))
     total = total.astype(bf16)

time: 165 us -> 159 us (0.964)
  waiting for transfers between devices: 74.3 us -> 57.7 us
  starting transfers between devices: 65.5 us -> 78.6 us
    ppermute x7, starting transfers between devices: 8.33 us -> 23.3 us  [across_cores(): return lax.ppermute(value, 'core', [(0, 1), (1, 0)])]
    ppermute x3, waiting for transfers between devices: 16.3 us -> 1.6 us  [on_device(): lax.ppermute(quarter, PLANE, along(2, k))]
    ppermute x3, waiting for transfers between devices: 16.7 us -> 8.05 us  [on_device(): grad = lax.ppermute(turn(grad, *held), 'z', next_section())]
    ppermute x3, starting transfers between devices: 3.88 us -> 9.71 us  [on_device(): grad = lax.ppermute(turn(grad, *held), 'z', next_section())]
    ppermute x3 -> x1, starting transfers between devices: 12.6 us -> 7.29 us  [on_device(): packed = lax.ppermute(packed, COLUMN, home_to_work(0))]
    ppermute x2, waiting for transfers between devices: 0.01 us -> 4.81 us  [on_device(): lax.ppermute(shard, COLUMN, home_to_work(flip))]
    ppermute x7, waiting for transfers between devices: 3.01 us -> 6.84 us  [across_cores(): return lax.ppermute(value, 'core', [(0, 1), (1, 0)])]
    ppermute x3 -> x1, waiting for transfers between devices: 3.81 us -> 0.01 us  [on_device(): packed = lax.ppermute(packed, COLUMN, home_to_work(0))]
  transfers between devices with their start and end apart: 30 -> 28, of which waited for: 15 -> 17; matrix products, arithmetic and copies ran while one was open for 2% -> 1% of each run, Pallas kernels for 3% -> 2%
where the time goes in v4:
time: 159 us; the launch traced here: 158 us
  starting transfers between devices  78.6 us (49%)
  waiting for transfers between devices  57.7 us (36%)
  Pallas kernels  14.9 us (9%)
  other arithmetic  3.6 us (2%)
    ppermute x7, starting transfers between devices, across_cores(): return lax.ppermute(value, 'core', [(0, 1), (1, 0)])  23.3 us
    ppermute x3, waiting for transfers between devices, on_device(): lax.ppermute(sums[k], PLANE, along(2, SIDE - k))  20.9 us
    pallas_call x12, Pallas kernels, call(): pl.pallas_call(body, out_shape=shapes, in_specs=[whole] * len(operands),...  14.9 us
    ppermute x2, starting transfers between devices, on_device(): lax.ppermute(shard, COLUMN, home_to_work(flip))  10.4 us
    ppermute x3, starting transfers between devices, on_device(): grad = lax.ppermute(turn(grad, *held), 'z', next_section())  9.71 us
    ppermute x3, waiting for transfers between devices, on_device(): grad = lax.ppermute(turn(grad, *held), 'z', next_section())  8.05 us
    ppermute x2, waiting for transfers between devices, on_device(): lax.ppermute(jnp.concatenate([total[flip * own:(flip + 1) * own], total[(...  7.91 us
    ppermute x1, starting transfers between devices, on_device(): packed = lax.ppermute(packed, COLUMN, home_to_work(0))  7.29 us
  transfers between devices with their start and end apart: 28, of which 17 were waited for; matrix products, arithmetic and copies ran while one was open for 1% of the time, Pallas kernels for 2%

profile of v4, /device:TPU:9, one launch (start us, length us, event | category | flops | bytes accessed | tf_op | source)
XLA Modules:
  0.0 158.4 jit_solution(12852837558840665894)
XLA Ops:
  3.7 6.1 %collective-permute-start.2 = (bf16[88,640]{1,0:T(8,128)(2,1)S(1)}, bf16[88,640]{1,0:T(8,128)(2,1)S(1)}, u32[]{:S(2)}, u32[]{:S(2)}) collective-permute-start(bf16[88,640]{1,0:T(8,128)(2,1)S(1)} %maximum_maximum_fusion), channel_id=1, source_target_pairs={{0,8},{1,9},{2,72},{3,73},{4,136},{5,137},{6,200},{7,201},{8,0},{9... | collective-permute-start | bytes 337928 | tf_op jit(solution)/shard_map/ppermute | solution.py:242
  9.8 4.2 %collective-permute-start.1 = (bf16[88,640]{1,0:T(8,128)(2,1)S(1)}, bf16[88,640]{1,0:T(8,128)(2,1)S(1)}, u32[]{:S(2)}, u32[]{:S(2)}) collective-permute-start(bf16[88,640]{1,0:T(8,128)(2,1)S(1)} %maximum_maximum_fusion), channel_id=1, source_target_pairs={{0,0},{1,1},{2,64},{3,65},{4,128},{5,129},{6,192},{7,193},{8,8},{9... | collective-permute-start | bytes 337928 | tf_op jit(solution)/shard_map/ppermute | solution.py:242
  14.0 3.5 %collective-permute-done.2 = bf16[88,640]{1,0:T(8,128)(2,1)S(1)} collective-permute-done((bf16[88,640]{1,0:T(8,128)(2,1)S(1)}, bf16[88,640]{1,0:T(8,128)(2,1)S(1)}, u32[]{:S(2)}, u32[]{:S(2)}) %collective-permute-start.2) | collective-permute-done | bytes 112672 | tf_op jit(solution)/shard_map/ppermute | solution.py:242
  19.1 2.2 %collective-permute-start.4 = (bf16[168,640]{1,0:T(8,128)(2,1)S(1)}, bf16[168,640]{1,0:T(8,128)(2,1)S(1)}, u32[]{:S(2)}, u32[]{:S(2)}) collective-permute-start(bf16[168,640]{1,0:T(8,128)(2,1)S(1)} %concatenate.32), channel_id=1, source_target_pairs={{0,32},{1,33},{16,48},{17,49},{32,0},{33,1},{48,16},{49,17},{64,65... | collective-permute-start | bytes 645128 | tf_op jit(solution)/shard_map/ppermute | solution.py:263
  21.4 2.0 %collective-permute-start.3 = (bf16[168,640]{1,0:T(8,128)(2,1)S(1)}, bf16[168,640]{1,0:T(8,128)(2,1)S(1)}, u32[]{:S(2)}, u32[]{:S(2)}) collective-permute-start(bf16[168,640]{1,0:T(8,128)(2,1)S(1)} %concatenate.32), channel_id=1, source_target_pairs={{0,16},{1,17},{16,32},{17,33},{32,48},{33,49},{48,0},{49,1},{64,19... | collective-permute-start | bytes 645128 | tf_op jit(solution)/shard_map/ppermute | solution.py:263
  23.9 3.0 %collective-permute-done.4 = bf16[168,640]{1,0:T(8,128)(2,1)S(1)} collective-permute-done((bf16[168,640]{1,0:T(8,128)(2,1)S(1)}, bf16[168,640]{1,0:T(8,128)(2,1)S(1)}, u32[]{:S(2)}, u32[]{:S(2)}) %collective-permute-start.4) | collective-permute-done | bytes 215072 | tf_op jit(solution)/shard_map/ppermute | solution.py:263
  30.1 7.3 %collective-permute-start = (bf16[272,640]{1,0:T(8,128)(2,1)S(1)}, bf16[272,640]{1,0:T(8,128)(2,1)S(1)}, u32[]{:S(2)}, u32[]{:S(2)}) collective-permute-start(bf16[272,640]{1,0:T(8,128)(2,1)S(1)} %concatenate.28), channel_id=1, source_target_pairs={{0,0},{1,1},{2,64},{3,65},{4,128},{5,129},{6,192},{7,193},{8,8},{9... | collective-permute-start | bytes 1044488 | tf_op jit(solution)/shard_map/ppermute | solution.py:246
  38.1 3.2 %collective-permute-start.8 = (bf16[672,640]{1,0:T(8,128)(2,1)S(1)}, bf16[672,640]{1,0:T(8,128)(2,1)S(1)}, u32[]{:S(2)}, u32[]{:S(2)}) collective-permute-start(bf16[672,640]{1,0:T(8,128)(2,1)S(1)} %concatenate.33.b0), channel_id=1, source_target_pairs={{0,64},{64,0},{1,65},{65,1},{2,66},{66,2},{3,67},{67,3},{4,68},{68... | collective-permute-start | bytes 2580488 | tf_op jit(solution)/shard_map/ppermute | solution.py:50
  42.9 13.4 %collective-permute-start.9 = (bf16[672,640]{1,0:T(8,128)(2,1)S(1)}, bf16[672,640]{1,0:T(8,128)(2,1)S(1)}, u32[]{:S(2)}, u32[]{:S(2)}) collective-permute-start(bf16[672,640]{1,0:T(8,128)(2,1)S(1)} %collective-permute-done.7.b1), channel_id=1, source_target_pairs={{0,64},{64,0},{1,65},{65,1},{2,66},{66,2},{3,67},{67,3},{4,68},{68... | collective-permute-start | bytes 2580488 | tf_op jit(solution)/shard_map/ppermute | solution.py:50
  59.4 3.0 %collective-permute-start.12 = (bf16[672,640]{1,0:T(8,128)(2,1)S(1)}, bf16[672,640]{1,0:T(8,128)(2,1)S(1)}, u32[]{:S(2)}, u32[]{:S(2)}) collective-permute-start(bf16[672,640]{1,0:T(8,128)(2,1)S(1)} %collective-permute-done.6.b1), channel_id=1, source_target_pairs={{0,64},{64,0},{1,65},{65,1},{2,66},{66,2},{3,67},{67,3},{4,68},{68... | collective-permute-start | bytes 2580488 | tf_op jit(solution)/shard_map/ppermute | solution.py:50
  65.5 2.0 %shard_map.124 = bf16[128,640]{1,0:T(8,128)(2,1)S(1)} custom-call(bf16[128,640]{1,0:T(8,128)(2,1)S(1)} %get-tuple-element.91.g, bf16[128,640]{1,0:T(8,128)(2,1)S(1)} %get-tuple-element.90.x_ref.x, f32[1,640]{1,0:T(1,128)S(1)} %slice_add_fusion.1.gain_ref.gain, bf16[640,640]{1,0:T(8,128)(2,1)S(1)} %get-tuple-element.55.refs_0_, ...), custom_call_target="tpu_custom_call" | custom-call | flops 838860800 | bytes 4194304 | tf_op jit(solution)/shard_map/pallas_call | solution.py:210
  67.5 3.0 %collective-permute-start.13 = (bf16[128,640]{1,0:T(8,128)(2,1)S(1)}, bf16[128,640]{1,0:T(8,128)(2,1)S(1)}, u32[]{:S(2)}, u32[]{:S(2)}) collective-permute-start(bf16[128,640]{1,0:T(8,128)(2,1)S(1)} %shard_map.124), channel_id=1, source_target_pairs={{0,14},{2,0},{4,2},{6,4},{8,6},{10,8},{12,10},{14,12},{1,15},{3,1}... | collective-permute-start | bytes 491528 | tf_op jit(solution)/shard_map/ppermute | solution.py:304
  70.5 3.2 %collective-permute-done.13.g = bf16[128,640]{1,0:T(8,128)(2,1)S(1)} collective-permute-done((bf16[128,640]{1,0:T(8,128)(2,1)S(1)}, bf16[128,640]{1,0:T(8,128)(2,1)S(1)}, u32[]{:S(2)}, u32[]{:S(2)}) %collective-permute-start.13) | collective-permute-done | bytes 163872 | tf_op jit(solution)/shard_map/ppermute | solution.py:304
  73.7 2.0 %shard_map.125 = bf16[128,640]{1,0:T(8,128)(2,1)S(1)} custom-call(bf16[128,640]{1,0:T(8,128)(2,1)S(1)} %collective-permute-done.13.g, bf16[128,640]{1,0:T(8,128)(2,1)S(1)} %get-tuple-element.90.x_ref.x, f32[1,640]{1,0:T(1,128)S(1)} %slice_add_fusion.1.gain_ref.gain, bf16[640,640]{1,0:T(8,128)(2,1)S(1)} %get-tuple-element.55.refs_0_, ...), custom_call_target="tpu_custom_call" | custom-call | flops 838860800 | bytes 4194304 | tf_op jit(solution)/shard_map/pallas_call | solution.py:210
  75.7 3.5 %collective-permute-start.14 = (bf16[128,640]{1,0:T(8,128)(2,1)S(1)}, bf16[128,640]{1,0:T(8,128)(2,1)S(1)}, u32[]{:S(2)}, u32[]{:S(2)}) collective-permute-start(bf16[128,640]{1,0:T(8,128)(2,1)S(1)} %shard_map.125), channel_id=1, source_target_pairs={{0,14},{2,0},{4,2},{6,4},{8,6},{10,8},{12,10},{14,12},{1,15},{3,1}... | collective-permute-start | bytes 491528 | tf_op jit(solution)/shard_map/ppermute | solution.py:304
  79.2 2.6 %collective-permute-done.14.g = bf16[128,640]{1,0:T(8,128)(2,1)S(1)} collective-permute-done((bf16[128,640]{1,0:T(8,128)(2,1)S(1)}, bf16[128,640]{1,0:T(8,128)(2,1)S(1)}, u32[]{:S(2)}, u32[]{:S(2)}) %collective-permute-start.14) | collective-permute-done | bytes 163872 | tf_op jit(solution)/shard_map/ppermute | solution.py:304
  81.8 2.0 %shard_map.126 = bf16[128,640]{1,0:T(8,128)(2,1)S(1)} custom-call(bf16[128,640]{1,0:T(8,128)(2,1)S(1)} %collective-permute-done.14.g, bf16[128,640]{1,0:T(8,128)(2,1)S(1)} %get-tuple-element.90.x_ref.x, f32[1,640]{1,0:T(1,128)S(1)} %slice_add_fusion.1.gain_ref.gain, bf16[640,640]{1,0:T(8,128)(2,1)S(1)} %get-tuple-element.55.refs_0_, ...), custom_call_target="tpu_custom_call" | custom-call | flops 838860800 | bytes 4194304 | tf_op jit(solution)/shard_map/pallas_call | solution.py:210
  83.8 3.2 %collective-permute-start.15 = (bf16[128,640]{1,0:T(8,128)(2,1)S(1)}, bf16[128,640]{1,0:T(8,128)(2,1)S(1)}, u32[]{:S(2)}, u32[]{:S(2)}) collective-permute-start(bf16[128,640]{1,0:T(8,128)(2,1)S(1)} %shard_map.126), channel_id=1, source_target_pairs={{0,14},{2,0},{4,2},{6,4},{8,6},{10,8},{12,10},{14,12},{1,15},{3,1}... | collective-permute-start | bytes 491528 | tf_op jit(solution)/shard_map/ppermute | solution.py:304
  87.0 2.3 %collective-permute-done.15 = bf16[128,640]{1,0:T(8,128)(2,1)S(1)} collective-permute-done((bf16[128,640]{1,0:T(8,128)(2,1)S(1)}, bf16[128,640]{1,0:T(8,128)(2,1)S(1)}, u32[]{:S(2)}, u32[]{:S(2)}) %collective-permute-start.15) | collective-permute-done | bytes 163872 | tf_op jit(solution)/shard_map/ppermute | solution.py:304
  89.3 2.3 %shard_map.127 = (bf16[128,640]{1,0:T(8,128)(2,1)S(1)}, f32[1,640]{1,0:T(1,128)S(1)}, bf16[128,640]{1,0:T(8,128)(2,1)S(1)}, bf16[128,640]{1,0:T(8,128)(2,1)S(1)}, bf16[1280,640]{1,0:T(8,128)(2,1)S(1)}) custom-call(bf16[128,640]{1,0:T(8,128)(2,1)S(1)} %add_add_fusion.g.right.grad, bf16[128,640]{1,0:T(8,128)(2,1)S(1)} %get-tuple-element.90.x_ref.x, ...), custom_call_target="tpu_custom_call" | custom-call | flops 1048576000 | bytes 4194304 | tf_op jit(solution)/shard_map/pallas_call | solution.py:210
  92.3 3.0 %collective-permute-start.17 = (bf16[1280,640]{1,0:T(8,128)(2,1)S(1)}, bf16[1280,640]{1,0:T(8,128)(2,1)S(1)}, u32[]{:S(2)}, u32[]{:S(2)}) collective-permute-start(bf16[1280,640]{1,0:T(8,128)(2,1)S(1)} %shard_map.128), channel_id=1, source_target_pairs={{0,64},{64,0},{1,65},{65,1},{2,66},{66,2},{3,67},{67,3},{4,68},{68... | collective-permute-start | bytes 4915208 | tf_op jit(solution)/shard_map/ppermute | solution.py:50
  95.8 5.0 %collective-permute-done.18.gain_there = f32[1,640]{1,0:T(1,128)S(1)} collective-permute-done((f32[1,640]{1,0:T(1,128)S(1)}, f32[1,640]{1,0:T(1,128)S(1)}, u32[]{:S(2)}, u32[]{:S(2)}) %collective-permute-start.18) | collective-permute-done | bytes 2592 | tf_op jit(solution)/shard_map/ppermute | solution.py:50
  101.8 1.7 %collective-permute-start.19 = (bf16[656,640]{1,0:T(8,128)(2,1)S(1)}, bf16[656,640]{1,0:T(8,128)(2,1)S(1)}, u32[]{:S(2)}, u32[]{:S(2)}) collective-permute-start(bf16[656,640]{1,0:T(8,128)(2,1)S(1)} %get-tuple-element.78), channel_id=1, source_target_pairs={{0,129},{1,128},{16,145},{17,144},{32,161},{33,160},{48,177},{49,1... | collective-permute-start | bytes 2519048 | tf_op jit(solution)/shard_map/ppermute | solution.py:330
  104.7 17.4 %collective-permute-done.19.s1 = bf16[656,640]{1,0:T(8,128)(2,1)S(1)} collective-permute-done((bf16[656,640]{1,0:T(8,128)(2,1)S(1)}, bf16[656,640]{1,0:T(8,128)(2,1)S(1)}, u32[]{:S(2)}, u32[]{:S(2)}) %collective-permute-start.19) | collective-permute-done | bytes 839712 | tf_op jit(solution)/shard_map/ppermute | solution.py:330
  122.1 3.5 %collective-permute-done.21.s3 = bf16[656,640]{1,0:T(8,128)(2,1)S(1)} collective-permute-done((bf16[656,640]{1,0:T(8,128)(2,1)S(1)}, bf16[656,640]{1,0:T(8,128)(2,1)S(1)}, u32[]{:S(2)}, u32[]{:S(2)}) %collective-permute-start.21) | collective-permute-done | bytes 839712 | tf_op jit(solution)/shard_map/ppermute | solution.py:330
  126.1 4.4 %collective-permute-start.22 = (bf16[176,640]{1,0:T(8,128)(2,1)S(1)}, bf16[176,640]{1,0:T(8,128)(2,1)S(1)}, u32[]{:S(2)}, u32[]{:S(2)}) collective-permute-start(bf16[176,640]{1,0:T(8,128)(2,1)S(1)} %get-tuple-element.82), channel_id=1, source_target_pairs={{0,48},{1,49},{16,0},{17,1},{32,16},{33,17},{48,32},{49,33},{64,19... | collective-permute-start | bytes 675848 | tf_op jit(solution)/shard_map/ppermute | solution.py:334
  131.8 6.7 %collective-permute-start.25 = (bf16[128,640]{1,0:T(8,128)(2,1)S(1)}, bf16[128,640]{1,0:T(8,128)(2,1)S(1)}, u32[]{:S(2)}, u32[]{:S(2)}) collective-permute-start(bf16[128,640]{1,0:T(8,128)(2,1)S(1)} %get-tuple-element.85), channel_id=1, source_target_pairs={{0,0},{1,1},{64,2},{65,3},{128,4},{129,5},{192,6},{193,7},{8,8},{9... | collective-permute-start | bytes 491528 | tf_op jit(solution)/shard_map/ppermute | solution.py:326
  138.4 3.0 %collective-permute-done.25.value = bf16[128,640]{1,0:T(8,128)(2,1)S(1)} collective-permute-done((bf16[128,640]{1,0:T(8,128)(2,1)S(1)}, bf16[128,640]{1,0:T(8,128)(2,1)S(1)}, u32[]{:S(2)}, u32[]{:S(2)}) %collective-permute-start.25) | collective-permute-done | bytes 163872 | tf_op jit(solution)/shard_map/ppermute | solution.py:326
  142.4 4.7 %collective-permute-start.27 = (bf16[88,640]{1,0:T(8,128)(2,1)S(1)}, bf16[88,640]{1,0:T(8,128)(2,1)S(1)}, u32[]{:S(2)}, u32[]{:S(2)}) collective-permute-start(bf16[88,640]{1,0:T(8,128)(2,1)S(1)} %concatenate.35), channel_id=1, source_target_pairs={{8,0},{9,1},{72,2},{73,3},{136,4},{137,5},{200,6},{201,7},{0,8},{1... | collective-permute-start | bytes 337928 | tf_op jit(solution)/shard_map/ppermute | solution.py:342
  147.2 1.9 %collective-permute-start.26 = (bf16[88,640]{1,0:T(8,128)(2,1)S(1)}, bf16[88,640]{1,0:T(8,128)(2,1)S(1)}, u32[]{:S(2)}, u32[]{:S(2)}) collective-permute-start(bf16[88,640]{1,0:T(8,128)(2,1)S(1)} %concatenate.34), channel_id=1, source_target_pairs={{0,0},{1,1},{64,2},{65,3},{128,4},{129,5},{192,6},{193,7},{8,8},{9... | collective-permute-start | bytes 337928 | tf_op jit(solution)/shard_map/ppermute | solution.py:342
  149.1 4.5 %collective-permute-done.27 = bf16[88,640]{1,0:T(8,128)(2,1)S(1)} collective-permute-done((bf16[88,640]{1,0:T(8,128)(2,1)S(1)}, bf16[88,640]{1,0:T(8,128)(2,1)S(1)}, u32[]{:S(2)}, u32[]{:S(2)}) %collective-permute-start.27) | collective-permute-done | bytes 112672 | tf_op jit(solution)/shard_map/ppermute | solution.py:342
  153.6 3.4 %collective-permute-done.26 = bf16[88,640]{1,0:T(8,128)(2,1)S(1)} collective-permute-done((bf16[88,640]{1,0:T(8,128)(2,1)S(1)}, bf16[88,640]{1,0:T(8,128)(2,1)S(1)}, u32[]{:S(2)}, u32[]{:S(2)}) %collective-permute-start.26) | collective-permute-done | bytes 112672 | tf_op jit(solution)/shard_map/ppermute | solution.py:342
  (87 shorter events, 24.0 us)
Async XLA Ops:
  0.6 1.7 %copy-start = (bf16[1,256,40]{1,2,0:T(8,128)(2,1)S(1)}, bf16[1,256,40]{1,2,0:T(8,128)(2,1)}, u32[]{:S(2)}) copy-start(bf16[1,256,40]{1,2,0:T(8,128)(2,1)} %param.14) | copy-start | bytes 61444
  3.7 13.9 %collective-permute-start.2 = (bf16[88,640]{1,0:T(8,128)(2,1)S(1)}, bf16[88,640]{1,0:T(8,128)(2,1)S(1)}, u32[]{:S(2)}, u32[]{:S(2)}) collective-permute-start(bf16[88,640]{1,0:T(8,128)(2,1)S(1)} %maximum_maximum_fusion), channel_id=1, source_target_pairs={{0,8},{1,9},{2,72},{3,73},{4,136},{5,137},{6,200},{7,201},{8,0},{9... | collective-permute-start | bytes 337928 | tf_op jit(solution)/shard_map/ppermute | solution.py:242
  9.8 9.1 %collective-permute-start.1 = (bf16[88,640]{1,0:T(8,128)(2,1)S(1)}, bf16[88,640]{1,0:T(8,128)(2,1)S(1)}, u32[]{:S(2)}, u32[]{:S(2)}) collective-permute-start(bf16[88,640]{1,0:T(8,128)(2,1)S(1)} %maximum_maximum_fusion), channel_id=1, source_target_pairs={{0,0},{1,1},{2,64},{3,65},{4,128},{5,129},{6,192},{7,193},{8,8},{9... | collective-permute-start | bytes 337928 | tf_op jit(solution)/shard_map/ppermute | solution.py:242
  18.9 10.8 %copy-start.3 = (f32[1,640]{1,0:T(1,128)S(1)}, f32[1,640]{1,0:T(1,128)}, u32[]{:S(2)}) copy-start(f32[1,640]{1,0:T(1,128)} %param.11) | copy-start | bytes 7684
  18.9 10.8 %copy-start.1 = (bf16[1,128,640]{2,1,0:T(8,128)(2,1)S(1)}, bf16[1,128,640]{2,1,0:T(8,128)(2,1)}, u32[]{:S(2)}) copy-start(bf16[1,128,640]{2,1,0:T(8,128)(2,1)} %param.9) | copy-start | bytes 491524
  18.9 10.8 %copy-start.2 = (bf16[128,640]{1,0:T(8,128)(2,1)S(1)}, bf16[128,640]{1,0:T(8,128)(2,1)}, u32[]{:S(2)}) copy-start(bf16[128,640]{1,0:T(8,128)(2,1)} %param.10) | copy-start | bytes 491524
  19.0 4.8 %collective-permute-start.5 = (bf16[168,640]{1,0:T(8,128)(2,1)S(1)}, bf16[168,640]{1,0:T(8,128)(2,1)S(1)}, u32[]{:S(2)}, u32[]{:S(2)}) collective-permute-start(bf16[168,640]{1,0:T(8,128)(2,1)S(1)} %concatenate.32), channel_id=1, source_target_pairs={{0,48},{1,49},{16,0},{17,1},{32,16},{33,17},{48,32},{49,33},{64,19... | collective-permute-start | bytes 645128 | tf_op jit(solution)/shard_map/ppermute | solution.py:263
  19.1 7.7 %collective-permute-start.4 = (bf16[168,640]{1,0:T(8,128)(2,1)S(1)}, bf16[168,640]{1,0:T(8,128)(2,1)S(1)}, u32[]{:S(2)}, u32[]{:S(2)}) collective-permute-start(bf16[168,640]{1,0:T(8,128)(2,1)S(1)} %concatenate.32), channel_id=1, source_target_pairs={{0,32},{1,33},{16,48},{17,49},{32,0},{33,1},{48,16},{49,17},{64,65... | collective-permute-start | bytes 645128 | tf_op jit(solution)/shard_map/ppermute | solution.py:263
  21.4 6.5 %collective-permute-start.3 = (bf16[168,640]{1,0:T(8,128)(2,1)S(1)}, bf16[168,640]{1,0:T(8,128)(2,1)S(1)}, u32[]{:S(2)}, u32[]{:S(2)}) collective-permute-start(bf16[168,640]{1,0:T(8,128)(2,1)S(1)} %concatenate.32), channel_id=1, source_target_pairs={{0,16},{1,17},{16,32},{17,33},{32,48},{33,49},{48,0},{49,1},{64,19... | collective-permute-start | bytes 645128 | tf_op jit(solution)/shard_map/ppermute | solution.py:263
  28.4 14.5 %collective-permute-start.7 = (bf16[672,640]{1,0:T(8,128)(2,1)S(1)}, bf16[672,640]{1,0:T(8,128)(2,1)S(1)}, u32[]{:S(2)}, u32[]{:S(2)}) collective-permute-start(bf16[672,640]{1,0:T(8,128)(2,1)S(1)} %concatenate.33.b0), channel_id=1, source_target_pairs={{0,128},{1,129},{16,144},{17,145},{32,160},{33,161},{48,176},{49,1... | collective-permute-start | bytes 2580488 | tf_op jit(solution)/shard_map/ppermute | solution.py:267
  30.1 26.5 %collective-permute-start = (bf16[272,640]{1,0:T(8,128)(2,1)S(1)}, bf16[272,640]{1,0:T(8,128)(2,1)S(1)}, u32[]{:S(2)}, u32[]{:S(2)}) collective-permute-start(bf16[272,640]{1,0:T(8,128)(2,1)S(1)} %concatenate.28), channel_id=1, source_target_pairs={{0,0},{1,1},{2,64},{3,65},{4,128},{5,129},{6,192},{7,193},{8,8},{9... | collective-permute-start | bytes 1044488 | tf_op jit(solution)/shard_map/ppermute | solution.py:246
  37.5 19.3 %collective-permute-start.10 = (bf16[672,640]{1,0:T(8,128)(2,1)S(1)}, bf16[672,640]{1,0:T(8,128)(2,1)S(1)}, u32[]{:S(2)}, u32[]{:S(2)}) collective-permute-start(bf16[672,640]{1,0:T(8,128)(2,1)S(1)} %concatenate.33.b0), channel_id=1, source_target_pairs={{0,1},{1,0},{16,17},{17,16},{32,33},{33,32},{48,49},{49,48},{64,96... | collective-permute-start | bytes 2580488 | tf_op jit(solution)/shard_map/ppermute | solution.py:267
  38.1 19.4 %collective-permute-start.8 = (bf16[672,640]{1,0:T(8,128)(2,1)S(1)}, bf16[672,640]{1,0:T(8,128)(2,1)S(1)}, u32[]{:S(2)}, u32[]{:S(2)}) collective-permute-start(bf16[672,640]{1,0:T(8,128)(2,1)S(1)} %concatenate.33.b0), channel_id=1, source_target_pairs={{0,64},{64,0},{1,65},{65,1},{2,66},{66,2},{3,67},{67,3},{4,68},{68... | collective-permute-start | bytes 2580488 | tf_op jit(solution)/shard_map/ppermute | solution.py:50
  41.3 18.1 %collective-permute-start.6 = (bf16[672,640]{1,0:T(8,128)(2,1)S(1)}, bf16[672,640]{1,0:T(8,128)(2,1)S(1)}, u32[]{:S(2)}, u32[]{:S(2)}) collective-permute-start(bf16[672,640]{1,0:T(8,128)(2,1)S(1)} %concatenate.33.b0), channel_id=1, source_target_pairs={{0,129},{1,128},{16,145},{17,144},{32,161},{33,160},{48,177},{49,1... | collective-permute-start | bytes 2580488 | tf_op jit(solution)/shard_map/ppermute | solution.py:267
  42.9 15.4 %collective-permute-start.9 = (bf16[672,640]{1,0:T(8,128)(2,1)S(1)}, bf16[672,640]{1,0:T(8,128)(2,1)S(1)}, u32[]{:S(2)}, u32[]{:S(2)}) collective-permute-start(bf16[672,640]{1,0:T(8,128)(2,1)S(1)} %collective-permute-done.7.b1), channel_id=1, source_target_pairs={{0,64},{64,0},{1,65},{65,1},{2,66},{66,2},{3,67},{67,3},{4,68},{68... | collective-permute-start | bytes 2580488 | tf_op jit(solution)/shard_map/ppermute | solution.py:50
  56.7 6.7 %collective-permute-start.11 = (bf16[672,640]{1,0:T(8,128)(2,1)S(1)}, bf16[672,640]{1,0:T(8,128)(2,1)S(1)}, u32[]{:S(2)}, u32[]{:S(2)}) collective-permute-start(bf16[672,640]{1,0:T(8,128)(2,1)S(1)} %collective-permute-done.10.b0), channel_id=1, source_target_pairs={{0,64},{64,0},{1,65},{65,1},{2,66},{66,2},{3,67},{67,3},{4,68},{68... | collective-permute-start | bytes 2580488 | tf_op jit(solution)/shard_map/ppermute | solution.py:50
  59.4 5.0 %collective-permute-start.12 = (bf16[672,640]{1,0:T(8,128)(2,1)S(1)}, bf16[672,640]{1,0:T(8,128)(2,1)S(1)}, u32[]{:S(2)}, u32[]{:S(2)}) collective-permute-start(bf16[672,640]{1,0:T(8,128)(2,1)S(1)} %collective-permute-done.6.b1), channel_id=1, source_target_pairs={{0,64},{64,0},{1,65},{65,1},{2,66},{66,2},{3,67},{67,3},{4,68},{68... | collective-permute-start | bytes 2580488 | tf_op jit(solution)/shard_map/ppermute | solution.py:50
  67.5 6.2 %collective-permute-start.13 = (bf16[128,640]{1,0:T(8,128)(2,1)S(1)}, bf16[128,640]{1,0:T(8,128)(2,1)S(1)}, u32[]{:S(2)}, u32[]{:S(2)}) collective-permute-start(bf16[128,640]{1,0:T(8,128)(2,1)S(1)} %shard_map.124), channel_id=1, source_target_pairs={{0,14},{2,0},{4,2},{6,4},{8,6},{10,8},{12,10},{14,12},{1,15},{3,1}... | collective-permute-start | bytes 491528 | tf_op jit(solution)/shard_map/ppermute | solution.py:304
  75.7 6.1 %collective-permute-start.14 = (bf16[128,640]{1,0:T(8,128)(2,1)S(1)}, bf16[128,640]{1,0:T(8,128)(2,1)S(1)}, u32[]{:S(2)}, u32[]{:S(2)}) collective-permute-start(bf16[128,640]{1,0:T(8,128)(2,1)S(1)} %shard_map.125), channel_id=1, source_target_pairs={{0,14},{2,0},{4,2},{6,4},{8,6},{10,8},{12,10},{14,12},{1,15},{3,1}... | collective-permute-start | bytes 491528 | tf_op jit(solution)/shard_map/ppermute | solution.py:304
  83.8 5.5 %collective-permute-start.15 = (bf16[128,640]{1,0:T(8,128)(2,1)S(1)}, bf16[128,640]{1,0:T(8,128)(2,1)S(1)}, u32[]{:S(2)}, u32[]{:S(2)}) collective-permute-start(bf16[128,640]{1,0:T(8,128)(2,1)S(1)} %shard_map.126), channel_id=1, source_target_pairs={{0,14},{2,0},{4,2},{6,4},{8,6},{10,8},{12,10},{14,12},{1,15},{3,1}... | collective-permute-start | bytes 491528 | tf_op jit(solution)/shard_map/ppermute | solution.py:304
  92.3 8.5 %collective-permute-start.17 = (bf16[1280,640]{1,0:T(8,128)(2,1)S(1)}, bf16[1280,640]{1,0:T(8,128)(2,1)S(1)}, u32[]{:S(2)}, u32[]{:S(2)}) collective-permute-start(bf16[1280,640]{1,0:T(8,128)(2,1)S(1)} %shard_map.128), channel_id=1, source_target_pairs={{0,64},{64,0},{1,65},{65,1},{2,66},{66,2},{3,67},{67,3},{4,68},{68... | collective-permute-start | bytes 4915208 | tf_op jit(solution)/shard_map/ppermute | solution.py:50
  95.3 5.5 %collective-permute-start.16 = (bf16[1280,640]{1,0:T(8,128)(2,1)S(1)}, bf16[1280,640]{1,0:T(8,128)(2,1)S(1)}, u32[]{:S(2)}, u32[]{:S(2)}) collective-permute-start(bf16[1280,640]{1,0:T(8,128)(2,1)S(1)} %get-tuple-element.71), channel_id=1, source_target_pairs={{0,64},{64,0},{1,65},{65,1},{2,66},{66,2},{3,67},{67,3},{4,68},{68... | collective-permute-start | bytes 4915208 | tf_op jit(solution)/shard_map/ppermute | solution.py:50
  95.4 5.4 %collective-permute-start.18 = (f32[1,640]{1,0:T(1,128)S(1)}, f32[1,640]{1,0:T(1,128)S(1)}, u32[]{:S(2)}, u32[]{:S(2)}) collective-permute-start(f32[1,640]{1,0:T(1,128)S(1)} %get-tuple-element.76.gain_here), channel_id=1, source_target_pairs={{0,64},{64,0},{1,65},{65,1},{2,66},{66,2},{3,67},{67,3},{4,68},{68... | collective-permute-start | bytes 7688 | tf_op jit(solution)/shard_map/ppermute | solution.py:50
  101.8 20.2 %collective-permute-start.19 = (bf16[656,640]{1,0:T(8,128)(2,1)S(1)}, bf16[656,640]{1,0:T(8,128)(2,1)S(1)}, u32[]{:S(2)}, u32[]{:S(2)}) collective-permute-start(bf16[656,640]{1,0:T(8,128)(2,1)S(1)} %get-tuple-element.78), channel_id=1, source_target_pairs={{0,129},{1,128},{16,145},{17,144},{32,161},{33,160},{48,177},{49,1... | collective-permute-start | bytes 2519048 | tf_op jit(solution)/shard_map/ppermute | solution.py:330
  103.6 18.5 %collective-permute-start.20 = (bf16[656,640]{1,0:T(8,128)(2,1)S(1)}, bf16[656,640]{1,0:T(8,128)(2,1)S(1)}, u32[]{:S(2)}, u32[]{:S(2)}) collective-permute-start(bf16[656,640]{1,0:T(8,128)(2,1)S(1)} %get-tuple-element.79), channel_id=1, source_target_pairs={{0,1},{1,0},{16,17},{17,16},{32,33},{33,32},{48,49},{49,48},{64,96... | collective-permute-start | bytes 2519048 | tf_op jit(solution)/shard_map/ppermute | solution.py:330
  104.4 21.2 %collective-permute-start.21 = (bf16[656,640]{1,0:T(8,128)(2,1)S(1)}, bf16[656,640]{1,0:T(8,128)(2,1)S(1)}, u32[]{:S(2)}, u32[]{:S(2)}) collective-permute-start(bf16[656,640]{1,0:T(8,128)(2,1)S(1)} %get-tuple-element.80), channel_id=1, source_target_pairs={{0,128},{1,129},{16,144},{17,145},{32,160},{33,161},{48,176},{49,1... | collective-permute-start | bytes 2519048 | tf_op jit(solution)/shard_map/ppermute | solution.py:330
  126.1 16.0 %collective-permute-start.22 = (bf16[176,640]{1,0:T(8,128)(2,1)S(1)}, bf16[176,640]{1,0:T(8,128)(2,1)S(1)}, u32[]{:S(2)}, u32[]{:S(2)}) collective-permute-start(bf16[176,640]{1,0:T(8,128)(2,1)S(1)} %get-tuple-element.82), channel_id=1, source_target_pairs={{0,48},{1,49},{16,0},{17,1},{32,16},{33,17},{48,32},{49,33},{64,19... | collective-permute-start | bytes 675848 | tf_op jit(solution)/shard_map/ppermute | solution.py:334
  130.5 11.6 %collective-permute-start.23 = (bf16[176,640]{1,0:T(8,128)(2,1)S(1)}, bf16[176,640]{1,0:T(8,128)(2,1)S(1)}, u32[]{:S(2)}, u32[]{:S(2)}) collective-permute-start(bf16[176,640]{1,0:T(8,128)(2,1)S(1)} %get-tuple-element.83), channel_id=1, source_target_pairs={{0,32},{1,33},{16,48},{17,49},{32,0},{33,1},{48,16},{49,17},{64,65... | collective-permute-start | bytes 675848 | tf_op jit(solution)/shard_map/ppermute | solution.py:334
  130.5 11.6 %collective-permute-start.24 = (bf16[176,640]{1,0:T(8,128)(2,1)S(1)}, bf16[176,640]{1,0:T(8,128)(2,1)S(1)}, u32[]{:S(2)}, u32[]{:S(2)}) collective-permute-start(bf16[176,640]{1,0:T(8,128)(2,1)S(1)} %get-tuple-element.84), channel_id=1, source_target_pairs={{0,16},{1,17},{16,32},{17,33},{32,48},{33,49},{48,0},{49,1},{64,19... | collective-permute-start | bytes 675848 | tf_op jit(solution)/shard_map/ppermute | solution.py:334
  131.8 9.7 %collective-permute-start.25 = (bf16[128,640]{1,0:T(8,128)(2,1)S(1)}, bf16[128,640]{1,0:T(8,128)(2,1)S(1)}, u32[]{:S(2)}, u32[]{:S(2)}) collective-permute-start(bf16[128,640]{1,0:T(8,128)(2,1)S(1)} %get-tuple-element.85), channel_id=1, source_target_pairs={{0,0},{1,1},{64,2},{65,3},{128,4},{129,5},{192,6},{193,7},{8,8},{9... | collective-permute-start | bytes 491528 | tf_op jit(solution)/shard_map/ppermute | solution.py:326
  142.4 11.2 %collective-permute-start.27 = (bf16[88,640]{1,0:T(8,128)(2,1)S(1)}, bf16[88,640]{1,0:T(8,128)(2,1)S(1)}, u32[]{:S(2)}, u32[]{:S(2)}) collective-permute-start(bf16[88,640]{1,0:T(8,128)(2,1)S(1)} %concatenate.35), channel_id=1, source_target_pairs={{8,0},{9,1},{72,2},{73,3},{136,4},{137,5},{200,6},{201,7},{0,8},{1... | collective-permute-start | bytes 337928 | tf_op jit(solution)/shard_map/ppermute | solution.py:342
  147.2 9.8 %collective-permute-start.26 = (bf16[88,640]{1,0:T(8,128)(2,1)S(1)}, bf16[88,640]{1,0:T(8,128)(2,1)S(1)}, u32[]{:S(2)}, u32[]{:S(2)}) collective-permute-start(bf16[88,640]{1,0:T(8,128)(2,1)S(1)} %concatenate.34), channel_id=1, source_target_pairs={{0,0},{1,1},{64,2},{65,3},{128,4},{129,5},{192,6},{193,7},{8,8},{9... | collective-permute-start | bytes 337928 | tf_op jit(solution)/shard_map/ppermute | solution.py:342

commit v5 on v4

--- a/solution.py
+++ b/solution.py
@@ -142,14 +142,12 @@
 
 def last_turn_kernel(g, x, gain, *refs):
     quarters = [refs[i : i + 3] for i in range(0, 12, 3)]
-    normed, out, gain_out, near_0, near_1, far_out = refs[12:]
+    out, gain_out = refs[12:14]
     grad_in, terms, pre_grads = turn_body(g, x, gain, quarters)
     out[...] = grad_in
     gain_out[...] = jnp.sum(terms, axis=0, keepdims=True)
-    near_0[...], near_1[...] = pre_grads[:2]
-    for n, pre_grad in enumerate(pre_grads[2:]):
-        rows = pl.ds(n * pre_grad.shape[1], pre_grad.shape[1])
-        far_out[rows, :] = dot_first(pre_grad, normed[...]).astype(jnp.bfloat16)
+    for ref, pre_grad in zip(refs[14:], pre_grads):
+        ref[...] = pre_grad
 
 
 def outer_kernel(left_0, left_1, right, out):
@@ -240,14 +238,6 @@
     )
 
     one, two = (lax.ppermute(shard, COLUMN, home_to_work(flip)) for flip in (0, 1))
-    packed = jnp.concatenate(
-        [checkpoints[0], cotangent, *three_parts(gains), jnp.zeros((PAD - 3, chan), bf16)], axis=0
-    )
-    packed = lax.ppermute(packed, COLUMN, home_to_work(0))
-    x_rows, cot_rows = packed[:rows], packed[rows : 2 * rows]
-    gain_row = packed[2 * rows : 2 * rows + 3].astype(f32)
-    gain_row = gain_row[0:1] + gain_row[1:2] + gain_row[2:3]
-
     chunk = jnp.concatenate(
         [
             one[:own],
@@ -264,6 +254,14 @@
     quarter = jnp.concatenate(
         [part[: 4 * own] for part in chunks] + [part[4 * own :] for part in chunks], axis=0
     )
+    packed = jnp.concatenate(
+        [checkpoints[0], cotangent, *three_parts(gains), jnp.zeros((PAD - 3, chan), bf16)], axis=0
+    )
+    packed = lax.ppermute(packed, COLUMN, home_to_work(0))
+    quarter, packed = lax.optimization_barrier((quarter, packed))
+    x_rows, cot_rows = packed[:rows], packed[rows : 2 * rows]
+    gain_row = packed[2 * rows : 2 * rows + 3].astype(f32)
+    gain_row = gain_row[0:1] + gain_row[1:2] + gain_row[2:3]
     near = [quarter] + [lax.ppermute(quarter, PLANE, along(2, k)) for k in range(1, SIDE)]
 
     width = half // 2
@@ -304,21 +302,18 @@
         grad = lax.ppermute(turn(grad, *held), "z", next_section())
         kept = kept + grad
 
-    far_out = kernel(outer_kernel, [((half, chan), bf16)], flops)(*hiddens[2:], kept)
+    outer = kernel(outer_kernel, [((half, chan), bf16)], flops)
+    far_out = outer(*hiddens[2:], kept)
+    kept, far_out = lax.optimization_barrier((kept, far_out))
     recv_out = across_cores(far_out)
     last_turn = kernel(
         last_turn_kernel,
-        [
-            ((rows, chan), bf16),
-            ((1, chan), f32),
-            ((rows, width), bf16),
-            ((rows, width), bf16),
-            ((half, chan), bf16),
-        ],
-        5 * flops,
-    )
-    grad_in, gain_part, pg_0, pg_1, far_in = last_turn(kept, *held, normed)
-    recv_in = across_cores(far_in)
+        [((rows, chan), bf16), ((1, chan), f32)] + [((rows, width), bf16)] * 4,
+        4 * flops,
+    )
+    grad_in, gain_part, pg_0, pg_1, *pg_far = last_turn(kept, *held)
+    *pg_far, recv_out = lax.optimization_barrier((*pg_far, recv_out))
+    recv_in = across_cores(outer(*pg_far, normed))
     gain_there = across_cores(gain_part)
     sums = kernel(near_kernel, [((SIDE * 4 * own + PAD, chan), bf16)] * SIDE, 2 * flops)(
         pg_0, pg_1, normed, recv_in, *hiddens[:2], kept, recv_out, gain_part, gain_there
@@ -329,12 +324,12 @@
     parts = [sums[0]] + [
         lax.ppermute(sums[k], PLANE, along(2, SIDE - k)) for k in range(1, SIDE)
     ]
+    *parts, grad_home = lax.optimization_barrier((*parts, grad_home))
     sums = kernel(stage_sum_kernel, [((4 * own + PAD, chan), bf16)] * SIDE)(*parts)
     parts = [sums[0]] + [
         lax.ppermute(sums[k], PLANE, along(1, SIDE - k)) for k in range(1, SIDE)
     ]
     total = sum(part.astype(f32) for part in parts)
-    total, grad_home = lax.optimization_barrier((total, grad_home))
     gain_lines = list(two_parts(total[4 * own : 4 * own + 1] + total[4 * own + 1 : 4 * own + 2]))
     gain_lines.append(jnp.zeros((6, chan), bf16))
     total = total.astype(bf16)

time: 159 us -> 161 us (1.013)
  starting transfers between devices: 78.6 us -> 69.6 us
  waiting for transfers between devices: 57.7 us -> 66.5 us
  local copies, waits for them, and re-layouts: 1.47 us -> 3.19 us
    ppermute x7, starting transfers between devices: 23.3 us -> 7.05 us  [across_cores(): return lax.ppermute(value, 'core', [(0, 1), (1, 0)])]
    ppermute x3, waiting for transfers between devices: 20.9 us -> 7.93 us  [on_device(): lax.ppermute(sums[k], PLANE, along(2, SIDE - k))]
    ppermute x3, waiting for transfers between devices: 1.6 us -> 13.9 us  [on_device(): lax.ppermute(quarter, PLANE, along(2, k))]
    ppermute x3, waiting for transfers between devices: 0.01 us -> 6.52 us  [on_device(): lax.ppermute(sums[k], PLANE, along(1, SIDE - k))]
    ppermute x3, waiting for transfers between devices: 4.53 us -> 10.6 us  [on_device(): lax.ppermute(chunk, PLANE, along(1, k))]
    ppermute x2, waiting for transfers between devices: 4.81 us -> 0.01 us  [on_device(): lax.ppermute(shard, COLUMN, home_to_work(flip))]
    ppermute x3, starting transfers between devices: 1.88 us -> 6.29 us  [on_device(): lax.ppermute(quarter, PLANE, along(2, k))]
    ppermute x2, starting transfers between devices: 6.66 us -> 10.8 us  [on_device(): lax.ppermute(jnp.concatenate([total[flip * own:(flip + 1) * own], total[(...]
  transfers between devices with their start and end apart: 28 -> 28, of which waited for: 17 -> 19; matrix products, arithmetic and copies ran while one was open for 1% -> 2% of each run, Pallas kernels for 2% -> 3%
where the time goes in v5:
time: 161 us
  starting transfers between devices  69.6 us (43%)
  waiting for transfers between devices  66.5 us (41%)
  Pallas kernels  15.1 us (9%)
  other arithmetic  4.27 us (3%)
  local copies, waits for them, and re-layouts  3.19 us (2%)
    pallas_call x13, Pallas kernels, call(): pl.pallas_call(body, out_shape=shapes, in_specs=[whole] * len(operands),...  15.1 us
    ppermute x3, waiting for transfers between devices, on_device(): lax.ppermute(quarter, PLANE, along(2, k))  13.9 us
    ppermute x2, starting transfers between devices, on_device(): lax.ppermute(jnp.concatenate([total[flip * own:(flip + 1) * own], total[(...  10.8 us
    ppermute x3, waiting for transfers between devices, on_device(): lax.ppermute(chunk, PLANE, along(1, k))  10.6 us
    ppermute x2, starting transfers between devices, on_device(): lax.ppermute(shard, COLUMN, home_to_work(flip))  10.4 us
    ppermute x3, starting transfers between devices, on_device(): grad = lax.ppermute(turn(grad, *held), 'z', next_section())  9.99 us
    ppermute x3, waiting for transfers between devices, on_device(): grad = lax.ppermute(turn(grad, *held), 'z', next_section())  9.92 us
    ppermute x2, waiting for transfers between devices, on_device(): lax.ppermute(jnp.concatenate([total[flip * own:(flip + 1) * own], total[(...  9.63 us
  transfers between devices with their start and end apart: 28, of which 19 were waited for; matrix products, arithmetic and copies ran while one was open for 2% of the time, Pallas kernels for 3%

profile of v5, /device:TPU:9, one launch (start us, length us, event | category | flops | bytes accessed | tf_op | source)
XLA Modules:
  0.0 160.8 jit_solution(15413684330976834301)
XLA Ops:
  3.7 6.1 %collective-permute-start.1 = (bf16[88,640]{1,0:T(8,128)(2,1)S(1)}, bf16[88,640]{1,0:T(8,128)(2,1)S(1)}, u32[]{:S(2)}, u32[]{:S(2)}) collective-permute-start(bf16[88,640]{1,0:T(8,128)(2,1)S(1)} %maximum_maximum_fusion), channel_id=1, source_target_pairs={{0,8},{1,9},{2,72},{3,73},{4,136},{5,137},{6,200},{7,201},{8,0},{9... | collective-permute-start | bytes 337928 | tf_op jit(solution)/shard_map/ppermute | solution.py:240
  9.8 4.2 %collective-permute-start = (bf16[88,640]{1,0:T(8,128)(2,1)S(1)}, bf16[88,640]{1,0:T(8,128)(2,1)S(1)}, u32[]{:S(2)}, u32[]{:S(2)}) collective-permute-start(bf16[88,640]{1,0:T(8,128)(2,1)S(1)} %maximum_maximum_fusion), channel_id=1, source_target_pairs={{0,0},{1,1},{2,64},{3,65},{4,128},{5,129},{6,192},{7,193},{8,8},{9... | collective-permute-start | bytes 337928 | tf_op jit(solution)/shard_map/ppermute | solution.py:240
  14.7 2.1 %concatenate.33 = bf16[272,640]{1,0:T(8,128)(2,1)S(1)} concatenate(bf16[128,640]{1,0:T(8,128)(2,1)} %bitcast.21, bf16[128,640]{1,0:T(8,128)(2,1)} %param.10, bf16[1,640]{1,0:T(2,128)(2,1)S(1)} %get-tuple-element.130, bf16[1,640]{1,0:T(2,128)(2,1)S(1)} %get-tuple-element.129, bf16[1,640]{1,0:T(2,128)(2,1)S(1)} %get-tuple-element.128, bf16[13,640]{1,0:T(8,128)(2,1)S(1)} %broadcast_in_dim.25), dimensions={0} | concatenate | bytes 696320 | tf_op jit(solution)/shard_map/concatenate | solution.py:257
  16.9 4.0 %collective-permute-start.5 = (bf16[272,640]{1,0:T(8,128)(2,1)S(1)}, bf16[272,640]{1,0:T(8,128)(2,1)S(1)}, u32[]{:S(2)}, u32[]{:S(2)}) collective-permute-start(bf16[272,640]{1,0:T(8,128)(2,1)S(1)} %concatenate.33), channel_id=1, source_target_pairs={{0,0},{1,1},{2,64},{3,65},{4,128},{5,129},{6,192},{7,193},{8,8},{9... | collective-permute-start | bytes 1044488 | tf_op jit(solution)/shard_map/ppermute | solution.py:260
  21.2 2.4 %collective-permute-start.3 = (bf16[168,640]{1,0:T(8,128)(2,1)S(1)}, bf16[168,640]{1,0:T(8,128)(2,1)S(1)}, u32[]{:S(2)}, u32[]{:S(2)}) collective-permute-start(bf16[168,640]{1,0:T(8,128)(2,1)S(1)} %concatenate.31), channel_id=1, source_target_pairs={{0,32},{1,33},{16,48},{17,49},{32,0},{33,1},{48,16},{49,17},{64,65... | collective-permute-start | bytes 645128 | tf_op jit(solution)/shard_map/ppermute | solution.py:253
  26.2 2.8 %collective-permute-done.3 = bf16[168,640]{1,0:T(8,128)(2,1)S(1)} collective-permute-done((bf16[168,640]{1,0:T(8,128)(2,1)S(1)}, bf16[168,640]{1,0:T(8,128)(2,1)S(1)}, u32[]{:S(2)}, u32[]{:S(2)}) %collective-permute-start.3) | collective-permute-done | bytes 215072 | tf_op jit(solution)/shard_map/ppermute | solution.py:253
  29.0 7.1 %collective-permute-done.2 = bf16[168,640]{1,0:T(8,128)(2,1)S(1)} collective-permute-done((bf16[168,640]{1,0:T(8,128)(2,1)S(1)}, bf16[168,640]{1,0:T(8,128)(2,1)S(1)}, u32[]{:S(2)}, u32[]{:S(2)}) %collective-permute-start.2) | collective-permute-done | bytes 215072 | tf_op jit(solution)/shard_map/ppermute | solution.py:253
  37.9 2.5 %collective-permute-start.10 = (bf16[672,640]{1,0:T(8,128)(2,1)S(1)}, bf16[672,640]{1,0:T(8,128)(2,1)S(1)}, u32[]{:S(2)}, u32[]{:S(2)}) collective-permute-start(bf16[672,640]{1,0:T(8,128)(2,1)S(1)} %concatenate.32.b0), channel_id=1, source_target_pairs={{0,1},{1,0},{16,17},{17,16},{32,33},{33,32},{48,49},{49,48},{64,96... | collective-permute-start | bytes 2580488 | tf_op jit(solution)/shard_map/ppermute | solution.py:265
  41.1 2.5 %collective-permute-start.6 = (bf16[672,640]{1,0:T(8,128)(2,1)S(1)}, bf16[672,640]{1,0:T(8,128)(2,1)S(1)}, u32[]{:S(2)}, u32[]{:S(2)}) collective-permute-start(bf16[672,640]{1,0:T(8,128)(2,1)S(1)} %concatenate.32.b0), channel_id=1, source_target_pairs={{0,129},{1,128},{16,145},{17,144},{32,161},{33,160},{48,177},{49,1... | collective-permute-start | bytes 2580488 | tf_op jit(solution)/shard_map/ppermute | solution.py:265
  43.6 6.1 %collective-permute-done.7.b1 = bf16[672,640]{1,0:T(8,128)(2,1)S(1)} collective-permute-done((bf16[672,640]{1,0:T(8,128)(2,1)S(1)}, bf16[672,640]{1,0:T(8,128)(2,1)S(1)}, u32[]{:S(2)}, u32[]{:S(2)}) %collective-permute-start.7) | collective-permute-done | bytes 860192 | tf_op jit(solution)/shard_map/ppermute | solution.py:265
  51.9 7.9 %collective-permute-done.10.b0 = bf16[672,640]{1,0:T(8,128)(2,1)S(1)} collective-permute-done((bf16[672,640]{1,0:T(8,128)(2,1)S(1)}, bf16[672,640]{1,0:T(8,128)(2,1)S(1)}, u32[]{:S(2)}, u32[]{:S(2)}) %collective-permute-start.10) | collective-permute-done | bytes 860192 | tf_op jit(solution)/shard_map/ppermute | solution.py:265
  65.4 2.0 %shard_map.124 = bf16[128,640]{1,0:T(8,128)(2,1)S(1)} custom-call(bf16[128,640]{1,0:T(8,128)(2,1)S(1)} %get-tuple-element.115.g, bf16[128,640]{1,0:T(8,128)(2,1)S(1)} %get-tuple-element.114.x_ref.x, f32[1,640]{1,0:T(1,128)S(1)} %slice_add_fusion.2.gain_ref.gain, bf16[640,640]{1,0:T(8,128)(2,1)S(1)} %get-tuple-element.68.refs_0_, ...), custom_call_target="tpu_custom_call" | custom-call | flops 838860800 | bytes 4194304 | tf_op jit(solution)/shard_map/pallas_call | solution.py:208
  67.7 5.4 %collective-permute-done.13.g = bf16[128,640]{1,0:T(8,128)(2,1)S(1)} collective-permute-done((bf16[128,640]{1,0:T(8,128)(2,1)S(1)}, bf16[128,640]{1,0:T(8,128)(2,1)S(1)}, u32[]{:S(2)}, u32[]{:S(2)}) %collective-permute-start.13) | collective-permute-done | bytes 163872 | tf_op jit(solution)/shard_map/ppermute | solution.py:302
  73.1 2.0 %shard_map.125 = bf16[128,640]{1,0:T(8,128)(2,1)S(1)} custom-call(bf16[128,640]{1,0:T(8,128)(2,1)S(1)} %collective-permute-done.13.g, bf16[128,640]{1,0:T(8,128)(2,1)S(1)} %get-tuple-element.114.x_ref.x, f32[1,640]{1,0:T(1,128)S(1)} %slice_add_fusion.2.gain_ref.gain, bf16[640,640]{1,0:T(8,128)(2,1)S(1)} %get-tuple-element.68.refs_0_, ...), custom_call_target="tpu_custom_call" | custom-call | flops 838860800 | bytes 4194304 | tf_op jit(solution)/shard_map/pallas_call | solution.py:208
  75.1 3.6 %collective-permute-start.14 = (bf16[128,640]{1,0:T(8,128)(2,1)S(1)}, bf16[128,640]{1,0:T(8,128)(2,1)S(1)}, u32[]{:S(2)}, u32[]{:S(2)}) collective-permute-start(bf16[128,640]{1,0:T(8,128)(2,1)S(1)} %shard_map.125), channel_id=1, source_target_pairs={{0,14},{2,0},{4,2},{6,4},{8,6},{10,8},{12,10},{14,12},{1,15},{3,1}... | collective-permute-start | bytes 491528 | tf_op jit(solution)/shard_map/ppermute | solution.py:302
  78.7 2.3 %collective-permute-done.14.g = bf16[128,640]{1,0:T(8,128)(2,1)S(1)} collective-permute-done((bf16[128,640]{1,0:T(8,128)(2,1)S(1)}, bf16[128,640]{1,0:T(8,128)(2,1)S(1)}, u32[]{:S(2)}, u32[]{:S(2)}) %collective-permute-start.14) | collective-permute-done | bytes 163872 | tf_op jit(solution)/shard_map/ppermute | solution.py:302
  80.9 2.0 %shard_map.126 = bf16[128,640]{1,0:T(8,128)(2,1)S(1)} custom-call(bf16[128,640]{1,0:T(8,128)(2,1)S(1)} %collective-permute-done.14.g, bf16[128,640]{1,0:T(8,128)(2,1)S(1)} %get-tuple-element.114.x_ref.x, f32[1,640]{1,0:T(1,128)S(1)} %slice_add_fusion.2.gain_ref.gain, bf16[640,640]{1,0:T(8,128)(2,1)S(1)} %get-tuple-element.68.refs_0_, ...), custom_call_target="tpu_custom_call" | custom-call | flops 838860800 | bytes 4194304 | tf_op jit(solution)/shard_map/pallas_call | solution.py:208
  82.9 6.1 %collective-permute-start.15 = (bf16[128,640]{1,0:T(8,128)(2,1)S(1)}, bf16[128,640]{1,0:T(8,128)(2,1)S(1)}, u32[]{:S(2)}, u32[]{:S(2)}) collective-permute-start(bf16[128,640]{1,0:T(8,128)(2,1)S(1)} %shard_map.126), channel_id=1, source_target_pairs={{0,14},{2,0},{4,2},{6,4},{8,6},{10,8},{12,10},{14,12},{1,15},{3,1}... | collective-permute-start | bytes 491528 | tf_op jit(solution)/shard_map/ppermute | solution.py:302
  89.0 2.3 %collective-permute-done.15 = bf16[128,640]{1,0:T(8,128)(2,1)S(1)} collective-permute-done((bf16[128,640]{1,0:T(8,128)(2,1)S(1)}, bf16[128,640]{1,0:T(8,128)(2,1)S(1)}, u32[]{:S(2)}, u32[]{:S(2)}) %collective-permute-start.15) | collective-permute-done | bytes 163872 | tf_op jit(solution)/shard_map/ppermute | solution.py:302
  92.0 3.1 %collective-permute-start.16 = (bf16[1280,640]{1,0:T(8,128)(2,1)S(1)}, bf16[1280,640]{1,0:T(8,128)(2,1)S(1)}, u32[]{:S(2)}, u32[]{:S(2)}) collective-permute-start(bf16[1280,640]{1,0:T(8,128)(2,1)S(1)} %shard_map.127), channel_id=1, source_target_pairs={{0,64},{64,0},{1,65},{65,1},{2,66},{66,2},{3,67},{67,3},{4,68},{68... | collective-permute-start | bytes 4915208 | tf_op jit(solution)/shard_map/ppermute | solution.py:50
  99.4 3.0 %collective-permute-done.18.gain_there = f32[1,640]{1,0:T(1,128)S(1)} collective-permute-done((f32[1,640]{1,0:T(1,128)S(1)}, f32[1,640]{1,0:T(1,128)S(1)}, u32[]{:S(2)}, u32[]{:S(2)}) %collective-permute-start.18) | collective-permute-done | bytes 2592 | tf_op jit(solution)/shard_map/ppermute | solution.py:50
  103.5 3.4 %collective-permute-start.19 = (bf16[656,640]{1,0:T(8,128)(2,1)S(1)}, bf16[656,640]{1,0:T(8,128)(2,1)S(1)}, u32[]{:S(2)}, u32[]{:S(2)}) collective-permute-start(bf16[656,640]{1,0:T(8,128)(2,1)S(1)} %get-tuple-element.97), channel_id=1, source_target_pairs={{0,129},{1,128},{16,145},{17,144},{32,161},{33,160},{48,177},{49,1... | collective-permute-start | bytes 2519048 | tf_op jit(solution)/shard_map/ppermute | solution.py:325
  107.6 9.5 %collective-permute-start.22 = (bf16[128,640]{1,0:T(8,128)(2,1)S(1)}, bf16[128,640]{1,0:T(8,128)(2,1)S(1)}, u32[]{:S(2)}, u32[]{:S(2)}) collective-permute-start(bf16[128,640]{1,0:T(8,128)(2,1)S(1)} %get-tuple-element.100), channel_id=1, source_target_pairs={{0,0},{1,1},{64,2},{65,3},{128,4},{129,5},{192,6},{193,7},{8,8},{9... | collective-permute-start | bytes 491528 | tf_op jit(solution)/shard_map/ppermute | solution.py:321
  117.1 2.9 %collective-permute-done.22.value = bf16[128,640]{1,0:T(8,128)(2,1)S(1)} collective-permute-done((bf16[128,640]{1,0:T(8,128)(2,1)S(1)}, bf16[128,640]{1,0:T(8,128)(2,1)S(1)}, u32[]{:S(2)}, u32[]{:S(2)}) %collective-permute-start.22) | collective-permute-done | bytes 163872 | tf_op jit(solution)/shard_map/ppermute | solution.py:321
  120.6 4.8 %collective-permute-done.19.s1 = bf16[656,640]{1,0:T(8,128)(2,1)S(1)} collective-permute-done((bf16[656,640]{1,0:T(8,128)(2,1)S(1)}, bf16[656,640]{1,0:T(8,128)(2,1)S(1)}, u32[]{:S(2)}, u32[]{:S(2)}) %collective-permute-start.19) | collective-permute-done | bytes 839712 | tf_op jit(solution)/shard_map/ppermute | solution.py:325
  125.4 3.1 %collective-permute-done.21.s3 = bf16[656,640]{1,0:T(8,128)(2,1)S(1)} collective-permute-done((bf16[656,640]{1,0:T(8,128)(2,1)S(1)}, bf16[656,640]{1,0:T(8,128)(2,1)S(1)}, u32[]{:S(2)}, u32[]{:S(2)}) %collective-permute-start.21) | collective-permute-done | bytes 839712 | tf_op jit(solution)/shard_map/ppermute | solution.py:325
  129.1 3.1 %collective-permute-start.24 = (bf16[176,640]{1,0:T(8,128)(2,1)S(1)}, bf16[176,640]{1,0:T(8,128)(2,1)S(1)}, u32[]{:S(2)}, u32[]{:S(2)}) collective-permute-start(bf16[176,640]{1,0:T(8,128)(2,1)S(1)} %get-tuple-element.108), channel_id=1, source_target_pairs={{0,32},{1,33},{16,48},{17,49},{32,0},{33,1},{48,16},{49,17},{64,65... | collective-permute-start | bytes 675848 | tf_op jit(solution)/shard_map/ppermute | solution.py:330
  132.2 2.2 %collective-permute-done.23 = bf16[176,640]{1,0:T(8,128)(2,1)S(1)} collective-permute-done((bf16[176,640]{1,0:T(8,128)(2,1)S(1)}, bf16[176,640]{1,0:T(8,128)(2,1)S(1)}, u32[]{:S(2)}, u32[]{:S(2)}) %collective-permute-start.23) | collective-permute-done | bytes 225312 | tf_op jit(solution)/shard_map/ppermute | solution.py:330
  134.4 3.6 %collective-permute-done.24 = bf16[176,640]{1,0:T(8,128)(2,1)S(1)} collective-permute-done((bf16[176,640]{1,0:T(8,128)(2,1)S(1)}, bf16[176,640]{1,0:T(8,128)(2,1)S(1)}, u32[]{:S(2)}, u32[]{:S(2)}) %collective-permute-start.24) | collective-permute-done | bytes 225312 | tf_op jit(solution)/shard_map/ppermute | solution.py:330
  139.0 10.7 %collective-permute-start.26 = (bf16[88,640]{1,0:T(8,128)(2,1)S(1)}, bf16[88,640]{1,0:T(8,128)(2,1)S(1)}, u32[]{:S(2)}, u32[]{:S(2)}) collective-permute-start(bf16[88,640]{1,0:T(8,128)(2,1)S(1)} %concatenate.34), channel_id=1, source_target_pairs={{0,0},{1,1},{64,2},{65,3},{128,4},{129,5},{192,6},{193,7},{8,8},{9... | collective-permute-start | bytes 337928 | tf_op jit(solution)/shard_map/ppermute | solution.py:337
  149.8 2.3 %collective-permute-done.26 = bf16[88,640]{1,0:T(8,128)(2,1)S(1)} collective-permute-done((bf16[88,640]{1,0:T(8,128)(2,1)S(1)}, bf16[88,640]{1,0:T(8,128)(2,1)S(1)}, u32[]{:S(2)}, u32[]{:S(2)}) %collective-permute-start.26) | collective-permute-done | bytes 112672 | tf_op jit(solution)/shard_map/ppermute | solution.py:337
  152.1 7.3 %collective-permute-done.27 = bf16[88,640]{1,0:T(8,128)(2,1)S(1)} collective-permute-done((bf16[88,640]{1,0:T(8,128)(2,1)S(1)}, bf16[88,640]{1,0:T(8,128)(2,1)S(1)}, u32[]{:S(2)}, u32[]{:S(2)}) %collective-permute-start.27) | collective-permute-done | bytes 112672 | tf_op jit(solution)/shard_map/ppermute | solution.py:337
  (81 shorter events, 27.4 us)
Async XLA Ops:
  0.6 1.7 %copy-start = (bf16[1,256,40]{1,2,0:T(8,128)(2,1)S(1)}, bf16[1,256,40]{1,2,0:T(8,128)(2,1)}, u32[]{:S(2)}) copy-start(bf16[1,256,40]{1,2,0:T(8,128)(2,1)} %param.14) | copy-start | bytes 61444
  3.7 17.2 %collective-permute-start.1 = (bf16[88,640]{1,0:T(8,128)(2,1)S(1)}, bf16[88,640]{1,0:T(8,128)(2,1)S(1)}, u32[]{:S(2)}, u32[]{:S(2)}) collective-permute-start(bf16[88,640]{1,0:T(8,128)(2,1)S(1)} %maximum_maximum_fusion), channel_id=1, source_target_pairs={{0,8},{1,9},{2,72},{3,73},{4,136},{5,137},{6,200},{7,201},{8,0},{9... | collective-permute-start | bytes 337928 | tf_op jit(solution)/shard_map/ppermute | solution.py:240
  9.8 11.1 %collective-permute-start = (bf16[88,640]{1,0:T(8,128)(2,1)S(1)}, bf16[88,640]{1,0:T(8,128)(2,1)S(1)}, u32[]{:S(2)}, u32[]{:S(2)}) collective-permute-start(bf16[88,640]{1,0:T(8,128)(2,1)S(1)} %maximum_maximum_fusion), channel_id=1, source_target_pairs={{0,0},{1,1},{2,64},{3,65},{4,128},{5,129},{6,192},{7,193},{8,8},{9... | collective-permute-start | bytes 337928 | tf_op jit(solution)/shard_map/ppermute | solution.py:240
  16.9 19.8 %collective-permute-start.5 = (bf16[272,640]{1,0:T(8,128)(2,1)S(1)}, bf16[272,640]{1,0:T(8,128)(2,1)S(1)}, u32[]{:S(2)}, u32[]{:S(2)}) collective-permute-start(bf16[272,640]{1,0:T(8,128)(2,1)S(1)} %concatenate.33), channel_id=1, source_target_pairs={{0,0},{1,1},{2,64},{3,65},{4,128},{5,129},{6,192},{7,193},{8,8},{9... | collective-permute-start | bytes 1044488 | tf_op jit(solution)/shard_map/ppermute | solution.py:260
  21.1 5.1 %collective-permute-start.4 = (bf16[168,640]{1,0:T(8,128)(2,1)S(1)}, bf16[168,640]{1,0:T(8,128)(2,1)S(1)}, u32[]{:S(2)}, u32[]{:S(2)}) collective-permute-start(bf16[168,640]{1,0:T(8,128)(2,1)S(1)} %concatenate.31), channel_id=1, source_target_pairs={{0,48},{1,49},{16,0},{17,1},{32,16},{33,17},{48,32},{49,33},{64,19... | collective-permute-start | bytes 645128 | tf_op jit(solution)/shard_map/ppermute | solution.py:253
  21.2 7.9 %collective-permute-start.3 = (bf16[168,640]{1,0:T(8,128)(2,1)S(1)}, bf16[168,640]{1,0:T(8,128)(2,1)S(1)}, u32[]{:S(2)}, u32[]{:S(2)}) collective-permute-start(bf16[168,640]{1,0:T(8,128)(2,1)S(1)} %concatenate.31), channel_id=1, source_target_pairs={{0,32},{1,33},{16,48},{17,49},{32,0},{33,1},{48,16},{49,17},{64,65... | collective-permute-start | bytes 645128 | tf_op jit(solution)/shard_map/ppermute | solution.py:253
  23.6 12.6 %collective-permute-start.2 = (bf16[168,640]{1,0:T(8,128)(2,1)S(1)}, bf16[168,640]{1,0:T(8,128)(2,1)S(1)}, u32[]{:S(2)}, u32[]{:S(2)}) collective-permute-start(bf16[168,640]{1,0:T(8,128)(2,1)S(1)} %concatenate.31), channel_id=1, source_target_pairs={{0,16},{1,17},{16,32},{17,33},{32,48},{33,49},{48,0},{49,1},{64,19... | collective-permute-start | bytes 645128 | tf_op jit(solution)/shard_map/ppermute | solution.py:253
  36.6 13.0 %collective-permute-start.7 = (bf16[672,640]{1,0:T(8,128)(2,1)S(1)}, bf16[672,640]{1,0:T(8,128)(2,1)S(1)}, u32[]{:S(2)}, u32[]{:S(2)}) collective-permute-start(bf16[672,640]{1,0:T(8,128)(2,1)S(1)} %concatenate.32.b0), channel_id=1, source_target_pairs={{0,128},{1,129},{16,144},{17,145},{32,160},{33,161},{48,176},{49,1... | collective-permute-start | bytes 2580488 | tf_op jit(solution)/shard_map/ppermute | solution.py:265
  37.9 21.8 %collective-permute-start.10 = (bf16[672,640]{1,0:T(8,128)(2,1)S(1)}, bf16[672,640]{1,0:T(8,128)(2,1)S(1)}, u32[]{:S(2)}, u32[]{:S(2)}) collective-permute-start(bf16[672,640]{1,0:T(8,128)(2,1)S(1)} %concatenate.32.b0), channel_id=1, source_target_pairs={{0,1},{1,0},{16,17},{17,16},{32,33},{33,32},{48,49},{49,48},{64,96... | collective-permute-start | bytes 2580488 | tf_op jit(solution)/shard_map/ppermute | solution.py:265
  40.5 19.9 %collective-permute-start.8 = (bf16[672,640]{1,0:T(8,128)(2,1)S(1)}, bf16[672,640]{1,0:T(8,128)(2,1)S(1)}, u32[]{:S(2)}, u32[]{:S(2)}) collective-permute-start(bf16[672,640]{1,0:T(8,128)(2,1)S(1)} %concatenate.32.b0), channel_id=1, source_target_pairs={{0,64},{64,0},{1,65},{65,1},{2,66},{66,2},{3,67},{67,3},{4,68},{68... | collective-permute-start | bytes 2580488 | tf_op jit(solution)/shard_map/ppermute | solution.py:50
  41.1 20.3 %collective-permute-start.6 = (bf16[672,640]{1,0:T(8,128)(2,1)S(1)}, bf16[672,640]{1,0:T(8,128)(2,1)S(1)}, u32[]{:S(2)}, u32[]{:S(2)}) collective-permute-start(bf16[672,640]{1,0:T(8,128)(2,1)S(1)} %concatenate.32.b0), channel_id=1, source_target_pairs={{0,129},{1,128},{16,145},{17,144},{32,161},{33,160},{48,177},{49,1... | collective-permute-start | bytes 2580488 | tf_op jit(solution)/shard_map/ppermute | solution.py:265
  49.7 10.7 %collective-permute-start.9 = (bf16[672,640]{1,0:T(8,128)(2,1)S(1)}, bf16[672,640]{1,0:T(8,128)(2,1)S(1)}, u32[]{:S(2)}, u32[]{:S(2)}) collective-permute-start(bf16[672,640]{1,0:T(8,128)(2,1)S(1)} %collective-permute-done.7.b1), channel_id=1, source_target_pairs={{0,64},{64,0},{1,65},{65,1},{2,66},{66,2},{3,67},{67,3},{4,68},{68... | collective-permute-start | bytes 2580488 | tf_op jit(solution)/shard_map/ppermute | solution.py:50
  59.7 3.6 %collective-permute-start.11 = (bf16[672,640]{1,0:T(8,128)(2,1)S(1)}, bf16[672,640]{1,0:T(8,128)(2,1)S(1)}, u32[]{:S(2)}, u32[]{:S(2)}) collective-permute-start(bf16[672,640]{1,0:T(8,128)(2,1)S(1)} %collective-permute-done.10.b0), channel_id=1, source_target_pairs={{0,64},{64,0},{1,65},{65,1},{2,66},{66,2},{3,67},{67,3},{4,68},{68... | collective-permute-start | bytes 2580488 | tf_op jit(solution)/shard_map/ppermute | solution.py:50
  61.4 2.9 %collective-permute-start.12 = (bf16[672,640]{1,0:T(8,128)(2,1)S(1)}, bf16[672,640]{1,0:T(8,128)(2,1)S(1)}, u32[]{:S(2)}, u32[]{:S(2)}) collective-permute-start(bf16[672,640]{1,0:T(8,128)(2,1)S(1)} %collective-permute-done.6.b1), channel_id=1, source_target_pairs={{0,64},{64,0},{1,65},{65,1},{2,66},{66,2},{3,67},{67,3},{4,68},{68... | collective-permute-start | bytes 2580488 | tf_op jit(solution)/shard_map/ppermute | solution.py:50
  67.4 5.7 %collective-permute-start.13 = (bf16[128,640]{1,0:T(8,128)(2,1)S(1)}, bf16[128,640]{1,0:T(8,128)(2,1)S(1)}, u32[]{:S(2)}, u32[]{:S(2)}) collective-permute-start(bf16[128,640]{1,0:T(8,128)(2,1)S(1)} %shard_map.124), channel_id=1, source_target_pairs={{0,14},{2,0},{4,2},{6,4},{8,6},{10,8},{12,10},{14,12},{1,15},{3,1}... | collective-permute-start | bytes 491528 | tf_op jit(solution)/shard_map/ppermute | solution.py:302
  75.1 5.9 %collective-permute-start.14 = (bf16[128,640]{1,0:T(8,128)(2,1)S(1)}, bf16[128,640]{1,0:T(8,128)(2,1)S(1)}, u32[]{:S(2)}, u32[]{:S(2)}) collective-permute-start(bf16[128,640]{1,0:T(8,128)(2,1)S(1)} %shard_map.125), channel_id=1, source_target_pairs={{0,14},{2,0},{4,2},{6,4},{8,6},{10,8},{12,10},{14,12},{1,15},{3,1}... | collective-permute-start | bytes 491528 | tf_op jit(solution)/shard_map/ppermute | solution.py:302
  82.9 8.4 %collective-permute-start.15 = (bf16[128,640]{1,0:T(8,128)(2,1)S(1)}, bf16[128,640]{1,0:T(8,128)(2,1)S(1)}, u32[]{:S(2)}, u32[]{:S(2)}) collective-permute-start(bf16[128,640]{1,0:T(8,128)(2,1)S(1)} %shard_map.126), channel_id=1, source_target_pairs={{0,14},{2,0},{4,2},{6,4},{8,6},{10,8},{12,10},{14,12},{1,15},{3,1}... | collective-permute-start | bytes 491528 | tf_op jit(solution)/shard_map/ppermute | solution.py:302
  92.0 6.2 %collective-permute-start.16 = (bf16[1280,640]{1,0:T(8,128)(2,1)S(1)}, bf16[1280,640]{1,0:T(8,128)(2,1)S(1)}, u32[]{:S(2)}, u32[]{:S(2)}) collective-permute-start(bf16[1280,640]{1,0:T(8,128)(2,1)S(1)} %shard_map.127), channel_id=1, source_target_pairs={{0,64},{64,0},{1,65},{65,1},{2,66},{66,2},{3,67},{67,3},{4,68},{68... | collective-permute-start | bytes 4915208 | tf_op jit(solution)/shard_map/ppermute | solution.py:50
  98.8 3.6 %collective-permute-start.17 = (bf16[1280,640]{1,0:T(8,128)(2,1)S(1)}, bf16[1280,640]{1,0:T(8,128)(2,1)S(1)}, u32[]{:S(2)}, u32[]{:S(2)}) collective-permute-start(bf16[1280,640]{1,0:T(8,128)(2,1)S(1)} %shard_map.129), channel_id=1, source_target_pairs={{0,64},{64,0},{1,65},{65,1},{2,66},{66,2},{3,67},{67,3},{4,68},{68... | collective-permute-start | bytes 4915208 | tf_op jit(solution)/shard_map/ppermute | solution.py:50
  99.3 3.1 %collective-permute-start.18 = (f32[1,640]{1,0:T(1,128)S(1)}, f32[1,640]{1,0:T(1,128)S(1)}, u32[]{:S(2)}, u32[]{:S(2)}) collective-permute-start(f32[1,640]{1,0:T(1,128)S(1)} %get-tuple-element.95.gain_here), channel_id=1, source_target_pairs={{0,64},{64,0},{1,65},{65,1},{2,66},{66,2},{3,67},{67,3},{4,68},{68... | collective-permute-start | bytes 7688 | tf_op jit(solution)/shard_map/ppermute | solution.py:50
  103.5 22.0 %collective-permute-start.19 = (bf16[656,640]{1,0:T(8,128)(2,1)S(1)}, bf16[656,640]{1,0:T(8,128)(2,1)S(1)}, u32[]{:S(2)}, u32[]{:S(2)}) collective-permute-start(bf16[656,640]{1,0:T(8,128)(2,1)S(1)} %get-tuple-element.97), channel_id=1, source_target_pairs={{0,129},{1,128},{16,145},{17,144},{32,161},{33,160},{48,177},{49,1... | collective-permute-start | bytes 2519048 | tf_op jit(solution)/shard_map/ppermute | solution.py:325
  106.9 18.5 %collective-permute-start.20 = (bf16[656,640]{1,0:T(8,128)(2,1)S(1)}, bf16[656,640]{1,0:T(8,128)(2,1)S(1)}, u32[]{:S(2)}, u32[]{:S(2)}) collective-permute-start(bf16[656,640]{1,0:T(8,128)(2,1)S(1)} %get-tuple-element.98), channel_id=1, source_target_pairs={{0,1},{1,0},{16,17},{17,16},{32,33},{33,32},{48,49},{49,48},{64,96... | collective-permute-start | bytes 2519048 | tf_op jit(solution)/shard_map/ppermute | solution.py:325
  106.9 21.6 %collective-permute-start.21 = (bf16[656,640]{1,0:T(8,128)(2,1)S(1)}, bf16[656,640]{1,0:T(8,128)(2,1)S(1)}, u32[]{:S(2)}, u32[]{:S(2)}) collective-permute-start(bf16[656,640]{1,0:T(8,128)(2,1)S(1)} %get-tuple-element.99), channel_id=1, source_target_pairs={{0,128},{1,129},{16,144},{17,145},{32,160},{33,161},{48,176},{49,1... | collective-permute-start | bytes 2519048 | tf_op jit(solution)/shard_map/ppermute | solution.py:325
  107.6 12.3 %collective-permute-start.22 = (bf16[128,640]{1,0:T(8,128)(2,1)S(1)}, bf16[128,640]{1,0:T(8,128)(2,1)S(1)}, u32[]{:S(2)}, u32[]{:S(2)}) collective-permute-start(bf16[128,640]{1,0:T(8,128)(2,1)S(1)} %get-tuple-element.100), channel_id=1, source_target_pairs={{0,0},{1,1},{64,2},{65,3},{128,4},{129,5},{192,6},{193,7},{8,8},{9... | collective-permute-start | bytes 491528 | tf_op jit(solution)/shard_map/ppermute | solution.py:321
  129.0 5.3 %collective-permute-start.23 = (bf16[176,640]{1,0:T(8,128)(2,1)S(1)}, bf16[176,640]{1,0:T(8,128)(2,1)S(1)}, u32[]{:S(2)}, u32[]{:S(2)}) collective-permute-start(bf16[176,640]{1,0:T(8,128)(2,1)S(1)} %get-tuple-element.107), channel_id=1, source_target_pairs={{0,48},{1,49},{16,0},{17,1},{32,16},{33,17},{48,32},{49,33},{64,19... | collective-permute-start | bytes 675848 | tf_op jit(solution)/shard_map/ppermute | solution.py:330
  129.1 8.8 %collective-permute-start.24 = (bf16[176,640]{1,0:T(8,128)(2,1)S(1)}, bf16[176,640]{1,0:T(8,128)(2,1)S(1)}, u32[]{:S(2)}, u32[]{:S(2)}) collective-permute-start(bf16[176,640]{1,0:T(8,128)(2,1)S(1)} %get-tuple-element.108), channel_id=1, source_target_pairs={{0,32},{1,33},{16,48},{17,49},{32,0},{33,1},{48,16},{49,17},{64,65... | collective-permute-start | bytes 675848 | tf_op jit(solution)/shard_map/ppermute | solution.py:330
  132.2 6.5 %collective-permute-start.25 = (bf16[176,640]{1,0:T(8,128)(2,1)S(1)}, bf16[176,640]{1,0:T(8,128)(2,1)S(1)}, u32[]{:S(2)}, u32[]{:S(2)}) collective-permute-start(bf16[176,640]{1,0:T(8,128)(2,1)S(1)} %get-tuple-element.109), channel_id=1, source_target_pairs={{0,16},{1,17},{16,32},{17,33},{32,48},{33,49},{48,0},{49,1},{64,19... | collective-permute-start | bytes 675848 | tf_op jit(solution)/shard_map/ppermute | solution.py:330
  139.0 13.1 %collective-permute-start.26 = (bf16[88,640]{1,0:T(8,128)(2,1)S(1)}, bf16[88,640]{1,0:T(8,128)(2,1)S(1)}, u32[]{:S(2)}, u32[]{:S(2)}) collective-permute-start(bf16[88,640]{1,0:T(8,128)(2,1)S(1)} %concatenate.34), channel_id=1, source_target_pairs={{0,0},{1,1},{64,2},{65,3},{128,4},{129,5},{192,6},{193,7},{8,8},{9... | collective-permute-start | bytes 337928 | tf_op jit(solution)/shard_map/ppermute | solution.py:337
  149.7 9.7 %collective-permute-start.27 = (bf16[88,640]{1,0:T(8,128)(2,1)S(1)}, bf16[88,640]{1,0:T(8,128)(2,1)S(1)}, u32[]{:S(2)}, u32[]{:S(2)}) collective-permute-start(bf16[88,640]{1,0:T(8,128)(2,1)S(1)} %concatenate.35), channel_id=1, source_target_pairs={{8,0},{9,1},{72,2},{73,3},{136,4},{137,5},{200,6},{201,7},{0,8},{1... | collective-permute-start | bytes 337928 | tf_op jit(solution)/shard_map/ppermute | solution.py:337

commit v6 on v5

--- a/solution.py
+++ b/solution.py
@@ -223,7 +223,6 @@
     own = w_in.shape[2]
     half = SIDE * SIDE * 2 * own
     grad_scale = float(rows * 64) ** (-0.5)
-    section = lax.axis_index("z") % 4
     sample = 2 * lax.axis_index("x") + lax.axis_index("z") // 4
     bf16, f32 = jnp.bfloat16, jnp.float32
 
@@ -234,7 +233,7 @@
     cond = dot_plain(time_feats, time_proj[0]) + dot_plain(picks, class_table[0])
     cond_row = jnp.concatenate([part.reshape(1, -1) for part in two_parts(cond)], axis=1)
     shard = jnp.concatenate(
-        [w_in[0].T, w_out[0], cond_row, jnp.zeros((7, chan), bf16)], axis=0
+        [w_in[0].T, w_out[0], cond_row, *three_parts(gains), jnp.zeros((4, chan), bf16)], axis=0
     )
 
     one, two = (lax.ppermute(shard, COLUMN, home_to_work(flip)) for flip in (0, 1))
@@ -254,14 +253,12 @@
     quarter = jnp.concatenate(
         [part[: 4 * own] for part in chunks] + [part[4 * own :] for part in chunks], axis=0
     )
-    packed = jnp.concatenate(
-        [checkpoints[0], cotangent, *three_parts(gains), jnp.zeros((PAD - 3, chan), bf16)], axis=0
-    )
-    packed = lax.ppermute(packed, COLUMN, home_to_work(0))
-    quarter, packed = lax.optimization_barrier((quarter, packed))
-    x_rows, cot_rows = packed[:rows], packed[rows : 2 * rows]
-    gain_row = packed[2 * rows : 2 * rows + 3].astype(f32)
+    gain_row = one[2 * own + 1 : 2 * own + 4].astype(f32)
     gain_row = gain_row[0:1] + gain_row[1:2] + gain_row[2:3]
+    x_rows = lax.ppermute(checkpoints[0], COLUMN, home_to_work(0))
+    cot_rows = lax.ppermute(
+        cotangent, COLUMN, [pair for pair in home_to_work(0) if pair[0] >> 4 == 3]
+    )
     near = [quarter] + [lax.ppermute(quarter, PLANE, along(2, k)) for k in range(1, SIDE)]
 
     width = half // 2
@@ -285,7 +282,7 @@
     )
     first_far = [across_cores(block) for block in near[:2]]
     first = [activate(x_rows, gain_row, select, *blocks) for blocks in (near[:2], first_far)]
-    last_near, *first = lax.optimization_barrier((near[3], *first))
+    last_near, cot_rows, *first = lax.optimization_barrier((near[3], cot_rows, *first))
     near, last_far = [near[2], last_near], [across_cores(near[2]), across_cores(last_near)]
     second = [activate(x_rows, gain_row, select, *blocks) for blocks in (near, last_far)]
     quarters = [first[0], second[0], first[1], second[1]]
@@ -296,8 +293,7 @@
         held += [w_in_rows, w_out_rows, slope]
 
     turn = kernel(turn_kernel, [((rows, chan), bf16)], 4 * flops)
-    grad = jnp.where(section == 3, cot_rows, jnp.zeros_like(cot_rows))
-    kept = grad
+    kept = grad = cot_rows
     for _ in range(3):
         grad = lax.ppermute(turn(grad, *held), "z", next_section())
         kept = kept + grad

time: 161 us -> 158 us (0.981)
  waiting for transfers between devices: 66.5 us -> 54 us
  starting transfers between devices: 69.6 us -> 80.7 us
    ppermute x3, waiting for transfers between devices: 13.9 us -> 2.1 us  [on_device(): lax.ppermute(quarter, PLANE, along(2, k))]
    ppermute x1 -> x2, starting transfers between devices: 4 us -> 15.8 us  [the longest x1 8.54 us: on_device(): lax.ppermute(cotangent, COLUMN, [pair for pair in home_to_work(0) if pair...]
    ppermute x7, starting transfers between devices: 7.05 us -> 15.5 us  [across_cores(): return lax.ppermute(value, 'core', [(0, 1), (1, 0)])]
    ppermute x3, starting transfers between devices: 9.99 us -> 2.8 us  [on_device(): grad = lax.ppermute(turn(grad, *held), 'z', next_section())]
    ppermute x3, waiting for transfers between devices: 10.6 us -> 4.52 us  [on_device(): lax.ppermute(chunk, PLANE, along(1, k))]
    ppermute x2, waiting for transfers between devices: 0.01 us -> 4.81 us  [on_device(): lax.ppermute(shard, COLUMN, home_to_work(flip))]
    ppermute x3, starting transfers between devices: 6.29 us -> 1.88 us  [on_device(): lax.ppermute(quarter, PLANE, along(2, k))]
    ppermute x3, starting transfers between devices: 3.14 us -> 7.22 us  [on_device(): lax.ppermute(sums[k], PLANE, along(1, SIDE - k))]
  transfers between devices with their start and end apart: 28 -> 29, of which waited for: 19 -> 20; matrix products, arithmetic and copies ran while one was open for 2% -> 0% of each run, Pallas kernels for 3% -> 3%
where the time goes in v6:
time: 158 us
  starting transfers between devices  80.7 us (51%)
  waiting for transfers between devices  54 us (34%)
  Pallas kernels  15.1 us (10%)
  other arithmetic  3.41 us (2%)
  local copies, waits for them, and re-layouts  2.66 us (2%)
    ppermute x7, starting transfers between devices, across_cores(): return lax.ppermute(value, 'core', [(0, 1), (1, 0)])  15.5 us
    pallas_call x13, Pallas kernels, call(): pl.pallas_call(body, out_shape=shapes, in_specs=[whole] * len(operands),...  15.1 us
    ppermute x3, waiting for transfers between devices, on_device(): grad = lax.ppermute(turn(grad, *held), 'z', next_section())  13.4 us
    ppermute x1, starting transfers between devices, on_device(): grad_home = lax.ppermute(grad_in, COLUMN, work_to_home(0))  12.2 us
    ppermute x2, starting transfers between devices, on_device(): lax.ppermute(shard, COLUMN, home_to_work(flip))  10.3 us
    ppermute x2, starting transfers between devices, on_device(): lax.ppermute(jnp.concatenate([total[flip * own:(flip + 1) * own], total[(...  9.18 us
    ppermute x2, waiting for transfers between devices, on_device(): lax.ppermute(jnp.concatenate([total[flip * own:(flip + 1) * own], total[(...  9.16 us
    ppermute x1, starting transfers between devices, on_device(): lax.ppermute(cotangent, COLUMN, [pair for pair in home_to_work(0) if pair...  8.54 us
  transfers between devices with their start and end apart: 29, of which 20 were waited for; matrix products, arithmetic and copies ran while one was open for 0% of the time, Pallas kernels for 3%

profile of v6, /device:TPU:9, one launch (start us, length us, event | category | flops | bytes accessed | tf_op | source)
XLA Modules:
  0.0 157.9 jit_solution(7129447580547755277)
XLA Ops:
  3.4 1.7 %concatenate.27 = bf16[88,640]{1,0:T(8,128)(2,1)S(1)} concatenate(bf16[40,640]{1,0:T(8,128)(2,1)} %bitcast.21, bf16[40,640]{1,0:T(8,128)(2,1)} %bitcast.22, bf16[1,640]{1,0:T(2,128)(2,1)S(1)} %pad_maximum_fusion, bf16[1,640]{1,0:T(2,128)(2,1)S(1)} %get-tuple-element.126, bf16[1,640]{1,0:T(2,128)(2,1)S(1)} %get-tuple-element.125, bf16[1,640]{1,0:T(2,128)(2,1)S(1)} %get-tuple-element.124, ...), dimensions={0} | concatenate | bytes 225280 | tf_op jit(solution)/shard_map/concatenate | solution.py:235
  5.1 6.1 %collective-permute-start.1 = (bf16[88,640]{1,0:T(8,128)(2,1)S(1)}, bf16[88,640]{1,0:T(8,128)(2,1)S(1)}, u32[]{:S(2)}, u32[]{:S(2)}) collective-permute-start(bf16[88,640]{1,0:T(8,128)(2,1)S(1)} %concatenate.27), channel_id=1, source_target_pairs={{0,8},{1,9},{2,72},{3,73},{4,136},{5,137},{6,200},{7,201},{8,0},{9... | collective-permute-start | bytes 337928 | tf_op jit(solution)/shard_map/ppermute | solution.py:239
  11.2 4.2 %collective-permute-start = (bf16[88,640]{1,0:T(8,128)(2,1)S(1)}, bf16[88,640]{1,0:T(8,128)(2,1)S(1)}, u32[]{:S(2)}, u32[]{:S(2)}) collective-permute-start(bf16[88,640]{1,0:T(8,128)(2,1)S(1)} %concatenate.27), channel_id=1, source_target_pairs={{0,0},{1,1},{2,64},{3,65},{4,128},{5,129},{6,192},{7,193},{8,8},{9... | collective-permute-start | bytes 337928 | tf_op jit(solution)/shard_map/ppermute | solution.py:239
  15.5 3.5 %collective-permute-done.1 = bf16[88,640]{1,0:T(8,128)(2,1)S(1)} collective-permute-done((bf16[88,640]{1,0:T(8,128)(2,1)S(1)}, bf16[88,640]{1,0:T(8,128)(2,1)S(1)}, u32[]{:S(2)}, u32[]{:S(2)}) %collective-permute-start.1) | collective-permute-done | bytes 112672 | tf_op jit(solution)/shard_map/ppermute | solution.py:239
  20.5 2.2 %collective-permute-start.3 = (bf16[168,640]{1,0:T(8,128)(2,1)S(1)}, bf16[168,640]{1,0:T(8,128)(2,1)S(1)}, u32[]{:S(2)}, u32[]{:S(2)}) collective-permute-start(bf16[168,640]{1,0:T(8,128)(2,1)S(1)} %concatenate.28), channel_id=1, source_target_pairs={{0,32},{1,33},{16,48},{17,49},{32,0},{33,1},{48,16},{49,17},{64,65... | collective-permute-start | bytes 645128 | tf_op jit(solution)/shard_map/ppermute | solution.py:252
  22.8 2.0 %collective-permute-start.2 = (bf16[168,640]{1,0:T(8,128)(2,1)S(1)}, bf16[168,640]{1,0:T(8,128)(2,1)S(1)}, u32[]{:S(2)}, u32[]{:S(2)}) collective-permute-start(bf16[168,640]{1,0:T(8,128)(2,1)S(1)} %concatenate.28), channel_id=1, source_target_pairs={{0,16},{1,17},{16,32},{17,33},{32,48},{33,49},{48,0},{49,1},{64,19... | collective-permute-start | bytes 645128 | tf_op jit(solution)/shard_map/ppermute | solution.py:252
  25.3 3.0 %collective-permute-done.3 = bf16[168,640]{1,0:T(8,128)(2,1)S(1)} collective-permute-done((bf16[168,640]{1,0:T(8,128)(2,1)S(1)}, bf16[168,640]{1,0:T(8,128)(2,1)S(1)}, u32[]{:S(2)}, u32[]{:S(2)}) %collective-permute-start.3) | collective-permute-done | bytes 215072 | tf_op jit(solution)/shard_map/ppermute | solution.py:252
  31.1 7.3 %collective-permute-start.7 = (bf16[128,640]{1,0:T(8,128)(2,1)S(1)}, bf16[128,640]{1,0:T(8,128)(2,1)S(1)}, u32[]{:S(2)}, u32[]{:S(2)}) collective-permute-start(bf16[128,640]{1,0:T(8,128)(2,1)S(1)} %bitcast.23), channel_id=1, source_target_pairs={{0,0},{1,1},{2,64},{3,65},{4,128},{5,129},{6,192},{7,193},{8,8},{9... | collective-permute-start | bytes 491528 | tf_op jit(solution)/shard_map/ppermute | solution.py:258
  39.0 3.2 %collective-permute-start.9 = (bf16[672,640]{1,0:T(8,128)(2,1)S(1)}, bf16[672,640]{1,0:T(8,128)(2,1)S(1)}, u32[]{:S(2)}, u32[]{:S(2)}) collective-permute-start(bf16[672,640]{1,0:T(8,128)(2,1)S(1)} %concatenate.29.b0), channel_id=1, source_target_pairs={{0,64},{64,0},{1,65},{65,1},{2,66},{66,2},{3,67},{67,3},{4,68},{68... | collective-permute-start | bytes 2580488 | tf_op jit(solution)/shard_map/ppermute | solution.py:50
  42.2 2.1 %collective-permute-done.8.b1 = bf16[672,640]{1,0:T(8,128)(2,1)S(1)} collective-permute-done((bf16[672,640]{1,0:T(8,128)(2,1)S(1)}, bf16[672,640]{1,0:T(8,128)(2,1)S(1)}, u32[]{:S(2)}, u32[]{:S(2)}) %collective-permute-start.8) | collective-permute-done | bytes 860192 | tf_op jit(solution)/shard_map/ppermute | solution.py:262
  44.3 8.7 %collective-permute-start.10 = (bf16[672,640]{1,0:T(8,128)(2,1)S(1)}, bf16[672,640]{1,0:T(8,128)(2,1)S(1)}, u32[]{:S(2)}, u32[]{:S(2)}) collective-permute-start(bf16[672,640]{1,0:T(8,128)(2,1)S(1)} %collective-permute-done.8.b1), channel_id=1, source_target_pairs={{0,64},{64,0},{1,65},{65,1},{2,66},{66,2},{3,67},{67,3},{4,68},{68... | collective-permute-start | bytes 2580488 | tf_op jit(solution)/shard_map/ppermute | solution.py:50
  53.4 8.5 %collective-permute-start.6 = (bf16[128,640]{1,0:T(8,128)(2,1)S(1)}, bf16[128,640]{1,0:T(8,128)(2,1)S(1)}, u32[]{:S(2)}, u32[]{:S(2)}) collective-permute-start(bf16[128,640]{1,0:T(8,128)(2,1)S(1)} %copy-done.2), channel_id=1, source_target_pairs={{192,6},{193,7},{194,70},{195,71},{196,134},{197,135},{198,198},{1... | collective-permute-start | bytes 491528 | tf_op jit(solution)/shard_map/ppermute | solution.py:259
  65.3 1.3 collective-permute-done.13.b1
  67.7 2.0 %shard_map.124 = bf16[128,640]{1,0:T(8,128)(2,1)S(1)} custom-call(bf16[128,640]{1,0:T(8,128)(2,1)S(1)} %collective-permute-done.6.g, bf16[128,640]{1,0:T(8,128)(2,1)S(1)} %collective-permute-done.7.x_ref.x, f32[1,640]{1,0:T(1,128)S(1)} %slice_add_fusion.2.gain_ref.gain, bf16[640,640]{1,0:T(8,128)(2,1)S(1)} %get-tuple-element.66.refs_0_, ...), custom_call_target="tpu_custom_call" | custom-call | flops 838860800 | bytes 4194304 | tf_op jit(solution)/shard_map/pallas_call | solution.py:208
  70.5 6.0 %collective-permute-done.14.g = bf16[128,640]{1,0:T(8,128)(2,1)S(1)} collective-permute-done((bf16[128,640]{1,0:T(8,128)(2,1)S(1)}, bf16[128,640]{1,0:T(8,128)(2,1)S(1)}, u32[]{:S(2)}, u32[]{:S(2)}) %collective-permute-start.14) | collective-permute-done | bytes 163872 | tf_op jit(solution)/shard_map/ppermute | solution.py:298
  76.5 2.0 %shard_map.125 = bf16[128,640]{1,0:T(8,128)(2,1)S(1)} custom-call(bf16[128,640]{1,0:T(8,128)(2,1)S(1)} %collective-permute-done.14.g, bf16[128,640]{1,0:T(8,128)(2,1)S(1)} %collective-permute-done.7.x_ref.x, f32[1,640]{1,0:T(1,128)S(1)} %slice_add_fusion.2.gain_ref.gain, bf16[640,640]{1,0:T(8,128)(2,1)S(1)} %get-tuple-element.66.refs_0_, ...), custom_call_target="tpu_custom_call" | custom-call | flops 838860800 | bytes 4194304 | tf_op jit(solution)/shard_map/pallas_call | solution.py:208
  79.1 4.4 %collective-permute-done.15.g = bf16[128,640]{1,0:T(8,128)(2,1)S(1)} collective-permute-done((bf16[128,640]{1,0:T(8,128)(2,1)S(1)}, bf16[128,640]{1,0:T(8,128)(2,1)S(1)}, u32[]{:S(2)}, u32[]{:S(2)}) %collective-permute-start.15) | collective-permute-done | bytes 163872 | tf_op jit(solution)/shard_map/ppermute | solution.py:298
  83.6 2.0 %shard_map.126 = bf16[128,640]{1,0:T(8,128)(2,1)S(1)} custom-call(bf16[128,640]{1,0:T(8,128)(2,1)S(1)} %collective-permute-done.15.g, bf16[128,640]{1,0:T(8,128)(2,1)S(1)} %collective-permute-done.7.x_ref.x, f32[1,640]{1,0:T(1,128)S(1)} %slice_add_fusion.2.gain_ref.gain, bf16[640,640]{1,0:T(8,128)(2,1)S(1)} %get-tuple-element.66.refs_0_, ...), custom_call_target="tpu_custom_call" | custom-call | flops 838860800 | bytes 4194304 | tf_op jit(solution)/shard_map/pallas_call | solution.py:208
  85.6 1.3 collective-permute-start.16
  86.9 2.9 %collective-permute-done.16 = bf16[128,640]{1,0:T(8,128)(2,1)S(1)} collective-permute-done((bf16[128,640]{1,0:T(8,128)(2,1)S(1)}, bf16[128,640]{1,0:T(8,128)(2,1)S(1)}, u32[]{:S(2)}, u32[]{:S(2)}) %collective-permute-start.16) | collective-permute-done | bytes 163872 | tf_op jit(solution)/shard_map/ppermute | solution.py:298
  90.5 2.8 %collective-permute-start.17 = (bf16[1280,640]{1,0:T(8,128)(2,1)S(1)}, bf16[1280,640]{1,0:T(8,128)(2,1)S(1)}, u32[]{:S(2)}, u32[]{:S(2)}) collective-permute-start(bf16[1280,640]{1,0:T(8,128)(2,1)S(1)} %shard_map.127), channel_id=1, source_target_pairs={{0,64},{64,0},{1,65},{65,1},{2,66},{66,2},{3,67},{67,3},{4,68},{68... | collective-permute-start | bytes 4915208 | tf_op jit(solution)/shard_map/ppermute | solution.py:50
  93.3 2.0 %shard_map.128 = (bf16[128,640]{1,0:T(8,128)(2,1)S(1)}, f32[1,640]{1,0:T(1,128)S(1)}, bf16[128,640]{1,0:T(8,128)(2,1)S(1)}, bf16[128,640]{1,0:T(8,128)(2,1)S(1)}...) custom-call(bf16[128,640]{1,0:T(8,128)(2,1)S(1)} %add_add_fusion.right.g.grad, ...), custom_call_target="tpu_custom_call" | custom-call | flops 838860800 | bytes 4194304 | tf_op jit(solution)/shard_map/pallas_call | solution.py:208
  97.7 3.0 %collective-permute-done.19.gain_there = f32[1,640]{1,0:T(1,128)S(1)} collective-permute-done((f32[1,640]{1,0:T(1,128)S(1)}, f32[1,640]{1,0:T(1,128)S(1)}, u32[]{:S(2)}, u32[]{:S(2)}) %collective-permute-start.19) | collective-permute-done | bytes 2592 | tf_op jit(solution)/shard_map/ppermute | solution.py:50
  103.3 12.2 %collective-permute-start.23 = (bf16[128,640]{1,0:T(8,128)(2,1)S(1)}, bf16[128,640]{1,0:T(8,128)(2,1)S(1)}, u32[]{:S(2)}, u32[]{:S(2)}) collective-permute-start(bf16[128,640]{1,0:T(8,128)(2,1)S(1)} %get-tuple-element.98), channel_id=1, source_target_pairs={{0,0},{1,1},{64,2},{65,3},{128,4},{129,5},{192,6},{193,7},{8,8},{9... | collective-permute-start | bytes 491528 | tf_op jit(solution)/shard_map/ppermute | solution.py:317
  115.5 3.2 %collective-permute-done.23.value = bf16[128,640]{1,0:T(8,128)(2,1)S(1)} collective-permute-done((bf16[128,640]{1,0:T(8,128)(2,1)S(1)}, bf16[128,640]{1,0:T(8,128)(2,1)S(1)}, u32[]{:S(2)}, u32[]{:S(2)}) %collective-permute-start.23) | collective-permute-done | bytes 163872 | tf_op jit(solution)/shard_map/ppermute | solution.py:317
  119.3 4.8 %collective-permute-done.22.s3 = bf16[656,640]{1,0:T(8,128)(2,1)S(1)} collective-permute-done((bf16[656,640]{1,0:T(8,128)(2,1)S(1)}, bf16[656,640]{1,0:T(8,128)(2,1)S(1)}, u32[]{:S(2)}, u32[]{:S(2)}) %collective-permute-start.22) | collective-permute-done | bytes 839712 | tf_op jit(solution)/shard_map/ppermute | solution.py:321
  124.7 5.9 %collective-permute-start.24 = (bf16[176,640]{1,0:T(8,128)(2,1)S(1)}, bf16[176,640]{1,0:T(8,128)(2,1)S(1)}, u32[]{:S(2)}, u32[]{:S(2)}) collective-permute-start(bf16[176,640]{1,0:T(8,128)(2,1)S(1)} %get-tuple-element.105), channel_id=1, source_target_pairs={{0,48},{1,49},{16,0},{17,1},{32,16},{33,17},{48,32},{49,33},{64,19... | collective-permute-start | bytes 675848 | tf_op jit(solution)/shard_map/ppermute | solution.py:326
  131.9 1.6 %collective-permute-done.24 = bf16[176,640]{1,0:T(8,128)(2,1)S(1)} collective-permute-done((bf16[176,640]{1,0:T(8,128)(2,1)S(1)}, bf16[176,640]{1,0:T(8,128)(2,1)S(1)}, u32[]{:S(2)}, u32[]{:S(2)}) %collective-permute-start.24) | collective-permute-done | bytes 225312 | tf_op jit(solution)/shard_map/ppermute | solution.py:326
  133.5 3.4 %collective-permute-done.25 = bf16[176,640]{1,0:T(8,128)(2,1)S(1)} collective-permute-done((bf16[176,640]{1,0:T(8,128)(2,1)S(1)}, bf16[176,640]{1,0:T(8,128)(2,1)S(1)}, u32[]{:S(2)}, u32[]{:S(2)}) %collective-permute-start.25) | collective-permute-done | bytes 225312 | tf_op jit(solution)/shard_map/ppermute | solution.py:326
  138.2 8.7 %collective-permute-start.27 = (bf16[88,640]{1,0:T(8,128)(2,1)S(1)}, bf16[88,640]{1,0:T(8,128)(2,1)S(1)}, u32[]{:S(2)}, u32[]{:S(2)}) collective-permute-start(bf16[88,640]{1,0:T(8,128)(2,1)S(1)} %concatenate.30), channel_id=1, source_target_pairs={{0,0},{1,1},{64,2},{65,3},{128,4},{129,5},{192,6},{193,7},{8,8},{9... | collective-permute-start | bytes 337928 | tf_op jit(solution)/shard_map/ppermute | solution.py:333
  147.4 3.2 %collective-permute-done.27 = bf16[88,640]{1,0:T(8,128)(2,1)S(1)} collective-permute-done((bf16[88,640]{1,0:T(8,128)(2,1)S(1)}, bf16[88,640]{1,0:T(8,128)(2,1)S(1)}, u32[]{:S(2)}, u32[]{:S(2)}) %collective-permute-start.27) | collective-permute-done | bytes 112672 | tf_op jit(solution)/shard_map/ppermute | solution.py:333
  150.7 5.9 %collective-permute-done.28 = bf16[88,640]{1,0:T(8,128)(2,1)S(1)} collective-permute-done((bf16[88,640]{1,0:T(8,128)(2,1)S(1)}, bf16[88,640]{1,0:T(8,128)(2,1)S(1)}, u32[]{:S(2)}, u32[]{:S(2)}) %collective-permute-start.28) | collective-permute-done | bytes 112672 | tf_op jit(solution)/shard_map/ppermute | solution.py:333
  (84 shorter events, 25.5 us)
Async XLA Ops:
  0.6 1.7 %copy-start = (bf16[1,256,40]{1,2,0:T(8,128)(2,1)S(1)}, bf16[1,256,40]{1,2,0:T(8,128)(2,1)}, u32[]{:S(2)}) copy-start(bf16[1,256,40]{1,2,0:T(8,128)(2,1)} %param.14) | copy-start | bytes 61444
  5.1 13.9 %collective-permute-start.1 = (bf16[88,640]{1,0:T(8,128)(2,1)S(1)}, bf16[88,640]{1,0:T(8,128)(2,1)S(1)}, u32[]{:S(2)}, u32[]{:S(2)}) collective-permute-start(bf16[88,640]{1,0:T(8,128)(2,1)S(1)} %concatenate.27), channel_id=1, source_target_pairs={{0,8},{1,9},{2,72},{3,73},{4,136},{5,137},{6,200},{7,201},{8,0},{9... | collective-permute-start | bytes 337928 | tf_op jit(solution)/shard_map/ppermute | solution.py:239
  11.2 9.1 %collective-permute-start = (bf16[88,640]{1,0:T(8,128)(2,1)S(1)}, bf16[88,640]{1,0:T(8,128)(2,1)S(1)}, u32[]{:S(2)}, u32[]{:S(2)}) collective-permute-start(bf16[88,640]{1,0:T(8,128)(2,1)S(1)} %concatenate.27), channel_id=1, source_target_pairs={{0,0},{1,1},{2,64},{3,65},{4,128},{5,129},{6,192},{7,193},{8,8},{9... | collective-permute-start | bytes 337928 | tf_op jit(solution)/shard_map/ppermute | solution.py:239
  20.3 10.7 %copy-start.1 = (bf16[1,128,640]{2,1,0:T(8,128)(2,1)S(1)}, bf16[1,128,640]{2,1,0:T(8,128)(2,1)}, u32[]{:S(2)}) copy-start(bf16[1,128,640]{2,1,0:T(8,128)(2,1)} %param.9) | copy-start | bytes 491524
  20.4 4.8 %collective-permute-start.4 = (bf16[168,640]{1,0:T(8,128)(2,1)S(1)}, bf16[168,640]{1,0:T(8,128)(2,1)S(1)}, u32[]{:S(2)}, u32[]{:S(2)}) collective-permute-start(bf16[168,640]{1,0:T(8,128)(2,1)S(1)} %concatenate.28), channel_id=1, source_target_pairs={{0,48},{1,49},{16,0},{17,1},{32,16},{33,17},{48,32},{49,33},{64,19... | collective-permute-start | bytes 645128 | tf_op jit(solution)/shard_map/ppermute | solution.py:252
  20.5 7.7 %collective-permute-start.3 = (bf16[168,640]{1,0:T(8,128)(2,1)S(1)}, bf16[168,640]{1,0:T(8,128)(2,1)S(1)}, u32[]{:S(2)}, u32[]{:S(2)}) collective-permute-start(bf16[168,640]{1,0:T(8,128)(2,1)S(1)} %concatenate.28), channel_id=1, source_target_pairs={{0,32},{1,33},{16,48},{17,49},{32,0},{33,1},{48,16},{49,17},{64,65... | collective-permute-start | bytes 645128 | tf_op jit(solution)/shard_map/ppermute | solution.py:252
  22.8 6.5 %collective-permute-start.2 = (bf16[168,640]{1,0:T(8,128)(2,1)S(1)}, bf16[168,640]{1,0:T(8,128)(2,1)S(1)}, u32[]{:S(2)}, u32[]{:S(2)}) collective-permute-start(bf16[168,640]{1,0:T(8,128)(2,1)S(1)} %concatenate.28), channel_id=1, source_target_pairs={{0,16},{1,17},{16,32},{17,33},{32,48},{33,49},{48,0},{49,1},{64,19... | collective-permute-start | bytes 645128 | tf_op jit(solution)/shard_map/ppermute | solution.py:252
  28.2 25.1 %copy-start.2 = (bf16[128,640]{1,0:T(8,128)(2,1)S(1)}, bf16[128,640]{1,0:T(8,128)(2,1)}, u32[]{:S(2)}) copy-start(bf16[128,640]{1,0:T(8,128)(2,1)} %param.10) | copy-start | bytes 491524
  29.8 14.5 %collective-permute-start.8 = (bf16[672,640]{1,0:T(8,128)(2,1)S(1)}, bf16[672,640]{1,0:T(8,128)(2,1)S(1)}, u32[]{:S(2)}, u32[]{:S(2)}) collective-permute-start(bf16[672,640]{1,0:T(8,128)(2,1)S(1)} %concatenate.29.b0), channel_id=1, source_target_pairs={{0,128},{1,129},{16,144},{17,145},{32,160},{33,161},{48,176},{49,1... | collective-permute-start | bytes 2580488 | tf_op jit(solution)/shard_map/ppermute | solution.py:262
  31.1 22.3 %collective-permute-start.7 = (bf16[128,640]{1,0:T(8,128)(2,1)S(1)}, bf16[128,640]{1,0:T(8,128)(2,1)S(1)}, u32[]{:S(2)}, u32[]{:S(2)}) collective-permute-start(bf16[128,640]{1,0:T(8,128)(2,1)S(1)} %bitcast.23), channel_id=1, source_target_pairs={{0,0},{1,1},{2,64},{3,65},{4,128},{5,129},{6,192},{7,193},{8,8},{9... | collective-permute-start | bytes 491528 | tf_op jit(solution)/shard_map/ppermute | solution.py:258
  38.4 23.6 %collective-permute-start.11 = (bf16[672,640]{1,0:T(8,128)(2,1)S(1)}, bf16[672,640]{1,0:T(8,128)(2,1)S(1)}, u32[]{:S(2)}, u32[]{:S(2)}) collective-permute-start(bf16[672,640]{1,0:T(8,128)(2,1)S(1)} %concatenate.29.b0), channel_id=1, source_target_pairs={{0,1},{1,0},{16,17},{17,16},{32,33},{33,32},{48,49},{49,48},{64,96... | collective-permute-start | bytes 2580488 | tf_op jit(solution)/shard_map/ppermute | solution.py:262
  39.0 23.7 %collective-permute-start.9 = (bf16[672,640]{1,0:T(8,128)(2,1)S(1)}, bf16[672,640]{1,0:T(8,128)(2,1)S(1)}, u32[]{:S(2)}, u32[]{:S(2)}) collective-permute-start(bf16[672,640]{1,0:T(8,128)(2,1)S(1)} %concatenate.29.b0), channel_id=1, source_target_pairs={{0,64},{64,0},{1,65},{65,1},{2,66},{66,2},{3,67},{67,3},{4,68},{68... | collective-permute-start | bytes 2580488 | tf_op jit(solution)/shard_map/ppermute | solution.py:50
  42.2 22.0 %collective-permute-start.5 = (bf16[672,640]{1,0:T(8,128)(2,1)S(1)}, bf16[672,640]{1,0:T(8,128)(2,1)S(1)}, u32[]{:S(2)}, u32[]{:S(2)}) collective-permute-start(bf16[672,640]{1,0:T(8,128)(2,1)S(1)} %concatenate.29.b0), channel_id=1, source_target_pairs={{0,129},{1,128},{16,145},{17,144},{32,161},{33,160},{48,177},{49,1... | collective-permute-start | bytes 2580488 | tf_op jit(solution)/shard_map/ppermute | solution.py:262
  44.3 18.4 %collective-permute-start.10 = (bf16[672,640]{1,0:T(8,128)(2,1)S(1)}, bf16[672,640]{1,0:T(8,128)(2,1)S(1)}, u32[]{:S(2)}, u32[]{:S(2)}) collective-permute-start(bf16[672,640]{1,0:T(8,128)(2,1)S(1)} %collective-permute-done.8.b1), channel_id=1, source_target_pairs={{0,64},{64,0},{1,65},{65,1},{2,66},{66,2},{3,67},{67,3},{4,68},{68... | collective-permute-start | bytes 2580488 | tf_op jit(solution)/shard_map/ppermute | solution.py:50
  53.4 10.8 %collective-permute-start.6 = (bf16[128,640]{1,0:T(8,128)(2,1)S(1)}, bf16[128,640]{1,0:T(8,128)(2,1)S(1)}, u32[]{:S(2)}, u32[]{:S(2)}) collective-permute-start(bf16[128,640]{1,0:T(8,128)(2,1)S(1)} %copy-done.2), channel_id=1, source_target_pairs={{192,6},{193,7},{194,70},{195,71},{196,134},{197,135},{198,198},{1... | collective-permute-start | bytes 491528 | tf_op jit(solution)/shard_map/ppermute | solution.py:259
  62.0 3.3 %collective-permute-start.12 = (bf16[672,640]{1,0:T(8,128)(2,1)S(1)}, bf16[672,640]{1,0:T(8,128)(2,1)S(1)}, u32[]{:S(2)}, u32[]{:S(2)}) collective-permute-start(bf16[672,640]{1,0:T(8,128)(2,1)S(1)} %collective-permute-done.11.b0), channel_id=1, source_target_pairs={{0,64},{64,0},{1,65},{65,1},{2,66},{66,2},{3,67},{67,3},{4,68},{68... | collective-permute-start | bytes 2580488 | tf_op jit(solution)/shard_map/ppermute | solution.py:50
  64.2 2.4 %collective-permute-start.13 = (bf16[672,640]{1,0:T(8,128)(2,1)S(1)}, bf16[672,640]{1,0:T(8,128)(2,1)S(1)}, u32[]{:S(2)}, u32[]{:S(2)}) collective-permute-start(bf16[672,640]{1,0:T(8,128)(2,1)S(1)} %collective-permute-done.5.b1), channel_id=1, source_target_pairs={{0,64},{64,0},{1,65},{65,1},{2,66},{66,2},{3,67},{67,3},{4,68},{68... | collective-permute-start | bytes 2580488 | tf_op jit(solution)/shard_map/ppermute | solution.py:50
  69.7 6.8 %collective-permute-start.14 = (bf16[128,640]{1,0:T(8,128)(2,1)S(1)}, bf16[128,640]{1,0:T(8,128)(2,1)S(1)}, u32[]{:S(2)}, u32[]{:S(2)}) collective-permute-start(bf16[128,640]{1,0:T(8,128)(2,1)S(1)} %shard_map.124), channel_id=1, source_target_pairs={{0,14},{2,0},{4,2},{6,4},{8,6},{10,8},{12,10},{14,12},{1,15},{3,1}... | collective-permute-start | bytes 491528 | tf_op jit(solution)/shard_map/ppermute | solution.py:298
  78.5 5.1 %collective-permute-start.15 = (bf16[128,640]{1,0:T(8,128)(2,1)S(1)}, bf16[128,640]{1,0:T(8,128)(2,1)S(1)}, u32[]{:S(2)}, u32[]{:S(2)}) collective-permute-start(bf16[128,640]{1,0:T(8,128)(2,1)S(1)} %shard_map.125), channel_id=1, source_target_pairs={{0,14},{2,0},{4,2},{6,4},{8,6},{10,8},{12,10},{14,12},{1,15},{3,1}... | collective-permute-start | bytes 491528 | tf_op jit(solution)/shard_map/ppermute | solution.py:298
  85.6 4.2 %collective-permute-start.16 = (bf16[128,640]{1,0:T(8,128)(2,1)S(1)}, bf16[128,640]{1,0:T(8,128)(2,1)S(1)}, u32[]{:S(2)}, u32[]{:S(2)}) collective-permute-start(bf16[128,640]{1,0:T(8,128)(2,1)S(1)} %shard_map.126), channel_id=1, source_target_pairs={{0,14},{2,0},{4,2},{6,4},{8,6},{10,8},{12,10},{14,12},{1,15},{3,1}... | collective-permute-start | bytes 491528 | tf_op jit(solution)/shard_map/ppermute | solution.py:298
  90.5 6.0 %collective-permute-start.17 = (bf16[1280,640]{1,0:T(8,128)(2,1)S(1)}, bf16[1280,640]{1,0:T(8,128)(2,1)S(1)}, u32[]{:S(2)}, u32[]{:S(2)}) collective-permute-start(bf16[1280,640]{1,0:T(8,128)(2,1)S(1)} %shard_map.127), channel_id=1, source_target_pairs={{0,64},{64,0},{1,65},{65,1},{2,66},{66,2},{3,67},{67,3},{4,68},{68... | collective-permute-start | bytes 4915208 | tf_op jit(solution)/shard_map/ppermute | solution.py:50
  97.1 3.6 %collective-permute-start.18 = (bf16[1280,640]{1,0:T(8,128)(2,1)S(1)}, bf16[1280,640]{1,0:T(8,128)(2,1)S(1)}, u32[]{:S(2)}, u32[]{:S(2)}) collective-permute-start(bf16[1280,640]{1,0:T(8,128)(2,1)S(1)} %shard_map.129), channel_id=1, source_target_pairs={{0,64},{64,0},{1,65},{65,1},{2,66},{66,2},{3,67},{67,3},{4,68},{68... | collective-permute-start | bytes 4915208 | tf_op jit(solution)/shard_map/ppermute | solution.py:50
  97.5 3.1 %collective-permute-start.19 = (f32[1,640]{1,0:T(1,128)S(1)}, f32[1,640]{1,0:T(1,128)S(1)}, u32[]{:S(2)}, u32[]{:S(2)}) collective-permute-start(f32[1,640]{1,0:T(1,128)S(1)} %get-tuple-element.93.gain_here), channel_id=1, source_target_pairs={{0,64},{64,0},{1,65},{65,1},{2,66},{66,2},{3,67},{67,3},{4,68},{68... | collective-permute-start | bytes 7688 | tf_op jit(solution)/shard_map/ppermute | solution.py:50
  101.7 17.6 %collective-permute-start.20 = (bf16[656,640]{1,0:T(8,128)(2,1)S(1)}, bf16[656,640]{1,0:T(8,128)(2,1)S(1)}, u32[]{:S(2)}, u32[]{:S(2)}) collective-permute-start(bf16[656,640]{1,0:T(8,128)(2,1)S(1)} %get-tuple-element.95), channel_id=1, source_target_pairs={{0,129},{1,128},{16,145},{17,144},{32,161},{33,160},{48,177},{49,1... | collective-permute-start | bytes 2519048 | tf_op jit(solution)/shard_map/ppermute | solution.py:321
  102.1 17.2 %collective-permute-start.21 = (bf16[656,640]{1,0:T(8,128)(2,1)S(1)}, bf16[656,640]{1,0:T(8,128)(2,1)S(1)}, u32[]{:S(2)}, u32[]{:S(2)}) collective-permute-start(bf16[656,640]{1,0:T(8,128)(2,1)S(1)} %get-tuple-element.96), channel_id=1, source_target_pairs={{0,1},{1,0},{16,17},{17,16},{32,33},{33,32},{48,49},{49,48},{64,96... | collective-permute-start | bytes 2519048 | tf_op jit(solution)/shard_map/ppermute | solution.py:321
  102.6 21.6 %collective-permute-start.22 = (bf16[656,640]{1,0:T(8,128)(2,1)S(1)}, bf16[656,640]{1,0:T(8,128)(2,1)S(1)}, u32[]{:S(2)}, u32[]{:S(2)}) collective-permute-start(bf16[656,640]{1,0:T(8,128)(2,1)S(1)} %get-tuple-element.97), channel_id=1, source_target_pairs={{0,128},{1,129},{16,144},{17,145},{32,160},{33,161},{48,176},{49,1... | collective-permute-start | bytes 2519048 | tf_op jit(solution)/shard_map/ppermute | solution.py:321
  103.3 15.4 %collective-permute-start.23 = (bf16[128,640]{1,0:T(8,128)(2,1)S(1)}, bf16[128,640]{1,0:T(8,128)(2,1)S(1)}, u32[]{:S(2)}, u32[]{:S(2)}) collective-permute-start(bf16[128,640]{1,0:T(8,128)(2,1)S(1)} %get-tuple-element.98), channel_id=1, source_target_pairs={{0,0},{1,1},{64,2},{65,3},{128,4},{129,5},{192,6},{193,7},{8,8},{9... | collective-permute-start | bytes 491528 | tf_op jit(solution)/shard_map/ppermute | solution.py:317
  124.7 8.9 %collective-permute-start.24 = (bf16[176,640]{1,0:T(8,128)(2,1)S(1)}, bf16[176,640]{1,0:T(8,128)(2,1)S(1)}, u32[]{:S(2)}, u32[]{:S(2)}) collective-permute-start(bf16[176,640]{1,0:T(8,128)(2,1)S(1)} %get-tuple-element.105), channel_id=1, source_target_pairs={{0,48},{1,49},{16,0},{17,1},{32,16},{33,17},{48,32},{49,33},{64,19... | collective-permute-start | bytes 675848 | tf_op jit(solution)/shard_map/ppermute | solution.py:326
  130.6 6.3 %collective-permute-start.25 = (bf16[176,640]{1,0:T(8,128)(2,1)S(1)}, bf16[176,640]{1,0:T(8,128)(2,1)S(1)}, u32[]{:S(2)}, u32[]{:S(2)}) collective-permute-start(bf16[176,640]{1,0:T(8,128)(2,1)S(1)} %get-tuple-element.106), channel_id=1, source_target_pairs={{0,32},{1,33},{16,48},{17,49},{32,0},{33,1},{48,16},{49,17},{64,65... | collective-permute-start | bytes 675848 | tf_op jit(solution)/shard_map/ppermute | solution.py:326
  131.1 6.8 %collective-permute-start.26 = (bf16[176,640]{1,0:T(8,128)(2,1)S(1)}, bf16[176,640]{1,0:T(8,128)(2,1)S(1)}, u32[]{:S(2)}, u32[]{:S(2)}) collective-permute-start(bf16[176,640]{1,0:T(8,128)(2,1)S(1)} %get-tuple-element.107), channel_id=1, source_target_pairs={{0,16},{1,17},{16,32},{17,33},{32,48},{33,49},{48,0},{49,1},{64,19... | collective-permute-start | bytes 675848 | tf_op jit(solution)/shard_map/ppermute | solution.py:326
  138.2 12.5 %collective-permute-start.27 = (bf16[88,640]{1,0:T(8,128)(2,1)S(1)}, bf16[88,640]{1,0:T(8,128)(2,1)S(1)}, u32[]{:S(2)}, u32[]{:S(2)}) collective-permute-start(bf16[88,640]{1,0:T(8,128)(2,1)S(1)} %concatenate.30), channel_id=1, source_target_pairs={{0,0},{1,1},{64,2},{65,3},{128,4},{129,5},{192,6},{193,7},{8,8},{9... | collective-permute-start | bytes 337928 | tf_op jit(solution)/shard_map/ppermute | solution.py:333
  147.0 9.6 %collective-permute-start.28 = (bf16[88,640]{1,0:T(8,128)(2,1)S(1)}, bf16[88,640]{1,0:T(8,128)(2,1)S(1)}, u32[]{:S(2)}, u32[]{:S(2)}) collective-permute-start(bf16[88,640]{1,0:T(8,128)(2,1)S(1)} %concatenate.31), channel_id=1, source_target_pairs={{8,0},{9,1},{72,2},{73,3},{136,4},{137,5},{200,6},{201,7},{0,8},{1... | collective-permute-start | bytes 337928 | tf_op jit(solution)/shard_map/ppermute | solution.py:333

commit v7 on v6

--- a/solution.py
+++ b/solution.py
@@ -11,6 +11,7 @@
 COLUMN = ("yl", "core", "z", "yh")
 PLANE = ("yl", "core", "x", "yh")
 SIDE = 4
+ORDER = (2, 1, 3)
 PAD = 16
 LINES = 8
 VMEM_LIMIT = 28 << 20
@@ -232,9 +233,11 @@
     ).astype(bf16)
     cond = dot_plain(time_feats, time_proj[0]) + dot_plain(picks, class_table[0])
     cond_row = jnp.concatenate([part.reshape(1, -1) for part in two_parts(cond)], axis=1)
-    shard = jnp.concatenate(
-        [w_in[0].T, w_out[0], cond_row, *three_parts(gains), jnp.zeros((4, chan), bf16)], axis=0
-    )
+    line = jnp.arange(8, dtype=jnp.int32)[:, None]
+    spare = jnp.zeros((8, chan), bf16)
+    for n, row in enumerate((cond_row, *three_parts(gains))):
+        spare = jnp.where(line == n, row, spare)
+    shard = jnp.concatenate([w_in[0].T, w_out[0], spare], axis=0)
 
     one, two = (lax.ppermute(shard, COLUMN, home_to_work(flip)) for flip in (0, 1))
     chunk = jnp.concatenate(
@@ -249,7 +252,7 @@
         ],
         axis=0,
     )
-    chunks = [chunk] + [lax.ppermute(chunk, PLANE, along(1, k)) for k in range(1, SIDE)]
+    chunks = [chunk] + [lax.ppermute(chunk, PLANE, along(1, k)) for k in ORDER]
     quarter = jnp.concatenate(
         [part[: 4 * own] for part in chunks] + [part[4 * own :] for part in chunks], axis=0
     )
@@ -259,7 +262,7 @@
     cot_rows = lax.ppermute(
         cotangent, COLUMN, [pair for pair in home_to_work(0) if pair[0] >> 4 == 3]
     )
-    near = [quarter] + [lax.ppermute(quarter, PLANE, along(2, k)) for k in range(1, SIDE)]
+    near = [quarter] + [lax.ppermute(quarter, PLANE, along(2, k)) for k in ORDER]
 
     width = half // 2
     entry = jnp.arange(chan, dtype=jnp.int32)[:, None]
@@ -318,12 +321,12 @@
     grad_home = kernel(copy_kernel, [((rows, chan), bf16)])(grad_home)
 
     parts = [sums[0]] + [
-        lax.ppermute(sums[k], PLANE, along(2, SIDE - k)) for k in range(1, SIDE)
+        lax.ppermute(part, PLANE, along(2, SIDE - k)) for k, part in zip(ORDER, sums[1:])
     ]
     *parts, grad_home = lax.optimization_barrier((*parts, grad_home))
     sums = kernel(stage_sum_kernel, [((4 * own + PAD, chan), bf16)] * SIDE)(*parts)
     parts = [sums[0]] + [
-        lax.ppermute(sums[k], PLANE, along(1, SIDE - k)) for k in range(1, SIDE)
+        lax.ppermute(part, PLANE, along(1, SIDE - k)) for k, part in zip(ORDER, sums[1:])
     ]
     total = sum(part.astype(f32) for part in parts)
     gain_lines = list(two_parts(total[4 * own : 4 * own + 1] + total[4 * own + 1 : 4 * own + 2]))

time: 158 us -> 157 us (level)
  waiting for transfers between devices: 54 us -> 49.3 us
  starting transfers between devices: 80.7 us -> 84.9 us
  local copies, waits for them, and re-layouts: 2.66 us -> 0.99 us
    ppermute x7, starting transfers between devices: 15.5 us -> 27.4 us  [across_cores(): return lax.ppermute(value, 'core', [(0, 1), (1, 0)])]
    ppermute x1, starting transfers between devices: 8.54 us -> 1.3 us  [on_device(): lax.ppermute(cotangent, COLUMN, [pair for pair in home_to_work(0) if pair...]
    ppermute x9, starting transfers between devices: 13.1 us -> 9.64 us  [the longest x3 4.91 us: on_device(): chunks = [chunk] + [lax.ppermute(chunk, PLANE, along(1, k)) for k in ORDER]]
    ppermute x1, starting transfers between devices: 12.2 us -> 9.1 us  [on_device(): grad_home = lax.ppermute(grad_in, COLUMN, work_to_home(0))]
    ppermute x3, waiting for transfers between devices: 13.4 us -> 10.6 us  [on_device(): grad = lax.ppermute(turn(grad, *held), 'z', next_section())]
    ppermute x3, starting transfers between devices: 2.8 us -> 5.05 us  [on_device(): grad = lax.ppermute(turn(grad, *held), 'z', next_section())]
    ppermute x3, waiting for transfers between devices: 2.1 us -> 0.01 us  [on_device(): lax.ppermute(quarter, PLANE, along(2, k))]
    ppermute x1, starting transfers between devices: 7.29 us -> 9.22 us  [on_device(): x_rows = lax.ppermute(checkpoints[0], COLUMN, home_to_work(0))]
  transfers between devices with their start and end apart: 29 -> 29, of which waited for: 20 -> 18; matrix products, arithmetic and copies ran while one was open for 0% -> 0% of each run, Pallas kernels for 3% -> 3%
where the time goes in v7:
time: 157 us
  starting transfers between devices  84.9 us (54%)
  waiting for transfers between devices  49.3 us (31%)
  Pallas kernels  15.1 us (10%)
  other arithmetic  4.34 us (3%)
    ppermute x7, starting transfers between devices, across_cores(): return lax.ppermute(value, 'core', [(0, 1), (1, 0)])  27.4 us
    pallas_call x13, Pallas kernels, call(): pl.pallas_call(body, out_shape=shapes, in_specs=[whole] * len(operands),...  15.1 us
    ppermute x3, waiting for transfers between devices, on_device(): grad = lax.ppermute(turn(grad, *held), 'z', next_section())  10.6 us
    ppermute x2, starting transfers between devices, on_device(): lax.ppermute(shard, COLUMN, home_to_work(flip))  10.4 us
    ppermute x2, starting transfers between devices, on_device(): lax.ppermute(jnp.concatenate([total[flip * own:(flip + 1) * own], total[(...  9.93 us
    ppermute x1, starting transfers between devices, on_device(): x_rows = lax.ppermute(checkpoints[0], COLUMN, home_to_work(0))  9.22 us
    ppermute x1, starting transfers between devices, on_device(): grad_home = lax.ppermute(grad_in, COLUMN, work_to_home(0))  9.1 us
    ppermute x2, waiting for transfers between devices, on_device(): lax.ppermute(jnp.concatenate([total[flip * own:(flip + 1) * own], total[(...  8.82 us
  transfers between devices with their start and end apart: 29, of which 18 were waited for; matrix products, arithmetic and copies ran while one was open for 0% of the time, Pallas kernels for 3%

profile of v7, /device:TPU:9, one launch (start us, length us, event | category | flops | bytes accessed | tf_op | source)
XLA Modules:
  0.0 156.6 jit_solution(20547771051180569)
XLA Ops:
  4.4 6.1 %collective-permute-start.1 = (bf16[88,640]{1,0:T(8,128)(2,1)S(1)}, bf16[88,640]{1,0:T(8,128)(2,1)S(1)}, u32[]{:S(2)}, u32[]{:S(2)}) collective-permute-start(bf16[88,640]{1,0:T(8,128)(2,1)S(1)} %pad_maximum_fusion), channel_id=1, source_target_pairs={{0,8},{1,9},{2,72},{3,73},{4,136},{5,137},{6,200},{7,201},{8,0},{9... | collective-permute-start | bytes 337928 | tf_op jit(solution)/shard_map/ppermute | solution.py:242
  10.5 4.2 %collective-permute-start = (bf16[88,640]{1,0:T(8,128)(2,1)S(1)}, bf16[88,640]{1,0:T(8,128)(2,1)S(1)}, u32[]{:S(2)}, u32[]{:S(2)}) collective-permute-start(bf16[88,640]{1,0:T(8,128)(2,1)S(1)} %pad_maximum_fusion), channel_id=1, source_target_pairs={{0,0},{1,1},{2,64},{3,65},{4,128},{5,129},{6,192},{7,193},{8,8},{9... | collective-permute-start | bytes 337928 | tf_op jit(solution)/shard_map/ppermute | solution.py:242
  14.7 3.5 %collective-permute-done.1 = bf16[88,640]{1,0:T(8,128)(2,1)S(1)} collective-permute-done((bf16[88,640]{1,0:T(8,128)(2,1)S(1)}, bf16[88,640]{1,0:T(8,128)(2,1)S(1)}, u32[]{:S(2)}, u32[]{:S(2)}) %collective-permute-start.1) | collective-permute-done | bytes 112672 | tf_op jit(solution)/shard_map/ppermute | solution.py:242
  21.3 3.4 %collective-permute-start.2 = (bf16[168,640]{1,0:T(8,128)(2,1)S(1)}, bf16[168,640]{1,0:T(8,128)(2,1)S(1)}, u32[]{:S(2)}, u32[]{:S(2)}) collective-permute-start(bf16[168,640]{1,0:T(8,128)(2,1)S(1)} %concatenate.28), channel_id=1, source_target_pairs={{0,32},{1,33},{16,48},{17,49},{32,0},{33,1},{48,16},{49,17},{64,65... | collective-permute-start | bytes 645128 | tf_op jit(solution)/shard_map/ppermute | solution.py:255
  24.7 1.7 %collective-permute-done.3 = bf16[168,640]{1,0:T(8,128)(2,1)S(1)} collective-permute-done((bf16[168,640]{1,0:T(8,128)(2,1)S(1)}, bf16[168,640]{1,0:T(8,128)(2,1)S(1)}, u32[]{:S(2)}, u32[]{:S(2)}) %collective-permute-start.3) | collective-permute-done | bytes 215072 | tf_op jit(solution)/shard_map/ppermute | solution.py:255
  26.4 1.5 collective-permute-done.2
  28.4 2.8 %collective-permute-start.8 = (bf16[672,640]{1,0:T(8,128)(2,1)S(1)}, bf16[672,640]{1,0:T(8,128)(2,1)S(1)}, u32[]{:S(2)}, u32[]{:S(2)}) collective-permute-start(bf16[672,640]{1,0:T(8,128)(2,1)S(1)} %concatenate.29.b0), channel_id=1, source_target_pairs={{0,1},{1,0},{16,17},{17,16},{32,33},{33,32},{48,49},{49,48},{64,96... | collective-permute-start | bytes 2580488 | tf_op jit(solution)/shard_map/ppermute | solution.py:265
  31.2 9.2 %collective-permute-start.7 = (bf16[128,640]{1,0:T(8,128)(2,1)S(1)}, bf16[128,640]{1,0:T(8,128)(2,1)S(1)}, u32[]{:S(2)}, u32[]{:S(2)}) collective-permute-start(bf16[128,640]{1,0:T(8,128)(2,1)S(1)} %bitcast.23), channel_id=1, source_target_pairs={{0,0},{1,1},{2,64},{3,65},{4,128},{5,129},{6,192},{7,193},{8,8},{9... | collective-permute-start | bytes 491528 | tf_op jit(solution)/shard_map/ppermute | solution.py:261
  40.5 6.2 %collective-permute-start.9 = (bf16[672,640]{1,0:T(8,128)(2,1)S(1)}, bf16[672,640]{1,0:T(8,128)(2,1)S(1)}, u32[]{:S(2)}, u32[]{:S(2)}) collective-permute-start(bf16[672,640]{1,0:T(8,128)(2,1)S(1)} %concatenate.29.b0), channel_id=1, source_target_pairs={{0,64},{64,0},{1,65},{65,1},{2,66},{66,2},{3,67},{67,3},{4,68},{68... | collective-permute-start | bytes 2580488 | tf_op jit(solution)/shard_map/ppermute | solution.py:51
  46.7 12.2 %collective-permute-start.10 = (bf16[672,640]{1,0:T(8,128)(2,1)S(1)}, bf16[672,640]{1,0:T(8,128)(2,1)S(1)}, u32[]{:S(2)}, u32[]{:S(2)}) collective-permute-start(bf16[672,640]{1,0:T(8,128)(2,1)S(1)} %collective-permute-done.8.b1), channel_id=1, source_target_pairs={{0,64},{64,0},{1,65},{65,1},{2,66},{66,2},{3,67},{67,3},{4,68},{68... | collective-permute-start | bytes 2580488 | tf_op jit(solution)/shard_map/ppermute | solution.py:51
  62.9 5.1 %collective-permute-start.13 = (bf16[672,640]{1,0:T(8,128)(2,1)S(1)}, bf16[672,640]{1,0:T(8,128)(2,1)S(1)}, u32[]{:S(2)}, u32[]{:S(2)}) collective-permute-start(bf16[672,640]{1,0:T(8,128)(2,1)S(1)} %collective-permute-done.5.b1), channel_id=1, source_target_pairs={{0,64},{64,0},{1,65},{65,1},{2,66},{66,2},{3,67},{67,3},{4,68},{68... | collective-permute-start | bytes 2580488 | tf_op jit(solution)/shard_map/ppermute | solution.py:51
  71.1 2.0 %shard_map.124 = bf16[128,640]{1,0:T(8,128)(2,1)S(1)} custom-call(bf16[128,640]{1,0:T(8,128)(2,1)S(1)} %collective-permute-done.6.g, bf16[128,640]{1,0:T(8,128)(2,1)S(1)} %collective-permute-done.7.x_ref.x, f32[1,640]{1,0:T(1,128)S(1)} %slice_add_fusion.2.gain_ref.gain, bf16[640,640]{1,0:T(8,128)(2,1)S(1)} %get-tuple-element.66.refs_0_, ...), custom_call_target="tpu_custom_call" | custom-call | flops 838860800 | bytes 4194304 | tf_op jit(solution)/shard_map/pallas_call | solution.py:209
  73.4 5.4 %collective-permute-done.14.g = bf16[128,640]{1,0:T(8,128)(2,1)S(1)} collective-permute-done((bf16[128,640]{1,0:T(8,128)(2,1)S(1)}, bf16[128,640]{1,0:T(8,128)(2,1)S(1)}, u32[]{:S(2)}, u32[]{:S(2)}) %collective-permute-start.14) | collective-permute-done | bytes 163872 | tf_op jit(solution)/shard_map/ppermute | solution.py:301
  78.8 2.0 %shard_map.125 = bf16[128,640]{1,0:T(8,128)(2,1)S(1)} custom-call(bf16[128,640]{1,0:T(8,128)(2,1)S(1)} %collective-permute-done.14.g, bf16[128,640]{1,0:T(8,128)(2,1)S(1)} %collective-permute-done.7.x_ref.x, f32[1,640]{1,0:T(1,128)S(1)} %slice_add_fusion.2.gain_ref.gain, bf16[640,640]{1,0:T(8,128)(2,1)S(1)} %get-tuple-element.66.refs_0_, ...), custom_call_target="tpu_custom_call" | custom-call | flops 838860800 | bytes 4194304 | tf_op jit(solution)/shard_map/pallas_call | solution.py:209
  80.8 1.6 %collective-permute-start.15 = (bf16[128,640]{1,0:T(8,128)(2,1)S(1)}, bf16[128,640]{1,0:T(8,128)(2,1)S(1)}, u32[]{:S(2)}, u32[]{:S(2)}) collective-permute-start(bf16[128,640]{1,0:T(8,128)(2,1)S(1)} %shard_map.125), channel_id=1, source_target_pairs={{0,14},{2,0},{4,2},{6,4},{8,6},{10,8},{12,10},{14,12},{1,15},{3,1}... | collective-permute-start | bytes 491528 | tf_op jit(solution)/shard_map/ppermute | solution.py:301
  82.4 2.9 %collective-permute-done.15.g = bf16[128,640]{1,0:T(8,128)(2,1)S(1)} collective-permute-done((bf16[128,640]{1,0:T(8,128)(2,1)S(1)}, bf16[128,640]{1,0:T(8,128)(2,1)S(1)}, u32[]{:S(2)}, u32[]{:S(2)}) %collective-permute-start.15) | collective-permute-done | bytes 163872 | tf_op jit(solution)/shard_map/ppermute | solution.py:301
  85.4 2.0 %shard_map.126 = bf16[128,640]{1,0:T(8,128)(2,1)S(1)} custom-call(bf16[128,640]{1,0:T(8,128)(2,1)S(1)} %collective-permute-done.15.g, bf16[128,640]{1,0:T(8,128)(2,1)S(1)} %collective-permute-done.7.x_ref.x, f32[1,640]{1,0:T(1,128)S(1)} %slice_add_fusion.2.gain_ref.gain, bf16[640,640]{1,0:T(8,128)(2,1)S(1)} %get-tuple-element.66.refs_0_, ...), custom_call_target="tpu_custom_call" | custom-call | flops 838860800 | bytes 4194304 | tf_op jit(solution)/shard_map/pallas_call | solution.py:209
  87.4 3.2 %collective-permute-start.16 = (bf16[128,640]{1,0:T(8,128)(2,1)S(1)}, bf16[128,640]{1,0:T(8,128)(2,1)S(1)}, u32[]{:S(2)}, u32[]{:S(2)}) collective-permute-start(bf16[128,640]{1,0:T(8,128)(2,1)S(1)} %shard_map.126), channel_id=1, source_target_pairs={{0,14},{2,0},{4,2},{6,4},{8,6},{10,8},{12,10},{14,12},{1,15},{3,1}... | collective-permute-start | bytes 491528 | tf_op jit(solution)/shard_map/ppermute | solution.py:301
  90.5 2.3 %collective-permute-done.16 = bf16[128,640]{1,0:T(8,128)(2,1)S(1)} collective-permute-done((bf16[128,640]{1,0:T(8,128)(2,1)S(1)}, bf16[128,640]{1,0:T(8,128)(2,1)S(1)}, u32[]{:S(2)}, u32[]{:S(2)}) %collective-permute-start.16) | collective-permute-done | bytes 163872 | tf_op jit(solution)/shard_map/ppermute | solution.py:301
  93.5 2.7 %collective-permute-start.17 = (bf16[1280,640]{1,0:T(8,128)(2,1)S(1)}, bf16[1280,640]{1,0:T(8,128)(2,1)S(1)}, u32[]{:S(2)}, u32[]{:S(2)}) collective-permute-start(bf16[1280,640]{1,0:T(8,128)(2,1)S(1)} %shard_map.127), channel_id=1, source_target_pairs={{0,64},{64,0},{1,65},{65,1},{2,66},{66,2},{3,67},{67,3},{4,68},{68... | collective-permute-start | bytes 4915208 | tf_op jit(solution)/shard_map/ppermute | solution.py:51
  96.2 2.0 %shard_map.128 = (bf16[128,640]{1,0:T(8,128)(2,1)S(1)}, f32[1,640]{1,0:T(1,128)S(1)}, bf16[128,640]{1,0:T(8,128)(2,1)S(1)}, bf16[128,640]{1,0:T(8,128)(2,1)S(1)}...) custom-call(bf16[128,640]{1,0:T(8,128)(2,1)S(1)} %add_add_fusion.right.g.grad, ...), custom_call_target="tpu_custom_call" | custom-call | flops 838860800 | bytes 4194304 | tf_op jit(solution)/shard_map/pallas_call | solution.py:209
  100.5 3.0 %collective-permute-done.19.gain_there = f32[1,640]{1,0:T(1,128)S(1)} collective-permute-done((f32[1,640]{1,0:T(1,128)S(1)}, f32[1,640]{1,0:T(1,128)S(1)}, u32[]{:S(2)}, u32[]{:S(2)}) %collective-permute-start.19) | collective-permute-done | bytes 2592 | tf_op jit(solution)/shard_map/ppermute | solution.py:51
  106.2 9.1 %collective-permute-start.23 = (bf16[128,640]{1,0:T(8,128)(2,1)S(1)}, bf16[128,640]{1,0:T(8,128)(2,1)S(1)}, u32[]{:S(2)}, u32[]{:S(2)}) collective-permute-start(bf16[128,640]{1,0:T(8,128)(2,1)S(1)} %get-tuple-element.98), channel_id=1, source_target_pairs={{0,0},{1,1},{64,2},{65,3},{128,4},{129,5},{192,6},{193,7},{8,8},{9... | collective-permute-start | bytes 491528 | tf_op jit(solution)/shard_map/ppermute | solution.py:320
  115.4 2.9 %collective-permute-done.23.value = bf16[128,640]{1,0:T(8,128)(2,1)S(1)} collective-permute-done((bf16[128,640]{1,0:T(8,128)(2,1)S(1)}, bf16[128,640]{1,0:T(8,128)(2,1)S(1)}, u32[]{:S(2)}, u32[]{:S(2)}) %collective-permute-start.23) | collective-permute-done | bytes 163872 | tf_op jit(solution)/shard_map/ppermute | solution.py:320
  119.0 4.9 %collective-permute-done.21.s2 = bf16[656,640]{1,0:T(8,128)(2,1)S(1)} collective-permute-done((bf16[656,640]{1,0:T(8,128)(2,1)S(1)}, bf16[656,640]{1,0:T(8,128)(2,1)S(1)}, u32[]{:S(2)}, u32[]{:S(2)}) %collective-permute-start.21) | collective-permute-done | bytes 839712 | tf_op jit(solution)/shard_map/ppermute | solution.py:324
  123.8 2.8 %collective-permute-done.22.s3 = bf16[656,640]{1,0:T(8,128)(2,1)S(1)} collective-permute-done((bf16[656,640]{1,0:T(8,128)(2,1)S(1)}, bf16[656,640]{1,0:T(8,128)(2,1)S(1)}, u32[]{:S(2)}, u32[]{:S(2)}) %collective-permute-start.22) | collective-permute-done | bytes 839712 | tf_op jit(solution)/shard_map/ppermute | solution.py:324
  127.1 1.6 %collective-permute-start.24 = (bf16[176,640]{1,0:T(8,128)(2,1)S(1)}, bf16[176,640]{1,0:T(8,128)(2,1)S(1)}, u32[]{:S(2)}, u32[]{:S(2)}) collective-permute-start(bf16[176,640]{1,0:T(8,128)(2,1)S(1)} %get-tuple-element.105), channel_id=1, source_target_pairs={{0,32},{1,33},{16,48},{17,49},{32,0},{33,1},{48,16},{49,17},{64,65... | collective-permute-start | bytes 675848 | tf_op jit(solution)/shard_map/ppermute | solution.py:329
  130.2 3.4 %collective-permute-done.24 = bf16[176,640]{1,0:T(8,128)(2,1)S(1)} collective-permute-done((bf16[176,640]{1,0:T(8,128)(2,1)S(1)}, bf16[176,640]{1,0:T(8,128)(2,1)S(1)}, u32[]{:S(2)}, u32[]{:S(2)}) %collective-permute-start.24) | collective-permute-done | bytes 225312 | tf_op jit(solution)/shard_map/ppermute | solution.py:329
  133.6 2.6 %collective-permute-done.25 = bf16[176,640]{1,0:T(8,128)(2,1)S(1)} collective-permute-done((bf16[176,640]{1,0:T(8,128)(2,1)S(1)}, bf16[176,640]{1,0:T(8,128)(2,1)S(1)}, u32[]{:S(2)}, u32[]{:S(2)}) %collective-permute-start.25) | collective-permute-done | bytes 225312 | tf_op jit(solution)/shard_map/ppermute | solution.py:329
  136.5 9.8 %collective-permute-start.27 = (bf16[88,640]{1,0:T(8,128)(2,1)S(1)}, bf16[88,640]{1,0:T(8,128)(2,1)S(1)}, u32[]{:S(2)}, u32[]{:S(2)}) collective-permute-start(bf16[88,640]{1,0:T(8,128)(2,1)S(1)} %concatenate.30), channel_id=1, source_target_pairs={{0,0},{1,1},{64,2},{65,3},{128,4},{129,5},{192,6},{193,7},{8,8},{9... | collective-permute-start | bytes 337928 | tf_op jit(solution)/shard_map/ppermute | solution.py:336
  146.5 3.6 %collective-permute-done.27 = bf16[88,640]{1,0:T(8,128)(2,1)S(1)} collective-permute-done((bf16[88,640]{1,0:T(8,128)(2,1)S(1)}, bf16[88,640]{1,0:T(8,128)(2,1)S(1)}, u32[]{:S(2)}, u32[]{:S(2)}) %collective-permute-start.27) | collective-permute-done | bytes 112672 | tf_op jit(solution)/shard_map/ppermute | solution.py:336
  150.1 5.2 %collective-permute-done.28 = bf16[88,640]{1,0:T(8,128)(2,1)S(1)} collective-permute-done((bf16[88,640]{1,0:T(8,128)(2,1)S(1)}, bf16[88,640]{1,0:T(8,128)(2,1)S(1)}, u32[]{:S(2)}, u32[]{:S(2)}) %collective-permute-start.28) | collective-permute-done | bytes 112672 | tf_op jit(solution)/shard_map/ppermute | solution.py:336
  (85 shorter events, 24.5 us)
Async XLA Ops:
  0.6 1.7 %copy-start = (bf16[1,256,40]{1,2,0:T(8,128)(2,1)S(1)}, bf16[1,256,40]{1,2,0:T(8,128)(2,1)}, u32[]{:S(2)}) copy-start(bf16[1,256,40]{1,2,0:T(8,128)(2,1)} %param.14) | copy-start | bytes 61444
  4.4 13.9 %collective-permute-start.1 = (bf16[88,640]{1,0:T(8,128)(2,1)S(1)}, bf16[88,640]{1,0:T(8,128)(2,1)S(1)}, u32[]{:S(2)}, u32[]{:S(2)}) collective-permute-start(bf16[88,640]{1,0:T(8,128)(2,1)S(1)} %pad_maximum_fusion), channel_id=1, source_target_pairs={{0,8},{1,9},{2,72},{3,73},{4,136},{5,137},{6,200},{7,201},{8,0},{9... | collective-permute-start | bytes 337928 | tf_op jit(solution)/shard_map/ppermute | solution.py:242
  10.5 9.1 %collective-permute-start = (bf16[88,640]{1,0:T(8,128)(2,1)S(1)}, bf16[88,640]{1,0:T(8,128)(2,1)S(1)}, u32[]{:S(2)}, u32[]{:S(2)}) collective-permute-start(bf16[88,640]{1,0:T(8,128)(2,1)S(1)} %pad_maximum_fusion), channel_id=1, source_target_pairs={{0,0},{1,1},{2,64},{3,65},{4,128},{5,129},{6,192},{7,193},{8,8},{9... | collective-permute-start | bytes 337928 | tf_op jit(solution)/shard_map/ppermute | solution.py:242
  19.6 11.6 %copy-start.1 = (bf16[1,128,640]{2,1,0:T(8,128)(2,1)S(1)}, bf16[1,128,640]{2,1,0:T(8,128)(2,1)}, u32[]{:S(2)}) copy-start(bf16[1,128,640]{2,1,0:T(8,128)(2,1)} %param.9) | copy-start | bytes 491524
  19.7 4.9 %collective-permute-start.4 = (bf16[168,640]{1,0:T(8,128)(2,1)S(1)}, bf16[168,640]{1,0:T(8,128)(2,1)S(1)}, u32[]{:S(2)}, u32[]{:S(2)}) collective-permute-start(bf16[168,640]{1,0:T(8,128)(2,1)S(1)} %concatenate.28), channel_id=1, source_target_pairs={{0,48},{1,49},{16,0},{17,1},{32,16},{33,17},{48,32},{49,33},{64,19... | collective-permute-start | bytes 645128 | tf_op jit(solution)/shard_map/ppermute | solution.py:255
  19.8 6.6 %collective-permute-start.3 = (bf16[168,640]{1,0:T(8,128)(2,1)S(1)}, bf16[168,640]{1,0:T(8,128)(2,1)S(1)}, u32[]{:S(2)}, u32[]{:S(2)}) collective-permute-start(bf16[168,640]{1,0:T(8,128)(2,1)S(1)} %concatenate.28), channel_id=1, source_target_pairs={{0,16},{1,17},{16,32},{17,33},{32,48},{33,49},{48,0},{49,1},{64,19... | collective-permute-start | bytes 645128 | tf_op jit(solution)/shard_map/ppermute | solution.py:255
  21.3 6.6 %collective-permute-start.2 = (bf16[168,640]{1,0:T(8,128)(2,1)S(1)}, bf16[168,640]{1,0:T(8,128)(2,1)S(1)}, u32[]{:S(2)}, u32[]{:S(2)}) collective-permute-start(bf16[168,640]{1,0:T(8,128)(2,1)S(1)} %concatenate.28), channel_id=1, source_target_pairs={{0,32},{1,33},{16,48},{17,49},{32,0},{33,1},{48,16},{49,17},{64,65... | collective-permute-start | bytes 645128 | tf_op jit(solution)/shard_map/ppermute | solution.py:255
  26.4 32.9 %copy-start.2 = (bf16[128,640]{1,0:T(8,128)(2,1)S(1)}, bf16[128,640]{1,0:T(8,128)(2,1)}, u32[]{:S(2)}) copy-start(bf16[128,640]{1,0:T(8,128)(2,1)} %param.10) | copy-start | bytes 491524
  28.4 18.4 %collective-permute-start.8 = (bf16[672,640]{1,0:T(8,128)(2,1)S(1)}, bf16[672,640]{1,0:T(8,128)(2,1)S(1)}, u32[]{:S(2)}, u32[]{:S(2)}) collective-permute-start(bf16[672,640]{1,0:T(8,128)(2,1)S(1)} %concatenate.29.b0), channel_id=1, source_target_pairs={{0,1},{1,0},{16,17},{17,16},{32,33},{33,32},{48,49},{49,48},{64,96... | collective-permute-start | bytes 2580488 | tf_op jit(solution)/shard_map/ppermute | solution.py:265
  31.2 28.2 %collective-permute-start.7 = (bf16[128,640]{1,0:T(8,128)(2,1)S(1)}, bf16[128,640]{1,0:T(8,128)(2,1)S(1)}, u32[]{:S(2)}, u32[]{:S(2)}) collective-permute-start(bf16[128,640]{1,0:T(8,128)(2,1)S(1)} %bitcast.23), channel_id=1, source_target_pairs={{0,0},{1,1},{2,64},{3,65},{4,128},{5,129},{6,192},{7,193},{8,8},{9... | collective-permute-start | bytes 491528 | tf_op jit(solution)/shard_map/ppermute | solution.py:261
  40.4 20.2 %collective-permute-start.11 = (bf16[672,640]{1,0:T(8,128)(2,1)S(1)}, bf16[672,640]{1,0:T(8,128)(2,1)S(1)}, u32[]{:S(2)}, u32[]{:S(2)}) collective-permute-start(bf16[672,640]{1,0:T(8,128)(2,1)S(1)} %concatenate.29.b0), channel_id=1, source_target_pairs={{0,128},{1,129},{16,144},{17,145},{32,160},{33,161},{48,176},{49,1... | collective-permute-start | bytes 2580488 | tf_op jit(solution)/shard_map/ppermute | solution.py:265
  40.5 21.2 %collective-permute-start.9 = (bf16[672,640]{1,0:T(8,128)(2,1)S(1)}, bf16[672,640]{1,0:T(8,128)(2,1)S(1)}, u32[]{:S(2)}, u32[]{:S(2)}) collective-permute-start(bf16[672,640]{1,0:T(8,128)(2,1)S(1)} %concatenate.29.b0), channel_id=1, source_target_pairs={{0,64},{64,0},{1,65},{65,1},{2,66},{66,2},{3,67},{67,3},{4,68},{68... | collective-permute-start | bytes 2580488 | tf_op jit(solution)/shard_map/ppermute | solution.py:51
  46.7 16.2 %collective-permute-start.5 = (bf16[672,640]{1,0:T(8,128)(2,1)S(1)}, bf16[672,640]{1,0:T(8,128)(2,1)S(1)}, u32[]{:S(2)}, u32[]{:S(2)}) collective-permute-start(bf16[672,640]{1,0:T(8,128)(2,1)S(1)} %concatenate.29.b0), channel_id=1, source_target_pairs={{0,129},{1,128},{16,145},{17,144},{32,161},{33,160},{48,177},{49,1... | collective-permute-start | bytes 2580488 | tf_op jit(solution)/shard_map/ppermute | solution.py:265
  46.7 15.0 %collective-permute-start.10 = (bf16[672,640]{1,0:T(8,128)(2,1)S(1)}, bf16[672,640]{1,0:T(8,128)(2,1)S(1)}, u32[]{:S(2)}, u32[]{:S(2)}) collective-permute-start(bf16[672,640]{1,0:T(8,128)(2,1)S(1)} %collective-permute-done.8.b1), channel_id=1, source_target_pairs={{0,64},{64,0},{1,65},{65,1},{2,66},{66,2},{3,67},{67,3},{4,68},{68... | collective-permute-start | bytes 2580488 | tf_op jit(solution)/shard_map/ppermute | solution.py:51
  59.3 3.6 %collective-permute-start.6 = (bf16[128,640]{1,0:T(8,128)(2,1)S(1)}, bf16[128,640]{1,0:T(8,128)(2,1)S(1)}, u32[]{:S(2)}, u32[]{:S(2)}) collective-permute-start(bf16[128,640]{1,0:T(8,128)(2,1)S(1)} %copy-done.2), channel_id=1, source_target_pairs={{192,6},{193,7},{194,70},{195,71},{196,134},{197,135},{198,198},{1... | collective-permute-start | bytes 491528 | tf_op jit(solution)/shard_map/ppermute | solution.py:262
  60.7 8.4 %collective-permute-start.12 = (bf16[672,640]{1,0:T(8,128)(2,1)S(1)}, bf16[672,640]{1,0:T(8,128)(2,1)S(1)}, u32[]{:S(2)}, u32[]{:S(2)}) collective-permute-start(bf16[672,640]{1,0:T(8,128)(2,1)S(1)} %collective-permute-done.11.b0), channel_id=1, source_target_pairs={{0,64},{64,0},{1,65},{65,1},{2,66},{66,2},{3,67},{67,3},{4,68},{68... | collective-permute-start | bytes 2580488 | tf_op jit(solution)/shard_map/ppermute | solution.py:51
  62.9 7.1 %collective-permute-start.13 = (bf16[672,640]{1,0:T(8,128)(2,1)S(1)}, bf16[672,640]{1,0:T(8,128)(2,1)S(1)}, u32[]{:S(2)}, u32[]{:S(2)}) collective-permute-start(bf16[672,640]{1,0:T(8,128)(2,1)S(1)} %collective-permute-done.5.b1), channel_id=1, source_target_pairs={{0,64},{64,0},{1,65},{65,1},{2,66},{66,2},{3,67},{67,3},{4,68},{68... | collective-permute-start | bytes 2580488 | tf_op jit(solution)/shard_map/ppermute | solution.py:51
  73.1 5.7 %collective-permute-start.14 = (bf16[128,640]{1,0:T(8,128)(2,1)S(1)}, bf16[128,640]{1,0:T(8,128)(2,1)S(1)}, u32[]{:S(2)}, u32[]{:S(2)}) collective-permute-start(bf16[128,640]{1,0:T(8,128)(2,1)S(1)} %shard_map.124), channel_id=1, source_target_pairs={{0,14},{2,0},{4,2},{6,4},{8,6},{10,8},{12,10},{14,12},{1,15},{3,1}... | collective-permute-start | bytes 491528 | tf_op jit(solution)/shard_map/ppermute | solution.py:301
  80.8 4.6 %collective-permute-start.15 = (bf16[128,640]{1,0:T(8,128)(2,1)S(1)}, bf16[128,640]{1,0:T(8,128)(2,1)S(1)}, u32[]{:S(2)}, u32[]{:S(2)}) collective-permute-start(bf16[128,640]{1,0:T(8,128)(2,1)S(1)} %shard_map.125), channel_id=1, source_target_pairs={{0,14},{2,0},{4,2},{6,4},{8,6},{10,8},{12,10},{14,12},{1,15},{3,1}... | collective-permute-start | bytes 491528 | tf_op jit(solution)/shard_map/ppermute | solution.py:301
  87.4 5.4 %collective-permute-start.16 = (bf16[128,640]{1,0:T(8,128)(2,1)S(1)}, bf16[128,640]{1,0:T(8,128)(2,1)S(1)}, u32[]{:S(2)}, u32[]{:S(2)}) collective-permute-start(bf16[128,640]{1,0:T(8,128)(2,1)S(1)} %shard_map.126), channel_id=1, source_target_pairs={{0,14},{2,0},{4,2},{6,4},{8,6},{10,8},{12,10},{14,12},{1,15},{3,1}... | collective-permute-start | bytes 491528 | tf_op jit(solution)/shard_map/ppermute | solution.py:301
  93.5 5.9 %collective-permute-start.17 = (bf16[1280,640]{1,0:T(8,128)(2,1)S(1)}, bf16[1280,640]{1,0:T(8,128)(2,1)S(1)}, u32[]{:S(2)}, u32[]{:S(2)}) collective-permute-start(bf16[1280,640]{1,0:T(8,128)(2,1)S(1)} %shard_map.127), channel_id=1, source_target_pairs={{0,64},{64,0},{1,65},{65,1},{2,66},{66,2},{3,67},{67,3},{4,68},{68... | collective-permute-start | bytes 4915208 | tf_op jit(solution)/shard_map/ppermute | solution.py:51
  100.0 3.6 %collective-permute-start.18 = (bf16[1280,640]{1,0:T(8,128)(2,1)S(1)}, bf16[1280,640]{1,0:T(8,128)(2,1)S(1)}, u32[]{:S(2)}, u32[]{:S(2)}) collective-permute-start(bf16[1280,640]{1,0:T(8,128)(2,1)S(1)} %shard_map.129), channel_id=1, source_target_pairs={{0,64},{64,0},{1,65},{65,1},{2,66},{66,2},{3,67},{67,3},{4,68},{68... | collective-permute-start | bytes 4915208 | tf_op jit(solution)/shard_map/ppermute | solution.py:51
  100.4 3.1 %collective-permute-start.19 = (f32[1,640]{1,0:T(1,128)S(1)}, f32[1,640]{1,0:T(1,128)S(1)}, u32[]{:S(2)}, u32[]{:S(2)}) collective-permute-start(f32[1,640]{1,0:T(1,128)S(1)} %get-tuple-element.93.gain_here), channel_id=1, source_target_pairs={{0,64},{64,0},{1,65},{65,1},{2,66},{66,2},{3,67},{67,3},{4,68},{68... | collective-permute-start | bytes 7688 | tf_op jit(solution)/shard_map/ppermute | solution.py:51
  104.6 14.4 %collective-permute-start.20 = (bf16[656,640]{1,0:T(8,128)(2,1)S(1)}, bf16[656,640]{1,0:T(8,128)(2,1)S(1)}, u32[]{:S(2)}, u32[]{:S(2)}) collective-permute-start(bf16[656,640]{1,0:T(8,128)(2,1)S(1)} %get-tuple-element.95), channel_id=1, source_target_pairs={{0,1},{1,0},{16,17},{17,16},{32,33},{33,32},{48,49},{49,48},{64,96... | collective-permute-start | bytes 2519048 | tf_op jit(solution)/shard_map/ppermute | solution.py:324
  104.7 19.1 %collective-permute-start.21 = (bf16[656,640]{1,0:T(8,128)(2,1)S(1)}, bf16[656,640]{1,0:T(8,128)(2,1)S(1)}, u32[]{:S(2)}, u32[]{:S(2)}) collective-permute-start(bf16[656,640]{1,0:T(8,128)(2,1)S(1)} %get-tuple-element.96), channel_id=1, source_target_pairs={{0,129},{1,128},{16,145},{17,144},{32,161},{33,160},{48,177},{49,1... | collective-permute-start | bytes 2519048 | tf_op jit(solution)/shard_map/ppermute | solution.py:324
  104.8 21.8 %collective-permute-start.22 = (bf16[656,640]{1,0:T(8,128)(2,1)S(1)}, bf16[656,640]{1,0:T(8,128)(2,1)S(1)}, u32[]{:S(2)}, u32[]{:S(2)}) collective-permute-start(bf16[656,640]{1,0:T(8,128)(2,1)S(1)} %get-tuple-element.97), channel_id=1, source_target_pairs={{0,128},{1,129},{16,144},{17,145},{32,160},{33,161},{48,176},{49,1... | collective-permute-start | bytes 2519048 | tf_op jit(solution)/shard_map/ppermute | solution.py:324
  106.2 12.0 %collective-permute-start.23 = (bf16[128,640]{1,0:T(8,128)(2,1)S(1)}, bf16[128,640]{1,0:T(8,128)(2,1)S(1)}, u32[]{:S(2)}, u32[]{:S(2)}) collective-permute-start(bf16[128,640]{1,0:T(8,128)(2,1)S(1)} %get-tuple-element.98), channel_id=1, source_target_pairs={{0,0},{1,1},{64,2},{65,3},{128,4},{129,5},{192,6},{193,7},{8,8},{9... | collective-permute-start | bytes 491528 | tf_op jit(solution)/shard_map/ppermute | solution.py:320
  127.1 6.5 %collective-permute-start.24 = (bf16[176,640]{1,0:T(8,128)(2,1)S(1)}, bf16[176,640]{1,0:T(8,128)(2,1)S(1)}, u32[]{:S(2)}, u32[]{:S(2)}) collective-permute-start(bf16[176,640]{1,0:T(8,128)(2,1)S(1)} %get-tuple-element.105), channel_id=1, source_target_pairs={{0,32},{1,33},{16,48},{17,49},{32,0},{33,1},{48,16},{49,17},{64,65... | collective-permute-start | bytes 675848 | tf_op jit(solution)/shard_map/ppermute | solution.py:329
  128.7 7.5 %collective-permute-start.25 = (bf16[176,640]{1,0:T(8,128)(2,1)S(1)}, bf16[176,640]{1,0:T(8,128)(2,1)S(1)}, u32[]{:S(2)}, u32[]{:S(2)}) collective-permute-start(bf16[176,640]{1,0:T(8,128)(2,1)S(1)} %get-tuple-element.106), channel_id=1, source_target_pairs={{0,48},{1,49},{16,0},{17,1},{32,16},{33,17},{48,32},{49,33},{64,19... | collective-permute-start | bytes 675848 | tf_op jit(solution)/shard_map/ppermute | solution.py:329
  129.3 6.9 %collective-permute-start.26 = (bf16[176,640]{1,0:T(8,128)(2,1)S(1)}, bf16[176,640]{1,0:T(8,128)(2,1)S(1)}, u32[]{:S(2)}, u32[]{:S(2)}) collective-permute-start(bf16[176,640]{1,0:T(8,128)(2,1)S(1)} %get-tuple-element.107), channel_id=1, source_target_pairs={{0,16},{1,17},{16,32},{17,33},{32,48},{33,49},{48,0},{49,1},{64,19... | collective-permute-start | bytes 675848 | tf_op jit(solution)/shard_map/ppermute | solution.py:329
  136.5 13.6 %collective-permute-start.27 = (bf16[88,640]{1,0:T(8,128)(2,1)S(1)}, bf16[88,640]{1,0:T(8,128)(2,1)S(1)}, u32[]{:S(2)}, u32[]{:S(2)}) collective-permute-start(bf16[88,640]{1,0:T(8,128)(2,1)S(1)} %concatenate.30), channel_id=1, source_target_pairs={{0,0},{1,1},{64,2},{65,3},{128,4},{129,5},{192,6},{193,7},{8,8},{9... | collective-permute-start | bytes 337928 | tf_op jit(solution)/shard_map/ppermute | solution.py:336
  146.4 8.9 %collective-permute-start.28 = (bf16[88,640]{1,0:T(8,128)(2,1)S(1)}, bf16[88,640]{1,0:T(8,128)(2,1)S(1)}, u32[]{:S(2)}, u32[]{:S(2)}) collective-permute-start(bf16[88,640]{1,0:T(8,128)(2,1)S(1)} %concatenate.31), channel_id=1, source_target_pairs={{8,0},{9,1},{72,2},{73,3},{136,4},{137,5},{200,6},{201,7},{0,8},{1... | collective-permute-start | bytes 337928 | tf_op jit(solution)/shard_map/ppermute | solution.py:336

commit v8 on v7

--- a/solution.py
+++ b/solution.py
@@ -252,17 +252,20 @@
         ],
         axis=0,
     )
-    chunks = [chunk] + [lax.ppermute(chunk, PLANE, along(1, k)) for k in ORDER]
+    chunk, x_rows = lax.optimization_barrier((chunk, checkpoints[0]))
+    x_rows = lax.ppermute(x_rows, COLUMN, home_to_work(0))
+    chunks = [chunk] + [lax.ppermute(chunk, PLANE, along(1, k)) for k in range(1, SIDE)]
     quarter = jnp.concatenate(
         [part[: 4 * own] for part in chunks] + [part[4 * own :] for part in chunks], axis=0
     )
+    quarter, x_rows = lax.optimization_barrier((quarter, x_rows))
     gain_row = one[2 * own + 1 : 2 * own + 4].astype(f32)
     gain_row = gain_row[0:1] + gain_row[1:2] + gain_row[2:3]
-    x_rows = lax.ppermute(checkpoints[0], COLUMN, home_to_work(0))
+    near = [quarter] + [lax.ppermute(quarter, PLANE, along(2, k)) for k in ORDER]
+    cotangent, near[1] = lax.optimization_barrier((cotangent, near[1]))
     cot_rows = lax.ppermute(
         cotangent, COLUMN, [pair for pair in home_to_work(0) if pair[0] >> 4 == 3]
     )
-    near = [quarter] + [lax.ppermute(quarter, PLANE, along(2, k)) for k in ORDER]
 
     width = half // 2
     entry = jnp.arange(chan, dtype=jnp.int32)[:, None]
@@ -326,7 +329,7 @@
     *parts, grad_home = lax.optimization_barrier((*parts, grad_home))
     sums = kernel(stage_sum_kernel, [((4 * own + PAD, chan), bf16)] * SIDE)(*parts)
     parts = [sums[0]] + [
-        lax.ppermute(part, PLANE, along(1, SIDE - k)) for k, part in zip(ORDER, sums[1:])
+        lax.ppermute(part, PLANE, along(1, SIDE - k)) for k, part in enumerate(sums[1:], 1)
     ]
     total = sum(part.astype(f32) for part in parts)
     gain_lines = list(two_parts(total[4 * own : 4 * own + 1] + total[4 * own + 1 : 4 * own + 2]))

time: 157 us -> 155 us (0.987)
  starting transfers between devices: 84.9 us -> 79.9 us
  waiting for transfers between devices: 49.3 us -> 51.9 us
    ppermute x7, starting transfers between devices: 27.4 us -> 14.2 us  [across_cores(): return lax.ppermute(value, 'core', [(0, 1), (1, 0)])]
    ppermute x3, waiting for transfers between devices: 0.01 us -> 5.88 us  [on_device(): lax.ppermute(quarter, PLANE, along(2, k))]
    ppermute x4, starting transfers between devices: 14.1 us -> 9.36 us  [the longest x1 5.06 us: on_device(): x_rows = lax.ppermute(x_rows, COLUMN, home_to_work(0))]
    ppermute x2, starting transfers between devices: 9.93 us -> 14.5 us  [on_device(): lax.ppermute(jnp.concatenate([total[flip * own:(flip + 1) * own], total[(...]
    ppermute x3, starting transfers between devices: 5.05 us -> 8.5 us  [on_device(): grad = lax.ppermute(turn(grad, *held), 'z', next_section())]
    ppermute x3, starting transfers between devices: 2.9 us -> 5.45 us  [on_device(): lax.ppermute(quarter, PLANE, along(2, k))]
    ppermute x2, waiting for transfers between devices: 8.82 us -> 6.29 us  [on_device(): lax.ppermute(jnp.concatenate([total[flip * own:(flip + 1) * own], total[(...]
    ppermute x3, starting transfers between devices: 1.63 us -> 4 us  [on_device(): lax.ppermute(part, PLANE, along(2, SIDE - k))]
  transfers between devices with their start and end apart: 29 -> 29, of which waited for: 18 -> 19; matrix products, arithmetic and copies ran while one was open for 0% -> 0% of each run, Pallas kernels for 3% -> 3%
where the time goes in v8:
time: 155 us; the launch traced here: 154 us
  starting transfers between devices  79.9 us (52%)
  waiting for transfers between devices  51.9 us (33%)
  Pallas kernels  15.1 us (10%)
  other arithmetic  4.34 us (3%)
    pallas_call x13, Pallas kernels, call(): pl.pallas_call(body, out_shape=shapes, in_specs=[whole] * len(operands),...  15.1 us
    ppermute x2, starting transfers between devices, on_device(): lax.ppermute(jnp.concatenate([total[flip * own:(flip + 1) * own], total[(...  14.5 us
    ppermute x7, starting transfers between devices, across_cores(): return lax.ppermute(value, 'core', [(0, 1), (1, 0)])  14.2 us
    ppermute x2, starting transfers between devices, on_device(): lax.ppermute(shard, COLUMN, home_to_work(flip))  10.4 us
    ppermute x3, waiting for transfers between devices, on_device(): grad = lax.ppermute(turn(grad, *held), 'z', next_section())  8.62 us
    ppermute x3, starting transfers between devices, on_device(): grad = lax.ppermute(turn(grad, *held), 'z', next_section())  8.5 us
    ppermute x1, starting transfers between devices, on_device(): grad_home = lax.ppermute(grad_in, COLUMN, work_to_home(0))  6.84 us
    ppermute x2, waiting for transfers between devices, on_device(): lax.ppermute(jnp.concatenate([total[flip * own:(flip + 1) * own], total[(...  6.29 us
  transfers between devices with their start and end apart: 29, of which 19 were waited for; matrix products, arithmetic and copies ran while one was open for 0% of the time, Pallas kernels for 3%

profile of v8, /device:TPU:9, one launch (start us, length us, event | category | flops | bytes accessed | tf_op | source)
XLA Modules:
  0.0 154.0 jit_solution(11444018813318228429)
XLA Ops:
  4.4 6.1 %collective-permute-start.1 = (bf16[88,640]{1,0:T(8,128)(2,1)S(1)}, bf16[88,640]{1,0:T(8,128)(2,1)S(1)}, u32[]{:S(2)}, u32[]{:S(2)}) collective-permute-start(bf16[88,640]{1,0:T(8,128)(2,1)S(1)} %pad_maximum_fusion), channel_id=1, source_target_pairs={{0,8},{1,9},{2,72},{3,73},{4,136},{5,137},{6,200},{7,201},{8,0},{9... | collective-permute-start | bytes 337928 | tf_op jit(solution)/shard_map/ppermute | solution.py:242
  10.5 4.2 %collective-permute-start = (bf16[88,640]{1,0:T(8,128)(2,1)S(1)}, bf16[88,640]{1,0:T(8,128)(2,1)S(1)}, u32[]{:S(2)}, u32[]{:S(2)}) collective-permute-start(bf16[88,640]{1,0:T(8,128)(2,1)S(1)} %pad_maximum_fusion), channel_id=1, source_target_pairs={{0,0},{1,1},{2,64},{3,65},{4,128},{5,129},{6,192},{7,193},{8,8},{9... | collective-permute-start | bytes 337928 | tf_op jit(solution)/shard_map/ppermute | solution.py:242
  14.7 3.5 %collective-permute-done.1 = bf16[88,640]{1,0:T(8,128)(2,1)S(1)} collective-permute-done((bf16[88,640]{1,0:T(8,128)(2,1)S(1)}, bf16[88,640]{1,0:T(8,128)(2,1)S(1)}, u32[]{:S(2)}, u32[]{:S(2)}) %collective-permute-start.1) | collective-permute-done | bytes 112672 | tf_op jit(solution)/shard_map/ppermute | solution.py:242
  19.8 2.2 %collective-permute-start.3 = (bf16[168,640]{1,0:T(8,128)(2,1)S(1)}, bf16[168,640]{1,0:T(8,128)(2,1)S(1)}, u32[]{:S(2)}, u32[]{:S(2)}) collective-permute-start(bf16[168,640]{1,0:T(8,128)(2,1)S(1)} %concatenate.25), channel_id=1, source_target_pairs={{0,32},{1,33},{16,48},{17,49},{32,0},{33,1},{48,16},{49,17},{64,65... | collective-permute-start | bytes 645128 | tf_op jit(solution)/shard_map/ppermute | solution.py:257
  24.0 5.1 %collective-permute-start.5 = (bf16[128,640]{1,0:T(8,128)(2,1)}, bf16[128,640]{1,0:T(8,128)(2,1)S(1)}, u32[]{:S(2)}, u32[]{:S(2)}) collective-permute-start(bf16[128,640]{1,0:T(8,128)(2,1)} %bitcast.23), channel_id=1, source_target_pairs={{0,0},{1,1},{2,64},{3,65},{4,128},{5,129},{6,192},{7,193},{8,8},{9... | collective-permute-start | bytes 491528 | tf_op jit(solution)/shard_map/ppermute | solution.py:256
  29.3 4.4 %collective-permute-done.5.x_ref.x = bf16[128,640]{1,0:T(8,128)(2,1)S(1)} collective-permute-done((bf16[128,640]{1,0:T(8,128)(2,1)}, bf16[128,640]{1,0:T(8,128)(2,1)S(1)}, u32[]{:S(2)}, u32[]{:S(2)}) %collective-permute-start.5) | collective-permute-done | bytes 163872 | tf_op jit(solution)/shard_map/ppermute | solution.py:256
  33.7 2.7 %collective-permute-start.7 = (bf16[672,640]{1,0:T(8,128)(2,1)S(1)}, bf16[672,640]{1,0:T(8,128)(2,1)S(1)}, u32[]{:S(2)}, u32[]{:S(2)}) collective-permute-start(bf16[672,640]{1,0:T(8,128)(2,1)S(1)} %constant_dynamic-update-slice_fusion.b0), channel_id=1, source_target_pairs={{0,1},{1,0},{16,17},{17,16},{32,33},{33,32},{48,49},{49,48},{64,96... | collective-permute-start | bytes 2580488 | tf_op jit(solution)/shard_map/ppermute | solution.py:264
  36.7 2.3 %collective-permute-start.9 = (bf16[672,640]{1,0:T(8,128)(2,1)S(1)}, bf16[672,640]{1,0:T(8,128)(2,1)S(1)}, u32[]{:S(2)}, u32[]{:S(2)}) collective-permute-start(bf16[672,640]{1,0:T(8,128)(2,1)S(1)} %constant_dynamic-update-slice_fusion.b0), channel_id=1, source_target_pairs={{0,64},{64,0},{1,65},{65,1},{2,66},{66,2},{3,67},{67,3},{4,68},{68... | collective-permute-start | bytes 2580488 | tf_op jit(solution)/shard_map/ppermute | solution.py:51
  39.0 2.5 %collective-permute-start.6 = (bf16[672,640]{1,0:T(8,128)(2,1)S(1)}, bf16[672,640]{1,0:T(8,128)(2,1)S(1)}, u32[]{:S(2)}, u32[]{:S(2)}) collective-permute-start(bf16[672,640]{1,0:T(8,128)(2,1)S(1)} %constant_dynamic-update-slice_fusion.b0), channel_id=1, source_target_pairs={{0,129},{1,128},{16,145},{17,144},{32,161},{33,160},{48,177},{49,1... | collective-permute-start | bytes 2580488 | tf_op jit(solution)/shard_map/ppermute | solution.py:264
  41.5 5.5 %collective-permute-done.7.b1 = bf16[672,640]{1,0:T(8,128)(2,1)S(1)} collective-permute-done((bf16[672,640]{1,0:T(8,128)(2,1)S(1)}, bf16[672,640]{1,0:T(8,128)(2,1)S(1)}, u32[]{:S(2)}, u32[]{:S(2)}) %collective-permute-start.7) | collective-permute-done | bytes 860192 | tf_op jit(solution)/shard_map/ppermute | solution.py:264
  47.0 5.2 %collective-permute-start.10 = (bf16[672,640]{1,0:T(8,128)(2,1)S(1)}, bf16[672,640]{1,0:T(8,128)(2,1)S(1)}, u32[]{:S(2)}, u32[]{:S(2)}) collective-permute-start(bf16[672,640]{1,0:T(8,128)(2,1)S(1)} %collective-permute-done.7.b1), channel_id=1, source_target_pairs={{0,64},{64,0},{1,65},{65,1},{2,66},{66,2},{3,67},{67,3},{4,68},{68... | collective-permute-start | bytes 2580488 | tf_op jit(solution)/shard_map/ppermute | solution.py:51
  52.5 3.1 %collective-permute-start.8 = (bf16[128,640]{1,0:T(8,128)(2,1)S(1)}, bf16[128,640]{1,0:T(8,128)(2,1)S(1)}, u32[]{:S(2)}, u32[]{:S(2)}) collective-permute-start(bf16[128,640]{1,0:T(8,128)(2,1)S(1)} %copy-done.1), channel_id=1, source_target_pairs={{192,6},{193,7},{194,70},{195,71},{196,134},{197,135},{198,198},{1... | collective-permute-start | bytes 491528 | tf_op jit(solution)/shard_map/ppermute | solution.py:266
  58.0 3.3 %collective-permute-start.13 = (bf16[672,640]{1,0:T(8,128)(2,1)S(1)}, bf16[672,640]{1,0:T(8,128)(2,1)S(1)}, u32[]{:S(2)}, u32[]{:S(2)}) collective-permute-start(bf16[672,640]{1,0:T(8,128)(2,1)S(1)} %collective-permute-done.6.b1), channel_id=1, source_target_pairs={{0,64},{64,0},{1,65},{65,1},{2,66},{66,2},{3,67},{67,3},{4,68},{68... | collective-permute-start | bytes 2580488 | tf_op jit(solution)/shard_map/ppermute | solution.py:51
  64.4 2.0 %shard_map.124 = bf16[128,640]{1,0:T(8,128)(2,1)S(1)} custom-call(bf16[128,640]{1,0:T(8,128)(2,1)S(1)} %collective-permute-done.8.g, bf16[128,640]{1,0:T(8,128)(2,1)S(1)} %collective-permute-done.5.x_ref.x, f32[1,640]{1,0:T(1,128)S(1)} %slice_add_fusion.2.gain_ref.gain, bf16[640,640]{1,0:T(8,128)(2,1)S(1)} %get-tuple-element.78.refs_0_, ...), custom_call_target="tpu_custom_call" | custom-call | flops 838860800 | bytes 4194304 | tf_op jit(solution)/shard_map/pallas_call | solution.py:209
  68.2 3.8 %collective-permute-done.14.g = bf16[128,640]{1,0:T(8,128)(2,1)S(1)} collective-permute-done((bf16[128,640]{1,0:T(8,128)(2,1)S(1)}, bf16[128,640]{1,0:T(8,128)(2,1)S(1)}, u32[]{:S(2)}, u32[]{:S(2)}) %collective-permute-start.14) | collective-permute-done | bytes 163872 | tf_op jit(solution)/shard_map/ppermute | solution.py:304
  74.0 3.1 %collective-permute-start.15 = (bf16[128,640]{1,0:T(8,128)(2,1)S(1)}, bf16[128,640]{1,0:T(8,128)(2,1)S(1)}, u32[]{:S(2)}, u32[]{:S(2)}) collective-permute-start(bf16[128,640]{1,0:T(8,128)(2,1)S(1)} %shard_map.125), channel_id=1, source_target_pairs={{0,14},{2,0},{4,2},{6,4},{8,6},{10,8},{12,10},{14,12},{1,15},{3,1}... | collective-permute-start | bytes 491528 | tf_op jit(solution)/shard_map/ppermute | solution.py:304
  77.2 2.6 %collective-permute-done.15.g = bf16[128,640]{1,0:T(8,128)(2,1)S(1)} collective-permute-done((bf16[128,640]{1,0:T(8,128)(2,1)S(1)}, bf16[128,640]{1,0:T(8,128)(2,1)S(1)}, u32[]{:S(2)}, u32[]{:S(2)}) %collective-permute-start.15) | collective-permute-done | bytes 163872 | tf_op jit(solution)/shard_map/ppermute | solution.py:304
  79.7 2.0 %shard_map.126 = bf16[128,640]{1,0:T(8,128)(2,1)S(1)} custom-call(bf16[128,640]{1,0:T(8,128)(2,1)S(1)} %collective-permute-done.15.g, bf16[128,640]{1,0:T(8,128)(2,1)S(1)} %collective-permute-done.5.x_ref.x, f32[1,640]{1,0:T(1,128)S(1)} %slice_add_fusion.2.gain_ref.gain, bf16[640,640]{1,0:T(8,128)(2,1)S(1)} %get-tuple-element.78.refs_0_, ...), custom_call_target="tpu_custom_call" | custom-call | flops 838860800 | bytes 4194304 | tf_op jit(solution)/shard_map/pallas_call | solution.py:209
  81.7 3.5 %collective-permute-start.16 = (bf16[128,640]{1,0:T(8,128)(2,1)S(1)}, bf16[128,640]{1,0:T(8,128)(2,1)S(1)}, u32[]{:S(2)}, u32[]{:S(2)}) collective-permute-start(bf16[128,640]{1,0:T(8,128)(2,1)S(1)} %shard_map.126), channel_id=1, source_target_pairs={{0,14},{2,0},{4,2},{6,4},{8,6},{10,8},{12,10},{14,12},{1,15},{3,1}... | collective-permute-start | bytes 491528 | tf_op jit(solution)/shard_map/ppermute | solution.py:304
  85.2 2.3 %collective-permute-done.16 = bf16[128,640]{1,0:T(8,128)(2,1)S(1)} collective-permute-done((bf16[128,640]{1,0:T(8,128)(2,1)S(1)}, bf16[128,640]{1,0:T(8,128)(2,1)S(1)}, u32[]{:S(2)}, u32[]{:S(2)}) %collective-permute-start.16) | collective-permute-done | bytes 163872 | tf_op jit(solution)/shard_map/ppermute | solution.py:304
  88.1 2.8 %collective-permute-start.17 = (bf16[1280,640]{1,0:T(8,128)(2,1)S(1)}, bf16[1280,640]{1,0:T(8,128)(2,1)S(1)}, u32[]{:S(2)}, u32[]{:S(2)}) collective-permute-start(bf16[1280,640]{1,0:T(8,128)(2,1)S(1)} %shard_map.127), channel_id=1, source_target_pairs={{0,64},{64,0},{1,65},{65,1},{2,66},{66,2},{3,67},{67,3},{4,68},{68... | collective-permute-start | bytes 4915208 | tf_op jit(solution)/shard_map/ppermute | solution.py:51
  91.0 2.0 %shard_map.128 = (bf16[128,640]{1,0:T(8,128)(2,1)S(1)}, f32[1,640]{1,0:T(1,128)S(1)}, bf16[128,640]{1,0:T(8,128)(2,1)S(1)}, bf16[128,640]{1,0:T(8,128)(2,1)S(1)}...) custom-call(bf16[128,640]{1,0:T(8,128)(2,1)S(1)} %add_add_fusion.right.g.grad, ...), custom_call_target="tpu_custom_call" | custom-call | flops 838860800 | bytes 4194304 | tf_op jit(solution)/shard_map/pallas_call | solution.py:209
  95.3 3.0 %collective-permute-done.19.gain_there = f32[1,640]{1,0:T(1,128)S(1)} collective-permute-done((f32[1,640]{1,0:T(1,128)S(1)}, f32[1,640]{1,0:T(1,128)S(1)}, u32[]{:S(2)}, u32[]{:S(2)}) %collective-permute-start.19) | collective-permute-done | bytes 2592 | tf_op jit(solution)/shard_map/ppermute | solution.py:51
  101.0 2.3 %collective-permute-start.21 = (bf16[656,640]{1,0:T(8,128)(2,1)S(1)}, bf16[656,640]{1,0:T(8,128)(2,1)S(1)}, u32[]{:S(2)}, u32[]{:S(2)}) collective-permute-start(bf16[656,640]{1,0:T(8,128)(2,1)S(1)} %get-tuple-element.108), channel_id=1, source_target_pairs={{0,129},{1,128},{16,145},{17,144},{32,161},{33,160},{48,177},{49,1... | collective-permute-start | bytes 2519048 | tf_op jit(solution)/shard_map/ppermute | solution.py:327
  103.4 6.8 %collective-permute-start.23 = (bf16[128,640]{1,0:T(8,128)(2,1)S(1)}, bf16[128,640]{1,0:T(8,128)(2,1)S(1)}, u32[]{:S(2)}, u32[]{:S(2)}) collective-permute-start(bf16[128,640]{1,0:T(8,128)(2,1)S(1)} %get-tuple-element.110), channel_id=1, source_target_pairs={{0,0},{1,1},{64,2},{65,3},{128,4},{129,5},{192,6},{193,7},{8,8},{9... | collective-permute-start | bytes 491528 | tf_op jit(solution)/shard_map/ppermute | solution.py:323
  110.2 4.4 %collective-permute-done.23.value = bf16[128,640]{1,0:T(8,128)(2,1)S(1)} collective-permute-done((bf16[128,640]{1,0:T(8,128)(2,1)S(1)}, bf16[128,640]{1,0:T(8,128)(2,1)S(1)}, u32[]{:S(2)}, u32[]{:S(2)}) %collective-permute-start.23) | collective-permute-done | bytes 163872 | tf_op jit(solution)/shard_map/ppermute | solution.py:323
  115.3 6.0 %collective-permute-done.21.s2 = bf16[656,640]{1,0:T(8,128)(2,1)S(1)} collective-permute-done((bf16[656,640]{1,0:T(8,128)(2,1)S(1)}, bf16[656,640]{1,0:T(8,128)(2,1)S(1)}, u32[]{:S(2)}, u32[]{:S(2)}) %collective-permute-start.21) | collective-permute-done | bytes 839712 | tf_op jit(solution)/shard_map/ppermute | solution.py:327
  121.9 2.4 %collective-permute-start.24 = (bf16[176,640]{1,0:T(8,128)(2,1)S(1)}, bf16[176,640]{1,0:T(8,128)(2,1)S(1)}, u32[]{:S(2)}, u32[]{:S(2)}) collective-permute-start(bf16[176,640]{1,0:T(8,128)(2,1)S(1)} %get-tuple-element.117), channel_id=1, source_target_pairs={{0,48},{1,49},{16,0},{17,1},{32,16},{33,17},{48,32},{49,33},{64,19... | collective-permute-start | bytes 675848 | tf_op jit(solution)/shard_map/ppermute | solution.py:332
  127.1 3.4 %collective-permute-done.25 = bf16[176,640]{1,0:T(8,128)(2,1)S(1)} collective-permute-done((bf16[176,640]{1,0:T(8,128)(2,1)S(1)}, bf16[176,640]{1,0:T(8,128)(2,1)S(1)}, u32[]{:S(2)}, u32[]{:S(2)}) %collective-permute-start.25) | collective-permute-done | bytes 225312 | tf_op jit(solution)/shard_map/ppermute | solution.py:332
  131.8 14.4 %collective-permute-start.27 = (bf16[88,640]{1,0:T(8,128)(2,1)S(1)}, bf16[88,640]{1,0:T(8,128)(2,1)S(1)}, u32[]{:S(2)}, u32[]{:S(2)}) collective-permute-start(bf16[88,640]{1,0:T(8,128)(2,1)S(1)} %concatenate.27), channel_id=1, source_target_pairs={{0,0},{1,1},{64,2},{65,3},{128,4},{129,5},{192,6},{193,7},{8,8},{9... | collective-permute-start | bytes 337928 | tf_op jit(solution)/shard_map/ppermute | solution.py:339
  146.4 3.1 %collective-permute-done.27 = bf16[88,640]{1,0:T(8,128)(2,1)S(1)} collective-permute-done((bf16[88,640]{1,0:T(8,128)(2,1)S(1)}, bf16[88,640]{1,0:T(8,128)(2,1)S(1)}, u32[]{:S(2)}, u32[]{:S(2)}) %collective-permute-start.27) | collective-permute-done | bytes 112672 | tf_op jit(solution)/shard_map/ppermute | solution.py:339
  149.5 3.1 %collective-permute-done.28 = bf16[88,640]{1,0:T(8,128)(2,1)S(1)} collective-permute-done((bf16[88,640]{1,0:T(8,128)(2,1)S(1)}, bf16[88,640]{1,0:T(8,128)(2,1)S(1)}, u32[]{:S(2)}, u32[]{:S(2)}) %collective-permute-start.28) | collective-permute-done | bytes 112672 | tf_op jit(solution)/shard_map/ppermute | solution.py:339
  (84 shorter events, 29.7 us)
Async XLA Ops:
  0.6 1.7 %copy-start = (bf16[1,256,40]{1,2,0:T(8,128)(2,1)S(1)}, bf16[1,256,40]{1,2,0:T(8,128)(2,1)}, u32[]{:S(2)}) copy-start(bf16[1,256,40]{1,2,0:T(8,128)(2,1)} %param.14) | copy-start | bytes 61444
  4.4 13.9 %collective-permute-start.1 = (bf16[88,640]{1,0:T(8,128)(2,1)S(1)}, bf16[88,640]{1,0:T(8,128)(2,1)S(1)}, u32[]{:S(2)}, u32[]{:S(2)}) collective-permute-start(bf16[88,640]{1,0:T(8,128)(2,1)S(1)} %pad_maximum_fusion), channel_id=1, source_target_pairs={{0,8},{1,9},{2,72},{3,73},{4,136},{5,137},{6,200},{7,201},{8,0},{9... | collective-permute-start | bytes 337928 | tf_op jit(solution)/shard_map/ppermute | solution.py:242
  10.5 9.1 %collective-permute-start = (bf16[88,640]{1,0:T(8,128)(2,1)S(1)}, bf16[88,640]{1,0:T(8,128)(2,1)S(1)}, u32[]{:S(2)}, u32[]{:S(2)}) collective-permute-start(bf16[88,640]{1,0:T(8,128)(2,1)S(1)} %pad_maximum_fusion), channel_id=1, source_target_pairs={{0,0},{1,1},{2,64},{3,65},{4,128},{5,129},{6,192},{7,193},{8,8},{9... | collective-permute-start | bytes 337928 | tf_op jit(solution)/shard_map/ppermute | solution.py:242
  19.6 32.9 %copy-start.1 = (bf16[128,640]{1,0:T(8,128)(2,1)S(1)}, bf16[128,640]{1,0:T(8,128)(2,1)}, u32[]{:S(2)}) copy-start(bf16[128,640]{1,0:T(8,128)(2,1)} %param.10) | copy-start | bytes 491524
  19.7 9.5 %collective-permute-start.4 = (bf16[168,640]{1,0:T(8,128)(2,1)S(1)}, bf16[168,640]{1,0:T(8,128)(2,1)S(1)}, u32[]{:S(2)}, u32[]{:S(2)}) collective-permute-start(bf16[168,640]{1,0:T(8,128)(2,1)S(1)} %concatenate.25), channel_id=1, source_target_pairs={{0,48},{1,49},{16,0},{17,1},{32,16},{33,17},{48,32},{49,33},{64,19... | collective-permute-start | bytes 645128 | tf_op jit(solution)/shard_map/ppermute | solution.py:257
  19.8 9.4 %collective-permute-start.3 = (bf16[168,640]{1,0:T(8,128)(2,1)S(1)}, bf16[168,640]{1,0:T(8,128)(2,1)S(1)}, u32[]{:S(2)}, u32[]{:S(2)}) collective-permute-start(bf16[168,640]{1,0:T(8,128)(2,1)S(1)} %concatenate.25), channel_id=1, source_target_pairs={{0,32},{1,33},{16,48},{17,49},{32,0},{33,1},{48,16},{49,17},{64,65... | collective-permute-start | bytes 645128 | tf_op jit(solution)/shard_map/ppermute | solution.py:257
  22.1 7.1 %collective-permute-start.2 = (bf16[168,640]{1,0:T(8,128)(2,1)S(1)}, bf16[168,640]{1,0:T(8,128)(2,1)S(1)}, u32[]{:S(2)}, u32[]{:S(2)}) collective-permute-start(bf16[168,640]{1,0:T(8,128)(2,1)S(1)} %concatenate.25), channel_id=1, source_target_pairs={{0,16},{1,17},{16,32},{17,33},{32,48},{33,49},{48,0},{49,1},{64,19... | collective-permute-start | bytes 645128 | tf_op jit(solution)/shard_map/ppermute | solution.py:257
  24.0 9.7 %collective-permute-start.5 = (bf16[128,640]{1,0:T(8,128)(2,1)}, bf16[128,640]{1,0:T(8,128)(2,1)S(1)}, u32[]{:S(2)}, u32[]{:S(2)}) collective-permute-start(bf16[128,640]{1,0:T(8,128)(2,1)} %bitcast.23), channel_id=1, source_target_pairs={{0,0},{1,1},{2,64},{3,65},{4,128},{5,129},{6,192},{7,193},{8,8},{9... | collective-permute-start | bytes 491528 | tf_op jit(solution)/shard_map/ppermute | solution.py:256
  33.7 13.2 %collective-permute-start.7 = (bf16[672,640]{1,0:T(8,128)(2,1)S(1)}, bf16[672,640]{1,0:T(8,128)(2,1)S(1)}, u32[]{:S(2)}, u32[]{:S(2)}) collective-permute-start(bf16[672,640]{1,0:T(8,128)(2,1)S(1)} %constant_dynamic-update-slice_fusion.b0), channel_id=1, source_target_pairs={{0,1},{1,0},{16,17},{17,16},{32,33},{33,32},{48,49},{49,48},{64,96... | collective-permute-start | bytes 2580488 | tf_op jit(solution)/shard_map/ppermute | solution.py:264
  36.4 19.7 %collective-permute-start.11 = (bf16[672,640]{1,0:T(8,128)(2,1)S(1)}, bf16[672,640]{1,0:T(8,128)(2,1)S(1)}, u32[]{:S(2)}, u32[]{:S(2)}) collective-permute-start(bf16[672,640]{1,0:T(8,128)(2,1)S(1)} %constant_dynamic-update-slice_fusion.b0), channel_id=1, source_target_pairs={{0,128},{1,129},{16,144},{17,145},{32,160},{33,161},{48,176},{49,1... | collective-permute-start | bytes 2580488 | tf_op jit(solution)/shard_map/ppermute | solution.py:264
  36.7 20.0 %collective-permute-start.9 = (bf16[672,640]{1,0:T(8,128)(2,1)S(1)}, bf16[672,640]{1,0:T(8,128)(2,1)S(1)}, u32[]{:S(2)}, u32[]{:S(2)}) collective-permute-start(bf16[672,640]{1,0:T(8,128)(2,1)S(1)} %constant_dynamic-update-slice_fusion.b0), channel_id=1, source_target_pairs={{0,64},{64,0},{1,65},{65,1},{2,66},{66,2},{3,67},{67,3},{4,68},{68... | collective-permute-start | bytes 2580488 | tf_op jit(solution)/shard_map/ppermute | solution.py:51
  39.0 18.7 %collective-permute-start.6 = (bf16[672,640]{1,0:T(8,128)(2,1)S(1)}, bf16[672,640]{1,0:T(8,128)(2,1)S(1)}, u32[]{:S(2)}, u32[]{:S(2)}) collective-permute-start(bf16[672,640]{1,0:T(8,128)(2,1)S(1)} %constant_dynamic-update-slice_fusion.b0), channel_id=1, source_target_pairs={{0,129},{1,128},{16,145},{17,144},{32,161},{33,160},{48,177},{49,1... | collective-permute-start | bytes 2580488 | tf_op jit(solution)/shard_map/ppermute | solution.py:264
  47.0 9.7 %collective-permute-start.10 = (bf16[672,640]{1,0:T(8,128)(2,1)S(1)}, bf16[672,640]{1,0:T(8,128)(2,1)S(1)}, u32[]{:S(2)}, u32[]{:S(2)}) collective-permute-start(bf16[672,640]{1,0:T(8,128)(2,1)S(1)} %collective-permute-done.7.b1), channel_id=1, source_target_pairs={{0,64},{64,0},{1,65},{65,1},{2,66},{66,2},{3,67},{67,3},{4,68},{68... | collective-permute-start | bytes 2580488 | tf_op jit(solution)/shard_map/ppermute | solution.py:51
  52.5 5.4 %collective-permute-start.8 = (bf16[128,640]{1,0:T(8,128)(2,1)S(1)}, bf16[128,640]{1,0:T(8,128)(2,1)S(1)}, u32[]{:S(2)}, u32[]{:S(2)}) collective-permute-start(bf16[128,640]{1,0:T(8,128)(2,1)S(1)} %copy-done.1), channel_id=1, source_target_pairs={{192,6},{193,7},{194,70},{195,71},{196,134},{197,135},{198,198},{1... | collective-permute-start | bytes 491528 | tf_op jit(solution)/shard_map/ppermute | solution.py:266
  56.1 6.2 %collective-permute-start.12 = (bf16[672,640]{1,0:T(8,128)(2,1)S(1)}, bf16[672,640]{1,0:T(8,128)(2,1)S(1)}, u32[]{:S(2)}, u32[]{:S(2)}) collective-permute-start(bf16[672,640]{1,0:T(8,128)(2,1)S(1)} %collective-permute-done.11.b0), channel_id=1, source_target_pairs={{0,64},{64,0},{1,65},{65,1},{2,66},{66,2},{3,67},{67,3},{4,68},{68... | collective-permute-start | bytes 2580488 | tf_op jit(solution)/shard_map/ppermute | solution.py:51
  58.0 5.3 %collective-permute-start.13 = (bf16[672,640]{1,0:T(8,128)(2,1)S(1)}, bf16[672,640]{1,0:T(8,128)(2,1)S(1)}, u32[]{:S(2)}, u32[]{:S(2)}) collective-permute-start(bf16[672,640]{1,0:T(8,128)(2,1)S(1)} %collective-permute-done.6.b1), channel_id=1, source_target_pairs={{0,64},{64,0},{1,65},{65,1},{2,66},{66,2},{3,67},{67,3},{4,68},{68... | collective-permute-start | bytes 2580488 | tf_op jit(solution)/shard_map/ppermute | solution.py:51
  66.4 5.7 %collective-permute-start.14 = (bf16[128,640]{1,0:T(8,128)(2,1)S(1)}, bf16[128,640]{1,0:T(8,128)(2,1)S(1)}, u32[]{:S(2)}, u32[]{:S(2)}) collective-permute-start(bf16[128,640]{1,0:T(8,128)(2,1)S(1)} %shard_map.124), channel_id=1, source_target_pairs={{0,14},{2,0},{4,2},{6,4},{8,6},{10,8},{12,10},{14,12},{1,15},{3,1}... | collective-permute-start | bytes 491528 | tf_op jit(solution)/shard_map/ppermute | solution.py:304
  74.0 5.7 %collective-permute-start.15 = (bf16[128,640]{1,0:T(8,128)(2,1)S(1)}, bf16[128,640]{1,0:T(8,128)(2,1)S(1)}, u32[]{:S(2)}, u32[]{:S(2)}) collective-permute-start(bf16[128,640]{1,0:T(8,128)(2,1)S(1)} %shard_map.125), channel_id=1, source_target_pairs={{0,14},{2,0},{4,2},{6,4},{8,6},{10,8},{12,10},{14,12},{1,15},{3,1}... | collective-permute-start | bytes 491528 | tf_op jit(solution)/shard_map/ppermute | solution.py:304
  81.7 5.8 %collective-permute-start.16 = (bf16[128,640]{1,0:T(8,128)(2,1)S(1)}, bf16[128,640]{1,0:T(8,128)(2,1)S(1)}, u32[]{:S(2)}, u32[]{:S(2)}) collective-permute-start(bf16[128,640]{1,0:T(8,128)(2,1)S(1)} %shard_map.126), channel_id=1, source_target_pairs={{0,14},{2,0},{4,2},{6,4},{8,6},{10,8},{12,10},{14,12},{1,15},{3,1}... | collective-permute-start | bytes 491528 | tf_op jit(solution)/shard_map/ppermute | solution.py:304
  88.1 5.9 %collective-permute-start.17 = (bf16[1280,640]{1,0:T(8,128)(2,1)S(1)}, bf16[1280,640]{1,0:T(8,128)(2,1)S(1)}, u32[]{:S(2)}, u32[]{:S(2)}) collective-permute-start(bf16[1280,640]{1,0:T(8,128)(2,1)S(1)} %shard_map.127), channel_id=1, source_target_pairs={{0,64},{64,0},{1,65},{65,1},{2,66},{66,2},{3,67},{67,3},{4,68},{68... | collective-permute-start | bytes 4915208 | tf_op jit(solution)/shard_map/ppermute | solution.py:51
  94.7 3.6 %collective-permute-start.18 = (bf16[1280,640]{1,0:T(8,128)(2,1)S(1)}, bf16[1280,640]{1,0:T(8,128)(2,1)S(1)}, u32[]{:S(2)}, u32[]{:S(2)}) collective-permute-start(bf16[1280,640]{1,0:T(8,128)(2,1)S(1)} %shard_map.129), channel_id=1, source_target_pairs={{0,64},{64,0},{1,65},{65,1},{2,66},{66,2},{3,67},{67,3},{4,68},{68... | collective-permute-start | bytes 4915208 | tf_op jit(solution)/shard_map/ppermute | solution.py:51
  95.2 3.1 %collective-permute-start.19 = (f32[1,640]{1,0:T(1,128)S(1)}, f32[1,640]{1,0:T(1,128)S(1)}, u32[]{:S(2)}, u32[]{:S(2)}) collective-permute-start(f32[1,640]{1,0:T(1,128)S(1)} %get-tuple-element.105.gain_here), channel_id=1, source_target_pairs={{0,64},{64,0},{1,65},{65,1},{2,66},{66,2},{3,67},{67,3},{4,68},{68... | collective-permute-start | bytes 7688 | tf_op jit(solution)/shard_map/ppermute | solution.py:51
  99.3 16.0 %collective-permute-start.20 = (bf16[656,640]{1,0:T(8,128)(2,1)S(1)}, bf16[656,640]{1,0:T(8,128)(2,1)S(1)}, u32[]{:S(2)}, u32[]{:S(2)}) collective-permute-start(bf16[656,640]{1,0:T(8,128)(2,1)S(1)} %get-tuple-element.107), channel_id=1, source_target_pairs={{0,1},{1,0},{16,17},{17,16},{32,33},{33,32},{48,49},{49,48},{64,96... | collective-permute-start | bytes 2519048 | tf_op jit(solution)/shard_map/ppermute | solution.py:327
  101.0 20.4 %collective-permute-start.21 = (bf16[656,640]{1,0:T(8,128)(2,1)S(1)}, bf16[656,640]{1,0:T(8,128)(2,1)S(1)}, u32[]{:S(2)}, u32[]{:S(2)}) collective-permute-start(bf16[656,640]{1,0:T(8,128)(2,1)S(1)} %get-tuple-element.108), channel_id=1, source_target_pairs={{0,129},{1,128},{16,145},{17,144},{32,161},{33,160},{48,177},{49,1... | collective-permute-start | bytes 2519048 | tf_op jit(solution)/shard_map/ppermute | solution.py:327
  103.3 18.0 %collective-permute-start.22 = (bf16[656,640]{1,0:T(8,128)(2,1)S(1)}, bf16[656,640]{1,0:T(8,128)(2,1)S(1)}, u32[]{:S(2)}, u32[]{:S(2)}) collective-permute-start(bf16[656,640]{1,0:T(8,128)(2,1)S(1)} %get-tuple-element.109), channel_id=1, source_target_pairs={{0,128},{1,129},{16,144},{17,145},{32,160},{33,161},{48,176},{49,1... | collective-permute-start | bytes 2519048 | tf_op jit(solution)/shard_map/ppermute | solution.py:327
  103.4 11.3 %collective-permute-start.23 = (bf16[128,640]{1,0:T(8,128)(2,1)S(1)}, bf16[128,640]{1,0:T(8,128)(2,1)S(1)}, u32[]{:S(2)}, u32[]{:S(2)}) collective-permute-start(bf16[128,640]{1,0:T(8,128)(2,1)S(1)} %get-tuple-element.110), channel_id=1, source_target_pairs={{0,0},{1,1},{64,2},{65,3},{128,4},{129,5},{192,6},{193,7},{8,8},{9... | collective-permute-start | bytes 491528 | tf_op jit(solution)/shard_map/ppermute | solution.py:323
  121.9 5.3 %collective-permute-start.24 = (bf16[176,640]{1,0:T(8,128)(2,1)S(1)}, bf16[176,640]{1,0:T(8,128)(2,1)S(1)}, u32[]{:S(2)}, u32[]{:S(2)}) collective-permute-start(bf16[176,640]{1,0:T(8,128)(2,1)S(1)} %get-tuple-element.117), channel_id=1, source_target_pairs={{0,48},{1,49},{16,0},{17,1},{32,16},{33,17},{48,32},{49,33},{64,19... | collective-permute-start | bytes 675848 | tf_op jit(solution)/shard_map/ppermute | solution.py:332
  124.2 6.3 %collective-permute-start.25 = (bf16[176,640]{1,0:T(8,128)(2,1)S(1)}, bf16[176,640]{1,0:T(8,128)(2,1)S(1)}, u32[]{:S(2)}, u32[]{:S(2)}) collective-permute-start(bf16[176,640]{1,0:T(8,128)(2,1)S(1)} %get-tuple-element.118), channel_id=1, source_target_pairs={{0,32},{1,33},{16,48},{17,49},{32,0},{33,1},{48,16},{49,17},{64,65... | collective-permute-start | bytes 675848 | tf_op jit(solution)/shard_map/ppermute | solution.py:332
  124.7 6.8 %collective-permute-start.26 = (bf16[176,640]{1,0:T(8,128)(2,1)S(1)}, bf16[176,640]{1,0:T(8,128)(2,1)S(1)}, u32[]{:S(2)}, u32[]{:S(2)}) collective-permute-start(bf16[176,640]{1,0:T(8,128)(2,1)S(1)} %get-tuple-element.119), channel_id=1, source_target_pairs={{0,16},{1,17},{16,32},{17,33},{32,48},{33,49},{48,0},{49,1},{64,19... | collective-permute-start | bytes 675848 | tf_op jit(solution)/shard_map/ppermute | solution.py:332
  131.8 17.7 %collective-permute-start.27 = (bf16[88,640]{1,0:T(8,128)(2,1)S(1)}, bf16[88,640]{1,0:T(8,128)(2,1)S(1)}, u32[]{:S(2)}, u32[]{:S(2)}) collective-permute-start(bf16[88,640]{1,0:T(8,128)(2,1)S(1)} %concatenate.27), channel_id=1, source_target_pairs={{0,0},{1,1},{64,2},{65,3},{128,4},{129,5},{192,6},{193,7},{8,8},{9... | collective-permute-start | bytes 337928 | tf_op jit(solution)/shard_map/ppermute | solution.py:339
  146.3 6.4 %collective-permute-start.28 = (bf16[88,640]{1,0:T(8,128)(2,1)S(1)}, bf16[88,640]{1,0:T(8,128)(2,1)S(1)}, u32[]{:S(2)}, u32[]{:S(2)}) collective-permute-start(bf16[88,640]{1,0:T(8,128)(2,1)S(1)} %concatenate.28), channel_id=1, source_target_pairs={{8,0},{9,1},{72,2},{73,3},{136,4},{137,5},{200,6},{201,7},{0,8},{1... | collective-permute-start | bytes 337928 | tf_op jit(solution)/shard_map/ppermute | solution.py:339

commit v9 on v8

--- a/solution.py
+++ b/solution.py
@@ -12,6 +12,7 @@
 PLANE = ("yl", "core", "x", "yh")
 SIDE = 4
 ORDER = (2, 1, 3)
+GRAD_SCALE = 8192.0 ** (-0.5)
 PAD = 16
 LINES = 8
 VMEM_LIMIT = 28 << 20
@@ -157,6 +158,19 @@
         out[rows, :] = dot_first(left[...], right[...]).astype(jnp.bfloat16)
 
 
+def first_outer_kernel(left_0, left_1, earlier, last, out, kept):
+    kept[...] = earlier[...] + last[...]
+    outer_kernel(left_0, left_1, kept, out)
+
+
+def home_kernel(part_0, part_1, w_in_out, w_out_out, gain_out):
+    own = w_in_out.shape[0]
+    total = (part_0[...].astype(jnp.float32) + part_1[...].astype(jnp.float32)) * GRAD_SCALE
+    w_in_out[...] = total[:own, :]
+    w_out_out[...] = total[own : 2 * own, :]
+    gain_out[...] = total[2 * own : 2 * own + 1, :] + total[2 * own + 1 : 2 * own + 2, :]
+
+
 def copy_kernel(value, out):
     out[...] = value[...]
 
@@ -223,7 +237,6 @@
     rows, chan = checkpoints.shape[1:]
     own = w_in.shape[2]
     half = SIDE * SIDE * 2 * own
-    grad_scale = float(rows * 64) ** (-0.5)
     sample = 2 * lax.axis_index("x") + lax.axis_index("z") // 4
     bf16, f32 = jnp.bfloat16, jnp.float32
 
@@ -299,13 +312,14 @@
         held += [w_in_rows, w_out_rows, slope]
 
     turn = kernel(turn_kernel, [((rows, chan), bf16)], 4 * flops)
-    kept = grad = cot_rows
+    grad, earlier = cot_rows, jnp.zeros_like(cot_rows)
     for _ in range(3):
+        earlier = earlier + grad
         grad = lax.ppermute(turn(grad, *held), "z", next_section())
-        kept = kept + grad
-
-    outer = kernel(outer_kernel, [((half, chan), bf16)], flops)
-    far_out = outer(*hiddens[2:], kept)
+
+    far_out, kept = kernel(
+        first_outer_kernel, [((half, chan), bf16), ((rows, chan), bf16)], flops
+    )(*hiddens[2:], earlier, grad)
     kept, far_out = lax.optimization_barrier((kept, far_out))
     recv_out = across_cores(far_out)
     last_turn = kernel(
@@ -314,8 +328,9 @@
         4 * flops,
     )
     grad_in, gain_part, pg_0, pg_1, *pg_far = last_turn(kept, *held)
-    *pg_far, recv_out = lax.optimization_barrier((*pg_far, recv_out))
-    recv_in = across_cores(outer(*pg_far, normed))
+    far_in = kernel(outer_kernel, [((half, chan), bf16)], flops)(*pg_far, normed)
+    far_in, recv_out = lax.optimization_barrier((far_in, recv_out))
+    recv_in = across_cores(far_in)
     gain_there = across_cores(gain_part)
     sums = kernel(near_kernel, [((SIDE * 4 * own + PAD, chan), bf16)] * SIDE, 2 * flops)(
         pg_0, pg_1, normed, recv_in, *hiddens[:2], kept, recv_out, gain_part, gain_there
@@ -335,7 +350,7 @@
     gain_lines = list(two_parts(total[4 * own : 4 * own + 1] + total[4 * own + 1 : 4 * own + 2]))
     gain_lines.append(jnp.zeros((6, chan), bf16))
     total = total.astype(bf16)
-    home = sum(
+    parts = [
         lax.ppermute(
             jnp.concatenate(
                 [
@@ -347,15 +362,13 @@
             ),
             COLUMN,
             work_to_home(flip),
-        ).astype(f32)
+        )
         for flip in (0, 1)
-    )
-    return (
-        grad_home[None],
-        (home[:own].T * grad_scale)[None],
-        (home[own : 2 * own] * grad_scale)[None],
-        (home[2 * own : 2 * own + 1] + home[2 * own + 1 : 2 * own + 2]) * grad_scale,
-    )
+    ]
+    w_in_home, w_out_home, gain_home = kernel(
+        home_kernel, [((own, chan), f32), ((own, chan), f32), ((1, chan), f32)]
+    )(*parts)
+    return grad_home[None], w_in_home.T[None], w_out_home[None], gain_home
 
 
 def solution(mesh):

time: 155 us -> 153 us (0.987)
    pallas_call x13 -> x14, Pallas kernels: 15.1 us -> 15.9 us  [call(): pl.pallas_call(body, out_shape=shapes, in_specs=[whole] * len(operands),...]
  transfers between devices with their start and end apart: 29 -> 29, of which waited for: 19 -> 19; matrix products, arithmetic and copies ran while one was open for 0% -> 0% of each run, Pallas kernels for 3% -> 4%
where the time goes in v9:
time: 153 us
  starting transfers between devices  79.9 us (52%)
  waiting for transfers between devices  51.2 us (33%)
  Pallas kernels  15.9 us (10%)
  other arithmetic  3.02 us (2%)
    pallas_call x14, Pallas kernels, call(): pl.pallas_call(body, out_shape=shapes, in_specs=[whole] * len(operands),...  15.9 us
    ppermute x2, starting transfers between devices, on_device(): lax.ppermute(jnp.concatenate([total[flip * own:(flip + 1) * own], total[(...  14.5 us
    ppermute x7, starting transfers between devices, across_cores(): return lax.ppermute(value, 'core', [(0, 1), (1, 0)])  14.1 us
    ppermute x2, starting transfers between devices, on_device(): lax.ppermute(shard, COLUMN, home_to_work(flip))  10.4 us
    ppermute x3, waiting for transfers between devices, on_device(): grad = lax.ppermute(turn(grad, *held), 'z', next_section())  8.58 us
    ppermute x3, starting transfers between devices, on_device(): grad = lax.ppermute(turn(grad, *held), 'z', next_section())  8.49 us
    ppermute x1, starting transfers between devices, on_device(): grad_home = lax.ppermute(grad_in, COLUMN, work_to_home(0))  6.85 us
    ppermute x2, waiting for transfers between devices, on_device(): lax.ppermute(jnp.concatenate([total[flip * own:(flip + 1) * own], total[(...  6.29 us
  transfers between devices with their start and end apart: 29, of which 19 were waited for; matrix products, arithmetic and copies ran while one was open for 0% of the time, Pallas kernels for 4%

profile of v9, /device:TPU:9, one launch (start us, length us, event | category | flops | bytes accessed | tf_op | source)
XLA Modules:
  0.0 152.6 jit_solution(6033083957453481233)
XLA Ops:
  4.4 6.1 %collective-permute-start.1 = (bf16[88,640]{1,0:T(8,128)(2,1)S(1)}, bf16[88,640]{1,0:T(8,128)(2,1)S(1)}, u32[]{:S(2)}, u32[]{:S(2)}) collective-permute-start(bf16[88,640]{1,0:T(8,128)(2,1)S(1)} %pad_maximum_fusion), channel_id=1, source_target_pairs={{0,8},{1,9},{2,72},{3,73},{4,136},{5,137},{6,200},{7,201},{8,0},{9... | collective-permute-start | bytes 337928 | tf_op jit(solution)/shard_map/ppermute | solution.py:255
  10.5 4.2 %collective-permute-start = (bf16[88,640]{1,0:T(8,128)(2,1)S(1)}, bf16[88,640]{1,0:T(8,128)(2,1)S(1)}, u32[]{:S(2)}, u32[]{:S(2)}) collective-permute-start(bf16[88,640]{1,0:T(8,128)(2,1)S(1)} %pad_maximum_fusion), channel_id=1, source_target_pairs={{0,0},{1,1},{2,64},{3,65},{4,128},{5,129},{6,192},{7,193},{8,8},{9... | collective-permute-start | bytes 337928 | tf_op jit(solution)/shard_map/ppermute | solution.py:255
  14.7 3.5 %collective-permute-done.1 = bf16[88,640]{1,0:T(8,128)(2,1)S(1)} collective-permute-done((bf16[88,640]{1,0:T(8,128)(2,1)S(1)}, bf16[88,640]{1,0:T(8,128)(2,1)S(1)}, u32[]{:S(2)}, u32[]{:S(2)}) %collective-permute-start.1) | collective-permute-done | bytes 112672 | tf_op jit(solution)/shard_map/ppermute | solution.py:255
  19.8 2.2 %collective-permute-start.3 = (bf16[168,640]{1,0:T(8,128)(2,1)S(1)}, bf16[168,640]{1,0:T(8,128)(2,1)S(1)}, u32[]{:S(2)}, u32[]{:S(2)}) collective-permute-start(bf16[168,640]{1,0:T(8,128)(2,1)S(1)} %concatenate.25), channel_id=1, source_target_pairs={{0,32},{1,33},{16,48},{17,49},{32,0},{33,1},{48,16},{49,17},{64,65... | collective-permute-start | bytes 645128 | tf_op jit(solution)/shard_map/ppermute | solution.py:270
  24.0 5.1 %collective-permute-start.5 = (bf16[128,640]{1,0:T(8,128)(2,1)}, bf16[128,640]{1,0:T(8,128)(2,1)S(1)}, u32[]{:S(2)}, u32[]{:S(2)}) collective-permute-start(bf16[128,640]{1,0:T(8,128)(2,1)} %bitcast.21), channel_id=1, source_target_pairs={{0,0},{1,1},{2,64},{3,65},{4,128},{5,129},{6,192},{7,193},{8,8},{9... | collective-permute-start | bytes 491528 | tf_op jit(solution)/shard_map/ppermute | solution.py:269
  29.3 4.4 %collective-permute-done.5.x_ref.x = bf16[128,640]{1,0:T(8,128)(2,1)S(1)} collective-permute-done((bf16[128,640]{1,0:T(8,128)(2,1)}, bf16[128,640]{1,0:T(8,128)(2,1)S(1)}, u32[]{:S(2)}, u32[]{:S(2)}) %collective-permute-start.5) | collective-permute-done | bytes 163872 | tf_op jit(solution)/shard_map/ppermute | solution.py:269
  33.7 2.7 %collective-permute-start.7 = (bf16[672,640]{1,0:T(8,128)(2,1)S(1)}, bf16[672,640]{1,0:T(8,128)(2,1)S(1)}, u32[]{:S(2)}, u32[]{:S(2)}) collective-permute-start(bf16[672,640]{1,0:T(8,128)(2,1)S(1)} %constant_dynamic-update-slice_fusion.b0), channel_id=1, source_target_pairs={{0,1},{1,0},{16,17},{17,16},{32,33},{33,32},{48,49},{49,48},{64,96... | collective-permute-start | bytes 2580488 | tf_op jit(solution)/shard_map/ppermute | solution.py:277
  36.7 2.3 %collective-permute-start.9 = (bf16[672,640]{1,0:T(8,128)(2,1)S(1)}, bf16[672,640]{1,0:T(8,128)(2,1)S(1)}, u32[]{:S(2)}, u32[]{:S(2)}) collective-permute-start(bf16[672,640]{1,0:T(8,128)(2,1)S(1)} %constant_dynamic-update-slice_fusion.b0), channel_id=1, source_target_pairs={{0,64},{64,0},{1,65},{65,1},{2,66},{66,2},{3,67},{67,3},{4,68},{68... | collective-permute-start | bytes 2580488 | tf_op jit(solution)/shard_map/ppermute | solution.py:52
  39.0 2.5 %collective-permute-start.6 = (bf16[672,640]{1,0:T(8,128)(2,1)S(1)}, bf16[672,640]{1,0:T(8,128)(2,1)S(1)}, u32[]{:S(2)}, u32[]{:S(2)}) collective-permute-start(bf16[672,640]{1,0:T(8,128)(2,1)S(1)} %constant_dynamic-update-slice_fusion.b0), channel_id=1, source_target_pairs={{0,129},{1,128},{16,145},{17,144},{32,161},{33,160},{48,177},{49,1... | collective-permute-start | bytes 2580488 | tf_op jit(solution)/shard_map/ppermute | solution.py:277
  41.5 5.5 %collective-permute-done.7.b1 = bf16[672,640]{1,0:T(8,128)(2,1)S(1)} collective-permute-done((bf16[672,640]{1,0:T(8,128)(2,1)S(1)}, bf16[672,640]{1,0:T(8,128)(2,1)S(1)}, u32[]{:S(2)}, u32[]{:S(2)}) %collective-permute-start.7) | collective-permute-done | bytes 860192 | tf_op jit(solution)/shard_map/ppermute | solution.py:277
  47.0 5.2 %collective-permute-start.10 = (bf16[672,640]{1,0:T(8,128)(2,1)S(1)}, bf16[672,640]{1,0:T(8,128)(2,1)S(1)}, u32[]{:S(2)}, u32[]{:S(2)}) collective-permute-start(bf16[672,640]{1,0:T(8,128)(2,1)S(1)} %collective-permute-done.7.b1), channel_id=1, source_target_pairs={{0,64},{64,0},{1,65},{65,1},{2,66},{66,2},{3,67},{67,3},{4,68},{68... | collective-permute-start | bytes 2580488 | tf_op jit(solution)/shard_map/ppermute | solution.py:52
  52.5 3.1 %collective-permute-start.8 = (bf16[128,640]{1,0:T(8,128)(2,1)S(1)}, bf16[128,640]{1,0:T(8,128)(2,1)S(1)}, u32[]{:S(2)}, u32[]{:S(2)}) collective-permute-start(bf16[128,640]{1,0:T(8,128)(2,1)S(1)} %copy-done.1), channel_id=1, source_target_pairs={{192,6},{193,7},{194,70},{195,71},{196,134},{197,135},{198,198},{1... | collective-permute-start | bytes 491528 | tf_op jit(solution)/shard_map/ppermute | solution.py:279
  58.0 3.3 %collective-permute-start.13 = (bf16[672,640]{1,0:T(8,128)(2,1)S(1)}, bf16[672,640]{1,0:T(8,128)(2,1)S(1)}, u32[]{:S(2)}, u32[]{:S(2)}) collective-permute-start(bf16[672,640]{1,0:T(8,128)(2,1)S(1)} %collective-permute-done.6.b1), channel_id=1, source_target_pairs={{0,64},{64,0},{1,65},{65,1},{2,66},{66,2},{3,67},{67,3},{4,68},{68... | collective-permute-start | bytes 2580488 | tf_op jit(solution)/shard_map/ppermute | solution.py:52
  68.2 3.8 %collective-permute-done.14.g = bf16[128,640]{1,0:T(8,128)(2,1)S(1)} collective-permute-done((bf16[128,640]{1,0:T(8,128)(2,1)S(1)}, bf16[128,640]{1,0:T(8,128)(2,1)S(1)}, u32[]{:S(2)}, u32[]{:S(2)}) %collective-permute-start.14) | collective-permute-done | bytes 163872 | tf_op jit(solution)/shard_map/ppermute | solution.py:318
  72.0 2.0 %shard_map.125 = bf16[128,640]{1,0:T(8,128)(2,1)S(1)} custom-call(bf16[128,640]{1,0:T(8,128)(2,1)S(1)} %collective-permute-done.14.g, bf16[128,640]{1,0:T(8,128)(2,1)S(1)} %collective-permute-done.5.x_ref.x, f32[1,640]{1,0:T(1,128)S(1)} %slice_add_fusion.1.gain_ref.gain, bf16[640,640]{1,0:T(8,128)(2,1)S(1)} %get-tuple-element.85.refs_0_, ...), custom_call_target="tpu_custom_call" | custom-call | flops 838860800 | bytes 4194304 | tf_op jit(solution)/shard_map/pallas_call | solution.py:223
  74.0 3.1 %collective-permute-start.15 = (bf16[128,640]{1,0:T(8,128)(2,1)S(1)}, bf16[128,640]{1,0:T(8,128)(2,1)S(1)}, u32[]{:S(2)}, u32[]{:S(2)}) collective-permute-start(bf16[128,640]{1,0:T(8,128)(2,1)S(1)} %shard_map.125), channel_id=1, source_target_pairs={{0,14},{2,0},{4,2},{6,4},{8,6},{10,8},{12,10},{14,12},{1,15},{3,1}... | collective-permute-start | bytes 491528 | tf_op jit(solution)/shard_map/ppermute | solution.py:318
  77.2 2.5 %collective-permute-done.15.g = bf16[128,640]{1,0:T(8,128)(2,1)S(1)} collective-permute-done((bf16[128,640]{1,0:T(8,128)(2,1)S(1)}, bf16[128,640]{1,0:T(8,128)(2,1)S(1)}, u32[]{:S(2)}, u32[]{:S(2)}) %collective-permute-start.15) | collective-permute-done | bytes 163872 | tf_op jit(solution)/shard_map/ppermute | solution.py:318
  79.7 2.0 %shard_map.126 = bf16[128,640]{1,0:T(8,128)(2,1)S(1)} custom-call(bf16[128,640]{1,0:T(8,128)(2,1)S(1)} %collective-permute-done.15.g, bf16[128,640]{1,0:T(8,128)(2,1)S(1)} %collective-permute-done.5.x_ref.x, f32[1,640]{1,0:T(1,128)S(1)} %slice_add_fusion.1.gain_ref.gain, bf16[640,640]{1,0:T(8,128)(2,1)S(1)} %get-tuple-element.85.refs_0_, ...), custom_call_target="tpu_custom_call" | custom-call | flops 838860800 | bytes 4194304 | tf_op jit(solution)/shard_map/pallas_call | solution.py:223
  81.7 3.5 %collective-permute-start.16 = (bf16[128,640]{1,0:T(8,128)(2,1)S(1)}, bf16[128,640]{1,0:T(8,128)(2,1)S(1)}, u32[]{:S(2)}, u32[]{:S(2)}) collective-permute-start(bf16[128,640]{1,0:T(8,128)(2,1)S(1)} %shard_map.126), channel_id=1, source_target_pairs={{0,14},{2,0},{4,2},{6,4},{8,6},{10,8},{12,10},{14,12},{1,15},{3,1}... | collective-permute-start | bytes 491528 | tf_op jit(solution)/shard_map/ppermute | solution.py:318
  85.3 2.2 %collective-permute-done.16.last = bf16[128,640]{1,0:T(8,128)(2,1)S(1)} collective-permute-done((bf16[128,640]{1,0:T(8,128)(2,1)S(1)}, bf16[128,640]{1,0:T(8,128)(2,1)S(1)}, u32[]{:S(2)}, u32[]{:S(2)}) %collective-permute-start.16) | collective-permute-done | bytes 163872 | tf_op jit(solution)/shard_map/ppermute | solution.py:318
  88.1 2.8 %collective-permute-start.17 = (bf16[1280,640]{1,0:T(8,128)(2,1)S(1)}, bf16[1280,640]{1,0:T(8,128)(2,1)S(1)}, u32[]{:S(2)}, u32[]{:S(2)}) collective-permute-start(bf16[1280,640]{1,0:T(8,128)(2,1)S(1)} %get-tuple-element.105), channel_id=1, source_target_pairs={{0,64},{64,0},{1,65},{65,1},{2,66},{66,2},{3,67},{67,3},{4,68},{68... | collective-permute-start | bytes 4915208 | tf_op jit(solution)/shard_map/ppermute | solution.py:52
  90.9 2.0 %shard_map.128 = (bf16[128,640]{1,0:T(8,128)(2,1)S(1)}, f32[1,640]{1,0:T(1,128)S(1)}, bf16[128,640]{1,0:T(8,128)(2,1)S(1)}, bf16[128,640]{1,0:T(8,128)(2,1)S(1)}...) custom-call(bf16[128,640]{1,0:T(8,128)(2,1)S(1)} %get-tuple-element.99.g.grad, ...), custom_call_target="tpu_custom_call" | custom-call | flops 838860800 | bytes 4194304 | tf_op jit(solution)/shard_map/pallas_call | solution.py:223
  94.6 3.0 %collective-permute-done.19.gain_there = f32[1,640]{1,0:T(1,128)S(1)} collective-permute-done((f32[1,640]{1,0:T(1,128)S(1)}, f32[1,640]{1,0:T(1,128)S(1)}, u32[]{:S(2)}, u32[]{:S(2)}) %collective-permute-start.19) | collective-permute-done | bytes 2592 | tf_op jit(solution)/shard_map/ppermute | solution.py:52
  100.3 2.3 %collective-permute-start.21 = (bf16[656,640]{1,0:T(8,128)(2,1)S(1)}, bf16[656,640]{1,0:T(8,128)(2,1)S(1)}, u32[]{:S(2)}, u32[]{:S(2)}) collective-permute-start(bf16[656,640]{1,0:T(8,128)(2,1)S(1)} %get-tuple-element.113), channel_id=1, source_target_pairs={{0,129},{1,128},{16,145},{17,144},{32,161},{33,160},{48,177},{49,1... | collective-permute-start | bytes 2519048 | tf_op jit(solution)/shard_map/ppermute | solution.py:342
  102.6 6.9 %collective-permute-start.23 = (bf16[128,640]{1,0:T(8,128)(2,1)S(1)}, bf16[128,640]{1,0:T(8,128)(2,1)S(1)}, u32[]{:S(2)}, u32[]{:S(2)}) collective-permute-start(bf16[128,640]{1,0:T(8,128)(2,1)S(1)} %get-tuple-element.115), channel_id=1, source_target_pairs={{0,0},{1,1},{64,2},{65,3},{128,4},{129,5},{192,6},{193,7},{8,8},{9... | collective-permute-start | bytes 491528 | tf_op jit(solution)/shard_map/ppermute | solution.py:338
  109.5 4.5 %collective-permute-done.23.value = bf16[128,640]{1,0:T(8,128)(2,1)S(1)} collective-permute-done((bf16[128,640]{1,0:T(8,128)(2,1)S(1)}, bf16[128,640]{1,0:T(8,128)(2,1)S(1)}, u32[]{:S(2)}, u32[]{:S(2)}) %collective-permute-start.23) | collective-permute-done | bytes 163872 | tf_op jit(solution)/shard_map/ppermute | solution.py:338
  114.6 6.0 %collective-permute-done.21.s2 = bf16[656,640]{1,0:T(8,128)(2,1)S(1)} collective-permute-done((bf16[656,640]{1,0:T(8,128)(2,1)S(1)}, bf16[656,640]{1,0:T(8,128)(2,1)S(1)}, u32[]{:S(2)}, u32[]{:S(2)}) %collective-permute-start.21) | collective-permute-done | bytes 839712 | tf_op jit(solution)/shard_map/ppermute | solution.py:342
  121.1 2.4 %collective-permute-start.24 = (bf16[176,640]{1,0:T(8,128)(2,1)S(1)}, bf16[176,640]{1,0:T(8,128)(2,1)S(1)}, u32[]{:S(2)}, u32[]{:S(2)}) collective-permute-start(bf16[176,640]{1,0:T(8,128)(2,1)S(1)} %get-tuple-element.122), channel_id=1, source_target_pairs={{0,48},{1,49},{16,0},{17,1},{32,16},{33,17},{48,32},{49,33},{64,19... | collective-permute-start | bytes 675848 | tf_op jit(solution)/shard_map/ppermute | solution.py:347
  126.4 3.4 %collective-permute-done.25 = bf16[176,640]{1,0:T(8,128)(2,1)S(1)} collective-permute-done((bf16[176,640]{1,0:T(8,128)(2,1)S(1)}, bf16[176,640]{1,0:T(8,128)(2,1)S(1)}, u32[]{:S(2)}, u32[]{:S(2)}) %collective-permute-start.25) | collective-permute-done | bytes 225312 | tf_op jit(solution)/shard_map/ppermute | solution.py:347
  131.1 14.4 %collective-permute-start.27 = (bf16[88,640]{1,0:T(8,128)(2,1)S(1)}, bf16[88,640]{1,0:T(8,128)(2,1)S(1)}, u32[]{:S(2)}, u32[]{:S(2)}) collective-permute-start(bf16[88,640]{1,0:T(8,128)(2,1)S(1)} %concatenate.27), channel_id=1, source_target_pairs={{0,0},{1,1},{64,2},{65,3},{128,4},{129,5},{192,6},{193,7},{8,8},{9... | collective-permute-start | bytes 337928 | tf_op jit(solution)/shard_map/ppermute | solution.py:354
  145.6 3.1 %collective-permute-done.27.part_0 = bf16[88,640]{1,0:T(8,128)(2,1)S(1)} collective-permute-done((bf16[88,640]{1,0:T(8,128)(2,1)S(1)}, bf16[88,640]{1,0:T(8,128)(2,1)S(1)}, u32[]{:S(2)}, u32[]{:S(2)}) %collective-permute-start.27) | collective-permute-done | bytes 112672 | tf_op jit(solution)/shard_map/ppermute | solution.py:354
  148.8 3.1 %collective-permute-done.28.part_1 = bf16[88,640]{1,0:T(8,128)(2,1)S(1)} collective-permute-done((bf16[88,640]{1,0:T(8,128)(2,1)S(1)}, bf16[88,640]{1,0:T(8,128)(2,1)S(1)}, u32[]{:S(2)}, u32[]{:S(2)}) %collective-permute-start.28) | collective-permute-done | bytes 112672 | tf_op jit(solution)/shard_map/ppermute | solution.py:354
  (82 shorter events, 28.3 us)
Async XLA Ops:
  0.6 1.7 %copy-start = (bf16[1,256,40]{1,2,0:T(8,128)(2,1)S(1)}, bf16[1,256,40]{1,2,0:T(8,128)(2,1)}, u32[]{:S(2)}) copy-start(bf16[1,256,40]{1,2,0:T(8,128)(2,1)} %param.14) | copy-start | bytes 61444
  4.4 13.9 %collective-permute-start.1 = (bf16[88,640]{1,0:T(8,128)(2,1)S(1)}, bf16[88,640]{1,0:T(8,128)(2,1)S(1)}, u32[]{:S(2)}, u32[]{:S(2)}) collective-permute-start(bf16[88,640]{1,0:T(8,128)(2,1)S(1)} %pad_maximum_fusion), channel_id=1, source_target_pairs={{0,8},{1,9},{2,72},{3,73},{4,136},{5,137},{6,200},{7,201},{8,0},{9... | collective-permute-start | bytes 337928 | tf_op jit(solution)/shard_map/ppermute | solution.py:255
  10.5 9.1 %collective-permute-start = (bf16[88,640]{1,0:T(8,128)(2,1)S(1)}, bf16[88,640]{1,0:T(8,128)(2,1)S(1)}, u32[]{:S(2)}, u32[]{:S(2)}) collective-permute-start(bf16[88,640]{1,0:T(8,128)(2,1)S(1)} %pad_maximum_fusion), channel_id=1, source_target_pairs={{0,0},{1,1},{2,64},{3,65},{4,128},{5,129},{6,192},{7,193},{8,8},{9... | collective-permute-start | bytes 337928 | tf_op jit(solution)/shard_map/ppermute | solution.py:255
  19.6 32.9 %copy-start.1 = (bf16[128,640]{1,0:T(8,128)(2,1)S(1)}, bf16[128,640]{1,0:T(8,128)(2,1)}, u32[]{:S(2)}) copy-start(bf16[128,640]{1,0:T(8,128)(2,1)} %param.10) | copy-start | bytes 491524
  19.7 9.5 %collective-permute-start.4 = (bf16[168,640]{1,0:T(8,128)(2,1)S(1)}, bf16[168,640]{1,0:T(8,128)(2,1)S(1)}, u32[]{:S(2)}, u32[]{:S(2)}) collective-permute-start(bf16[168,640]{1,0:T(8,128)(2,1)S(1)} %concatenate.25), channel_id=1, source_target_pairs={{0,48},{1,49},{16,0},{17,1},{32,16},{33,17},{48,32},{49,33},{64,19... | collective-permute-start | bytes 645128 | tf_op jit(solution)/shard_map/ppermute | solution.py:270
  19.8 9.4 %collective-permute-start.3 = (bf16[168,640]{1,0:T(8,128)(2,1)S(1)}, bf16[168,640]{1,0:T(8,128)(2,1)S(1)}, u32[]{:S(2)}, u32[]{:S(2)}) collective-permute-start(bf16[168,640]{1,0:T(8,128)(2,1)S(1)} %concatenate.25), channel_id=1, source_target_pairs={{0,32},{1,33},{16,48},{17,49},{32,0},{33,1},{48,16},{49,17},{64,65... | collective-permute-start | bytes 645128 | tf_op jit(solution)/shard_map/ppermute | solution.py:270
  22.1 7.1 %collective-permute-start.2 = (bf16[168,640]{1,0:T(8,128)(2,1)S(1)}, bf16[168,640]{1,0:T(8,128)(2,1)S(1)}, u32[]{:S(2)}, u32[]{:S(2)}) collective-permute-start(bf16[168,640]{1,0:T(8,128)(2,1)S(1)} %concatenate.25), channel_id=1, source_target_pairs={{0,16},{1,17},{16,32},{17,33},{32,48},{33,49},{48,0},{49,1},{64,19... | collective-permute-start | bytes 645128 | tf_op jit(solution)/shard_map/ppermute | solution.py:270
  24.0 9.7 %collective-permute-start.5 = (bf16[128,640]{1,0:T(8,128)(2,1)}, bf16[128,640]{1,0:T(8,128)(2,1)S(1)}, u32[]{:S(2)}, u32[]{:S(2)}) collective-permute-start(bf16[128,640]{1,0:T(8,128)(2,1)} %bitcast.21), channel_id=1, source_target_pairs={{0,0},{1,1},{2,64},{3,65},{4,128},{5,129},{6,192},{7,193},{8,8},{9... | collective-permute-start | bytes 491528 | tf_op jit(solution)/shard_map/ppermute | solution.py:269
  33.7 13.2 %collective-permute-start.7 = (bf16[672,640]{1,0:T(8,128)(2,1)S(1)}, bf16[672,640]{1,0:T(8,128)(2,1)S(1)}, u32[]{:S(2)}, u32[]{:S(2)}) collective-permute-start(bf16[672,640]{1,0:T(8,128)(2,1)S(1)} %constant_dynamic-update-slice_fusion.b0), channel_id=1, source_target_pairs={{0,1},{1,0},{16,17},{17,16},{32,33},{33,32},{48,49},{49,48},{64,96... | collective-permute-start | bytes 2580488 | tf_op jit(solution)/shard_map/ppermute | solution.py:277
  36.4 19.7 %collective-permute-start.11 = (bf16[672,640]{1,0:T(8,128)(2,1)S(1)}, bf16[672,640]{1,0:T(8,128)(2,1)S(1)}, u32[]{:S(2)}, u32[]{:S(2)}) collective-permute-start(bf16[672,640]{1,0:T(8,128)(2,1)S(1)} %constant_dynamic-update-slice_fusion.b0), channel_id=1, source_target_pairs={{0,128},{1,129},{16,144},{17,145},{32,160},{33,161},{48,176},{49,1... | collective-permute-start | bytes 2580488 | tf_op jit(solution)/shard_map/ppermute | solution.py:277
  36.7 20.0 %collective-permute-start.9 = (bf16[672,640]{1,0:T(8,128)(2,1)S(1)}, bf16[672,640]{1,0:T(8,128)(2,1)S(1)}, u32[]{:S(2)}, u32[]{:S(2)}) collective-permute-start(bf16[672,640]{1,0:T(8,128)(2,1)S(1)} %constant_dynamic-update-slice_fusion.b0), channel_id=1, source_target_pairs={{0,64},{64,0},{1,65},{65,1},{2,66},{66,2},{3,67},{67,3},{4,68},{68... | collective-permute-start | bytes 2580488 | tf_op jit(solution)/shard_map/ppermute | solution.py:52
  39.0 18.7 %collective-permute-start.6 = (bf16[672,640]{1,0:T(8,128)(2,1)S(1)}, bf16[672,640]{1,0:T(8,128)(2,1)S(1)}, u32[]{:S(2)}, u32[]{:S(2)}) collective-permute-start(bf16[672,640]{1,0:T(8,128)(2,1)S(1)} %constant_dynamic-update-slice_fusion.b0), channel_id=1, source_target_pairs={{0,129},{1,128},{16,145},{17,144},{32,161},{33,160},{48,177},{49,1... | collective-permute-start | bytes 2580488 | tf_op jit(solution)/shard_map/ppermute | solution.py:277
  47.0 9.7 %collective-permute-start.10 = (bf16[672,640]{1,0:T(8,128)(2,1)S(1)}, bf16[672,640]{1,0:T(8,128)(2,1)S(1)}, u32[]{:S(2)}, u32[]{:S(2)}) collective-permute-start(bf16[672,640]{1,0:T(8,128)(2,1)S(1)} %collective-permute-done.7.b1), channel_id=1, source_target_pairs={{0,64},{64,0},{1,65},{65,1},{2,66},{66,2},{3,67},{67,3},{4,68},{68... | collective-permute-start | bytes 2580488 | tf_op jit(solution)/shard_map/ppermute | solution.py:52
  52.5 5.4 %collective-permute-start.8 = (bf16[128,640]{1,0:T(8,128)(2,1)S(1)}, bf16[128,640]{1,0:T(8,128)(2,1)S(1)}, u32[]{:S(2)}, u32[]{:S(2)}) collective-permute-start(bf16[128,640]{1,0:T(8,128)(2,1)S(1)} %copy-done.1), channel_id=1, source_target_pairs={{192,6},{193,7},{194,70},{195,71},{196,134},{197,135},{198,198},{1... | collective-permute-start | bytes 491528 | tf_op jit(solution)/shard_map/ppermute | solution.py:279
  56.1 6.2 %collective-permute-start.12 = (bf16[672,640]{1,0:T(8,128)(2,1)S(1)}, bf16[672,640]{1,0:T(8,128)(2,1)S(1)}, u32[]{:S(2)}, u32[]{:S(2)}) collective-permute-start(bf16[672,640]{1,0:T(8,128)(2,1)S(1)} %collective-permute-done.11.b0), channel_id=1, source_target_pairs={{0,64},{64,0},{1,65},{65,1},{2,66},{66,2},{3,67},{67,3},{4,68},{68... | collective-permute-start | bytes 2580488 | tf_op jit(solution)/shard_map/ppermute | solution.py:52
  58.0 5.3 %collective-permute-start.13 = (bf16[672,640]{1,0:T(8,128)(2,1)S(1)}, bf16[672,640]{1,0:T(8,128)(2,1)S(1)}, u32[]{:S(2)}, u32[]{:S(2)}) collective-permute-start(bf16[672,640]{1,0:T(8,128)(2,1)S(1)} %collective-permute-done.6.b1), channel_id=1, source_target_pairs={{0,64},{64,0},{1,65},{65,1},{2,66},{66,2},{3,67},{67,3},{4,68},{68... | collective-permute-start | bytes 2580488 | tf_op jit(solution)/shard_map/ppermute | solution.py:52
  66.4 5.7 %collective-permute-start.14 = (bf16[128,640]{1,0:T(8,128)(2,1)S(1)}, bf16[128,640]{1,0:T(8,128)(2,1)S(1)}, u32[]{:S(2)}, u32[]{:S(2)}) collective-permute-start(bf16[128,640]{1,0:T(8,128)(2,1)S(1)} %shard_map.124), channel_id=1, source_target_pairs={{0,14},{2,0},{4,2},{6,4},{8,6},{10,8},{12,10},{14,12},{1,15},{3,1}... | collective-permute-start | bytes 491528 | tf_op jit(solution)/shard_map/ppermute | solution.py:318
  74.0 5.7 %collective-permute-start.15 = (bf16[128,640]{1,0:T(8,128)(2,1)S(1)}, bf16[128,640]{1,0:T(8,128)(2,1)S(1)}, u32[]{:S(2)}, u32[]{:S(2)}) collective-permute-start(bf16[128,640]{1,0:T(8,128)(2,1)S(1)} %shard_map.125), channel_id=1, source_target_pairs={{0,14},{2,0},{4,2},{6,4},{8,6},{10,8},{12,10},{14,12},{1,15},{3,1}... | collective-permute-start | bytes 491528 | tf_op jit(solution)/shard_map/ppermute | solution.py:318
  81.7 5.8 %collective-permute-start.16 = (bf16[128,640]{1,0:T(8,128)(2,1)S(1)}, bf16[128,640]{1,0:T(8,128)(2,1)S(1)}, u32[]{:S(2)}, u32[]{:S(2)}) collective-permute-start(bf16[128,640]{1,0:T(8,128)(2,1)S(1)} %shard_map.126), channel_id=1, source_target_pairs={{0,14},{2,0},{4,2},{6,4},{8,6},{10,8},{12,10},{14,12},{1,15},{3,1}... | collective-permute-start | bytes 491528 | tf_op jit(solution)/shard_map/ppermute | solution.py:318
  88.1 5.9 %collective-permute-start.17 = (bf16[1280,640]{1,0:T(8,128)(2,1)S(1)}, bf16[1280,640]{1,0:T(8,128)(2,1)S(1)}, u32[]{:S(2)}, u32[]{:S(2)}) collective-permute-start(bf16[1280,640]{1,0:T(8,128)(2,1)S(1)} %get-tuple-element.105), channel_id=1, source_target_pairs={{0,64},{64,0},{1,65},{65,1},{2,66},{66,2},{3,67},{67,3},{4,68},{68... | collective-permute-start | bytes 4915208 | tf_op jit(solution)/shard_map/ppermute | solution.py:52
  94.1 3.5 %collective-permute-start.18 = (bf16[1280,640]{1,0:T(8,128)(2,1)S(1)}, bf16[1280,640]{1,0:T(8,128)(2,1)S(1)}, u32[]{:S(2)}, u32[]{:S(2)}) collective-permute-start(bf16[1280,640]{1,0:T(8,128)(2,1)S(1)} %shard_map.129), channel_id=1, source_target_pairs={{0,64},{64,0},{1,65},{65,1},{2,66},{66,2},{3,67},{67,3},{4,68},{68... | collective-permute-start | bytes 4915208 | tf_op jit(solution)/shard_map/ppermute | solution.py:52
  94.4 3.1 %collective-permute-start.19 = (f32[1,640]{1,0:T(1,128)S(1)}, f32[1,640]{1,0:T(1,128)S(1)}, u32[]{:S(2)}, u32[]{:S(2)}) collective-permute-start(f32[1,640]{1,0:T(1,128)S(1)} %get-tuple-element.110.gain_here), channel_id=1, source_target_pairs={{0,64},{64,0},{1,65},{65,1},{2,66},{66,2},{3,67},{67,3},{4,68},{68... | collective-permute-start | bytes 7688 | tf_op jit(solution)/shard_map/ppermute | solution.py:52
  98.6 16.0 %collective-permute-start.20 = (bf16[656,640]{1,0:T(8,128)(2,1)S(1)}, bf16[656,640]{1,0:T(8,128)(2,1)S(1)}, u32[]{:S(2)}, u32[]{:S(2)}) collective-permute-start(bf16[656,640]{1,0:T(8,128)(2,1)S(1)} %get-tuple-element.112), channel_id=1, source_target_pairs={{0,1},{1,0},{16,17},{17,16},{32,33},{33,32},{48,49},{49,48},{64,96... | collective-permute-start | bytes 2519048 | tf_op jit(solution)/shard_map/ppermute | solution.py:342
  100.3 20.4 %collective-permute-start.21 = (bf16[656,640]{1,0:T(8,128)(2,1)S(1)}, bf16[656,640]{1,0:T(8,128)(2,1)S(1)}, u32[]{:S(2)}, u32[]{:S(2)}) collective-permute-start(bf16[656,640]{1,0:T(8,128)(2,1)S(1)} %get-tuple-element.113), channel_id=1, source_target_pairs={{0,129},{1,128},{16,145},{17,144},{32,161},{33,160},{48,177},{49,1... | collective-permute-start | bytes 2519048 | tf_op jit(solution)/shard_map/ppermute | solution.py:342
  102.6 18.0 %collective-permute-start.22 = (bf16[656,640]{1,0:T(8,128)(2,1)S(1)}, bf16[656,640]{1,0:T(8,128)(2,1)S(1)}, u32[]{:S(2)}, u32[]{:S(2)}) collective-permute-start(bf16[656,640]{1,0:T(8,128)(2,1)S(1)} %get-tuple-element.114), channel_id=1, source_target_pairs={{0,128},{1,129},{16,144},{17,145},{32,160},{33,161},{48,176},{49,1... | collective-permute-start | bytes 2519048 | tf_op jit(solution)/shard_map/ppermute | solution.py:342
  102.6 11.3 %collective-permute-start.23 = (bf16[128,640]{1,0:T(8,128)(2,1)S(1)}, bf16[128,640]{1,0:T(8,128)(2,1)S(1)}, u32[]{:S(2)}, u32[]{:S(2)}) collective-permute-start(bf16[128,640]{1,0:T(8,128)(2,1)S(1)} %get-tuple-element.115), channel_id=1, source_target_pairs={{0,0},{1,1},{64,2},{65,3},{128,4},{129,5},{192,6},{193,7},{8,8},{9... | collective-permute-start | bytes 491528 | tf_op jit(solution)/shard_map/ppermute | solution.py:338
  121.1 5.3 %collective-permute-start.24 = (bf16[176,640]{1,0:T(8,128)(2,1)S(1)}, bf16[176,640]{1,0:T(8,128)(2,1)S(1)}, u32[]{:S(2)}, u32[]{:S(2)}) collective-permute-start(bf16[176,640]{1,0:T(8,128)(2,1)S(1)} %get-tuple-element.122), channel_id=1, source_target_pairs={{0,48},{1,49},{16,0},{17,1},{32,16},{33,17},{48,32},{49,33},{64,19... | collective-permute-start | bytes 675848 | tf_op jit(solution)/shard_map/ppermute | solution.py:347
  123.5 6.3 %collective-permute-start.25 = (bf16[176,640]{1,0:T(8,128)(2,1)S(1)}, bf16[176,640]{1,0:T(8,128)(2,1)S(1)}, u32[]{:S(2)}, u32[]{:S(2)}) collective-permute-start(bf16[176,640]{1,0:T(8,128)(2,1)S(1)} %get-tuple-element.123), channel_id=1, source_target_pairs={{0,32},{1,33},{16,48},{17,49},{32,0},{33,1},{48,16},{49,17},{64,65... | collective-permute-start | bytes 675848 | tf_op jit(solution)/shard_map/ppermute | solution.py:347
  124.0 6.8 %collective-permute-start.26 = (bf16[176,640]{1,0:T(8,128)(2,1)S(1)}, bf16[176,640]{1,0:T(8,128)(2,1)S(1)}, u32[]{:S(2)}, u32[]{:S(2)}) collective-permute-start(bf16[176,640]{1,0:T(8,128)(2,1)S(1)} %get-tuple-element.124), channel_id=1, source_target_pairs={{0,16},{1,17},{16,32},{17,33},{32,48},{33,49},{48,0},{49,1},{64,19... | collective-permute-start | bytes 675848 | tf_op jit(solution)/shard_map/ppermute | solution.py:347
  131.1 17.7 %collective-permute-start.27 = (bf16[88,640]{1,0:T(8,128)(2,1)S(1)}, bf16[88,640]{1,0:T(8,128)(2,1)S(1)}, u32[]{:S(2)}, u32[]{:S(2)}) collective-permute-start(bf16[88,640]{1,0:T(8,128)(2,1)S(1)} %concatenate.27), channel_id=1, source_target_pairs={{0,0},{1,1},{64,2},{65,3},{128,4},{129,5},{192,6},{193,7},{8,8},{9... | collective-permute-start | bytes 337928 | tf_op jit(solution)/shard_map/ppermute | solution.py:354
  145.5 6.4 %collective-permute-start.28 = (bf16[88,640]{1,0:T(8,128)(2,1)S(1)}, bf16[88,640]{1,0:T(8,128)(2,1)S(1)}, u32[]{:S(2)}, u32[]{:S(2)}) collective-permute-start(bf16[88,640]{1,0:T(8,128)(2,1)S(1)} %concatenate.28), channel_id=1, source_target_pairs={{8,0},{9,1},{72,2},{73,3},{136,4},{137,5},{200,6},{201,7},{0,8},{1... | collective-permute-start | bytes 337928 | tf_op jit(solution)/shard_map/ppermute | solution.py:354

commit v10 on v9

--- a/solution.py
+++ b/solution.py
@@ -363,7 +363,7 @@
             COLUMN,
             work_to_home(flip),
         )
-        for flip in (0, 1)
+        for flip in (1, 0)
     ]
     w_in_home, w_out_home, gain_home = kernel(
         home_kernel, [((own, chan), f32), ((own, chan), f32), ((1, chan), f32)]

time: 153 us -> 152 us (level)
  waiting for transfers between devices: 51.2 us -> 49.2 us
    ppermute x2, waiting for transfers between devices: 6.29 us -> 4.31 us  [on_device(): lax.ppermute(jnp.concatenate([total[flip * own:(flip + 1) * own], total[(...]
  transfers between devices with their start and end apart: 29 -> 29, of which waited for: 19 -> 18; matrix products, arithmetic and copies ran while one was open for 0% -> 0% of each run, Pallas kernels for 4% -> 4%
where the time goes in v10:
time: 152 us; the launch traced here: 151 us
  starting transfers between devices  79.9 us (53%)
  waiting for transfers between devices  49.2 us (32%)
  Pallas kernels  15.9 us (10%)
  other arithmetic  3.02 us (2%)
    pallas_call x14, Pallas kernels, call(): pl.pallas_call(body, out_shape=shapes, in_specs=[whole] * len(operands),...  15.9 us
    ppermute x2, starting transfers between devices, on_device(): lax.ppermute(jnp.concatenate([total[flip * own:(flip + 1) * own], total[(...  14.5 us
    ppermute x7, starting transfers between devices, across_cores(): return lax.ppermute(value, 'core', [(0, 1), (1, 0)])  14.1 us
    ppermute x2, starting transfers between devices, on_device(): lax.ppermute(shard, COLUMN, home_to_work(flip))  10.4 us
    ppermute x3, waiting for transfers between devices, on_device(): grad = lax.ppermute(turn(grad, *held), 'z', next_section())  8.58 us
    ppermute x3, starting transfers between devices, on_device(): grad = lax.ppermute(turn(grad, *held), 'z', next_section())  8.49 us
    ppermute x1, starting transfers between devices, on_device(): grad_home = lax.ppermute(grad_in, COLUMN, work_to_home(0))  6.85 us
    ppermute x3, waiting for transfers between devices, on_device(): lax.ppermute(part, PLANE, along(1, SIDE - k))  6.04 us
  transfers between devices with their start and end apart: 29, of which 18 were waited for; matrix products, arithmetic and copies ran while one was open for 0% of the time, Pallas kernels for 4%

profile of v10, /device:TPU:9, one launch (start us, length us, event | category | flops | bytes accessed | tf_op | source)
XLA Modules:
  0.0 150.6 jit_solution(1350184919922787574)
XLA Ops:
  4.4 6.1 %collective-permute-start.1 = (bf16[88,640]{1,0:T(8,128)(2,1)S(1)}, bf16[88,640]{1,0:T(8,128)(2,1)S(1)}, u32[]{:S(2)}, u32[]{:S(2)}) collective-permute-start(bf16[88,640]{1,0:T(8,128)(2,1)S(1)} %pad_maximum_fusion), channel_id=1, source_target_pairs={{0,8},{1,9},{2,72},{3,73},{4,136},{5,137},{6,200},{7,201},{8,0},{9... | collective-permute-start | bytes 337928 | tf_op jit(solution)/shard_map/ppermute | solution.py:255
  10.5 4.2 %collective-permute-start = (bf16[88,640]{1,0:T(8,128)(2,1)S(1)}, bf16[88,640]{1,0:T(8,128)(2,1)S(1)}, u32[]{:S(2)}, u32[]{:S(2)}) collective-permute-start(bf16[88,640]{1,0:T(8,128)(2,1)S(1)} %pad_maximum_fusion), channel_id=1, source_target_pairs={{0,0},{1,1},{2,64},{3,65},{4,128},{5,129},{6,192},{7,193},{8,8},{9... | collective-permute-start | bytes 337928 | tf_op jit(solution)/shard_map/ppermute | solution.py:255
  14.7 3.5 %collective-permute-done.1 = bf16[88,640]{1,0:T(8,128)(2,1)S(1)} collective-permute-done((bf16[88,640]{1,0:T(8,128)(2,1)S(1)}, bf16[88,640]{1,0:T(8,128)(2,1)S(1)}, u32[]{:S(2)}, u32[]{:S(2)}) %collective-permute-start.1) | collective-permute-done | bytes 112672 | tf_op jit(solution)/shard_map/ppermute | solution.py:255
  19.8 2.2 %collective-permute-start.3 = (bf16[168,640]{1,0:T(8,128)(2,1)S(1)}, bf16[168,640]{1,0:T(8,128)(2,1)S(1)}, u32[]{:S(2)}, u32[]{:S(2)}) collective-permute-start(bf16[168,640]{1,0:T(8,128)(2,1)S(1)} %concatenate.25), channel_id=1, source_target_pairs={{0,32},{1,33},{16,48},{17,49},{32,0},{33,1},{48,16},{49,17},{64,65... | collective-permute-start | bytes 645128 | tf_op jit(solution)/shard_map/ppermute | solution.py:270
  24.0 5.1 %collective-permute-start.5 = (bf16[128,640]{1,0:T(8,128)(2,1)}, bf16[128,640]{1,0:T(8,128)(2,1)S(1)}, u32[]{:S(2)}, u32[]{:S(2)}) collective-permute-start(bf16[128,640]{1,0:T(8,128)(2,1)} %bitcast.21), channel_id=1, source_target_pairs={{0,0},{1,1},{2,64},{3,65},{4,128},{5,129},{6,192},{7,193},{8,8},{9... | collective-permute-start | bytes 491528 | tf_op jit(solution)/shard_map/ppermute | solution.py:269
  29.3 4.4 %collective-permute-done.5.x_ref.x = bf16[128,640]{1,0:T(8,128)(2,1)S(1)} collective-permute-done((bf16[128,640]{1,0:T(8,128)(2,1)}, bf16[128,640]{1,0:T(8,128)(2,1)S(1)}, u32[]{:S(2)}, u32[]{:S(2)}) %collective-permute-start.5) | collective-permute-done | bytes 163872 | tf_op jit(solution)/shard_map/ppermute | solution.py:269
  33.7 2.7 %collective-permute-start.7 = (bf16[672,640]{1,0:T(8,128)(2,1)S(1)}, bf16[672,640]{1,0:T(8,128)(2,1)S(1)}, u32[]{:S(2)}, u32[]{:S(2)}) collective-permute-start(bf16[672,640]{1,0:T(8,128)(2,1)S(1)} %constant_dynamic-update-slice_fusion.b0), channel_id=1, source_target_pairs={{0,1},{1,0},{16,17},{17,16},{32,33},{33,32},{48,49},{49,48},{64,96... | collective-permute-start | bytes 2580488 | tf_op jit(solution)/shard_map/ppermute | solution.py:277
  36.7 2.3 %collective-permute-start.9 = (bf16[672,640]{1,0:T(8,128)(2,1)S(1)}, bf16[672,640]{1,0:T(8,128)(2,1)S(1)}, u32[]{:S(2)}, u32[]{:S(2)}) collective-permute-start(bf16[672,640]{1,0:T(8,128)(2,1)S(1)} %constant_dynamic-update-slice_fusion.b0), channel_id=1, source_target_pairs={{0,64},{64,0},{1,65},{65,1},{2,66},{66,2},{3,67},{67,3},{4,68},{68... | collective-permute-start | bytes 2580488 | tf_op jit(solution)/shard_map/ppermute | solution.py:52
  39.0 2.5 %collective-permute-start.6 = (bf16[672,640]{1,0:T(8,128)(2,1)S(1)}, bf16[672,640]{1,0:T(8,128)(2,1)S(1)}, u32[]{:S(2)}, u32[]{:S(2)}) collective-permute-start(bf16[672,640]{1,0:T(8,128)(2,1)S(1)} %constant_dynamic-update-slice_fusion.b0), channel_id=1, source_target_pairs={{0,129},{1,128},{16,145},{17,144},{32,161},{33,160},{48,177},{49,1... | collective-permute-start | bytes 2580488 | tf_op jit(solution)/shard_map/ppermute | solution.py:277
  41.5 5.5 %collective-permute-done.7.b1 = bf16[672,640]{1,0:T(8,128)(2,1)S(1)} collective-permute-done((bf16[672,640]{1,0:T(8,128)(2,1)S(1)}, bf16[672,640]{1,0:T(8,128)(2,1)S(1)}, u32[]{:S(2)}, u32[]{:S(2)}) %collective-permute-start.7) | collective-permute-done | bytes 860192 | tf_op jit(solution)/shard_map/ppermute | solution.py:277
  47.0 5.2 %collective-permute-start.10 = (bf16[672,640]{1,0:T(8,128)(2,1)S(1)}, bf16[672,640]{1,0:T(8,128)(2,1)S(1)}, u32[]{:S(2)}, u32[]{:S(2)}) collective-permute-start(bf16[672,640]{1,0:T(8,128)(2,1)S(1)} %collective-permute-done.7.b1), channel_id=1, source_target_pairs={{0,64},{64,0},{1,65},{65,1},{2,66},{66,2},{3,67},{67,3},{4,68},{68... | collective-permute-start | bytes 2580488 | tf_op jit(solution)/shard_map/ppermute | solution.py:52
  52.5 3.1 %collective-permute-start.8 = (bf16[128,640]{1,0:T(8,128)(2,1)S(1)}, bf16[128,640]{1,0:T(8,128)(2,1)S(1)}, u32[]{:S(2)}, u32[]{:S(2)}) collective-permute-start(bf16[128,640]{1,0:T(8,128)(2,1)S(1)} %copy-done.1), channel_id=1, source_target_pairs={{192,6},{193,7},{194,70},{195,71},{196,134},{197,135},{198,198},{1... | collective-permute-start | bytes 491528 | tf_op jit(solution)/shard_map/ppermute | solution.py:279
  58.0 3.3 %collective-permute-start.13 = (bf16[672,640]{1,0:T(8,128)(2,1)S(1)}, bf16[672,640]{1,0:T(8,128)(2,1)S(1)}, u32[]{:S(2)}, u32[]{:S(2)}) collective-permute-start(bf16[672,640]{1,0:T(8,128)(2,1)S(1)} %collective-permute-done.6.b1), channel_id=1, source_target_pairs={{0,64},{64,0},{1,65},{65,1},{2,66},{66,2},{3,67},{67,3},{4,68},{68... | collective-permute-start | bytes 2580488 | tf_op jit(solution)/shard_map/ppermute | solution.py:52
  68.2 3.8 %collective-permute-done.14.g = bf16[128,640]{1,0:T(8,128)(2,1)S(1)} collective-permute-done((bf16[128,640]{1,0:T(8,128)(2,1)S(1)}, bf16[128,640]{1,0:T(8,128)(2,1)S(1)}, u32[]{:S(2)}, u32[]{:S(2)}) %collective-permute-start.14) | collective-permute-done | bytes 163872 | tf_op jit(solution)/shard_map/ppermute | solution.py:318
  72.0 2.0 %shard_map.125 = bf16[128,640]{1,0:T(8,128)(2,1)S(1)} custom-call(bf16[128,640]{1,0:T(8,128)(2,1)S(1)} %collective-permute-done.14.g, bf16[128,640]{1,0:T(8,128)(2,1)S(1)} %collective-permute-done.5.x_ref.x, f32[1,640]{1,0:T(1,128)S(1)} %slice_add_fusion.1.gain_ref.gain, bf16[640,640]{1,0:T(8,128)(2,1)S(1)} %get-tuple-element.85.refs_0_, ...), custom_call_target="tpu_custom_call" | custom-call | flops 838860800 | bytes 4194304 | tf_op jit(solution)/shard_map/pallas_call | solution.py:223
  74.0 3.1 %collective-permute-start.15 = (bf16[128,640]{1,0:T(8,128)(2,1)S(1)}, bf16[128,640]{1,0:T(8,128)(2,1)S(1)}, u32[]{:S(2)}, u32[]{:S(2)}) collective-permute-start(bf16[128,640]{1,0:T(8,128)(2,1)S(1)} %shard_map.125), channel_id=1, source_target_pairs={{0,14},{2,0},{4,2},{6,4},{8,6},{10,8},{12,10},{14,12},{1,15},{3,1}... | collective-permute-start | bytes 491528 | tf_op jit(solution)/shard_map/ppermute | solution.py:318
  77.2 2.5 %collective-permute-done.15.g = bf16[128,640]{1,0:T(8,128)(2,1)S(1)} collective-permute-done((bf16[128,640]{1,0:T(8,128)(2,1)S(1)}, bf16[128,640]{1,0:T(8,128)(2,1)S(1)}, u32[]{:S(2)}, u32[]{:S(2)}) %collective-permute-start.15) | collective-permute-done | bytes 163872 | tf_op jit(solution)/shard_map/ppermute | solution.py:318
  79.7 2.0 %shard_map.126 = bf16[128,640]{1,0:T(8,128)(2,1)S(1)} custom-call(bf16[128,640]{1,0:T(8,128)(2,1)S(1)} %collective-permute-done.15.g, bf16[128,640]{1,0:T(8,128)(2,1)S(1)} %collective-permute-done.5.x_ref.x, f32[1,640]{1,0:T(1,128)S(1)} %slice_add_fusion.1.gain_ref.gain, bf16[640,640]{1,0:T(8,128)(2,1)S(1)} %get-tuple-element.85.refs_0_, ...), custom_call_target="tpu_custom_call" | custom-call | flops 838860800 | bytes 4194304 | tf_op jit(solution)/shard_map/pallas_call | solution.py:223
  81.7 3.5 %collective-permute-start.16 = (bf16[128,640]{1,0:T(8,128)(2,1)S(1)}, bf16[128,640]{1,0:T(8,128)(2,1)S(1)}, u32[]{:S(2)}, u32[]{:S(2)}) collective-permute-start(bf16[128,640]{1,0:T(8,128)(2,1)S(1)} %shard_map.126), channel_id=1, source_target_pairs={{0,14},{2,0},{4,2},{6,4},{8,6},{10,8},{12,10},{14,12},{1,15},{3,1}... | collective-permute-start | bytes 491528 | tf_op jit(solution)/shard_map/ppermute | solution.py:318
  85.3 2.2 %collective-permute-done.16.last = bf16[128,640]{1,0:T(8,128)(2,1)S(1)} collective-permute-done((bf16[128,640]{1,0:T(8,128)(2,1)S(1)}, bf16[128,640]{1,0:T(8,128)(2,1)S(1)}, u32[]{:S(2)}, u32[]{:S(2)}) %collective-permute-start.16) | collective-permute-done | bytes 163872 | tf_op jit(solution)/shard_map/ppermute | solution.py:318
  88.1 2.8 %collective-permute-start.17 = (bf16[1280,640]{1,0:T(8,128)(2,1)S(1)}, bf16[1280,640]{1,0:T(8,128)(2,1)S(1)}, u32[]{:S(2)}, u32[]{:S(2)}) collective-permute-start(bf16[1280,640]{1,0:T(8,128)(2,1)S(1)} %get-tuple-element.105), channel_id=1, source_target_pairs={{0,64},{64,0},{1,65},{65,1},{2,66},{66,2},{3,67},{67,3},{4,68},{68... | collective-permute-start | bytes 4915208 | tf_op jit(solution)/shard_map/ppermute | solution.py:52
  90.9 2.0 %shard_map.128 = (bf16[128,640]{1,0:T(8,128)(2,1)S(1)}, f32[1,640]{1,0:T(1,128)S(1)}, bf16[128,640]{1,0:T(8,128)(2,1)S(1)}, bf16[128,640]{1,0:T(8,128)(2,1)S(1)}...) custom-call(bf16[128,640]{1,0:T(8,128)(2,1)S(1)} %get-tuple-element.99.g.grad, ...), custom_call_target="tpu_custom_call" | custom-call | flops 838860800 | bytes 4194304 | tf_op jit(solution)/shard_map/pallas_call | solution.py:223
  94.6 3.0 %collective-permute-done.19.gain_there = f32[1,640]{1,0:T(1,128)S(1)} collective-permute-done((f32[1,640]{1,0:T(1,128)S(1)}, f32[1,640]{1,0:T(1,128)S(1)}, u32[]{:S(2)}, u32[]{:S(2)}) %collective-permute-start.19) | collective-permute-done | bytes 2592 | tf_op jit(solution)/shard_map/ppermute | solution.py:52
  100.3 2.3 %collective-permute-start.21 = (bf16[656,640]{1,0:T(8,128)(2,1)S(1)}, bf16[656,640]{1,0:T(8,128)(2,1)S(1)}, u32[]{:S(2)}, u32[]{:S(2)}) collective-permute-start(bf16[656,640]{1,0:T(8,128)(2,1)S(1)} %get-tuple-element.113), channel_id=1, source_target_pairs={{0,129},{1,128},{16,145},{17,144},{32,161},{33,160},{48,177},{49,1... | collective-permute-start | bytes 2519048 | tf_op jit(solution)/shard_map/ppermute | solution.py:342
  102.6 6.9 %collective-permute-start.23 = (bf16[128,640]{1,0:T(8,128)(2,1)S(1)}, bf16[128,640]{1,0:T(8,128)(2,1)S(1)}, u32[]{:S(2)}, u32[]{:S(2)}) collective-permute-start(bf16[128,640]{1,0:T(8,128)(2,1)S(1)} %get-tuple-element.115), channel_id=1, source_target_pairs={{0,0},{1,1},{64,2},{65,3},{128,4},{129,5},{192,6},{193,7},{8,8},{9... | collective-permute-start | bytes 491528 | tf_op jit(solution)/shard_map/ppermute | solution.py:338
  109.5 4.5 %collective-permute-done.23.value = bf16[128,640]{1,0:T(8,128)(2,1)S(1)} collective-permute-done((bf16[128,640]{1,0:T(8,128)(2,1)S(1)}, bf16[128,640]{1,0:T(8,128)(2,1)S(1)}, u32[]{:S(2)}, u32[]{:S(2)}) %collective-permute-start.23) | collective-permute-done | bytes 163872 | tf_op jit(solution)/shard_map/ppermute | solution.py:338
  114.6 6.0 %collective-permute-done.21.s2 = bf16[656,640]{1,0:T(8,128)(2,1)S(1)} collective-permute-done((bf16[656,640]{1,0:T(8,128)(2,1)S(1)}, bf16[656,640]{1,0:T(8,128)(2,1)S(1)}, u32[]{:S(2)}, u32[]{:S(2)}) %collective-permute-start.21) | collective-permute-done | bytes 839712 | tf_op jit(solution)/shard_map/ppermute | solution.py:342
  121.1 2.4 %collective-permute-start.24 = (bf16[176,640]{1,0:T(8,128)(2,1)S(1)}, bf16[176,640]{1,0:T(8,128)(2,1)S(1)}, u32[]{:S(2)}, u32[]{:S(2)}) collective-permute-start(bf16[176,640]{1,0:T(8,128)(2,1)S(1)} %get-tuple-element.122), channel_id=1, source_target_pairs={{0,48},{1,49},{16,0},{17,1},{32,16},{33,17},{48,32},{49,33},{64,19... | collective-permute-start | bytes 675848 | tf_op jit(solution)/shard_map/ppermute | solution.py:347
  126.4 3.4 %collective-permute-done.25 = bf16[176,640]{1,0:T(8,128)(2,1)S(1)} collective-permute-done((bf16[176,640]{1,0:T(8,128)(2,1)S(1)}, bf16[176,640]{1,0:T(8,128)(2,1)S(1)}, u32[]{:S(2)}, u32[]{:S(2)}) %collective-permute-start.25) | collective-permute-done | bytes 225312 | tf_op jit(solution)/shard_map/ppermute | solution.py:347
  131.1 9.5 %collective-permute-start.27 = (bf16[88,640]{1,0:T(8,128)(2,1)S(1)}, bf16[88,640]{1,0:T(8,128)(2,1)S(1)}, u32[]{:S(2)}, u32[]{:S(2)}) collective-permute-start(bf16[88,640]{1,0:T(8,128)(2,1)S(1)} %concatenate.27), channel_id=1, source_target_pairs={{8,0},{9,1},{72,2},{73,3},{136,4},{137,5},{200,6},{201,7},{0,8},{1... | collective-permute-start | bytes 337928 | tf_op jit(solution)/shard_map/ppermute | solution.py:354
  140.7 4.9 %collective-permute-start.28 = (bf16[88,640]{1,0:T(8,128)(2,1)S(1)}, bf16[88,640]{1,0:T(8,128)(2,1)S(1)}, u32[]{:S(2)}, u32[]{:S(2)}) collective-permute-start(bf16[88,640]{1,0:T(8,128)(2,1)S(1)} %concatenate.28), channel_id=1, source_target_pairs={{0,0},{1,1},{64,2},{65,3},{128,4},{129,5},{192,6},{193,7},{8,8},{9... | collective-permute-start | bytes 337928 | tf_op jit(solution)/shard_map/ppermute | solution.py:354
  145.6 4.3 %collective-permute-done.28.part_1 = bf16[88,640]{1,0:T(8,128)(2,1)S(1)} collective-permute-done((bf16[88,640]{1,0:T(8,128)(2,1)S(1)}, bf16[88,640]{1,0:T(8,128)(2,1)S(1)}, u32[]{:S(2)}, u32[]{:S(2)}) %collective-permute-start.28) | collective-permute-done | bytes 112672 | tf_op jit(solution)/shard_map/ppermute | solution.py:354
  (82 shorter events, 28.2 us)
Async XLA Ops:
  0.6 1.7 %copy-start = (bf16[1,256,40]{1,2,0:T(8,128)(2,1)S(1)}, bf16[1,256,40]{1,2,0:T(8,128)(2,1)}, u32[]{:S(2)}) copy-start(bf16[1,256,40]{1,2,0:T(8,128)(2,1)} %param.14) | copy-start | bytes 61444
  4.4 13.9 %collective-permute-start.1 = (bf16[88,640]{1,0:T(8,128)(2,1)S(1)}, bf16[88,640]{1,0:T(8,128)(2,1)S(1)}, u32[]{:S(2)}, u32[]{:S(2)}) collective-permute-start(bf16[88,640]{1,0:T(8,128)(2,1)S(1)} %pad_maximum_fusion), channel_id=1, source_target_pairs={{0,8},{1,9},{2,72},{3,73},{4,136},{5,137},{6,200},{7,201},{8,0},{9... | collective-permute-start | bytes 337928 | tf_op jit(solution)/shard_map/ppermute | solution.py:255
  10.5 9.1 %collective-permute-start = (bf16[88,640]{1,0:T(8,128)(2,1)S(1)}, bf16[88,640]{1,0:T(8,128)(2,1)S(1)}, u32[]{:S(2)}, u32[]{:S(2)}) collective-permute-start(bf16[88,640]{1,0:T(8,128)(2,1)S(1)} %pad_maximum_fusion), channel_id=1, source_target_pairs={{0,0},{1,1},{2,64},{3,65},{4,128},{5,129},{6,192},{7,193},{8,8},{9... | collective-permute-start | bytes 337928 | tf_op jit(solution)/shard_map/ppermute | solution.py:255
  19.6 32.9 %copy-start.1 = (bf16[128,640]{1,0:T(8,128)(2,1)S(1)}, bf16[128,640]{1,0:T(8,128)(2,1)}, u32[]{:S(2)}) copy-start(bf16[128,640]{1,0:T(8,128)(2,1)} %param.10) | copy-start | bytes 491524
  19.7 9.5 %collective-permute-start.4 = (bf16[168,640]{1,0:T(8,128)(2,1)S(1)}, bf16[168,640]{1,0:T(8,128)(2,1)S(1)}, u32[]{:S(2)}, u32[]{:S(2)}) collective-permute-start(bf16[168,640]{1,0:T(8,128)(2,1)S(1)} %concatenate.25), channel_id=1, source_target_pairs={{0,48},{1,49},{16,0},{17,1},{32,16},{33,17},{48,32},{49,33},{64,19... | collective-permute-start | bytes 645128 | tf_op jit(solution)/shard_map/ppermute | solution.py:270
  19.8 9.4 %collective-permute-start.3 = (bf16[168,640]{1,0:T(8,128)(2,1)S(1)}, bf16[168,640]{1,0:T(8,128)(2,1)S(1)}, u32[]{:S(2)}, u32[]{:S(2)}) collective-permute-start(bf16[168,640]{1,0:T(8,128)(2,1)S(1)} %concatenate.25), channel_id=1, source_target_pairs={{0,32},{1,33},{16,48},{17,49},{32,0},{33,1},{48,16},{49,17},{64,65... | collective-permute-start | bytes 645128 | tf_op jit(solution)/shard_map/ppermute | solution.py:270
  22.1 7.1 %collective-permute-start.2 = (bf16[168,640]{1,0:T(8,128)(2,1)S(1)}, bf16[168,640]{1,0:T(8,128)(2,1)S(1)}, u32[]{:S(2)}, u32[]{:S(2)}) collective-permute-start(bf16[168,640]{1,0:T(8,128)(2,1)S(1)} %concatenate.25), channel_id=1, source_target_pairs={{0,16},{1,17},{16,32},{17,33},{32,48},{33,49},{48,0},{49,1},{64,19... | collective-permute-start | bytes 645128 | tf_op jit(solution)/shard_map/ppermute | solution.py:270
  24.0 9.7 %collective-permute-start.5 = (bf16[128,640]{1,0:T(8,128)(2,1)}, bf16[128,640]{1,0:T(8,128)(2,1)S(1)}, u32[]{:S(2)}, u32[]{:S(2)}) collective-permute-start(bf16[128,640]{1,0:T(8,128)(2,1)} %bitcast.21), channel_id=1, source_target_pairs={{0,0},{1,1},{2,64},{3,65},{4,128},{5,129},{6,192},{7,193},{8,8},{9... | collective-permute-start | bytes 491528 | tf_op jit(solution)/shard_map/ppermute | solution.py:269
  33.7 13.2 %collective-permute-start.7 = (bf16[672,640]{1,0:T(8,128)(2,1)S(1)}, bf16[672,640]{1,0:T(8,128)(2,1)S(1)}, u32[]{:S(2)}, u32[]{:S(2)}) collective-permute-start(bf16[672,640]{1,0:T(8,128)(2,1)S(1)} %constant_dynamic-update-slice_fusion.b0), channel_id=1, source_target_pairs={{0,1},{1,0},{16,17},{17,16},{32,33},{33,32},{48,49},{49,48},{64,96... | collective-permute-start | bytes 2580488 | tf_op jit(solution)/shard_map/ppermute | solution.py:277
  36.4 19.7 %collective-permute-start.11 = (bf16[672,640]{1,0:T(8,128)(2,1)S(1)}, bf16[672,640]{1,0:T(8,128)(2,1)S(1)}, u32[]{:S(2)}, u32[]{:S(2)}) collective-permute-start(bf16[672,640]{1,0:T(8,128)(2,1)S(1)} %constant_dynamic-update-slice_fusion.b0), channel_id=1, source_target_pairs={{0,128},{1,129},{16,144},{17,145},{32,160},{33,161},{48,176},{49,1... | collective-permute-start | bytes 2580488 | tf_op jit(solution)/shard_map/ppermute | solution.py:277
  36.7 20.0 %collective-permute-start.9 = (bf16[672,640]{1,0:T(8,128)(2,1)S(1)}, bf16[672,640]{1,0:T(8,128)(2,1)S(1)}, u32[]{:S(2)}, u32[]{:S(2)}) collective-permute-start(bf16[672,640]{1,0:T(8,128)(2,1)S(1)} %constant_dynamic-update-slice_fusion.b0), channel_id=1, source_target_pairs={{0,64},{64,0},{1,65},{65,1},{2,66},{66,2},{3,67},{67,3},{4,68},{68... | collective-permute-start | bytes 2580488 | tf_op jit(solution)/shard_map/ppermute | solution.py:52
  39.0 18.7 %collective-permute-start.6 = (bf16[672,640]{1,0:T(8,128)(2,1)S(1)}, bf16[672,640]{1,0:T(8,128)(2,1)S(1)}, u32[]{:S(2)}, u32[]{:S(2)}) collective-permute-start(bf16[672,640]{1,0:T(8,128)(2,1)S(1)} %constant_dynamic-update-slice_fusion.b0), channel_id=1, source_target_pairs={{0,129},{1,128},{16,145},{17,144},{32,161},{33,160},{48,177},{49,1... | collective-permute-start | bytes 2580488 | tf_op jit(solution)/shard_map/ppermute | solution.py:277
  47.0 9.7 %collective-permute-start.10 = (bf16[672,640]{1,0:T(8,128)(2,1)S(1)}, bf16[672,640]{1,0:T(8,128)(2,1)S(1)}, u32[]{:S(2)}, u32[]{:S(2)}) collective-permute-start(bf16[672,640]{1,0:T(8,128)(2,1)S(1)} %collective-permute-done.7.b1), channel_id=1, source_target_pairs={{0,64},{64,0},{1,65},{65,1},{2,66},{66,2},{3,67},{67,3},{4,68},{68... | collective-permute-start | bytes 2580488 | tf_op jit(solution)/shard_map/ppermute | solution.py:52
  52.5 5.4 %collective-permute-start.8 = (bf16[128,640]{1,0:T(8,128)(2,1)S(1)}, bf16[128,640]{1,0:T(8,128)(2,1)S(1)}, u32[]{:S(2)}, u32[]{:S(2)}) collective-permute-start(bf16[128,640]{1,0:T(8,128)(2,1)S(1)} %copy-done.1), channel_id=1, source_target_pairs={{192,6},{193,7},{194,70},{195,71},{196,134},{197,135},{198,198},{1... | collective-permute-start | bytes 491528 | tf_op jit(solution)/shard_map/ppermute | solution.py:279
  56.1 6.2 %collective-permute-start.12 = (bf16[672,640]{1,0:T(8,128)(2,1)S(1)}, bf16[672,640]{1,0:T(8,128)(2,1)S(1)}, u32[]{:S(2)}, u32[]{:S(2)}) collective-permute-start(bf16[672,640]{1,0:T(8,128)(2,1)S(1)} %collective-permute-done.11.b0), channel_id=1, source_target_pairs={{0,64},{64,0},{1,65},{65,1},{2,66},{66,2},{3,67},{67,3},{4,68},{68... | collective-permute-start | bytes 2580488 | tf_op jit(solution)/shard_map/ppermute | solution.py:52
  58.0 5.3 %collective-permute-start.13 = (bf16[672,640]{1,0:T(8,128)(2,1)S(1)}, bf16[672,640]{1,0:T(8,128)(2,1)S(1)}, u32[]{:S(2)}, u32[]{:S(2)}) collective-permute-start(bf16[672,640]{1,0:T(8,128)(2,1)S(1)} %collective-permute-done.6.b1), channel_id=1, source_target_pairs={{0,64},{64,0},{1,65},{65,1},{2,66},{66,2},{3,67},{67,3},{4,68},{68... | collective-permute-start | bytes 2580488 | tf_op jit(solution)/shard_map/ppermute | solution.py:52
  66.4 5.7 %collective-permute-start.14 = (bf16[128,640]{1,0:T(8,128)(2,1)S(1)}, bf16[128,640]{1,0:T(8,128)(2,1)S(1)}, u32[]{:S(2)}, u32[]{:S(2)}) collective-permute-start(bf16[128,640]{1,0:T(8,128)(2,1)S(1)} %shard_map.124), channel_id=1, source_target_pairs={{0,14},{2,0},{4,2},{6,4},{8,6},{10,8},{12,10},{14,12},{1,15},{3,1}... | collective-permute-start | bytes 491528 | tf_op jit(solution)/shard_map/ppermute | solution.py:318
  74.0 5.7 %collective-permute-start.15 = (bf16[128,640]{1,0:T(8,128)(2,1)S(1)}, bf16[128,640]{1,0:T(8,128)(2,1)S(1)}, u32[]{:S(2)}, u32[]{:S(2)}) collective-permute-start(bf16[128,640]{1,0:T(8,128)(2,1)S(1)} %shard_map.125), channel_id=1, source_target_pairs={{0,14},{2,0},{4,2},{6,4},{8,6},{10,8},{12,10},{14,12},{1,15},{3,1}... | collective-permute-start | bytes 491528 | tf_op jit(solution)/shard_map/ppermute | solution.py:318
  81.7 5.8 %collective-permute-start.16 = (bf16[128,640]{1,0:T(8,128)(2,1)S(1)}, bf16[128,640]{1,0:T(8,128)(2,1)S(1)}, u32[]{:S(2)}, u32[]{:S(2)}) collective-permute-start(bf16[128,640]{1,0:T(8,128)(2,1)S(1)} %shard_map.126), channel_id=1, source_target_pairs={{0,14},{2,0},{4,2},{6,4},{8,6},{10,8},{12,10},{14,12},{1,15},{3,1}... | collective-permute-start | bytes 491528 | tf_op jit(solution)/shard_map/ppermute | solution.py:318
  88.1 5.9 %collective-permute-start.17 = (bf16[1280,640]{1,0:T(8,128)(2,1)S(1)}, bf16[1280,640]{1,0:T(8,128)(2,1)S(1)}, u32[]{:S(2)}, u32[]{:S(2)}) collective-permute-start(bf16[1280,640]{1,0:T(8,128)(2,1)S(1)} %get-tuple-element.105), channel_id=1, source_target_pairs={{0,64},{64,0},{1,65},{65,1},{2,66},{66,2},{3,67},{67,3},{4,68},{68... | collective-permute-start | bytes 4915208 | tf_op jit(solution)/shard_map/ppermute | solution.py:52
  94.1 3.5 %collective-permute-start.18 = (bf16[1280,640]{1,0:T(8,128)(2,1)S(1)}, bf16[1280,640]{1,0:T(8,128)(2,1)S(1)}, u32[]{:S(2)}, u32[]{:S(2)}) collective-permute-start(bf16[1280,640]{1,0:T(8,128)(2,1)S(1)} %shard_map.129), channel_id=1, source_target_pairs={{0,64},{64,0},{1,65},{65,1},{2,66},{66,2},{3,67},{67,3},{4,68},{68... | collective-permute-start | bytes 4915208 | tf_op jit(solution)/shard_map/ppermute | solution.py:52
  94.4 3.1 %collective-permute-start.19 = (f32[1,640]{1,0:T(1,128)S(1)}, f32[1,640]{1,0:T(1,128)S(1)}, u32[]{:S(2)}, u32[]{:S(2)}) collective-permute-start(f32[1,640]{1,0:T(1,128)S(1)} %get-tuple-element.110.gain_here), channel_id=1, source_target_pairs={{0,64},{64,0},{1,65},{65,1},{2,66},{66,2},{3,67},{67,3},{4,68},{68... | collective-permute-start | bytes 7688 | tf_op jit(solution)/shard_map/ppermute | solution.py:52
  98.6 16.0 %collective-permute-start.20 = (bf16[656,640]{1,0:T(8,128)(2,1)S(1)}, bf16[656,640]{1,0:T(8,128)(2,1)S(1)}, u32[]{:S(2)}, u32[]{:S(2)}) collective-permute-start(bf16[656,640]{1,0:T(8,128)(2,1)S(1)} %get-tuple-element.112), channel_id=1, source_target_pairs={{0,1},{1,0},{16,17},{17,16},{32,33},{33,32},{48,49},{49,48},{64,96... | collective-permute-start | bytes 2519048 | tf_op jit(solution)/shard_map/ppermute | solution.py:342
  100.3 20.4 %collective-permute-start.21 = (bf16[656,640]{1,0:T(8,128)(2,1)S(1)}, bf16[656,640]{1,0:T(8,128)(2,1)S(1)}, u32[]{:S(2)}, u32[]{:S(2)}) collective-permute-start(bf16[656,640]{1,0:T(8,128)(2,1)S(1)} %get-tuple-element.113), channel_id=1, source_target_pairs={{0,129},{1,128},{16,145},{17,144},{32,161},{33,160},{48,177},{49,1... | collective-permute-start | bytes 2519048 | tf_op jit(solution)/shard_map/ppermute | solution.py:342
  102.6 18.0 %collective-permute-start.22 = (bf16[656,640]{1,0:T(8,128)(2,1)S(1)}, bf16[656,640]{1,0:T(8,128)(2,1)S(1)}, u32[]{:S(2)}, u32[]{:S(2)}) collective-permute-start(bf16[656,640]{1,0:T(8,128)(2,1)S(1)} %get-tuple-element.114), channel_id=1, source_target_pairs={{0,128},{1,129},{16,144},{17,145},{32,160},{33,161},{48,176},{49,1... | collective-permute-start | bytes 2519048 | tf_op jit(solution)/shard_map/ppermute | solution.py:342
  102.6 11.3 %collective-permute-start.23 = (bf16[128,640]{1,0:T(8,128)(2,1)S(1)}, bf16[128,640]{1,0:T(8,128)(2,1)S(1)}, u32[]{:S(2)}, u32[]{:S(2)}) collective-permute-start(bf16[128,640]{1,0:T(8,128)(2,1)S(1)} %get-tuple-element.115), channel_id=1, source_target_pairs={{0,0},{1,1},{64,2},{65,3},{128,4},{129,5},{192,6},{193,7},{8,8},{9... | collective-permute-start | bytes 491528 | tf_op jit(solution)/shard_map/ppermute | solution.py:338
  121.1 5.3 %collective-permute-start.24 = (bf16[176,640]{1,0:T(8,128)(2,1)S(1)}, bf16[176,640]{1,0:T(8,128)(2,1)S(1)}, u32[]{:S(2)}, u32[]{:S(2)}) collective-permute-start(bf16[176,640]{1,0:T(8,128)(2,1)S(1)} %get-tuple-element.122), channel_id=1, source_target_pairs={{0,48},{1,49},{16,0},{17,1},{32,16},{33,17},{48,32},{49,33},{64,19... | collective-permute-start | bytes 675848 | tf_op jit(solution)/shard_map/ppermute | solution.py:347
  123.5 6.3 %collective-permute-start.25 = (bf16[176,640]{1,0:T(8,128)(2,1)S(1)}, bf16[176,640]{1,0:T(8,128)(2,1)S(1)}, u32[]{:S(2)}, u32[]{:S(2)}) collective-permute-start(bf16[176,640]{1,0:T(8,128)(2,1)S(1)} %get-tuple-element.123), channel_id=1, source_target_pairs={{0,32},{1,33},{16,48},{17,49},{32,0},{33,1},{48,16},{49,17},{64,65... | collective-permute-start | bytes 675848 | tf_op jit(solution)/shard_map/ppermute | solution.py:347
  124.0 6.8 %collective-permute-start.26 = (bf16[176,640]{1,0:T(8,128)(2,1)S(1)}, bf16[176,640]{1,0:T(8,128)(2,1)S(1)}, u32[]{:S(2)}, u32[]{:S(2)}) collective-permute-start(bf16[176,640]{1,0:T(8,128)(2,1)S(1)} %get-tuple-element.124), channel_id=1, source_target_pairs={{0,16},{1,17},{16,32},{17,33},{32,48},{33,49},{48,0},{49,1},{64,19... | collective-permute-start | bytes 675848 | tf_op jit(solution)/shard_map/ppermute | solution.py:347
  131.1 14.5 %collective-permute-start.27 = (bf16[88,640]{1,0:T(8,128)(2,1)S(1)}, bf16[88,640]{1,0:T(8,128)(2,1)S(1)}, u32[]{:S(2)}, u32[]{:S(2)}) collective-permute-start(bf16[88,640]{1,0:T(8,128)(2,1)S(1)} %concatenate.27), channel_id=1, source_target_pairs={{8,0},{9,1},{72,2},{73,3},{136,4},{137,5},{200,6},{201,7},{0,8},{1... | collective-permute-start | bytes 337928 | tf_op jit(solution)/shard_map/ppermute | solution.py:354
  140.7 9.2 %collective-permute-start.28 = (bf16[88,640]{1,0:T(8,128)(2,1)S(1)}, bf16[88,640]{1,0:T(8,128)(2,1)S(1)}, u32[]{:S(2)}, u32[]{:S(2)}) collective-permute-start(bf16[88,640]{1,0:T(8,128)(2,1)S(1)} %concatenate.28), channel_id=1, source_target_pairs={{0,0},{1,1},{64,2},{65,3},{128,4},{129,5},{192,6},{193,7},{8,8},{9... | collective-permute-start | bytes 337928 | tf_op jit(solution)/shard_map/ppermute | solution.py:354
